TPU v7x, 512 devices: a whole 4x8x8 slice. The times are simulated.
512 devices in a mesh: seq: 128 (over z, y, core), chan: 4 (over x).
Axes of the slice: x: 4, y: 8, z: 8, core: 2. Of those that a mesh axis runs over, the one named last changes fastest.
Arguments:
- tokens: bfloat16 [65536, 4096], P('seq', 'chan'), may hold values from -24 to 24
- grad_out: bfloat16 [65536, 4096], P('seq', 'chan'), may hold values from -0.09375 to 0.09375
- in_weight: bfloat16 [4096, 3, 256], P('seq', None, 'chan'), may hold values from -0.09375 to 0.09375
- out_weight: bfloat16 [4096, 256], P('seq', 'chan'), may hold values from -0.09375 to 0.09375
- conv_out: bfloat16 [65536, 256], P('seq', 'chan'), may hold values from -6 to 6
- residues: float32 [16, 128], P(None, 'chan'), may hold values from -1.5 to 1.5
- decay_length: float32 [16, 128], P(None, 'chan'), may hold values from 8 to 4194304
Outputs:
- grad_in_weight: float32 [4096, 3, 256], P('seq', None, 'chan')
- grad_out_weight: float32 [4096, 256], P('seq', 'chan')
All inputs are finite; a program needn't handle non-finite values.
Results may differ from a plain program's by a relative error of at most 0.0041.
Values may be sent and summed in bfloat16 or wider, within the bound.
No kernel may reach another device: no remote copies, remote signals or barrier semaphores. Data moves between devices by JAX's collectives and lax.ppermute only.
A program may use at most 64 MiB of HBM per device.

v0:
```python
import math

import jax
import jax.numpy as jnp
from jax import lax
from jax.sharding import Mesh
from jax.sharding import PartitionSpec as P

SEQ = ("seq_0", "seq_1", "seq_2")


precise = lax.Precision.HIGHEST


def cut_along(value, dim, devices):
    dims = value.shape
    tiles = value.reshape(*dims[:dim], devices, dims[dim] // devices, *dims[dim + 1 :])
    return jnp.moveaxis(tiles, dim, 0)


def in_order(tiles, dim):
    dims = list(tiles.shape[1:])
    dims[dim] *= tiles.shape[0]
    return jnp.moveaxis(tiles, 0, dim).reshape(dims)


def moved_by_axis(tiles, axes, order):
    inside = tiles.shape[1:]
    filled = tiles.reshape(*(lax.axis_size(a) for a in axes), *inside)
    for k in order:
        filled = lax.all_to_all(filled, axes[k], k, k, tiled=True)
    return filled.reshape(-1, *inside)


def exchange_by_chip(value, groups, order, split_dim, concat_dim):
    devices = lax.axis_size(groups[0]) * lax.axis_size(groups[1])
    tiles = cut_along(value, split_dim, devices)
    return in_order(moved_by_axis(tiles, groups, order), concat_dim)


def in_one_piece(arrays, axis, dim, along):
    widths = [a.shape[along] for a in arrays]
    both = jnp.concatenate(arrays, axis=along)
    filled = lax.all_gather(both, axis, axis=dim, tiled=True)
    return tuple(jnp.split(filled, [sum(widths[:k]) for k in range(1, len(widths))], axis=along))


def sum_in_order(tiles, axes, order):
    dims = [lax.axis_size(a) for a in axes]
    tiles = tiles.reshape(*dims, *tiles.shape[1:])
    tiles = tiles.transpose(*order, *range(len(axes), tiles.ndim))
    tiles = tiles.reshape(-1, *tiles.shape[len(axes) :])
    for k in order:
        tiles = lax.psum_scatter(tiles, axes[k], scatter_dimension=0, tiled=True)
    return tiles[0]


def sum_by_axis(value, axes, order, dim):
    devices = lax.axis_size(axes)
    return sum_in_order(cut_along(value, dim, devices), axes, order)


def rotate(packed, radians):
    real_part = packed[..., 0, :]
    imag_part = packed[..., 1, :]
    cosine = jnp.cos(radians)
    sine_value = jnp.sin(radians)
    return jnp.stack(
        [real_part * cosine + imag_part * sine_value, imag_part * cosine - real_part * sine_value],
        axis=-2,
    )


def angle_tables(height, breadth, period):
    row_index = jnp.arange(height, dtype=jnp.int32)
    col_index = jnp.arange(breadth, dtype=jnp.int32)
    product = row_index[:, None] * col_index[None, :] % period
    radians = product.astype(jnp.float32) * (2.0 * math.pi / period)
    return (jnp.cos(radians), jnp.sin(radians))


def transform(formula, packed, cosine, sine_table, direction):
    along_cos = jnp.einsum(formula, cosine, packed, precision=precise)
    along_sin = jnp.einsum(formula, sine_table, packed, precision=precise)
    real_part = along_cos[..., 0, :] + direction * along_sin[..., 1, :]
    imag_part = along_cos[..., 1, :] - direction * along_sin[..., 0, :]
    return jnp.stack([real_part, imag_part], axis=-2)


def filter_spectrum(residues, decay_length, low_freq, local_rows, devices_seq):
    period = 2 * local_rows * devices_seq
    sequence = local_rows * devices_seq
    frequency = (
        low_freq[:, None] + 2 * devices_seq * jnp.arange(local_rows, dtype=jnp.int32)[None, :]
    )
    signed_freq = jnp.where(frequency > period // 2, frequency - period, frequency)
    phase_angle = signed_freq.astype(jnp.float32) * (2.0 * math.pi / period)
    parity = 1.0 - 2.0 * (low_freq % 2).astype(jnp.float32)
    inverse_len = 1.0 / decay_length
    decay_rate = jnp.exp(-inverse_len)
    weight = residues * jnp.sqrt(-jnp.expm1(-2.0 * inverse_len))
    remnant = jnp.exp(-inverse_len * sequence)
    half_sine = jnp.sin(0.5 * phase_angle)[None, :, :, None]
    full_sine = jnp.sin(phase_angle)[None, :, :, None]
    real_den = (
        -jnp.expm1(-inverse_len)[:, None, None, :]
        + 2.0 * decay_rate[:, None, None, :] * half_sine * half_sine
    )
    imag_den = decay_rate[:, None, None, :] * full_sine
    numerator = weight[:, None, None, :] * (
        1.0 - remnant[:, None, None, :] * parity[None, :, None, None]
    )
    factor = numerator / (real_den * real_den + imag_den * imag_den)
    return (jnp.sum(factor * real_den, axis=0), jnp.sum(factor * imag_den, axis=0))


def correlate(signal, residues, decay_length):
    local_rows, channels = signal.shape
    devices_seq = lax.axis_size(SEQ)
    position = lax.axis_index(SEQ)
    period = 2 * local_rows * devices_seq
    paired = channels // 2
    packed = signal.reshape(local_rows, paired, 2).transpose(0, 2, 1)
    spread = lax.all_to_all(packed, SEQ, split_axis=0, concat_axis=0, tiled=True)
    spread = spread.reshape(devices_seq, local_rows // devices_seq, 2, paired)
    cosine, sine_table = angle_tables(2 * devices_seq, devices_seq, 2 * devices_seq)
    mixed = transform("kp,pmrf->kmrf", spread, cosine, sine_table, 1.0)
    spectral = lax.all_to_all(mixed, SEQ, split_axis=0, concat_axis=1, tiled=True)
    low_freq = 2 * position
    low_freq = low_freq + jnp.arange(2, dtype=jnp.int32)
    offsets = jnp.arange(local_rows, dtype=jnp.int32)
    twiddles = (low_freq[:, None] * offsets[None, :] % period).astype(jnp.float32) * (
        2.0 * math.pi / period
    )
    twiddles = twiddles[:, :, None]
    cosine, sine_table = angle_tables(local_rows, local_rows, local_rows)
    spectrum = transform("km,emrf->ekrf", rotate(spectral, twiddles), cosine, sine_table, 1.0)
    resp_real, resp_imag = filter_spectrum(
        residues, decay_length, low_freq, local_rows, devices_seq
    )
    spec_real = spectrum[:, :, 0, :]
    spec_imag = spectrum[:, :, 1, :]
    weighted = jnp.stack(
        [
            spec_real * resp_real - spec_imag * resp_imag,
            spec_real * resp_imag + spec_imag * resp_real,
        ],
        axis=2,
    )
    returned = rotate(transform("km,emrf->ekrf", weighted, cosine, sine_table, -1.0), -twiddles)
    collected = lax.all_to_all(returned, SEQ, split_axis=1, concat_axis=0, tiled=True)
    cosine, sine_table = angle_tables(devices_seq, 2 * devices_seq, 2 * devices_seq)
    folded = transform("pk,kmrf->pmrf", collected, cosine, sine_table, -1.0)
    result = exchange_by_chip(folded, (("seq_0", "seq_1"), "seq_2"), (1, 0), 0, 1)[0]
    result = result * (1.0 / period)
    return result.transpose(0, 2, 1).reshape(local_rows, channels)


def local(tokens, grad_out, in_weight, out_weight, conv_out, residues, decay_length):
    local_rows = tokens.shape[0]
    channels = out_weight.shape[1]
    owned_rows = in_weight.shape[0]
    full_tokens, full_grads = in_one_piece((tokens, grad_out), "chan", 1, 0)
    pieces = (
        lax.all_gather(in_weight, SEQ, axis=0, tiled=True),
        lax.all_gather(out_weight, SEQ, axis=0, tiled=True),
    )
    piece_rows = pieces[0].shape[0]
    token_cols = full_tokens
    grad_cols = full_grads
    projected = jnp.dot(
        token_cols, pieces[0].reshape(piece_rows, 3 * channels), preferred_element_type=jnp.float32
    )
    upstream = jnp.dot(grad_cols, pieces[1], preferred_element_type=jnp.float32)
    projected, upstream = (projected, upstream)
    streams = projected.astype(jnp.bfloat16).reshape(local_rows, 3, channels)
    gate_first = streams[:, 0].astype(jnp.float32)
    gate_second = streams[:, 1].astype(jnp.float32)
    value_stream = streams[:, 2].astype(jnp.float32)
    conv_value = conv_out.astype(jnp.float32)
    gated = (gate_second * conv_value).astype(jnp.bfloat16)
    grad_second = (upstream * conv_value).astype(jnp.bfloat16)
    grad_conv = upstream * gate_second
    grad_source = correlate(grad_conv, residues, decay_length)
    grad_first = (grad_source * value_stream).astype(jnp.bfloat16)
    grad_value = (grad_source * gate_first).astype(jnp.bfloat16)
    grad_streams = jnp.stack([grad_first, grad_second, grad_value], axis=1).reshape(
        local_rows, 3 * channels
    )
    token_cols = full_tokens
    grad_cols = full_grads
    inward = lax.dot_general(
        token_cols, grad_streams, (((0,), (0,)), ((), ())), preferred_element_type=jnp.float32
    )
    outward = lax.dot_general(
        grad_cols, gated, (((0,), (0,)), ((), ())), preferred_element_type=jnp.float32
    )
    owned = sum_by_axis(jnp.concatenate([inward, outward], axis=1), SEQ, (2, 0, 1), 0)
    grad_in = owned[:, : 3 * channels].reshape(owned_rows, 3, channels)
    grad_proj = owned[:, 3 * channels :]
    return (grad_in, grad_proj)


def solution(mesh):
    finer = Mesh(
        mesh.devices.reshape(8, 8, 2, mesh.shape["chan"]), ("seq_0", "seq_1", "seq_2", "chan")
    )
    in_specs = (
        P(SEQ, "chan"),
        P(SEQ, "chan"),
        P(SEQ, None, "chan"),
        P(SEQ, "chan"),
        P(SEQ, "chan"),
        P(None, "chan"),
        P(None, "chan"),
    )
    out_specs = (P(SEQ, None, "chan"), P(SEQ, "chan"))
    return jax.shard_map(local, mesh=finer, in_specs=in_specs, out_specs=out_specs, check_vma=False)
```

profile of v0, /device:TPU:6, one launch (start us, length us, event | category | flops | bytes accessed | tf_op | source)
XLA Modules:
  0.0 453.4 jit_solution(13654914969769010621)
XLA Ops:
  8.0 3.1 pad_maximum_fusion.1
  11.2 57.9 %all_gather.10 = bf16[4096,64]{1,0:T(8,128)(2,1)S(1)} all-gather(bf16[32,64]{1,0:T(8,128)(2,1)S(1)} %copy-done.2), channel_id=1, replica_groups=mesh['seq_0'=8,'seq_1'=8,'seq_2'=2,'chan'=4] {'seq_0','seq_1','seq_2'}, dimensions={0}, use_global_device_ids=true | all-gather | bytes 528384 | tf_op jit(solution)/shard_map/all_gather | solution.py:166
  69.1 29.6 %all-gather.5.cloned.1.call-done = bf16[4096,3,64]{2,0,1:T(8,128)(2,1)} async-done(((bf16[32,3,64]{2,0,1:T(8,128)(2,1)}), bf16[4096,3,64]{2,0,1:T(8,128)(2,1)}) %all-gather.5.cloned.1.call-update) | async-done | bytes 1572880 | tf_op jit(solution)/shard_map/all_gather | solution.py:165
  98.7 3.1 copy.98
  101.8 82.0 %all-gather.3.cloned.1.call-done = bf16[1024,4096]{1,0:T(8,128)(2,1)} async-done(((bf16[1024,1024]{1,0:T(8,128)(2,1)}), bf16[1024,4096]{1,0:T(8,128)(2,1)}) %all-gather.3.cloned.1.call-update) | async-done | bytes 8388624 | tf_op jit(solution)/shard_map/all_gather | solution.py:44
  183.8 3.9 fusion.11
  191.4 15.3 %all-to-all-start = ((f32[128,1,256]{2,1,0:T(1,128)}), f32[128,1,256]{2,1,0:T(1,128)S(1)}, u32[]{:S(2)}, u32[]{:S(2)}) async-start(f32[128,1,256]{2,1,0:T(1,128)} %reshape.271), calls=%async_computation | async-start | bytes 262144 | tf_op jit(solution)/shard_map/all_to_all | solution.py:124
  206.8 12.1 %all-to-all-done = f32[128,1,256]{2,1,0:T(1,128)S(1)} async-done(((f32[128,1,256]{2,1,0:T(1,128)}), f32[128,1,256]{2,1,0:T(1,128)S(1)}, u32[]{:S(2)}, u32[]{:S(2)}) %all-to-all-start) | async-done | bytes 131104 | tf_op jit(solution)/shard_map/all_to_all | solution.py:124
  225.4 6.2 %all-to-all-start.1 = ((f32[128,1,512]{2,1,0:T(1,128)}), f32[128,1,512]{2,1,0:T(1,128)S(1)}, u32[]{:S(2)}, u32[]{:S(2)}) async-start(f32[128,1,512]{2,1,0:T(1,128)} %reshape.273), calls=%async_computation.1 | async-start | bytes 524288 | tf_op jit(solution)/shard_map/all_to_all | solution.py:128
  233.5 12.8 %all-to-all-done.1 = f32[128,1,512]{2,1,0:T(1,128)S(1)} async-done(((f32[128,1,512]{2,1,0:T(1,128)}), f32[128,1,512]{2,1,0:T(1,128)S(1)}, u32[]{:S(2)}, u32[]{:S(2)}) %all-to-all-start.1) | async-done | bytes 262176 | tf_op jit(solution)/shard_map/all_to_all | solution.py:128
  249.8 4.9 %convolution_bitcast_fusion.3 = f32[2,512,2,32]{1,3,2,0:T(8,128)S(1)} fusion(f32[2,512,1,32]{1,3,2,0:T(8,128)S(1)} %get-tuple-element.25, f32[2,512,1,32]{1,3,2,0:T(8,128)S(1)} %get-tuple-element.24), kind=kOutput, calls=%fused_computation.24 | convolution fusion | flops 406388736 | bytes 524288 | tf_op jit(solution)/shard_map/km,emrf->ekrf/dot_general | solution.py:83
  254.8 5.1 %convolution_bitcast_fusion.2 = f32[2,512,2,32]{1,3,2,0:T(8,128)S(1)} fusion(f32[2,512,1,32]{1,3,2,0:T(8,128)S(1)} %get-tuple-element.25, f32[2,512,1,32]{1,3,2,0:T(8,128)S(1)} %get-tuple-element.24), kind=kOutput, calls=%fused_computation.23 | convolution fusion | flops 406388736 | bytes 524288 | tf_op jit(solution)/shard_map/km,emrf->ekrf/dot_general | solution.py:84
  260.0 4.9 %convolution_bitcast_fusion.1 = f32[2,512,2,32]{1,3,2,0:T(8,128)S(1)} fusion(f32[2,512,1,32]{1,3,2,0:T(8,128)S(1)} %get-tuple-element.17, f32[2,512,1,32]{1,3,2,0:T(8,128)S(1)} %get-tuple-element.16), kind=kOutput, calls=%fused_computation.22 | convolution fusion | flops 406388736 | bytes 524288 | tf_op jit(solution)/shard_map/km,emrf->ekrf/dot_general | solution.py:83
  264.9 4.9 %convolution_bitcast_fusion = f32[2,512,2,32]{1,3,2,0:T(8,128)S(1)} fusion(f32[2,512,1,32]{1,3,2,0:T(8,128)S(1)} %get-tuple-element.17, f32[2,512,1,32]{1,3,2,0:T(8,128)S(1)} %get-tuple-element.16), kind=kOutput, calls=%fused_computation.21 | convolution fusion | flops 406388736 | bytes 524288 | tf_op jit(solution)/shard_map/km,emrf->ekrf/dot_general | solution.py:84
  271.7 20.7 %all_to_all.51 = f32[128,1,512]{2,1,0:T(1,128)S(1)} all-to-all(f32[128,1,512]{2,1,0:T(1,128)S(1)} %reshape.275), channel_id=1, replica_groups=mesh['seq_0'=8,'seq_1'=8,'seq_2'=2,'chan'=4] {'seq_0','seq_1','seq_2'}, dimensions={0} | all-to-all | bytes 524288 | tf_op jit(solution)/shard_map/all_to_all | solution.py:151
  298.5 3.8 all_to_all.52
  305.1 4.6 %all-to-all-start.4 = ((f32[64,1,512]{2,1,0:T(1,128)}), f32[64,1,512]{2,1,0:T(1,128)S(1)}, u32[]{:S(2)}, u32[]{:S(2)}) async-start(f32[64,1,512]{2,1,0:T(1,128)} %reshape.279), calls=%async_computation.4 | async-start | bytes 262144 | tf_op jit(solution)/shard_map/all_to_all | solution.py:31
  313.0 9.9 %all-to-all-done.4 = f32[64,1,512]{2,1,0:T(1,128)S(1)} async-done(((f32[64,1,512]{2,1,0:T(1,128)}), f32[64,1,512]{2,1,0:T(1,128)S(1)}, u32[]{:S(2)}, u32[]{:S(2)}) %all-to-all-start.4) | async-done | bytes 131104 | tf_op jit(solution)/shard_map/all_to_all | solution.py:31
  325.4 3.2 fusion
  330.8 5.6 %copy.120 = f32[4096,256]{1,0:T(8,128)} copy(f32[4096,256]{0,1:T(8,128)} %pad_maximum_fusion) | data formatting | bytes 8388608 | tf_op jit(solution)/shard_map/concatenate | solution.py:198
  336.5 4.8 %copy.121 = f32[2,8,8,32,256]{4,3,2,1,0:T(8,128)} copy(f32[2,8,8,32,256]{4,3,0,2,1:T(8,128)} %bitcast.96) | data formatting | bytes 8388608 | tf_op jit(solution)/shard_map/transpose | solution.py:51
  341.3 12.6 %reduce-scatter.4.cloned.1.call-done = f32[64,32,256]{2,1,0:T(8,128)} async-done(((f32[128,32,256]{2,1,0:T(8,128)}), f32[64,32,256]{2,1,0:T(8,128)}) %reduce-scatter.4.cloned.1.call-update) | async-done | bytes 2097168 | tf_op jit(solution)/shard_map/reduce_scatter | solution.py:54
  354.0 50.0 %reduce-scatter.6.cloned.1.call-done = f32[8,32,256]{2,1,0:T(8,128)} async-done(((f32[64,32,256]{2,1,0:T(8,128)}), f32[8,32,256]{2,1,0:T(8,128)}) %reduce-scatter.6.cloned.1.call-update) | async-done | bytes 262160 | tf_op jit(solution)/shard_map/reduce_scatter | solution.py:54
  404.0 39.9 %reduce-scatter.8.cloned.1.call-done = f32[1,32,256]{2,1,0:T(8,128)} async-done(((f32[8,32,256]{2,1,0:T(8,128)}), f32[1,32,256]{2,1,0:T(8,128)}) %reduce-scatter.8.cloned.1.call-update) | async-done | bytes 32784 | tf_op jit(solution)/shard_map/reduce_scatter | solution.py:54
  (86 shorter events, 38.1 us)
Async XLA Ops:
  7.2 91.6 %all-gather.5.cloned.1.call-start = ((), (), s32[]{:S(2)}) async-start(), calls=%async_computation.9 | async-start | bytes 3170304 | tf_op jit(solution)/shard_map/all_gather | solution.py:165
  7.9 3.3 copy-start.2
  7.9 61.1 %copy-start.3 = (f32[16,32]{1,0:T(8,128)S(1)}, f32[16,32]{1,0:T(8,128)}, u32[]{:S(2)}) copy-start(f32[16,32]{1,0:T(8,128)} %param.12) | copy-start | bytes 6148
  7.9 61.1 %copy-start.4 = (f32[16,32]{1,0:T(8,128)S(1)}, f32[16,32]{1,0:T(8,128)}, u32[]{:S(2)}) copy-start(f32[16,32]{1,0:T(8,128)} %param.13) | copy-start | bytes 6148
  7.9 175.9 %all-gather.3.cloned.1.call-start = ((), (), s32[]{:S(2)}) async-start(), calls=%async_computation.8 | async-start | bytes 10485760 | tf_op jit(solution)/shard_map/all_gather | solution.py:44
  183.8 4.6 %copy-start = (bf16[1024,4096]{1,0:T(8,128)(2,1)S(1)}, bf16[1024,4096]{1,0:T(8,128)(2,1)}, u32[]{:S(2)}) copy-start(bf16[1024,4096]{1,0:T(8,128)(2,1)} %all-gather.3.cloned.1.call-done) | copy-start | bytes 25165828
  183.8 4.6 %copy-start.1 = (bf16[512,64]{0,1:T(8,128)(2,1)S(1)}, bf16[512,64]{0,1:T(8,128)(2,1)}, u32[]{:S(2)}) copy-start(bf16[512,64]{0,1:T(8,128)(2,1)} %param.11) | copy-start | bytes 196612
  191.4 27.5 %all-to-all-start = ((f32[128,1,256]{2,1,0:T(1,128)}), f32[128,1,256]{2,1,0:T(1,128)S(1)}, u32[]{:S(2)}, u32[]{:S(2)}) async-start(f32[128,1,256]{2,1,0:T(1,128)} %reshape.271), calls=%async_computation | async-start | bytes 262144 | tf_op jit(solution)/shard_map/all_to_all | solution.py:124
  225.4 20.9 %all-to-all-start.1 = ((f32[128,1,512]{2,1,0:T(1,128)}), f32[128,1,512]{2,1,0:T(1,128)S(1)}, u32[]{:S(2)}, u32[]{:S(2)}) async-start(f32[128,1,512]{2,1,0:T(1,128)} %reshape.273), calls=%async_computation.1 | async-start | bytes 524288 | tf_op jit(solution)/shard_map/all_to_all | solution.py:128
  305.1 17.8 %all-to-all-start.4 = ((f32[64,1,512]{2,1,0:T(1,128)}), f32[64,1,512]{2,1,0:T(1,128)S(1)}, u32[]{:S(2)}, u32[]{:S(2)}) async-start(f32[64,1,512]{2,1,0:T(1,128)} %reshape.279), calls=%async_computation.4 | async-start | bytes 262144 | tf_op jit(solution)/shard_map/all_to_all | solution.py:31
  309.8 44.1 %reduce-scatter.4.cloned.1.call-start = ((), (), s32[]{:S(2)}) async-start(), calls=%async_computation.10 | async-start | bytes 6291456 | tf_op jit(solution)/shard_map/reduce_scatter | solution.py:54
  341.2 62.7 %reduce-scatter.6.cloned.1.call-start = ((), (), s32[]{:S(2)}) async-start(), calls=%async_computation.11 | async-start | bytes 2359296 | tf_op jit(solution)/shard_map/reduce_scatter | solution.py:54
  353.9 89.9 %reduce-scatter.8.cloned.1.call-start = ((), (), s32[]{:S(2)}) async-start(), calls=%async_computation.12 | async-start | bytes 294912 | tf_op jit(solution)/shard_map/reduce_scatter | solution.py:54
Sparse Core Ops, SparseCore 0:
  11.1 87.6 all-gather.4
  100.8 82.9 all-gather.2
  341.4 12.4 reduce-scatter.3
  356.8 47.0 reduce-scatter.5
  406.8 36.9 reduce-scatter.7
where the time goes:
time: 461 us; the launch traced here: 453 us
  waiting for transfers between devices  250 us (54%)
  blocking collectives  82.4 us (18%)
  matrix products  34.9 us (8%)
  local copies, waits for them, and re-layouts  32.2 us (7%)
  starting transfers between devices  26.4 us (6%)
  between operations  14.4 us (3%)
  other arithmetic  13.5 us (3%)
    reduce_scatter x3, waiting for transfers between devices, sum_in_order(): tiles = lax.psum_scatter(tiles, axes[k], scatter_dimension=0, tiled=True)  102 us
    all_gather x1, waiting for transfers between devices, in_one_piece(): filled = lax.all_gather(both, axis, axis=dim, tiled=True)  82 us
    all_gather x1, blocking collectives, local(): lax.all_gather(out_weight, SEQ, axis=0, tiled=True)  57.9 us
    all_gather x1, waiting for transfers between devices, local(): lax.all_gather(in_weight, SEQ, axis=0, tiled=True)  29.6 us
    all_to_all x1, blocking collectives, correlate(): lax.all_to_all(returned, SEQ, split_axis=1, concat_axis=0, tiled=True)  20.7 us
    all_to_all x1, starting transfers between devices, correlate(): lax.all_to_all(packed, SEQ, split_axis=0, concat_axis=0, tiled=True)  15.3 us
    all_to_all x1, waiting for transfers between devices, correlate(): lax.all_to_all(mixed, SEQ, split_axis=0, concat_axis=1, tiled=True)  12.8 us
    all_to_all x1, waiting for transfers between devices, correlate(): lax.all_to_all(packed, SEQ, split_axis=0, concat_axis=0, tiled=True)  12.1 us
  transfers between devices with their start and end apart: 8, of which 8 were waited for; matrix products, arithmetic and copies ran while one was open for 2% of the time, Pallas kernels for 0%

commit v1 on v0

v1 whole, which is shorter than its diff:
```python
import jax
import jax.numpy as jnp
from jax import lax
from jax.experimental import pallas as pl
from jax.experimental.pallas import tpu as pltpu
from jax.sharding import Mesh
from jax.sharding import PartitionSpec as P

SEQ = ("seq_0", "seq_1", "seq_2")
CHIPS = ("seq_0", "seq_1")
STEPS = 64
MODE_ROWS = 4
GROUPS = 4
F32 = jnp.float32
BF16 = jnp.bfloat16
VMEM = 48 * 1024 * 1024


def call(body, out_shape, scratch=(), flops=0, moved=0):
    return pl.pallas_call(
        body,
        out_shape=out_shape,
        scratch_shapes=list(scratch),
        compiler_params=pltpu.CompilerParams(vmem_limit_bytes=VMEM),
        cost_estimate=pl.CostEstimate(flops=flops, bytes_accessed=moved, transcendentals=0),
    )


def lane_group(shape):
    lane = lax.broadcasted_iota(jnp.int32, shape, len(shape) - 1)
    return lane // 32


def turn(x, by):
    return pltpu.roll(x, by, x.ndim - 1)


def transpose_body(a_ref, b_ref, out_ref):
    half = a_ref.shape[0]
    out_ref[:, :half] = a_ref[...].T
    out_ref[:, half:] = b_ref[...].T


def project_body(own_t, other_t, own_g, other_g, w_ref, out_ref):
    half = own_t.shape[0]
    for at, (t_ref, g_ref) in enumerate(((own_t, own_g), (other_t, other_g))):
        for c in range(0, w_ref.shape[0], 2):
            w = jnp.concatenate([w_ref[c], w_ref[c + 1]], axis=1)
            from_t = jnp.dot(t_ref[...], w, preferred_element_type=F32)
            from_g = jnp.dot(g_ref[...], w, preferred_element_type=F32)
            both = jnp.where(lane_group(from_t.shape) % GROUPS < 3, from_t, from_g)
            out_ref[c, at * half : (at + 1) * half] = both[:, :128]
            out_ref[c + 1, at * half : (at + 1) * half] = both[:, 128:]


def signal_of(x):
    product = x * turn(x, 64)
    return jnp.where(lane_group(x.shape) % 2 == 1, product, turn(product, 32))


def chunk_rows(core, q_half, step, rows):
    half = rows // 2
    start = half * core if q_half == 0 else half * (1 - core)
    return pl.ds(start + step, half // STEPS, stride=STEPS)


def first_body(core_ref, part_ref, decay_ref, far_ref, x_ref, left_ref, state_ref, sig, st):
    core = core_ref[0]
    rows = x_ref.shape[0]
    total = part_ref[0]
    for k in range(1, part_ref.shape[0]):
        total = total + part_ref[k]
    rounded = total.astype(BF16).astype(F32)
    x = jnp.where(lane_group(total.shape) < 3, rounded, total)
    x_ref[...] = x
    sig[...] = signal_of(x)
    decay = [decay_ref[m : m + 1, :] for m in range(MODE_ROWS)]
    chunks = rows // STEPS
    per = chunks // 2

    def step(i, held):
        t = STEPS - 1 - i
        g = [sig[chunk_rows(core, h, t, rows), :] for h in range(2)]
        return tuple(
            decay[m] * held[2 * m + h] + g[h] for m in range(MODE_ROWS) for h in range(2)
        )

    zero = jnp.zeros((per, 128), F32)
    held = lax.fori_loop(0, STEPS, step, (zero,) * (2 * MODE_ROWS), unroll=8)
    for m in range(MODE_ROWS):
        for h in range(2):
            st[m * chunks + h * per : m * chunks + (h + 1) * per, :] = held[2 * m + h]
    far = far_ref[...]
    acc = jnp.zeros((MODE_ROWS, 128), F32)
    for q in reversed(range(chunks)):
        where = pl.ds(q, MODE_ROWS, stride=chunks)
        left_ref[where, :] = acc
        acc = st[where, :] + far * acc
    state_ref[...] = jnp.broadcast_to(acc[None], state_ref.shape)


def second_body(
    core_ref, x_ref, left_ref, states_ref, reach_ref, power_ref, decay_ref, weight_ref, conv_ref,
    out_ref, sig, ys,
):
    core = core_ref[0]
    rows = x_ref.shape[0]
    chunks = rows // STEPS
    per = chunks // 2
    sig[...] = signal_of(x_ref[...])
    carry = jnp.sum(states_ref[...] * reach_ref[...], axis=0)
    decay = [decay_ref[m : m + 1, :] for m in range(MODE_ROWS)]
    weight = [weight_ref[m : m + 1, :] for m in range(MODE_ROWS)]
    begin = []
    for m in range(MODE_ROWS):
        here = slice(m * chunks, (m + 1) * chunks)
        c = left_ref[here, :] + power_ref[here, :] * carry[m : m + 1, :]
        begin += [c[:per], c[per:]]

    def step(i, held):
        t = STEPS - 1 - i
        new = []
        for h in range(2):
            g = sig[chunk_rows(core, h, t, rows), :]
            states = [decay[m] * held[2 * m + h] + g for m in range(MODE_ROWS)]
            y = weight[0] * states[0]
            for m in range(1, MODE_ROWS):
                y = y + weight[m] * states[m]
            ys[chunk_rows(core, h, t, rows), :] = y
            new.append(states)
        return tuple(new[h][m] for m in range(MODE_ROWS) for h in range(2))

    lax.fori_loop(0, STEPS, step, tuple(begin), unroll=8)
    y = ys[...]
    y = y + turn(y, 64)
    y = y + turn(y, 32)
    factor = jnp.where(lane_group(y.shape) % 2 == 0, y, conv_ref[...].astype(F32))
    out = (turn(x_ref[...], 64) * factor).astype(BF16)
    for k in range(out_ref.shape[0]):
        out_ref[k] = out


def weigh_body(tt_ref, gt_ref, grads_ref, out_ref):
    depth = tt_ref.shape[0]
    block = 512
    for r in range(0, depth, block):
        for c in range(0, grads_ref.shape[0], 2):
            g = jnp.concatenate([grads_ref[c], grads_ref[c + 1]], axis=1)
            from_t = jnp.dot(tt_ref[r : r + block, :], g, preferred_element_type=F32)
            from_g = jnp.dot(gt_ref[r : r + block, :], g, preferred_element_type=F32)
            both = jnp.where(lane_group(from_t.shape) % GROUPS < 3, from_t, from_g).astype(BF16)
            out_ref[c, r : r + block] = both[:, :128]
            out_ref[c + 1, r : r + block] = both[:, 128:]


def by_lanes(table):
    wide = jnp.repeat(table, 2, axis=1)
    channels = wide.shape[1]
    return wide.reshape(GROUPS, MODE_ROWS, channels).transpose(1, 0, 2).reshape(MODE_ROWS, -1)


def local(tokens, grad_out, in_weight, out_weight, conv_out, residues, decay_length):
    half = tokens.shape[0]
    depth = tokens.shape[1]
    rows = 2 * half
    owned = in_weight.shape[0]
    channels = out_weight.shape[1]
    mine = channels // 2
    size_z, size_y, size_x = (lax.axis_size(a) for a in ("seq_0", "seq_1", "chan"))
    chips = size_z * size_y
    fold = size_z // size_x
    core = lax.axis_index("seq_2")
    place = lax.axis_index(CHIPS)

    def transposed(value, swap):
        pairs = []
        for z in range(size_z):
            for k in range(2):
                for x in range(size_x):
                    c, l = z // fold, z % fold
                    source = (z * 2 + k) * size_x + x
                    target = ((fold * x + l) * 2 + (1 - k if swap else k)) * size_x + c
                    pairs.append((source, target))
        return lax.ppermute(value, ("seq_0", "seq_2", "chan"), pairs)

    def swapped(value):
        return lax.ppermute(value, "seq_2", [(0, 1), (1, 0)])

    packed = jnp.concatenate([in_weight, out_weight[:, None, :]], axis=1)
    packed = packed.reshape(owned, GROUPS, 2, mine).transpose(2, 0, 1, 3).reshape(2, owned, 128)
    kept, given = (
        jnp.where(core == 0, packed[0], packed[1]),
        jnp.where(core == 0, packed[1], packed[0]),
    )
    kept = transposed(kept, False)
    given = transposed(given, True)
    low = jnp.where(core == 0, kept, given)
    high = jnp.where(core == 0, given, kept)
    piece = jnp.concatenate([low, high], axis=0)
    piece = jnp.broadcast_to(piece[None], (chips, 2 * owned, 128))
    weights = lax.all_to_all(piece, CHIPS, 0, 0, tiled=True).reshape(size_x, depth, 128)

    tokens_too = swapped(tokens)
    grads_too = swapped(grad_out)
    conv_own = jnp.where(core == 0, conv_out[:, :mine], conv_out[:, mine:])
    conv_sent = jnp.where(core == 0, conv_out[:, mine:], conv_out[:, :mine])
    conv = jnp.concatenate([conv_own, swapped(conv_sent)], axis=0)
    conv = jnp.tile(conv, (1, GROUPS))
    flip = call(
        transpose_body, jax.ShapeDtypeStruct((depth, rows), BF16), moved=4 * depth * rows
    )
    tokens_t = flip(tokens, tokens_too)
    grads_t = flip(grad_out, grads_too)

    pick = residues.shape[1] // 2
    res = jnp.where(core == 0, residues[:, :pick], residues[:, pick:])
    length = jnp.where(core == 0, decay_length[:, :pick], decay_length[:, pick:])
    rate_raw = 1.0 / length
    weight = by_lanes(res * jnp.sqrt(-jnp.expm1(-2.0 * rate_raw)))
    rate = by_lanes(rate_raw)
    decay = jnp.exp(-rate)
    far = jnp.exp(-float(STEPS) * rate)
    chunks = rows // STEPS
    left_of = (chunks - 1 - jnp.arange(chunks)).astype(F32) * float(STEPS)
    power = jnp.exp(-left_of[None, :, None] * rate[:, None, :]).reshape(-1, 128)
    ahead = jnp.arange(chips) - place - 1
    reach = jnp.where(
        (ahead >= 0)[:, None, None],
        jnp.exp(-(jnp.maximum(ahead, 0) * rows).astype(F32)[:, None, None] * rate[None]),
        0.0,
    )
    core_at = core.astype(jnp.int32).reshape(1)

    project = call(
        project_body,
        jax.ShapeDtypeStruct((size_x, rows, 128), F32),
        flops=4 * rows * depth * size_x * 128,
        moved=8 * rows * depth,
    )
    parts = project(tokens, tokens_too, grad_out, grads_too, weights)
    parts = lax.all_to_all(parts, "chan", 0, 0, tiled=True)

    smem = pl.BlockSpec(memory_space=pltpu.SMEM)
    full = pl.BlockSpec(memory_space=pltpu.VMEM)
    x, left, state = pl.pallas_call(
        first_body,
        out_shape=(
            jax.ShapeDtypeStruct((rows, 128), F32),
            jax.ShapeDtypeStruct((MODE_ROWS * chunks, 128), F32),
            jax.ShapeDtypeStruct((chips, MODE_ROWS, 128), F32),
        ),
        in_specs=[smem, full, full, full],
        out_specs=(full, full, full),
        scratch_shapes=[pltpu.VMEM((rows, 128), F32), pltpu.VMEM((MODE_ROWS * chunks, 128), F32)],
        compiler_params=pltpu.CompilerParams(vmem_limit_bytes=VMEM),
    )(core_at, parts, decay, far)
    states = lax.all_to_all(state, CHIPS, 0, 0, tiled=True)
    grads = pl.pallas_call(
        second_body,
        out_shape=jax.ShapeDtypeStruct((size_x, rows, 128), BF16),
        in_specs=[smem] + [full] * 8,
        out_specs=full,
        scratch_shapes=[pltpu.VMEM((rows, 128), F32), pltpu.VMEM((rows, 128), F32)],
        compiler_params=pltpu.CompilerParams(vmem_limit_bytes=VMEM),
    )(core_at, x, left, states, reach, power, decay, weight, conv)
    grads = lax.all_to_all(grads, "chan", 0, 0, tiled=True)

    weigh = call(
        weigh_body,
        jax.ShapeDtypeStruct((size_x, depth, 128), BF16),
        flops=4 * rows * depth * size_x * 128,
        moved=8 * rows * depth,
    )
    partial = weigh(tokens_t, grads_t, grads).reshape(chips, 2 * owned, 128)
    partial = lax.all_to_all(partial, CHIPS, 0, 0, tiled=True)
    total = jnp.sum(partial.astype(F32), axis=0)
    kept = transposed(jnp.where(core == 0, total[:owned], total[owned:]), False)
    given = transposed(jnp.where(core == 0, total[owned:], total[:owned]), True)
    low = jnp.where(core == 0, kept, given)
    high = jnp.where(core == 0, given, kept)
    result = jnp.stack([low, high]).reshape(2, owned, GROUPS, mine)
    result = result.transpose(1, 2, 0, 3).reshape(owned, GROUPS, channels)
    return (result[:, :3], result[:, 3])


def solution(mesh):
    finer = Mesh(
        mesh.devices.reshape(8, 8, 2, mesh.shape["chan"]), ("seq_0", "seq_1", "seq_2", "chan")
    )
    in_specs = (
        P(SEQ, "chan"),
        P(SEQ, "chan"),
        P(SEQ, None, "chan"),
        P(SEQ, "chan"),
        P(SEQ, "chan"),
        P(None, "chan"),
        P(None, "chan"),
    )
    out_specs = (P(SEQ, None, "chan"), P(SEQ, "chan"))
    return jax.shard_map(local, mesh=finer, in_specs=in_specs, out_specs=out_specs, check_vma=False)
```

time: 461 us -> 194 us (0.42)
  the two profiles are of different devices: /device:TPU:6 before, /device:TPU:4 now
where the time goes in v1:
time: 194 us; the launch traced here: 193 us
  waiting for transfers between devices  74.8 us (39%)
  starting transfers between devices  59.2 us (31%)
  blocking collectives  29.6 us (15%)
  local copies, waits for them, and re-layouts  15 us (8%)
  Pallas kernels  13.1 us (7%)
    all_to_all x1, blocking collectives, local(): partial = lax.all_to_all(partial, CHIPS, 0, 0, tiled=True)  29.6 us
    all_to_all x1, waiting for transfers between devices, local(): lax.all_to_all(piece, CHIPS, 0, 0, tiled=True).reshape(size_x, depth, 128)  21.9 us
    ppermute x4, starting transfers between devices, transposed(): return lax.ppermute(value, ('seq_0', 'seq_2', 'chan'), pairs)  21.9 us
    ppermute x4, waiting for transfers between devices, transposed(): return lax.ppermute(value, ('seq_0', 'seq_2', 'chan'), pairs)  18.8 us
    all_to_all x1, waiting for transfers between devices, local(): parts = lax.all_to_all(parts, 'chan', 0, 0, tiled=True)  17.9 us
    all_to_all x1, waiting for transfers between devices, local(): states = lax.all_to_all(state, CHIPS, 0, 0, tiled=True)  11.7 us
    unnamed x28, local copies, waits for them, and re-layouts  9.11 us
    all_to_all x1, starting transfers between devices, local(): lax.all_to_all(piece, CHIPS, 0, 0, tiled=True).reshape(size_x, depth, 128)  9.02 us
  transfers between devices with their start and end apart: 11, of which 9 were waited for; matrix products, arithmetic and copies ran while one was open for 1% of the time, Pallas kernels for 2%

profile of v1, /device:TPU:4, one launch (start us, length us, event | category | flops | bytes accessed | tf_op | source)
XLA Modules:
  0.0 193.5 jit_solution(3002999474156251760)
XLA Ops:
  2.7 10.8 %collective-permute-start.2 = (bf16[32,128]{1,0:T(8,128)(2,1)S(1)}, bf16[32,128]{1,0:T(8,128)(2,1)S(1)}, u32[]{:S(2)}, u32[]{:S(2)}) collective-permute-start(bf16[32,128]{1,0:T(8,128)(2,1)S(1)} %select_n.77), channel_id=1, source_target_pairs={{0,0},{1,128},{2,256},{3,384},{4,4},{5,132},{6,260},{7,388},{64,64... | collective-permute-start | bytes 24584 | tf_op jit(solution)/shard_map/ppermute | solution.py:184
  13.7 1.9 collective-permute-start.3
  15.6 9.3 %collective-permute-done.3 = bf16[32,128]{1,0:T(8,128)(2,1)S(1)} collective-permute-done((bf16[32,128]{1,0:T(8,128)(2,1)S(1)}, bf16[32,128]{1,0:T(8,128)(2,1)S(1)}, u32[]{:S(2)}, u32[]{:S(2)}) %collective-permute-start.3) | collective-permute-done | bytes 8224 | tf_op jit(solution)/shard_map/ppermute | solution.py:184
  26.2 9.0 %all-to-all-start = ((bf16[64,64,128]{2,1,0:T(8,128)(2,1)}), bf16[64,64,128]{2,1,0:T(8,128)(2,1)S(1)}, u32[]{:S(2)}, u32[]{:S(2)}) async-start(bf16[64,64,128]{2,1,0:T(8,128)(2,1)} %broadcast_in_dim.28), calls=%async_computation | async-start | bytes 2097152 | tf_op jit(solution)/shard_map/all_to_all | solution.py:201
  35.3 1.9 collective-permute-start
  37.2 2.4 %collective-permute-start.1 = (bf16[512,1024]{1,0:T(8,128)(2,1)S(1)}, bf16[512,1024]{1,0:T(8,128)(2,1)S(1)}, u32[]{:S(2)}, u32[]{:S(2)}) collective-permute-start(bf16[512,1024]{1,0:T(8,128)(2,1)S(1)} %copy-done.3), channel_id=1, source_target_pairs={{0,4},{4,0},{1,5},{5,1},{2,6},{6,2},{3,7},{7,3},{8,12},{12,8},{9,1... | collective-permute-start | bytes 3145736 | tf_op jit(solution)/shard_map/ppermute | solution.py:187
  42.8 21.9 %all-to-all-done = bf16[64,64,128]{2,1,0:T(8,128)(2,1)S(1)} async-done(((bf16[64,64,128]{2,1,0:T(8,128)(2,1)}), bf16[64,64,128]{2,1,0:T(8,128)(2,1)S(1)}, u32[]{:S(2)}, u32[]{:S(2)}) %all-to-all-start) | async-done | bytes 1048608 | tf_op jit(solution)/shard_map/all_to_all | solution.py:201
  67.2 3.7 %shard_map.88 = f32[4,1024,128]{2,1,0:T(8,128)} custom-call(bf16[512,1024]{1,0:T(8,128)(2,1)S(1)} %copy-done.1, bf16[512,1024]{1,0:T(8,128)(2,1)S(1)} %copy-done.6, bf16[512,1024]{1,0:T(8,128)(2,1)S(1)} %copy-done.3, bf16[512,1024]{1,0:T(8,128)(2,1)S(1)} %copy-done.9, bf16[4,1024,128]{2,1,0:T(8,128)(2,1)S(1)} %bitcast.24), custom_call_target="tpu_custom_call" | custom-call | flops 2147483648 | bytes 8388608 | tf_op jit(solution)/shard_map/pallas_call | solution.py:240
  70.9 7.4 %all-to-all-start.1 = ((f32[4,1024,128]{2,1,0:T(8,128)}), f32[4,1024,128]{2,1,0:T(8,128)S(1)}, u32[]{:S(2)}, u32[]{:S(2)}) async-start(f32[4,1024,128]{2,1,0:T(8,128)} %shard_map.88), calls=%async_computation.1 | async-start | bytes 4194304 | tf_op jit(solution)/shard_map/all_to_all | solution.py:241
  78.3 1.9 collective-permute-start.4
  80.8 17.9 %all-to-all-done.1.part_ref = f32[4,1024,128]{2,1,0:T(8,128)S(1)} async-done(((f32[4,1024,128]{2,1,0:T(8,128)}), f32[4,1024,128]{2,1,0:T(8,128)S(1)}, u32[]{:S(2)}, u32[]{:S(2)}) %all-to-all-start.1) | async-done | bytes 2097184 | tf_op jit(solution)/shard_map/all_to_all | solution.py:241
  98.6 1.7 shard_map.89
  100.3 8.3 %all-to-all-start.2 = ((f32[64,4,128]{2,1,0:T(4,128)}), f32[64,4,128]{2,1,0:T(4,128)S(1)}, u32[]{:S(2)}, u32[]{:S(2)}) async-start(f32[64,4,128]{2,1,0:T(4,128)} %get-tuple-element.7), calls=%async_computation.2 | async-start | bytes 262144 | tf_op jit(solution)/shard_map/all_to_all | solution.py:257
  109.6 11.7 %all-to-all-done.2.states_ref = f32[64,4,128]{2,1,0:T(4,128)S(1)} async-done(((f32[64,4,128]{2,1,0:T(4,128)}), f32[64,4,128]{2,1,0:T(4,128)S(1)}, u32[]{:S(2)}, u32[]{:S(2)}) %all-to-all-start.2) | async-done | bytes 131104 | tf_op jit(solution)/shard_map/all_to_all | solution.py:257
  121.3 2.6 %shard_map.90 = bf16[4,1024,128]{2,1,0:T(8,128)(2,1)} custom-call(s32[1]{0:T(128)} %bitcast.core_ref, f32[1024,128]{1,0:T(8,128)S(1)} %get-tuple-element.5.x_ref, f32[64,128]{1,0:T(8,128)S(1)} %get-tuple-element.6.left_ref, f32[64,4,128]{2,1,0:T(4,128)S(1)} %all-to-all-done.2.states_ref, f32[64,4,128]{2,1,0:T(4,128)S(1)} %exponential_select_fusion.reach_ref, ...), custom_call_target="tpu_custom_call" | custom-call | tf_op jit(solution)/shard_map/pallas_call | solution.py:258
  123.9 6.4 %all-to-all-start.3 = ((bf16[4,1024,128]{2,1,0:T(8,128)(2,1)}), bf16[4,1024,128]{2,1,0:T(8,128)(2,1)S(1)}, u32[]{:S(2)}, u32[]{:S(2)}) async-start(bf16[4,1024,128]{2,1,0:T(8,128)(2,1)} %shard_map.90), calls=%async_computation.3 | async-start | bytes 2097152 | tf_op jit(solution)/shard_map/all_to_all | solution.py:266
  135.0 1.3 copy-done
  136.3 3.2 %all-to-all-done.3.grads_ref = bf16[4,1024,128]{2,1,0:T(8,128)(2,1)S(1)} async-done(((bf16[4,1024,128]{2,1,0:T(8,128)(2,1)}), bf16[4,1024,128]{2,1,0:T(8,128)(2,1)S(1)}, u32[]{:S(2)}, u32[]{:S(2)}) %all-to-all-start.3) | async-done | bytes 1048608 | tf_op jit(solution)/shard_map/all_to_all | solution.py:266
  139.5 3.9 %shard_map.91 = bf16[4,1024,128]{2,1,0:T(8,128)(2,1)S(1)} custom-call(bf16[1024,1024]{1,0:T(8,128)(2,1)S(1)} %shard_map.86.tt_ref, bf16[1024,1024]{1,0:T(8,128)(2,1)} %copy-done, bf16[4,1024,128]{2,1,0:T(8,128)(2,1)S(1)} %all-to-all-done.3.grads_ref), custom_call_target="tpu_custom_call" | custom-call | flops 2147483648 | bytes 8388608 | tf_op jit(solution)/shard_map/pallas_call | solution.py:274
  143.4 29.6 %all_to_all.25 = bf16[64,64,128]{2,1,0:T(8,128)(2,1)S(1)} all-to-all(bf16[64,64,128]{2,1,0:T(8,128)(2,1)S(1)} %bitcast.25), channel_id=1, replica_groups=mesh['seq_0'=8,'seq_1'=8,'seq_2'=2,'chan'=4] {'seq_0','seq_1'}, dimensions={0} | all-to-all | bytes 2097152 | tf_op jit(solution)/shard_map/all_to_all | solution.py:275
  173.2 7.2 %collective-permute-start.5 = (f32[32,128]{1,0:T(8,128)S(1)}, f32[32,128]{1,0:T(8,128)S(1)}, u32[]{:S(2)}, u32[]{:S(2)}) collective-permute-start(f32[32,128]{1,0:T(8,128)S(1)} %get-tuple-element.16), channel_id=1, source_target_pairs={{0,0},{1,128},{2,256},{3,384},{4,4},{5,132},{6,260},{7,388},{64,64... | collective-permute-start | bytes 49160 | tf_op jit(solution)/shard_map/ppermute | solution.py:184
  180.4 1.9 collective-permute-start.6
  182.3 2.9 %collective-permute-done.5 = f32[32,128]{1,0:T(8,128)S(1)} collective-permute-done((f32[32,128]{1,0:T(8,128)S(1)}, f32[32,128]{1,0:T(8,128)S(1)}, u32[]{:S(2)}, u32[]{:S(2)}) %collective-permute-start.5) | collective-permute-done | bytes 16416 | tf_op jit(solution)/shard_map/ppermute | solution.py:184
  185.2 6.6 %collective-permute-done.6 = f32[32,128]{1,0:T(8,128)S(1)} collective-permute-done((f32[32,128]{1,0:T(8,128)S(1)}, f32[32,128]{1,0:T(8,128)S(1)}, u32[]{:S(2)}, u32[]{:S(2)}) %collective-permute-start.6) | collective-permute-done | bytes 16416 | tf_op jit(solution)/shard_map/ppermute | solution.py:184
  (77 shorter events, 17.0 us)
Async XLA Ops:
  0.6 34.6 %copy-start.1 = (bf16[512,1024]{1,0:T(8,128)(2,1)S(1)}, bf16[512,1024]{1,0:T(8,128)(2,1)}, u32[]{:S(2)}) copy-start(bf16[512,1024]{1,0:T(8,128)(2,1)} %own_t.1) | copy-start | bytes 3145732
  0.6 36.5 %copy-start.3 = (bf16[512,1024]{1,0:T(8,128)(2,1)S(1)}, bf16[512,1024]{1,0:T(8,128)(2,1)}, u32[]{:S(2)}) copy-start(bf16[512,1024]{1,0:T(8,128)(2,1)} %own_g.1) | copy-start | bytes 3145732
  2.7 12.9 %collective-permute-start.2 = (bf16[32,128]{1,0:T(8,128)(2,1)S(1)}, bf16[32,128]{1,0:T(8,128)(2,1)S(1)}, u32[]{:S(2)}, u32[]{:S(2)}) collective-permute-start(bf16[32,128]{1,0:T(8,128)(2,1)S(1)} %select_n.77), channel_id=1, source_target_pairs={{0,0},{1,128},{2,256},{3,384},{4,4},{5,132},{6,260},{7,388},{64,64... | collective-permute-start | bytes 24584 | tf_op jit(solution)/shard_map/ppermute | solution.py:184
  13.7 11.3 %collective-permute-start.3 = (bf16[32,128]{1,0:T(8,128)(2,1)S(1)}, bf16[32,128]{1,0:T(8,128)(2,1)S(1)}, u32[]{:S(2)}, u32[]{:S(2)}) collective-permute-start(bf16[32,128]{1,0:T(8,128)(2,1)S(1)} %select_n.79), channel_id=1, source_target_pairs={{0,4},{1,132},{2,260},{3,388},{4,0},{5,128},{6,256},{7,384},{64,68... | collective-permute-start | bytes 24584 | tf_op jit(solution)/shard_map/ppermute | solution.py:184
  26.2 38.5 %all-to-all-start = ((bf16[64,64,128]{2,1,0:T(8,128)(2,1)}), bf16[64,64,128]{2,1,0:T(8,128)(2,1)S(1)}, u32[]{:S(2)}, u32[]{:S(2)}) async-start(bf16[64,64,128]{2,1,0:T(8,128)(2,1)} %broadcast_in_dim.28), calls=%async_computation | async-start | bytes 2097152 | tf_op jit(solution)/shard_map/all_to_all | solution.py:201
  35.3 4.6 %collective-permute-start = (bf16[512,1024]{1,0:T(8,128)(2,1)S(1)}, bf16[512,1024]{1,0:T(8,128)(2,1)S(1)}, u32[]{:S(2)}, u32[]{:S(2)}) collective-permute-start(bf16[512,1024]{1,0:T(8,128)(2,1)S(1)} %copy-done.1), channel_id=1, source_target_pairs={{0,4},{4,0},{1,5},{5,1},{2,6},{6,2},{3,7},{7,3},{8,12},{12,8},{9,1... | collective-permute-start | bytes 3145736 | tf_op jit(solution)/shard_map/ppermute | solution.py:187
  37.2 4.7 %collective-permute-start.1 = (bf16[512,1024]{1,0:T(8,128)(2,1)S(1)}, bf16[512,1024]{1,0:T(8,128)(2,1)S(1)}, u32[]{:S(2)}, u32[]{:S(2)}) collective-permute-start(bf16[512,1024]{1,0:T(8,128)(2,1)S(1)} %copy-done.3), channel_id=1, source_target_pairs={{0,4},{4,0},{1,5},{5,1},{2,6},{6,2},{3,7},{7,3},{8,12},{12,8},{9,1... | collective-permute-start | bytes 3145736 | tf_op jit(solution)/shard_map/ppermute | solution.py:187
  39.8 1.0 copy-start.5
  64.8 1.2 copy-start.6
  66.0 1.2 copy-start.9
  70.9 7.4 %copy-start.11 = (bf16[512,64]{0,1:T(8,128)(2,1)S(1)}, bf16[512,64]{0,1:T(8,128)(2,1)}, u32[]{:S(2)}) copy-start(bf16[512,64]{0,1:T(8,128)(2,1)} %param.11) | copy-start | bytes 196612
  70.9 9.3 %copy-start.12 = (f32[16,32]{1,0:T(8,128)S(1)}, f32[16,32]{1,0:T(8,128)}, u32[]{:S(2)}) copy-start(f32[16,32]{1,0:T(8,128)} %param.12) | copy-start | bytes 6148
  70.9 9.3 %copy-start.13 = (f32[16,32]{1,0:T(8,128)S(1)}, f32[16,32]{1,0:T(8,128)}, u32[]{:S(2)}) copy-start(f32[16,32]{1,0:T(8,128)} %param.13) | copy-start | bytes 6148
  70.9 27.7 %all-to-all-start.1 = ((f32[4,1024,128]{2,1,0:T(8,128)}), f32[4,1024,128]{2,1,0:T(8,128)S(1)}, u32[]{:S(2)}, u32[]{:S(2)}) async-start(f32[4,1024,128]{2,1,0:T(8,128)} %shard_map.88), calls=%async_computation.1 | async-start | bytes 4194304 | tf_op jit(solution)/shard_map/all_to_all | solution.py:241
  78.3 31.1 %collective-permute-start.4 = (bf16[512,32]{0,1:T(8,128)(2,1)S(1)}, bf16[512,32]{0,1:T(8,128)(2,1)S(1)}, u32[]{:S(2)}, u32[]{:S(2)}) collective-permute-start(bf16[512,32]{0,1:T(8,128)(2,1)S(1)} %get-tuple-element.11), channel_id=1, source_target_pairs={{0,4},{4,0},{1,5},{5,1},{2,6},{6,2},{3,7},{7,3},{8,12},{12,8},{9,1... | collective-permute-start | bytes 98312 | tf_op jit(solution)/shard_map/ppermute | solution.py:187
  100.3 21.0 %all-to-all-start.2 = ((f32[64,4,128]{2,1,0:T(4,128)}), f32[64,4,128]{2,1,0:T(4,128)S(1)}, u32[]{:S(2)}, u32[]{:S(2)}) async-start(f32[64,4,128]{2,1,0:T(4,128)} %get-tuple-element.7), calls=%async_computation.2 | async-start | bytes 262144 | tf_op jit(solution)/shard_map/all_to_all | solution.py:257
  123.9 15.6 %all-to-all-start.3 = ((bf16[4,1024,128]{2,1,0:T(8,128)(2,1)}), bf16[4,1024,128]{2,1,0:T(8,128)(2,1)S(1)}, u32[]{:S(2)}, u32[]{:S(2)}) async-start(bf16[4,1024,128]{2,1,0:T(8,128)(2,1)} %shard_map.90), calls=%async_computation.3 | async-start | bytes 2097152 | tf_op jit(solution)/shard_map/all_to_all | solution.py:266
  130.3 1.2 copy-start.2
  131.5 1.2 copy-start.7
  132.8 1.2 copy-start.4
  132.8 1.5 copy-start.10
  134.9 1.4 copy-start
  173.2 12.0 %collective-permute-start.5 = (f32[32,128]{1,0:T(8,128)S(1)}, f32[32,128]{1,0:T(8,128)S(1)}, u32[]{:S(2)}, u32[]{:S(2)}) collective-permute-start(f32[32,128]{1,0:T(8,128)S(1)} %get-tuple-element.16), channel_id=1, source_target_pairs={{0,0},{1,128},{2,256},{3,384},{4,4},{5,132},{6,260},{7,388},{64,64... | collective-permute-start | bytes 49160 | tf_op jit(solution)/shard_map/ppermute | solution.py:184
  180.4 11.4 %collective-permute-start.6 = (f32[32,128]{1,0:T(8,128)S(1)}, f32[32,128]{1,0:T(8,128)S(1)}, u32[]{:S(2)}, u32[]{:S(2)}) collective-permute-start(f32[32,128]{1,0:T(8,128)S(1)} %get-tuple-element.17), channel_id=1, source_target_pairs={{0,4},{1,132},{2,260},{3,388},{4,0},{5,128},{6,256},{7,384},{64,68... | collective-permute-start | bytes 49160 | tf_op jit(solution)/shard_map/ppermute | solution.py:184
  (1 other events, 1.0 us)

commit v2 on v1

--- a/solution.py
+++ b/solution.py
@@ -13,17 +13,33 @@
 GROUPS = 4
 F32 = jnp.float32
 BF16 = jnp.bfloat16
-VMEM = 48 * 1024 * 1024
-
-
-def call(body, out_shape, scratch=(), flops=0, moved=0):
+MIB = 1024 * 1024
+
+OFFSETS = ((5, 4), (2, 3), (0, 1), (6, 7))
+
+
+def call(body, out_shape, mib, scratch=(), flops=0, moved=0, inputs=None):
+    specs = {}
+    if inputs is not None:
+        specs["in_specs"] = [pl.BlockSpec(memory_space=pltpu.SMEM)] + [
+            pl.BlockSpec(memory_space=pltpu.VMEM)
+        ] * (inputs - 1)
     return pl.pallas_call(
         body,
         out_shape=out_shape,
         scratch_shapes=list(scratch),
-        compiler_params=pltpu.CompilerParams(vmem_limit_bytes=VMEM),
+        compiler_params=pltpu.CompilerParams(vmem_limit_bytes=mib * MIB),
         cost_estimate=pl.CostEstimate(flops=flops, bytes_accessed=moved, transcendentals=0),
-    )
+        **specs,
+    )
+
+
+def holder(plane, c, l):
+    e = lax.rem(c + len(OFFSETS) - plane, len(OFFSETS))
+    o = OFFSETS[0][l]
+    for k in range(1, len(OFFSETS)):
+        o = jnp.where(e == k, OFFSETS[k][l], o)
+    return lax.rem(2 * plane + o, 2 * len(OFFSETS))
 
 
 def lane_group(shape):
@@ -41,11 +57,65 @@
     out_ref[:, half:] = b_ref[...].T
 
 
-def project_body(own_t, other_t, own_g, other_g, w_ref, out_ref):
+def pack_body(at_ref, in_ref, out_w_ref, kept_ref, given_ref):
+    core = at_ref[0]
+    width = out_w_ref.shape[1]
+    row = lax.broadcasted_iota(jnp.int32, (width, 128), 0)
+    lane = lax.broadcasted_iota(jnp.int32, (width, 128), 1)
+    streams = [in_ref[0], in_ref[1], in_ref[2], out_w_ref[...]]
+    for half, ref in ((core, kept_ref), (1 - core, given_ref)):
+        total = jnp.zeros(ref.shape, F32)
+        for s, w in enumerate(streams):
+            chosen = (lane // 32 == s) & (row == half * 32 + lane % 32)
+            total = total + jnp.dot(w, chosen.astype(F32).astype(BF16), preferred_element_type=F32)
+        ref[...] = total.astype(BF16)
+
+
+def spread_body(at_ref, kept_ref, given_ref, out_ref):
+    first = at_ref[0] == 0
+    kept = kept_ref[...].astype(F32)
+    given = given_ref[...].astype(F32)
+    low = jnp.where(first, kept, given)
+    high = jnp.where(first, given, kept)
+    piece = jnp.concatenate([low, high], axis=0).astype(BF16)
+    for k in range(out_ref.shape[0]):
+        out_ref[k] = piece
+
+
+def total_body(at_ref, part_ref, kept_ref, given_ref):
+    first = at_ref[0] == 0
+    owned = kept_ref.shape[0]
+    total = part_ref[0].astype(F32)
+    for k in range(1, part_ref.shape[0]):
+        total = total + part_ref[k].astype(F32)
+    kept_ref[...] = jnp.where(first, total[:owned], total[owned:])
+    given_ref[...] = jnp.where(first, total[owned:], total[:owned])
+
+
+def unpack_body(at_ref, kept_ref, given_ref, in_ref, out_w_ref):
+    first = at_ref[0] == 0
+    low = jnp.where(first, kept_ref[...], given_ref[...])
+    high = jnp.where(first, given_ref[...], kept_ref[...])
+    for s in range(GROUPS):
+        left = low if s == 0 else turn(low, 128 - 32 * s)
+        right = high if s == 1 else turn(high, (160 - 32 * s) % 128)
+        both = jnp.where(lane_group(low.shape) == 0, left, right)[:, : out_w_ref.shape[1]]
+        if s < 3:
+            in_ref[s] = both
+        else:
+            out_w_ref[...] = both
+
+
+def project_body(at_ref, own_t, other_t, own_g, other_g, w_ref, out_ref):
     half = own_t.shape[0]
-    for at, (t_ref, g_ref) in enumerate(((own_t, own_g), (other_t, other_g))):
-        for c in range(0, w_ref.shape[0], 2):
-            w = jnp.concatenate([w_ref[c], w_ref[c + 1]], axis=1)
+    plane = at_ref[1]
+
+    def columns(c):
+        return jnp.concatenate([w_ref[holder(plane, c, l)] for l in range(2)], axis=0)
+
+    for c in range(0, out_ref.shape[0], 2):
+        w = jnp.concatenate([columns(c), columns(c + 1)], axis=1)
+        for at, (t_ref, g_ref) in enumerate(((own_t, own_g), (other_t, other_g))):
             from_t = jnp.dot(t_ref[...], w, preferred_element_type=F32)
             from_g = jnp.dot(g_ref[...], w, preferred_element_type=F32)
             both = jnp.where(lane_group(from_t.shape) % GROUPS < 3, from_t, from_g)
@@ -64,8 +134,8 @@
     return pl.ds(start + step, half // STEPS, stride=STEPS)
 
 
-def first_body(core_ref, part_ref, decay_ref, far_ref, x_ref, left_ref, state_ref, sig, st):
-    core = core_ref[0]
+def first_body(at_ref, part_ref, decay_ref, far_ref, x_ref, left_ref, state_ref, sig, st):
+    core = at_ref[0]
     rows = x_ref.shape[0]
     total = part_ref[0]
     for k in range(1, part_ref.shape[0]):
@@ -100,10 +170,10 @@
 
 
 def second_body(
-    core_ref, x_ref, left_ref, states_ref, reach_ref, power_ref, decay_ref, weight_ref, conv_ref,
+    at_ref, x_ref, left_ref, states_ref, reach_ref, power_ref, decay_ref, weight_ref, conv_ref,
     out_ref, sig, ys,
 ):
-    core = core_ref[0]
+    core = at_ref[0]
     rows = x_ref.shape[0]
     chunks = rows // STEPS
     per = chunks // 2
@@ -140,17 +210,18 @@
         out_ref[k] = out
 
 
-def weigh_body(tt_ref, gt_ref, grads_ref, out_ref):
-    depth = tt_ref.shape[0]
-    block = 512
-    for r in range(0, depth, block):
+def weigh_body(at_ref, tt_ref, gt_ref, grads_ref, out_ref):
+    plane = at_ref[1]
+    block = out_ref.shape[1]
+    for l in range(2):
+        r = l * block
         for c in range(0, grads_ref.shape[0], 2):
             g = jnp.concatenate([grads_ref[c], grads_ref[c + 1]], axis=1)
             from_t = jnp.dot(tt_ref[r : r + block, :], g, preferred_element_type=F32)
             from_g = jnp.dot(gt_ref[r : r + block, :], g, preferred_element_type=F32)
             both = jnp.where(lane_group(from_t.shape) % GROUPS < 3, from_t, from_g).astype(BF16)
-            out_ref[c, r : r + block] = both[:, :128]
-            out_ref[c + 1, r : r + block] = both[:, 128:]
+            out_ref[holder(plane, c, l)] = both[:, :128]
+            out_ref[holder(plane, c + 1, l)] = both[:, 128:]
 
 
 def by_lanes(table):
@@ -168,37 +239,36 @@
     mine = channels // 2
     size_z, size_y, size_x = (lax.axis_size(a) for a in ("seq_0", "seq_1", "chan"))
     chips = size_z * size_y
-    fold = size_z // size_x
     core = lax.axis_index("seq_2")
     place = lax.axis_index(CHIPS)
 
-    def transposed(value, swap):
+    at = jnp.stack([core, lax.axis_index("chan")]).astype(jnp.int32)
+
+    def transposed(value, swap, to_owner):
         pairs = []
         for z in range(size_z):
             for k in range(2):
                 for x in range(size_x):
-                    c, l = z // fold, z % fold
-                    source = (z * 2 + k) * size_x + x
-                    target = ((fold * x + l) * 2 + (1 - k if swap else k)) * size_x + c
-                    pairs.append((source, target))
+                    j, l = z // 2, z % 2
+                    held_z = (2 * j + OFFSETS[(x - j) % size_x][l]) % size_z
+                    owner = (z * 2 + k) * size_x + x
+                    held = (held_z * 2 + (1 - k if swap else k)) * size_x + j
+                    pairs.append((held, owner) if to_owner else (owner, held))
         return lax.ppermute(value, ("seq_0", "seq_2", "chan"), pairs)
 
     def swapped(value):
         return lax.ppermute(value, "seq_2", [(0, 1), (1, 0)])
 
-    packed = jnp.concatenate([in_weight, out_weight[:, None, :]], axis=1)
-    packed = packed.reshape(owned, GROUPS, 2, mine).transpose(2, 0, 1, 3).reshape(2, owned, 128)
-    kept, given = (
-        jnp.where(core == 0, packed[0], packed[1]),
-        jnp.where(core == 0, packed[1], packed[0]),
-    )
-    kept = transposed(kept, False)
-    given = transposed(given, True)
-    low = jnp.where(core == 0, kept, given)
-    high = jnp.where(core == 0, given, kept)
-    piece = jnp.concatenate([low, high], axis=0)
-    piece = jnp.broadcast_to(piece[None], (chips, 2 * owned, 128))
-    weights = lax.all_to_all(piece, CHIPS, 0, 0, tiled=True).reshape(size_x, depth, 128)
+    piece = jax.ShapeDtypeStruct((owned, 128), BF16)
+    kept, given = call(pack_body, (piece, piece), 4, inputs=3)(
+        at, in_weight.transpose(1, 0, 2), out_weight
+    )
+    kept = transposed(kept, False, False)
+    given = transposed(given, True, False)
+    spread = call(
+        spread_body, jax.ShapeDtypeStruct((chips, 2 * owned, 128), BF16), 4, inputs=3
+    )(at, kept, given)
+    weights = lax.all_to_all(spread, CHIPS, 0, 0, tiled=True).reshape(size_z, -1, 128)
 
     tokens_too = swapped(tokens)
     grads_too = swapped(grad_out)
@@ -207,7 +277,7 @@
     conv = jnp.concatenate([conv_own, swapped(conv_sent)], axis=0)
     conv = jnp.tile(conv, (1, GROUPS))
     flip = call(
-        transpose_body, jax.ShapeDtypeStruct((depth, rows), BF16), moved=4 * depth * rows
+        transpose_body, jax.ShapeDtypeStruct((depth, rows), BF16), 8, moved=4 * depth * rows
     )
     tokens_t = flip(tokens, tokens_too)
     grads_t = flip(grad_out, grads_too)
@@ -229,58 +299,66 @@
         jnp.exp(-(jnp.maximum(ahead, 0) * rows).astype(F32)[:, None, None] * rate[None]),
         0.0,
     )
-    core_at = core.astype(jnp.int32).reshape(1)
 
     project = call(
         project_body,
         jax.ShapeDtypeStruct((size_x, rows, 128), F32),
+        48,
+        inputs=6,
         flops=4 * rows * depth * size_x * 128,
         moved=8 * rows * depth,
     )
-    parts = project(tokens, tokens_too, grad_out, grads_too, weights)
+    weights, tokens_t, grads_t = lax.optimization_barrier((weights, tokens_t, grads_t))
+    parts = project(at, tokens, tokens_too, grad_out, grads_too, weights)
     parts = lax.all_to_all(parts, "chan", 0, 0, tiled=True)
 
-    smem = pl.BlockSpec(memory_space=pltpu.SMEM)
-    full = pl.BlockSpec(memory_space=pltpu.VMEM)
-    x, left, state = pl.pallas_call(
+    first = call(
         first_body,
-        out_shape=(
+        (
             jax.ShapeDtypeStruct((rows, 128), F32),
             jax.ShapeDtypeStruct((MODE_ROWS * chunks, 128), F32),
             jax.ShapeDtypeStruct((chips, MODE_ROWS, 128), F32),
         ),
-        in_specs=[smem, full, full, full],
-        out_specs=(full, full, full),
-        scratch_shapes=[pltpu.VMEM((rows, 128), F32), pltpu.VMEM((MODE_ROWS * chunks, 128), F32)],
-        compiler_params=pltpu.CompilerParams(vmem_limit_bytes=VMEM),
-    )(core_at, parts, decay, far)
+        10,
+        scratch=[pltpu.VMEM((rows, 128), F32), pltpu.VMEM((MODE_ROWS * chunks, 128), F32)],
+        inputs=4,
+    )
+    x, left, state = first(at, parts, decay, far)
     states = lax.all_to_all(state, CHIPS, 0, 0, tiled=True)
-    grads = pl.pallas_call(
+    second = call(
         second_body,
-        out_shape=jax.ShapeDtypeStruct((size_x, rows, 128), BF16),
-        in_specs=[smem] + [full] * 8,
-        out_specs=full,
-        scratch_shapes=[pltpu.VMEM((rows, 128), F32), pltpu.VMEM((rows, 128), F32)],
-        compiler_params=pltpu.CompilerParams(vmem_limit_bytes=VMEM),
-    )(core_at, x, left, states, reach, power, decay, weight, conv)
+        jax.ShapeDtypeStruct((size_x, rows, 128), BF16),
+        10,
+        scratch=[pltpu.VMEM((rows, 128), F32), pltpu.VMEM((rows, 128), F32)],
+        inputs=9,
+    )
+    grads = second(at, x, left, states, reach, power, decay, weight, conv)
     grads = lax.all_to_all(grads, "chan", 0, 0, tiled=True)
 
     weigh = call(
         weigh_body,
-        jax.ShapeDtypeStruct((size_x, depth, 128), BF16),
+        jax.ShapeDtypeStruct((size_z, depth // 2, 128), BF16),
+        16,
+        inputs=4,
         flops=4 * rows * depth * size_x * 128,
         moved=8 * rows * depth,
     )
-    partial = weigh(tokens_t, grads_t, grads).reshape(chips, 2 * owned, 128)
+    partial = weigh(at, tokens_t, grads_t, grads).reshape(chips, 2 * owned, 128)
     partial = lax.all_to_all(partial, CHIPS, 0, 0, tiled=True)
-    total = jnp.sum(partial.astype(F32), axis=0)
-    kept = transposed(jnp.where(core == 0, total[:owned], total[owned:]), False)
-    given = transposed(jnp.where(core == 0, total[owned:], total[:owned]), True)
-    low = jnp.where(core == 0, kept, given)
-    high = jnp.where(core == 0, given, kept)
-    result = jnp.stack([low, high]).reshape(2, owned, GROUPS, mine)
-    result = result.transpose(1, 2, 0, 3).reshape(owned, GROUPS, channels)
-    return (result[:, :3], result[:, 3])
+    piece = jax.ShapeDtypeStruct((owned, 128), F32)
+    kept, given = call(total_body, (piece, piece), 6, inputs=2)(at, partial)
+    kept = transposed(kept, False, True)
+    given = transposed(given, True, True)
+    grad_in, grad_proj = call(
+        unpack_body,
+        (
+            jax.ShapeDtypeStruct((3, owned, channels), F32),
+            jax.ShapeDtypeStruct((owned, channels), F32),
+        ),
+        4,
+        inputs=3,
+    )(at, kept, given)
+    return (grad_in.transpose(1, 0, 2), grad_proj)
 
 
 def solution(mesh):

time: 194 us -> 186 us (0.959)
  the two profiles are of different devices: /device:TPU:4 before, /device:TPU:6 now
where the time goes in v2:
time: 186 us; the launch traced here: 185 us
  waiting for transfers between devices  65.6 us (35%)
  starting transfers between devices  47.7 us (26%)
  blocking collectives  44.5 us (24%)
  Pallas kernels  17.1 us (9%)
  local copies, waits for them, and re-layouts  8.67 us (5%)
    all_to_all x1, blocking collectives, local(): partial = lax.all_to_all(partial, CHIPS, 0, 0, tiled=True)  29.8 us
    all_to_all x1, waiting for transfers between devices, local(): lax.all_to_all(spread, CHIPS, 0, 0, tiled=True).reshape(size_z, -1, 128)  20 us
    ppermute x4, starting transfers between devices, transposed(): return lax.ppermute(value, ('seq_0', 'seq_2', 'chan'), pairs)  19.4 us
    all_to_all x1, waiting for transfers between devices, local(): parts = lax.all_to_all(parts, 'chan', 0, 0, tiled=True)  18.9 us
    ppermute x4, waiting for transfers between devices, transposed(): return lax.ppermute(value, ('seq_0', 'seq_2', 'chan'), pairs)  14.7 us
    all_to_all x1, blocking collectives, local(): grads = lax.all_to_all(grads, 'chan', 0, 0, tiled=True)  14.7 us
    all_to_all x1, waiting for transfers between devices, local(): states = lax.all_to_all(state, CHIPS, 0, 0, tiled=True)  11.8 us
    all_to_all x1, starting transfers between devices, local(): lax.all_to_all(spread, CHIPS, 0, 0, tiled=True).reshape(size_z, -1, 128)  9.09 us
  transfers between devices with their start and end apart: 10, of which 8 were waited for; matrix products, arithmetic and copies ran while one was open for 1% of the time, Pallas kernels for 2%

profile of v2, /device:TPU:6, one launch (start us, length us, event | category | flops | bytes accessed | tf_op | source)
XLA Modules:
  0.0 185.0 jit_solution(9447934141027351904)
XLA Ops:
  3.0 10.9 %collective-permute-start = (bf16[32,128]{1,0:T(8,128)(2,1)S(1)}, bf16[32,128]{1,0:T(8,128)(2,1)S(1)}, u32[]{:S(2)}, u32[]{:S(2)}) collective-permute-start(bf16[32,128]{1,0:T(8,128)(2,1)S(1)} %get-tuple-element.14), channel_id=1, source_target_pairs={{0,320},{1,128},{2,0},{3,384},{4,324},{5,132},{6,4},{7,388},{64,25... | collective-permute-start | bytes 24584 | tf_op jit(solution)/shard_map/ppermute | solution.py:257
  13.9 1.9 %collective-permute-start.1 = (bf16[32,128]{1,0:T(8,128)(2,1)S(1)}, bf16[32,128]{1,0:T(8,128)(2,1)S(1)}, u32[]{:S(2)}, u32[]{:S(2)}) collective-permute-start(bf16[32,128]{1,0:T(8,128)(2,1)S(1)} %get-tuple-element.15), channel_id=1, source_target_pairs={{0,324},{1,132},{2,4},{3,388},{4,320},{5,128},{6,0},{7,384},{64,26... | collective-permute-start | bytes 24584 | tf_op jit(solution)/shard_map/ppermute | solution.py:257
  15.8 7.3 %collective-permute-done.1.given_ref = bf16[32,128]{1,0:T(8,128)(2,1)S(1)} collective-permute-done((bf16[32,128]{1,0:T(8,128)(2,1)S(1)}, bf16[32,128]{1,0:T(8,128)(2,1)S(1)}, u32[]{:S(2)}, u32[]{:S(2)}) %collective-permute-start.1) | collective-permute-done | bytes 8224 | tf_op jit(solution)/shard_map/ppermute | solution.py:257
  23.0 1.7 shard_map.87
  24.7 9.1 %all-to-all-start = ((bf16[64,64,128]{2,1,0:T(8,128)(2,1)}), bf16[64,64,128]{2,1,0:T(8,128)(2,1)S(1)}, u32[]{:S(2)}, u32[]{:S(2)}) async-start(bf16[64,64,128]{2,1,0:T(8,128)(2,1)} %shard_map.87), calls=%async_computation | async-start | bytes 2097152 | tf_op jit(solution)/shard_map/all_to_all | solution.py:271
  33.8 1.9 %collective-permute-start.2 = (bf16[512,1024]{1,0:T(8,128)(2,1)S(1)}, bf16[512,1024]{1,0:T(8,128)(2,1)S(1)}, u32[]{:S(2)}, u32[]{:S(2)}) collective-permute-start(bf16[512,1024]{1,0:T(8,128)(2,1)S(1)} %copy-done.4), channel_id=1, source_target_pairs={{0,4},{4,0},{1,5},{5,1},{2,6},{6,2},{3,7},{7,3},{8,12},{12,8},{9,1... | collective-permute-start | bytes 3145736 | tf_op jit(solution)/shard_map/ppermute | solution.py:260
  35.8 2.4 %collective-permute-start.3 = (bf16[512,1024]{1,0:T(8,128)(2,1)S(1)}, bf16[512,1024]{1,0:T(8,128)(2,1)S(1)}, u32[]{:S(2)}, u32[]{:S(2)}) collective-permute-start(bf16[512,1024]{1,0:T(8,128)(2,1)S(1)} %copy-done.5), channel_id=1, source_target_pairs={{0,4},{4,0},{1,5},{5,1},{2,6},{6,2},{3,7},{7,3},{8,12},{12,8},{9,1... | collective-permute-start | bytes 3145736 | tf_op jit(solution)/shard_map/ppermute | solution.py:260
  39.0 1.3 copy-done
  43.4 20.0 %all-to-all-done = bf16[64,64,128]{2,1,0:T(8,128)(2,1)S(1)} async-done(((bf16[64,64,128]{2,1,0:T(8,128)(2,1)}), bf16[64,64,128]{2,1,0:T(8,128)(2,1)S(1)}, u32[]{:S(2)}, u32[]{:S(2)}) %all-to-all-start) | async-done | bytes 1048608 | tf_op jit(solution)/shard_map/all_to_all | solution.py:271
  65.8 4.3 %shard_map.90 = f32[4,1024,128]{2,1,0:T(8,128)} custom-call(s32[2]{0:T(128)S(1)} %pad_add_fusion.at_ref, bf16[512,1024]{1,0:T(8,128)(2,1)S(1)} %copy-done.4, bf16[512,1024]{1,0:T(8,128)(2,1)S(1)} %copy-done.7, bf16[512,1024]{1,0:T(8,128)(2,1)S(1)} %copy-done.5, bf16[512,1024]{1,0:T(8,128)(2,1)S(1)} %copy-done.9, bf16[8,512,128]{2,1,0:T(8,128)(2,1)S(1)} %bitcast.17), custom_call_target="tpu_custom_call" | custom-call | flops 2147483648 | bytes 8388608 | tf_op jit(solution)/shard_map/pallas_call | solution.py:312
  70.1 4.6 %all-to-all-start.1 = ((f32[4,1024,128]{2,1,0:T(8,128)}), f32[4,1024,128]{2,1,0:T(8,128)S(1)}, u32[]{:S(2)}, u32[]{:S(2)}) async-start(f32[4,1024,128]{2,1,0:T(8,128)} %shard_map.90), calls=%async_computation.1 | async-start | bytes 4194304 | tf_op jit(solution)/shard_map/all_to_all | solution.py:313
  74.7 1.9 %collective-permute-start.4 = (bf16[512,32]{0,1:T(8,128)(2,1)S(1)}, bf16[512,32]{0,1:T(8,128)(2,1)S(1)}, u32[]{:S(2)}, u32[]{:S(2)}) collective-permute-start(bf16[512,32]{0,1:T(8,128)(2,1)S(1)} %get-tuple-element.29), channel_id=1, source_target_pairs={{0,4},{4,0},{1,5},{5,1},{2,6},{6,2},{3,7},{7,3},{8,12},{12,8},{9,1... | collective-permute-start | bytes 98312 | tf_op jit(solution)/shard_map/ppermute | solution.py:260
  77.2 18.9 %all-to-all-done.1.part_ref = f32[4,1024,128]{2,1,0:T(8,128)S(1)} async-done(((f32[4,1024,128]{2,1,0:T(8,128)}), f32[4,1024,128]{2,1,0:T(8,128)S(1)}, u32[]{:S(2)}, u32[]{:S(2)}) %all-to-all-start.1) | async-done | bytes 2097184 | tf_op jit(solution)/shard_map/all_to_all | solution.py:313
  96.1 2.2 %shard_map.91 = (f32[1024,128]{1,0:T(8,128)S(1)}, f32[64,128]{1,0:T(8,128)S(1)}, f32[64,4,128]{2,1,0:T(4,128)}) custom-call(s32[2]{0:T(128)S(1)} %pad_add_fusion.at_ref, f32[4,1024,128]{2,1,0:T(8,128)S(1)} %all-to-all-done.1.part_ref, f32[4,128]{1,0:T(4,128)S(1)} %get-tuple-element.31.decay_ref, f32[4,128]{1,0:T(4,128)S(1)} %get-tuple-element.30.far_ref), custom_call_target="tpu_custom_call" | custom-call | tf_op jit(solution)/shard_map/pallas_call | solution.py:326
  98.3 8.3 %all-to-all-start.2 = ((f32[64,4,128]{2,1,0:T(4,128)}), f32[64,4,128]{2,1,0:T(4,128)S(1)}, u32[]{:S(2)}, u32[]{:S(2)}) async-start(f32[64,4,128]{2,1,0:T(4,128)} %get-tuple-element.21), calls=%async_computation.2 | async-start | bytes 262144 | tf_op jit(solution)/shard_map/all_to_all | solution.py:327
  107.6 11.8 %all-to-all-done.2.states_ref = f32[64,4,128]{2,1,0:T(4,128)S(1)} async-done(((f32[64,4,128]{2,1,0:T(4,128)}), f32[64,4,128]{2,1,0:T(4,128)S(1)}, u32[]{:S(2)}, u32[]{:S(2)}) %all-to-all-start.2) | async-done | bytes 131104 | tf_op jit(solution)/shard_map/all_to_all | solution.py:327
  119.4 2.1 %shard_map.92 = bf16[4,1024,128]{2,1,0:T(8,128)(2,1)S(1)} custom-call(s32[2]{0:T(128)S(1)} %pad_add_fusion.at_ref, f32[1024,128]{1,0:T(8,128)S(1)} %get-tuple-element.19.x_ref, f32[64,128]{1,0:T(8,128)S(1)} %get-tuple-element.20.left_ref, f32[64,4,128]{2,1,0:T(4,128)S(1)} %all-to-all-done.2.states_ref, f32[64,4,128]{2,1,0:T(4,128)S(1)} %exponential_select_fusion.reach_ref, ...), custom_call_target="tpu_custom_call" | custom-call | tf_op jit(solution)/shard_map/pallas_call | solution.py:335
  121.5 14.7 %all_to_all.25.grads_ref = bf16[4,1024,128]{2,1,0:T(8,128)(2,1)S(1)} all-to-all(bf16[4,1024,128]{2,1,0:T(8,128)(2,1)S(1)} %shard_map.92), channel_id=1, replica_groups=mesh['seq_0'=8,'seq_1'=8,'seq_2'=2,'chan'=4] {'chan'}, dimensions={0} | all-to-all | bytes 2097152 | tf_op jit(solution)/shard_map/all_to_all | solution.py:336
  136.1 2.9 %shard_map.93 = bf16[8,512,128]{2,1,0:T(8,128)(2,1)S(1)} custom-call(s32[2]{0:T(128)S(1)} %pad_add_fusion.at_ref, bf16[1024,1024]{1,0:T(8,128)(2,1)S(1)} %copy-done.1, bf16[1024,1024]{1,0:T(8,128)(2,1)S(1)} %copy-done.3, bf16[4,1024,128]{2,1,0:T(8,128)(2,1)S(1)} %all_to_all.25.grads_ref), custom_call_target="tpu_custom_call" | custom-call | flops 2147483648 | bytes 8388608 | tf_op jit(solution)/shard_map/pallas_call | solution.py:346
  139.0 29.8 %all_to_all.26.part_ref = bf16[64,64,128]{2,1,0:T(8,128)(2,1)S(1)} all-to-all(bf16[64,64,128]{2,1,0:T(8,128)(2,1)S(1)} %bitcast.18), channel_id=1, replica_groups=mesh['seq_0'=8,'seq_1'=8,'seq_2'=2,'chan'=4] {'seq_0','seq_1'}, dimensions={0} | all-to-all | bytes 2097152 | tf_op jit(solution)/shard_map/all_to_all | solution.py:347
  169.6 4.7 %collective-permute-start.5 = (f32[32,128]{1,0:T(8,128)S(1)}, f32[32,128]{1,0:T(8,128)S(1)}, u32[]{:S(2)}, u32[]{:S(2)}) collective-permute-start(f32[32,128]{1,0:T(8,128)S(1)} %get-tuple-element.22), channel_id=1, source_target_pairs={{320,0},{128,1},{0,2},{384,3},{324,4},{132,5},{4,6},{388,7},{256,6... | collective-permute-start | bytes 49160 | tf_op jit(solution)/shard_map/ppermute | solution.py:257
  174.3 1.9 %collective-permute-start.6 = (f32[32,128]{1,0:T(8,128)S(1)}, f32[32,128]{1,0:T(8,128)S(1)}, u32[]{:S(2)}, u32[]{:S(2)}) collective-permute-start(f32[32,128]{1,0:T(8,128)S(1)} %get-tuple-element.23), channel_id=1, source_target_pairs={{324,0},{132,1},{4,2},{388,3},{320,4},{128,5},{0,6},{384,7},{260,6... | collective-permute-start | bytes 49160 | tf_op jit(solution)/shard_map/ppermute | solution.py:257
  176.3 3.2 %collective-permute-done.5.kept_ref = f32[32,128]{1,0:T(8,128)S(1)} collective-permute-done((f32[32,128]{1,0:T(8,128)S(1)}, f32[32,128]{1,0:T(8,128)S(1)}, u32[]{:S(2)}, u32[]{:S(2)}) %collective-permute-start.5) | collective-permute-done | bytes 16416 | tf_op jit(solution)/shard_map/ppermute | solution.py:257
  179.4 4.3 %collective-permute-done.6.given_ref = f32[32,128]{1,0:T(8,128)S(1)} collective-permute-done((f32[32,128]{1,0:T(8,128)S(1)}, f32[32,128]{1,0:T(8,128)S(1)}, u32[]{:S(2)}, u32[]{:S(2)}) %collective-permute-start.6) | collective-permute-done | bytes 16416 | tf_op jit(solution)/shard_map/ppermute | solution.py:257
  (62 shorter events, 12.0 us)
Async XLA Ops:
  0.6 33.2 %copy-start.4 = (bf16[512,1024]{1,0:T(8,128)(2,1)S(1)}, bf16[512,1024]{1,0:T(8,128)(2,1)}, u32[]{:S(2)}) copy-start(bf16[512,1024]{1,0:T(8,128)(2,1)} %own_t.1) | copy-start | bytes 3145732
  0.6 35.1 %copy-start.5 = (bf16[512,1024]{1,0:T(8,128)(2,1)S(1)}, bf16[512,1024]{1,0:T(8,128)(2,1)}, u32[]{:S(2)}) copy-start(bf16[512,1024]{1,0:T(8,128)(2,1)} %own_g.1) | copy-start | bytes 3145732
  0.7 0.9 copy-start.10
  3.0 12.8 %collective-permute-start = (bf16[32,128]{1,0:T(8,128)(2,1)S(1)}, bf16[32,128]{1,0:T(8,128)(2,1)S(1)}, u32[]{:S(2)}, u32[]{:S(2)}) collective-permute-start(bf16[32,128]{1,0:T(8,128)(2,1)S(1)} %get-tuple-element.14), channel_id=1, source_target_pairs={{0,320},{1,128},{2,0},{3,384},{4,324},{5,132},{6,4},{7,388},{64,25... | collective-permute-start | bytes 24584 | tf_op jit(solution)/shard_map/ppermute | solution.py:257
  13.9 9.2 %collective-permute-start.1 = (bf16[32,128]{1,0:T(8,128)(2,1)S(1)}, bf16[32,128]{1,0:T(8,128)(2,1)S(1)}, u32[]{:S(2)}, u32[]{:S(2)}) collective-permute-start(bf16[32,128]{1,0:T(8,128)(2,1)S(1)} %get-tuple-element.15), channel_id=1, source_target_pairs={{0,324},{1,132},{2,4},{3,388},{4,320},{5,128},{6,0},{7,384},{64,26... | collective-permute-start | bytes 24584 | tf_op jit(solution)/shard_map/ppermute | solution.py:257
  24.7 38.6 %all-to-all-start = ((bf16[64,64,128]{2,1,0:T(8,128)(2,1)}), bf16[64,64,128]{2,1,0:T(8,128)(2,1)S(1)}, u32[]{:S(2)}, u32[]{:S(2)}) async-start(bf16[64,64,128]{2,1,0:T(8,128)(2,1)} %shard_map.87), calls=%async_computation | async-start | bytes 2097152 | tf_op jit(solution)/shard_map/all_to_all | solution.py:271
  33.8 4.6 %collective-permute-start.2 = (bf16[512,1024]{1,0:T(8,128)(2,1)S(1)}, bf16[512,1024]{1,0:T(8,128)(2,1)S(1)}, u32[]{:S(2)}, u32[]{:S(2)}) collective-permute-start(bf16[512,1024]{1,0:T(8,128)(2,1)S(1)} %copy-done.4), channel_id=1, source_target_pairs={{0,4},{4,0},{1,5},{5,1},{2,6},{6,2},{3,7},{7,3},{8,12},{12,8},{9,1... | collective-permute-start | bytes 3145736 | tf_op jit(solution)/shard_map/ppermute | solution.py:260
  35.8 4.7 %collective-permute-start.3 = (bf16[512,1024]{1,0:T(8,128)(2,1)S(1)}, bf16[512,1024]{1,0:T(8,128)(2,1)S(1)}, u32[]{:S(2)}, u32[]{:S(2)}) collective-permute-start(bf16[512,1024]{1,0:T(8,128)(2,1)S(1)} %copy-done.5), channel_id=1, source_target_pairs={{0,4},{4,0},{1,5},{5,1},{2,6},{6,2},{3,7},{7,3},{8,12},{12,8},{9,1... | collective-permute-start | bytes 3145736 | tf_op jit(solution)/shard_map/ppermute | solution.py:260
  38.4 2.1 %copy-start.6 = (bf16[512,1024]{1,0:T(8,128)(2,1)}, bf16[512,1024]{1,0:T(8,128)(2,1)S(1)}, u32[]{:S(2)}) copy-start(bf16[512,1024]{1,0:T(8,128)(2,1)S(1)} %collective-permute-done.2.b_ref.other_t) | copy-start | bytes 3145732
  39.0 1.4 copy-start
  41.1 1.3 copy-start.2
  42.4 1.0 copy-start.8
  63.3 1.2 copy-start.7
  64.6 1.2 copy-start.9
  70.1 4.6 %copy-start.12 = (bf16[512,64]{0,1:T(8,128)(2,1)S(1)}, bf16[512,64]{0,1:T(8,128)(2,1)}, u32[]{:S(2)}) copy-start(bf16[512,64]{0,1:T(8,128)(2,1)} %param.11) | copy-start | bytes 196612
  70.1 6.6 %copy-start.13 = (f32[16,32]{1,0:T(8,128)S(1)}, f32[16,32]{1,0:T(8,128)}, u32[]{:S(2)}) copy-start(f32[16,32]{1,0:T(8,128)} %param.12) | copy-start | bytes 6148
  70.1 6.6 %copy-start.14 = (f32[16,32]{1,0:T(8,128)S(1)}, f32[16,32]{1,0:T(8,128)}, u32[]{:S(2)}) copy-start(f32[16,32]{1,0:T(8,128)} %param.13) | copy-start | bytes 6148
  70.1 26.1 %all-to-all-start.1 = ((f32[4,1024,128]{2,1,0:T(8,128)}), f32[4,1024,128]{2,1,0:T(8,128)S(1)}, u32[]{:S(2)}, u32[]{:S(2)}) async-start(f32[4,1024,128]{2,1,0:T(8,128)} %shard_map.90), calls=%async_computation.1 | async-start | bytes 4194304 | tf_op jit(solution)/shard_map/all_to_all | solution.py:313
  74.7 32.7 %collective-permute-start.4 = (bf16[512,32]{0,1:T(8,128)(2,1)S(1)}, bf16[512,32]{0,1:T(8,128)(2,1)S(1)}, u32[]{:S(2)}, u32[]{:S(2)}) collective-permute-start(bf16[512,32]{0,1:T(8,128)(2,1)S(1)} %get-tuple-element.29), channel_id=1, source_target_pairs={{0,4},{4,0},{1,5},{5,1},{2,6},{6,2},{3,7},{7,3},{8,12},{12,8},{9,1... | collective-permute-start | bytes 98312 | tf_op jit(solution)/shard_map/ppermute | solution.py:260
  98.3 21.0 %all-to-all-start.2 = ((f32[64,4,128]{2,1,0:T(4,128)}), f32[64,4,128]{2,1,0:T(4,128)S(1)}, u32[]{:S(2)}, u32[]{:S(2)}) async-start(f32[64,4,128]{2,1,0:T(4,128)} %get-tuple-element.21), calls=%async_computation.2 | async-start | bytes 262144 | tf_op jit(solution)/shard_map/all_to_all | solution.py:327
  119.4 16.8 %copy-start.1 = (bf16[1024,1024]{1,0:T(8,128)(2,1)S(1)}, bf16[1024,1024]{1,0:T(8,128)(2,1)}, u32[]{:S(2)}) copy-start(bf16[1024,1024]{1,0:T(8,128)(2,1)} %copy-done) | copy-start | bytes 6291460
  119.4 16.8 %copy-start.3 = (bf16[1024,1024]{1,0:T(8,128)(2,1)S(1)}, bf16[1024,1024]{1,0:T(8,128)(2,1)}, u32[]{:S(2)}) copy-start(bf16[1024,1024]{1,0:T(8,128)(2,1)} %copy-done.2) | copy-start | bytes 6291460
  169.6 9.9 %collective-permute-start.5 = (f32[32,128]{1,0:T(8,128)S(1)}, f32[32,128]{1,0:T(8,128)S(1)}, u32[]{:S(2)}, u32[]{:S(2)}) collective-permute-start(f32[32,128]{1,0:T(8,128)S(1)} %get-tuple-element.22), channel_id=1, source_target_pairs={{320,0},{128,1},{0,2},{384,3},{324,4},{132,5},{4,6},{388,7},{256,6... | collective-permute-start | bytes 49160 | tf_op jit(solution)/shard_map/ppermute | solution.py:257
  174.3 9.4 %collective-permute-start.6 = (f32[32,128]{1,0:T(8,128)S(1)}, f32[32,128]{1,0:T(8,128)S(1)}, u32[]{:S(2)}, u32[]{:S(2)}) collective-permute-start(f32[32,128]{1,0:T(8,128)S(1)} %get-tuple-element.23), channel_id=1, source_target_pairs={{324,0},{132,1},{4,2},{388,3},{320,4},{128,5},{0,6},{384,7},{260,6... | collective-permute-start | bytes 49160 | tf_op jit(solution)/shard_map/ppermute | solution.py:257
  (1 other events, 0.7 us)

commit v3 on v2

--- a/solution.py
+++ b/solution.py
@@ -34,12 +34,16 @@
     )
 
 
-def holder(plane, c, l):
-    e = lax.rem(c + len(OFFSETS) - plane, len(OFFSETS))
-    o = OFFSETS[0][l]
-    for k in range(1, len(OFFSETS)):
-        o = jnp.where(e == k, OFFSETS[k][l], o)
-    return lax.rem(2 * plane + o, 2 * len(OFFSETS))
+def holder(plane, e, l):
+    return lax.rem(2 * plane + OFFSETS[e][l], 2 * len(OFFSETS))
+
+
+def chunk_of(plane, e):
+    return lax.rem(plane + e, len(OFFSETS))
+
+
+def in_hbm(x):
+    return pltpu.with_memory_space_constraint(x, pltpu.HBM)
 
 
 def lane_group(shape):
@@ -96,9 +100,9 @@
     first = at_ref[0] == 0
     low = jnp.where(first, kept_ref[...], given_ref[...])
     high = jnp.where(first, given_ref[...], kept_ref[...])
-    for s in range(GROUPS):
-        left = low if s == 0 else turn(low, 128 - 32 * s)
-        right = high if s == 1 else turn(high, (160 - 32 * s) % 128)
+    for s, group in enumerate((0, 3, 2, 1)):
+        left = low if group == 0 else turn(low, 128 - 32 * group)
+        right = high if group == 1 else turn(high, (160 - 32 * group) % 128)
         both = jnp.where(lane_group(low.shape) == 0, left, right)[:, : out_w_ref.shape[1]]
         if s < 3:
             in_ref[s] = both
@@ -106,26 +110,41 @@
             out_w_ref[...] = both
 
 
-def project_body(at_ref, own_t, other_t, own_g, other_g, w_ref, out_ref):
+def project_body(at_ref, own_t, other_t, own_g, other_g, w_ref, out_ref, late_ref):
+    plane = at_ref[1]
     half = own_t.shape[0]
-    plane = at_ref[1]
-
-    def columns(c):
-        return jnp.concatenate([w_ref[holder(plane, c, l)] for l in range(2)], axis=0)
-
-    for c in range(0, out_ref.shape[0], 2):
-        w = jnp.concatenate([columns(c), columns(c + 1)], axis=1)
-        for at, (t_ref, g_ref) in enumerate(((own_t, own_g), (other_t, other_g))):
+
+    def columns(e):
+        return jnp.concatenate([w_ref[holder(plane, e, l)] for l in range(2)], axis=0)
+
+    for e in range(0, out_ref.shape[0], 2):
+        w = jnp.concatenate([columns(e), columns(e + 1)], axis=1)
+        both = []
+        for t_ref, g_ref in ((own_t, own_g), (other_t, other_g)):
             from_t = jnp.dot(t_ref[...], w, preferred_element_type=F32)
             from_g = jnp.dot(g_ref[...], w, preferred_element_type=F32)
-            both = jnp.where(lane_group(from_t.shape) % GROUPS < 3, from_t, from_g)
-            out_ref[c, at * half : (at + 1) * half] = both[:, :128]
-            out_ref[c + 1, at * half : (at + 1) * half] = both[:, 128:]
-
-
-def signal_of(x):
+            both.append(jnp.where(lane_group(from_t.shape) % GROUPS < 3, from_t, from_g))
+        for k in range(2):
+            own, other = (b[:, 128 * k : 128 * (k + 1)] for b in both)
+            odd = lane_group(own.shape) % 2 == 1
+            chunk = chunk_of(plane, e + k)
+            early = jnp.where(odd, own, turn(other, 96))
+            high = early.astype(BF16)
+            late = jnp.where(odd, turn(other, 32), own)
+            out_ref[chunk, :half] = high
+            out_ref[chunk, half : 2 * half] = (early - high.astype(F32)).astype(BF16)
+            out_ref[chunk, 2 * half :] = late.astype(BF16)
+            if e + k == 0:
+                late_ref[...] = late
+
+
+def store_signal(x, sig):
+    half = x.shape[0]
     product = x * turn(x, 64)
-    return jnp.where(lane_group(x.shape) % 2 == 1, product, turn(product, 32))
+    turned = turn(product, 32)
+    odd = lane_group(x.shape) % 2 == 1
+    sig[:half] = jnp.where(odd, product, turned)
+    sig[half:] = jnp.where(odd, turned, product)
 
 
 def chunk_rows(core, q_half, step, rows):
@@ -134,16 +153,22 @@
     return pl.ds(start + step, half // STEPS, stride=STEPS)
 
 
-def first_body(at_ref, part_ref, decay_ref, far_ref, x_ref, left_ref, state_ref, sig, st):
+def first_body(
+    at_ref, part_ref, own_late_ref, decay_ref, far_ref, x_ref, late_ref, left_ref, state_ref, sig, st
+):
     core = at_ref[0]
-    rows = x_ref.shape[0]
-    total = part_ref[0]
-    for k in range(1, part_ref.shape[0]):
-        total = total + part_ref[k]
+    rows = sig.shape[0]
+    half = rows // 2
+    total = jnp.zeros(x_ref.shape, F32)
+    late = own_late_ref[...]
+    for k in range(part_ref.shape[0]):
+        total = total + (part_ref[k, :half].astype(F32) + part_ref[k, half : 2 * half].astype(F32))
+        late = late + jnp.where(at_ref[1] == k, 0.0, part_ref[k, 2 * half :].astype(F32))
+    late_ref[...] = late.astype(BF16).astype(F32)
     rounded = total.astype(BF16).astype(F32)
-    x = jnp.where(lane_group(total.shape) < 3, rounded, total)
+    x = jnp.where(lane_group(total.shape) < 2, rounded, total)
     x_ref[...] = x
-    sig[...] = signal_of(x)
+    store_signal(x, sig)
     decay = [decay_ref[m : m + 1, :] for m in range(MODE_ROWS)]
     chunks = rows // STEPS
     per = chunks // 2
@@ -170,14 +195,15 @@
 
 
 def second_body(
-    at_ref, x_ref, left_ref, states_ref, reach_ref, power_ref, decay_ref, weight_ref, conv_ref,
-    out_ref, sig, ys,
+    at_ref, x_ref, late_ref, left_ref, states_ref, reach_ref, power_ref, decay_ref, weight_ref,
+    conv_ref, out_ref, sig, ys,
 ):
     core = at_ref[0]
-    rows = x_ref.shape[0]
+    rows = sig.shape[0]
+    half = rows // 2
     chunks = rows // STEPS
     per = chunks // 2
-    sig[...] = signal_of(x_ref[...])
+    store_signal(x_ref[...], sig)
     carry = jnp.sum(states_ref[...] * reach_ref[...], axis=0)
     decay = [decay_ref[m : m + 1, :] for m in range(MODE_ROWS)]
     weight = [weight_ref[m : m + 1, :] for m in range(MODE_ROWS)]
@@ -204,8 +230,12 @@
     y = ys[...]
     y = y + turn(y, 64)
     y = y + turn(y, 32)
-    factor = jnp.where(lane_group(y.shape) % 2 == 0, y, conv_ref[...].astype(F32))
-    out = (turn(x_ref[...], 64) * factor).astype(BF16)
+    odd = lane_group((half, 128)) % 2 == 1
+    late = turn(late_ref[...], 64) * jnp.where(odd, y[half:], y[:half])
+    early = x_ref[...] * conv_ref[...].astype(F32)
+    own = jnp.where(odd, early, late)
+    other = turn(jnp.where(odd, late, turn(early, 64)), 96)
+    out = jnp.concatenate([own, other], axis=0).astype(BF16)
     for k in range(out_ref.shape[0]):
         out_ref[k] = out
 
@@ -216,10 +246,10 @@
     for l in range(2):
         r = l * block
         for c in range(0, grads_ref.shape[0], 2):
-            g = jnp.concatenate([grads_ref[c], grads_ref[c + 1]], axis=1)
+            g = jnp.concatenate([grads_ref[chunk_of(plane, c + k)] for k in range(2)], axis=1)
             from_t = jnp.dot(tt_ref[r : r + block, :], g, preferred_element_type=F32)
             from_g = jnp.dot(gt_ref[r : r + block, :], g, preferred_element_type=F32)
-            both = jnp.where(lane_group(from_t.shape) % GROUPS < 3, from_t, from_g).astype(BF16)
+            both = jnp.where(lane_group(from_t.shape) % GROUPS != 1, from_t, from_g).astype(BF16)
             out_ref[holder(plane, c, l)] = both[:, :128]
             out_ref[holder(plane, c + 1, l)] = both[:, 128:]
 
@@ -261,21 +291,25 @@
 
     piece = jax.ShapeDtypeStruct((owned, 128), BF16)
     kept, given = call(pack_body, (piece, piece), 4, inputs=3)(
-        at, in_weight.transpose(1, 0, 2), out_weight
+        at, in_hbm(in_weight.transpose(1, 0, 2)), in_hbm(out_weight)
     )
     kept = transposed(kept, False, False)
     given = transposed(given, True, False)
+    tokens_too = swapped(tokens)
+    grads_too = swapped(grad_out)
+    kept, given, tokens_too, grads_too = lax.optimization_barrier(
+        (kept, given, tokens_too, grads_too)
+    )
     spread = call(
         spread_body, jax.ShapeDtypeStruct((chips, 2 * owned, 128), BF16), 4, inputs=3
     )(at, kept, given)
     weights = lax.all_to_all(spread, CHIPS, 0, 0, tiled=True).reshape(size_z, -1, 128)
 
-    tokens_too = swapped(tokens)
-    grads_too = swapped(grad_out)
+
     conv_own = jnp.where(core == 0, conv_out[:, :mine], conv_out[:, mine:])
     conv_sent = jnp.where(core == 0, conv_out[:, mine:], conv_out[:, :mine])
-    conv = jnp.concatenate([conv_own, swapped(conv_sent)], axis=0)
-    conv = jnp.tile(conv, (1, GROUPS))
+    conv = jnp.concatenate([swapped(conv_sent), conv_own], axis=1)
+    conv = jnp.tile(conv, (1, 2))
     flip = call(
         transpose_body, jax.ShapeDtypeStruct((depth, rows), BF16), 8, moved=4 * depth * rows
     )
@@ -302,37 +336,40 @@
 
     project = call(
         project_body,
-        jax.ShapeDtypeStruct((size_x, rows, 128), F32),
+        (pltpu.HBM((size_x, 3 * half, 128), BF16), jax.ShapeDtypeStruct((half, 128), F32)),
         48,
         inputs=6,
         flops=4 * rows * depth * size_x * 128,
         moved=8 * rows * depth,
     )
     weights, tokens_t, grads_t = lax.optimization_barrier((weights, tokens_t, grads_t))
-    parts = project(at, tokens, tokens_too, grad_out, grads_too, weights)
+    parts, own_late = project(
+        at, in_hbm(tokens), in_hbm(tokens_too), in_hbm(grad_out), in_hbm(grads_too), weights
+    )
     parts = lax.all_to_all(parts, "chan", 0, 0, tiled=True)
 
     first = call(
         first_body,
         (
-            jax.ShapeDtypeStruct((rows, 128), F32),
+            jax.ShapeDtypeStruct((half, 128), F32),
+            jax.ShapeDtypeStruct((half, 128), F32),
             jax.ShapeDtypeStruct((MODE_ROWS * chunks, 128), F32),
             jax.ShapeDtypeStruct((chips, MODE_ROWS, 128), F32),
         ),
         10,
         scratch=[pltpu.VMEM((rows, 128), F32), pltpu.VMEM((MODE_ROWS * chunks, 128), F32)],
-        inputs=4,
-    )
-    x, left, state = first(at, parts, decay, far)
+        inputs=5,
+    )
+    x, late, left, state = first(at, parts, own_late, decay, far)
     states = lax.all_to_all(state, CHIPS, 0, 0, tiled=True)
     second = call(
         second_body,
         jax.ShapeDtypeStruct((size_x, rows, 128), BF16),
         10,
         scratch=[pltpu.VMEM((rows, 128), F32), pltpu.VMEM((rows, 128), F32)],
-        inputs=9,
-    )
-    grads = second(at, x, left, states, reach, power, decay, weight, conv)
+        inputs=10,
+    )
+    grads = second(at, x, late, left, states, reach, power, decay, weight, conv)
     grads = lax.all_to_all(grads, "chan", 0, 0, tiled=True)
 
     weigh = call(

time: 186 us -> 184 us (0.989)
  local copies, waits for them, and re-layouts: 8.67 us -> 6.46 us
    all_to_all x1, waiting for transfers between devices: 18.9 us -> 13.8 us  [local(): parts = lax.all_to_all(parts, 'chan', 0, 0, tiled=True)]
    all_to_all x1, waiting for transfers between devices: 20 us -> 24.7 us  [local(): lax.all_to_all(spread, CHIPS, 0, 0, tiled=True).reshape(size_z, -1, 128)]
    unnamed x30 -> x26, local copies, waits for them, and re-layouts: 7.67 us -> 5.51 us
  transfers between devices with their start and end apart: 10 -> 10, of which waited for: 8 -> 6; matrix products, arithmetic and copies ran while one was open for 1% -> 1% of each run, Pallas kernels for 2% -> 2%
where the time goes in v3:
time: 184 us
  waiting for transfers between devices  65 us (35%)
  starting transfers between devices  47.6 us (26%)
  blocking collectives  44.3 us (24%)
  Pallas kernels  18.8 us (10%)
  local copies, waits for them, and re-layouts  6.46 us (4%)
    all_to_all x1, blocking collectives, local(): partial = lax.all_to_all(partial, CHIPS, 0, 0, tiled=True)  29.7 us
    all_to_all x1, waiting for transfers between devices, local(): lax.all_to_all(spread, CHIPS, 0, 0, tiled=True).reshape(size_z, -1, 128)  24.7 us
    ppermute x4, starting transfers between devices, transposed(): return lax.ppermute(value, ('seq_0', 'seq_2', 'chan'), pairs)  19.4 us
    ppermute x4, waiting for transfers between devices, transposed(): return lax.ppermute(value, ('seq_0', 'seq_2', 'chan'), pairs)  14.7 us
    all_to_all x1, blocking collectives, local(): grads = lax.all_to_all(grads, 'chan', 0, 0, tiled=True)  14.6 us
    all_to_all x1, waiting for transfers between devices, local(): parts = lax.all_to_all(parts, 'chan', 0, 0, tiled=True)  13.8 us
    all_to_all x1, waiting for transfers between devices, local(): states = lax.all_to_all(state, CHIPS, 0, 0, tiled=True)  11.8 us
    all_to_all x1, starting transfers between devices, local(): lax.all_to_all(spread, CHIPS, 0, 0, tiled=True).reshape(size_z, -1, 128)  9.17 us
  transfers between devices with their start and end apart: 10, of which 6 were waited for; matrix products, arithmetic and copies ran while one was open for 1% of the time, Pallas kernels for 2%

profile of v3, /device:TPU:6, one launch (start us, length us, event | category | flops | bytes accessed | tf_op | source)
XLA Modules:
  0.0 183.7 jit_solution(7563794313190293797)
XLA Ops:
  0.6 2.1 %collective-permute-start.2 = (bf16[512,1024]{1,0:T(8,128)(2,1)}, bf16[512,1024]{1,0:T(8,128)(2,1)S(1)}, u32[]{:S(2)}, u32[]{:S(2)}) collective-permute-start(bf16[512,1024]{1,0:T(8,128)(2,1)} %own_t.1), channel_id=1, source_target_pairs={{0,4},{4,0},{1,5},{5,1},{2,6},{6,2},{3,7},{7,3},{8,12},{12,8},{9,1... | collective-permute-start | bytes 3145736 | tf_op jit(solution)/shard_map/ppermute | solution.py:290
  2.7 2.4 %collective-permute-start.3 = (bf16[512,1024]{1,0:T(8,128)(2,1)}, bf16[512,1024]{1,0:T(8,128)(2,1)S(1)}, u32[]{:S(2)}, u32[]{:S(2)}) collective-permute-start(bf16[512,1024]{1,0:T(8,128)(2,1)} %own_g.1), channel_id=1, source_target_pairs={{0,4},{4,0},{1,5},{5,1},{2,6},{6,2},{3,7},{7,3},{8,12},{12,8},{9,1... | collective-permute-start | bytes 3145736 | tf_op jit(solution)/shard_map/ppermute | solution.py:290
  6.1 10.9 %collective-permute-start = (bf16[32,128]{1,0:T(8,128)(2,1)S(1)}, bf16[32,128]{1,0:T(8,128)(2,1)S(1)}, u32[]{:S(2)}, u32[]{:S(2)}) collective-permute-start(bf16[32,128]{1,0:T(8,128)(2,1)S(1)} %get-tuple-element.21), channel_id=1, source_target_pairs={{0,320},{1,128},{2,0},{3,384},{4,324},{5,132},{6,4},{7,388},{64,25... | collective-permute-start | bytes 24584 | tf_op jit(solution)/shard_map/ppermute | solution.py:287
  17.0 1.9 %collective-permute-start.1 = (bf16[32,128]{1,0:T(8,128)(2,1)S(1)}, bf16[32,128]{1,0:T(8,128)(2,1)S(1)}, u32[]{:S(2)}, u32[]{:S(2)}) collective-permute-start(bf16[32,128]{1,0:T(8,128)(2,1)S(1)} %get-tuple-element.22), channel_id=1, source_target_pairs={{0,324},{1,132},{2,4},{3,388},{4,320},{5,128},{6,0},{7,384},{64,26... | collective-permute-start | bytes 24584 | tf_op jit(solution)/shard_map/ppermute | solution.py:287
  18.9 7.3 %collective-permute-done.1.given_ref = bf16[32,128]{1,0:T(8,128)(2,1)S(1)} collective-permute-done((bf16[32,128]{1,0:T(8,128)(2,1)S(1)}, bf16[32,128]{1,0:T(8,128)(2,1)S(1)}, u32[]{:S(2)}, u32[]{:S(2)}) %collective-permute-start.1) | collective-permute-done | bytes 8224 | tf_op jit(solution)/shard_map/ppermute | solution.py:287
  26.2 1.7 shard_map.87
  27.9 9.2 %all-to-all-start = ((bf16[64,64,128]{2,1,0:T(8,128)(2,1)}), bf16[64,64,128]{2,1,0:T(8,128)(2,1)S(1)}, u32[]{:S(2)}, u32[]{:S(2)}) async-start(bf16[64,64,128]{2,1,0:T(8,128)(2,1)} %shard_map.87), calls=%async_computation | async-start | bytes 2097152 | tf_op jit(solution)/shard_map/all_to_all | solution.py:306
  42.3 24.7 %all-to-all-done = bf16[64,64,128]{2,1,0:T(8,128)(2,1)S(1)} async-done(((bf16[64,64,128]{2,1,0:T(8,128)(2,1)}), bf16[64,64,128]{2,1,0:T(8,128)(2,1)S(1)}, u32[]{:S(2)}, u32[]{:S(2)}) %all-to-all-start) | async-done | bytes 1048608 | tf_op jit(solution)/shard_map/all_to_all | solution.py:306
  67.0 5.8 %shard_map.90 = (bf16[4,1536,128]{2,1,0:T(8,128)(2,1)}, f32[512,128]{1,0:T(8,128)S(1)}) custom-call(s32[2]{0:T(128)S(1)} %pad_add_fusion.at_ref, bf16[512,1024]{1,0:T(8,128)(2,1)} %own_t.1, bf16[512,1024]{1,0:T(8,128)(2,1)} %copy-done.6, bf16[512,1024]{1,0:T(8,128)(2,1)} %own_g.1, bf16[512,1024]{1,0:T(8,128)(2,1)} %copy-done.8, bf16[8,512,128]{2,1,0:T(8,128)(2,1)S(1)} %bitcast.17), custom_call_target="tpu_custom_call" | custom-call | flops 2147483648 | bytes 8388608 | tf_op jit(solution)/shard_map/pallas_call | solution.py:346
  72.9 4.6 %all-to-all-start.1 = ((bf16[4,1536,128]{2,1,0:T(8,128)(2,1)}), bf16[4,1536,128]{2,1,0:T(8,128)(2,1)S(1)}, u32[]{:S(2)}, u32[]{:S(2)}) async-start(bf16[4,1536,128]{2,1,0:T(8,128)(2,1)} %get-tuple-element.30), calls=%async_computation.1 | async-start | bytes 3145728 | tf_op jit(solution)/shard_map/all_to_all | solution.py:349
  77.5 1.9 %collective-permute-start.4 = (bf16[512,32]{0,1:T(8,128)(2,1)S(1)}, bf16[512,32]{0,1:T(8,128)(2,1)S(1)}, u32[]{:S(2)}, u32[]{:S(2)}) collective-permute-start(bf16[512,32]{0,1:T(8,128)(2,1)S(1)} %get-tuple-element.42), channel_id=1, source_target_pairs={{0,4},{4,0},{1,5},{5,1},{2,6},{6,2},{3,7},{7,3},{8,12},{12,8},{9,1... | collective-permute-start | bytes 98312 | tf_op jit(solution)/shard_map/ppermute | solution.py:290
  80.0 13.8 %all-to-all-done.1.part_ref = bf16[4,1536,128]{2,1,0:T(8,128)(2,1)S(1)} async-done(((bf16[4,1536,128]{2,1,0:T(8,128)(2,1)}), bf16[4,1536,128]{2,1,0:T(8,128)(2,1)S(1)}, u32[]{:S(2)}, u32[]{:S(2)}) %all-to-all-start.1) | async-done | bytes 1572896 | tf_op jit(solution)/shard_map/all_to_all | solution.py:349
  93.7 2.3 %shard_map.91 = (f32[512,128]{1,0:T(8,128)S(1)}, f32[512,128]{1,0:T(8,128)S(1)}, f32[64,128]{1,0:T(8,128)S(1)}, f32[64,4,128]{2,1,0:T(4,128)}) custom-call(s32[2]{0:T(128)S(1)} %pad_add_fusion.at_ref, bf16[4,1536,128]{2,1,0:T(8,128)(2,1)S(1)} %all-to-all-done.1.part_ref, f32[512,128]{1,0:T(8,128)S(1)} %get-tuple-element.31.own_late_ref, ...), custom_call_target="tpu_custom_call" | custom-call | tf_op jit(solution)/shard_map/pallas_call | solution.py:363
  96.0 8.0 %all-to-all-start.2 = ((f32[64,4,128]{2,1,0:T(4,128)}), f32[64,4,128]{2,1,0:T(4,128)S(1)}, u32[]{:S(2)}, u32[]{:S(2)}) async-start(f32[64,4,128]{2,1,0:T(4,128)} %get-tuple-element.35), calls=%async_computation.2 | async-start | bytes 262144 | tf_op jit(solution)/shard_map/all_to_all | solution.py:364
  104.9 11.8 %all-to-all-done.2.states_ref = f32[64,4,128]{2,1,0:T(4,128)S(1)} async-done(((f32[64,4,128]{2,1,0:T(4,128)}), f32[64,4,128]{2,1,0:T(4,128)S(1)}, u32[]{:S(2)}, u32[]{:S(2)}) %all-to-all-start.2) | async-done | bytes 131104 | tf_op jit(solution)/shard_map/all_to_all | solution.py:364
  116.8 2.0 %shard_map.92 = bf16[4,1024,128]{2,1,0:T(8,128)(2,1)S(1)} custom-call(s32[2]{0:T(128)S(1)} %pad_add_fusion.at_ref, f32[512,128]{1,0:T(8,128)S(1)} %get-tuple-element.32.x_ref, f32[512,128]{1,0:T(8,128)S(1)} %get-tuple-element.33.late_ref, f32[64,128]{1,0:T(8,128)S(1)} %get-tuple-element.34.left_ref, f32[64,4,128]{2,1,0:T(4,128)S(1)} %all-to-all-done.2.states_ref, ...), custom_call_target="tpu_custom_call" | custom-call | tf_op jit(solution)/shard_map/pallas_call | solution.py:372
  118.8 14.6 %all_to_all.25.grads_ref = bf16[4,1024,128]{2,1,0:T(8,128)(2,1)S(1)} all-to-all(bf16[4,1024,128]{2,1,0:T(8,128)(2,1)S(1)} %shard_map.92), channel_id=1, replica_groups=mesh['seq_0'=8,'seq_1'=8,'seq_2'=2,'chan'=4] {'chan'}, dimensions={0} | all-to-all | bytes 2097152 | tf_op jit(solution)/shard_map/all_to_all | solution.py:373
  133.3 1.6 copy-done.3
  134.9 2.9 %shard_map.93 = bf16[8,512,128]{2,1,0:T(8,128)(2,1)S(1)} custom-call(s32[2]{0:T(128)S(1)} %pad_add_fusion.at_ref, bf16[1024,1024]{1,0:T(8,128)(2,1)S(1)} %copy-done.1, bf16[1024,1024]{1,0:T(8,128)(2,1)S(1)} %copy-done.3, bf16[4,1024,128]{2,1,0:T(8,128)(2,1)S(1)} %all_to_all.25.grads_ref), custom_call_target="tpu_custom_call" | custom-call | flops 2147483648 | bytes 8388608 | tf_op jit(solution)/shard_map/pallas_call | solution.py:383
  137.9 29.7 %all_to_all.26.part_ref = bf16[64,64,128]{2,1,0:T(8,128)(2,1)S(1)} all-to-all(bf16[64,64,128]{2,1,0:T(8,128)(2,1)S(1)} %bitcast.18), channel_id=1, replica_groups=mesh['seq_0'=8,'seq_1'=8,'seq_2'=2,'chan'=4] {'seq_0','seq_1'}, dimensions={0} | all-to-all | bytes 2097152 | tf_op jit(solution)/shard_map/all_to_all | solution.py:384
  168.3 4.7 %collective-permute-start.5 = (f32[32,128]{1,0:T(8,128)S(1)}, f32[32,128]{1,0:T(8,128)S(1)}, u32[]{:S(2)}, u32[]{:S(2)}) collective-permute-start(f32[32,128]{1,0:T(8,128)S(1)} %get-tuple-element.36), channel_id=1, source_target_pairs={{320,0},{128,1},{0,2},{384,3},{324,4},{132,5},{4,6},{388,7},{256,6... | collective-permute-start | bytes 49160 | tf_op jit(solution)/shard_map/ppermute | solution.py:287
  173.1 1.9 %collective-permute-start.6 = (f32[32,128]{1,0:T(8,128)S(1)}, f32[32,128]{1,0:T(8,128)S(1)}, u32[]{:S(2)}, u32[]{:S(2)}) collective-permute-start(f32[32,128]{1,0:T(8,128)S(1)} %get-tuple-element.37), channel_id=1, source_target_pairs={{324,0},{132,1},{4,2},{388,3},{320,4},{128,5},{0,6},{384,7},{260,6... | collective-permute-start | bytes 49160 | tf_op jit(solution)/shard_map/ppermute | solution.py:287
  175.0 3.2 %collective-permute-done.5.kept_ref = f32[32,128]{1,0:T(8,128)S(1)} collective-permute-done((f32[32,128]{1,0:T(8,128)S(1)}, f32[32,128]{1,0:T(8,128)S(1)}, u32[]{:S(2)}, u32[]{:S(2)}) %collective-permute-start.5) | collective-permute-done | bytes 16416 | tf_op jit(solution)/shard_map/ppermute | solution.py:287
  178.2 4.3 %collective-permute-done.6.given_ref = f32[32,128]{1,0:T(8,128)S(1)} collective-permute-done((f32[32,128]{1,0:T(8,128)S(1)}, f32[32,128]{1,0:T(8,128)S(1)}, u32[]{:S(2)}, u32[]{:S(2)}) %collective-permute-start.6) | collective-permute-done | bytes 16416 | tf_op jit(solution)/shard_map/ppermute | solution.py:287
  (58 shorter events, 9.5 us)
Async XLA Ops:
  0.6 36.5 %copy-start.4 = (bf16[512,1024]{1,0:T(8,128)(2,1)S(1)}, bf16[512,1024]{1,0:T(8,128)(2,1)}, u32[]{:S(2)}) copy-start(bf16[512,1024]{1,0:T(8,128)(2,1)} %own_t.1) | copy-start | bytes 3145732
  0.6 25.5 %collective-permute-start.2 = (bf16[512,1024]{1,0:T(8,128)(2,1)}, bf16[512,1024]{1,0:T(8,128)(2,1)S(1)}, u32[]{:S(2)}, u32[]{:S(2)}) collective-permute-start(bf16[512,1024]{1,0:T(8,128)(2,1)} %own_t.1), channel_id=1, source_target_pairs={{0,4},{4,0},{1,5},{5,1},{2,6},{6,2},{3,7},{7,3},{8,12},{12,8},{9,1... | collective-permute-start | bytes 3145736 | tf_op jit(solution)/shard_map/ppermute | solution.py:290
  2.7 23.5 %collective-permute-start.3 = (bf16[512,1024]{1,0:T(8,128)(2,1)}, bf16[512,1024]{1,0:T(8,128)(2,1)S(1)}, u32[]{:S(2)}, u32[]{:S(2)}) collective-permute-start(bf16[512,1024]{1,0:T(8,128)(2,1)} %own_g.1), channel_id=1, source_target_pairs={{0,4},{4,0},{1,5},{5,1},{2,6},{6,2},{3,7},{7,3},{8,12},{12,8},{9,1... | collective-permute-start | bytes 3145736 | tf_op jit(solution)/shard_map/ppermute | solution.py:290
  6.1 12.8 %collective-permute-start = (bf16[32,128]{1,0:T(8,128)(2,1)S(1)}, bf16[32,128]{1,0:T(8,128)(2,1)S(1)}, u32[]{:S(2)}, u32[]{:S(2)}) collective-permute-start(bf16[32,128]{1,0:T(8,128)(2,1)S(1)} %get-tuple-element.21), channel_id=1, source_target_pairs={{0,320},{1,128},{2,0},{3,384},{4,324},{5,132},{6,4},{7,388},{64,25... | collective-permute-start | bytes 24584 | tf_op jit(solution)/shard_map/ppermute | solution.py:287
  17.0 9.2 %collective-permute-start.1 = (bf16[32,128]{1,0:T(8,128)(2,1)S(1)}, bf16[32,128]{1,0:T(8,128)(2,1)S(1)}, u32[]{:S(2)}, u32[]{:S(2)}) collective-permute-start(bf16[32,128]{1,0:T(8,128)(2,1)S(1)} %get-tuple-element.22), channel_id=1, source_target_pairs={{0,324},{1,132},{2,4},{3,388},{4,320},{5,128},{6,0},{7,384},{64,26... | collective-permute-start | bytes 24584 | tf_op jit(solution)/shard_map/ppermute | solution.py:287
  26.2 1.7 copy-start.6
  26.2 1.7 copy-start.8
  27.9 39.1 %all-to-all-start = ((bf16[64,64,128]{2,1,0:T(8,128)(2,1)}), bf16[64,64,128]{2,1,0:T(8,128)(2,1)S(1)}, u32[]{:S(2)}, u32[]{:S(2)}) async-start(bf16[64,64,128]{2,1,0:T(8,128)(2,1)} %shard_map.87), calls=%async_computation | async-start | bytes 2097152 | tf_op jit(solution)/shard_map/all_to_all | solution.py:306
  37.1 1.2 copy-start.7
  38.3 2.0 %copy-start.5 = (bf16[512,1024]{1,0:T(8,128)(2,1)S(1)}, bf16[512,1024]{1,0:T(8,128)(2,1)}, u32[]{:S(2)}) copy-start(bf16[512,1024]{1,0:T(8,128)(2,1)} %own_g.1) | copy-start | bytes 3145732
  38.3 2.0 %copy-start.9 = (bf16[512,1024]{1,0:T(8,128)(2,1)S(1)}, bf16[512,1024]{1,0:T(8,128)(2,1)}, u32[]{:S(2)}) copy-start(bf16[512,1024]{1,0:T(8,128)(2,1)} %copy-done.8) | copy-start | bytes 3145732
  39.0 1.4 copy-start
  41.0 1.3 copy-start.2
  72.8 4.7 %copy-start.10 = (bf16[512,64]{0,1:T(8,128)(2,1)S(1)}, bf16[512,64]{0,1:T(8,128)(2,1)}, u32[]{:S(2)}) copy-start(bf16[512,64]{0,1:T(8,128)(2,1)} %param.11) | copy-start | bytes 196612
  72.8 6.6 %copy-start.11 = (f32[16,32]{1,0:T(8,128)S(1)}, f32[16,32]{1,0:T(8,128)}, u32[]{:S(2)}) copy-start(f32[16,32]{1,0:T(8,128)} %param.12) | copy-start | bytes 6148
  72.9 6.6 %copy-start.12 = (f32[16,32]{1,0:T(8,128)S(1)}, f32[16,32]{1,0:T(8,128)}, u32[]{:S(2)}) copy-start(f32[16,32]{1,0:T(8,128)} %param.13) | copy-start | bytes 6148
  72.9 20.9 %all-to-all-start.1 = ((bf16[4,1536,128]{2,1,0:T(8,128)(2,1)}), bf16[4,1536,128]{2,1,0:T(8,128)(2,1)S(1)}, u32[]{:S(2)}, u32[]{:S(2)}) async-start(bf16[4,1536,128]{2,1,0:T(8,128)(2,1)} %get-tuple-element.30), calls=%async_computation.1 | async-start | bytes 3145728 | tf_op jit(solution)/shard_map/all_to_all | solution.py:349
  77.5 27.3 %collective-permute-start.4 = (bf16[512,32]{0,1:T(8,128)(2,1)S(1)}, bf16[512,32]{0,1:T(8,128)(2,1)S(1)}, u32[]{:S(2)}, u32[]{:S(2)}) collective-permute-start(bf16[512,32]{0,1:T(8,128)(2,1)S(1)} %get-tuple-element.42), channel_id=1, source_target_pairs={{0,4},{4,0},{1,5},{5,1},{2,6},{6,2},{3,7},{7,3},{8,12},{12,8},{9,1... | collective-permute-start | bytes 98312 | tf_op jit(solution)/shard_map/ppermute | solution.py:290
  96.0 20.8 %all-to-all-start.2 = ((f32[64,4,128]{2,1,0:T(4,128)}), f32[64,4,128]{2,1,0:T(4,128)S(1)}, u32[]{:S(2)}, u32[]{:S(2)}) async-start(f32[64,4,128]{2,1,0:T(4,128)} %get-tuple-element.35), calls=%async_computation.2 | async-start | bytes 262144 | tf_op jit(solution)/shard_map/all_to_all | solution.py:364
  104.9 28.4 %copy-start.1 = (bf16[1024,1024]{1,0:T(8,128)(2,1)S(1)}, bf16[1024,1024]{1,0:T(8,128)(2,1)}, u32[]{:S(2)}) copy-start(bf16[1024,1024]{1,0:T(8,128)(2,1)} %copy-done) | copy-start | bytes 6291460
  133.3 1.6 copy-start.3
  168.3 9.9 %collective-permute-start.5 = (f32[32,128]{1,0:T(8,128)S(1)}, f32[32,128]{1,0:T(8,128)S(1)}, u32[]{:S(2)}, u32[]{:S(2)}) collective-permute-start(f32[32,128]{1,0:T(8,128)S(1)} %get-tuple-element.36), channel_id=1, source_target_pairs={{320,0},{128,1},{0,2},{384,3},{324,4},{132,5},{4,6},{388,7},{256,6... | collective-permute-start | bytes 49160 | tf_op jit(solution)/shard_map/ppermute | solution.py:287
  173.1 9.4 %collective-permute-start.6 = (f32[32,128]{1,0:T(8,128)S(1)}, f32[32,128]{1,0:T(8,128)S(1)}, u32[]{:S(2)}, u32[]{:S(2)}) collective-permute-start(f32[32,128]{1,0:T(8,128)S(1)} %get-tuple-element.37), channel_id=1, source_target_pairs={{324,0},{132,1},{4,2},{388,3},{320,4},{128,5},{0,6},{384,7},{260,6... | collective-permute-start | bytes 49160 | tf_op jit(solution)/shard_map/ppermute | solution.py:287

commit v4 on v3

--- a/solution.py
+++ b/solution.py
@@ -110,7 +110,7 @@
             out_w_ref[...] = both
 
 
-def project_body(at_ref, own_t, other_t, own_g, other_g, w_ref, out_ref, late_ref):
+def project_body(at_ref, own_t, other_t, own_g, other_g, w_ref, out_ref, own_ref):
     plane = at_ref[1]
     half = own_t.shape[0]
 
@@ -129,13 +129,12 @@
             odd = lane_group(own.shape) % 2 == 1
             chunk = chunk_of(plane, e + k)
             early = jnp.where(odd, own, turn(other, 96))
-            high = early.astype(BF16)
             late = jnp.where(odd, turn(other, 32), own)
-            out_ref[chunk, :half] = high
-            out_ref[chunk, half : 2 * half] = (early - high.astype(F32)).astype(BF16)
-            out_ref[chunk, 2 * half :] = late.astype(BF16)
+            out_ref[chunk, :half] = early.astype(BF16)
+            out_ref[chunk, half:] = late.astype(BF16)
             if e + k == 0:
-                late_ref[...] = late
+                own_ref[:half] = early
+                own_ref[half:] = late
 
 
 def store_signal(x, sig):
@@ -154,20 +153,17 @@
 
 
 def first_body(
-    at_ref, part_ref, own_late_ref, decay_ref, far_ref, x_ref, late_ref, left_ref, state_ref, sig, st
+    at_ref, part_ref, own_ref, decay_ref, far_ref, x_ref, late_ref, left_ref, state_ref, sig, st
 ):
     core = at_ref[0]
     rows = sig.shape[0]
     half = rows // 2
-    total = jnp.zeros(x_ref.shape, F32)
-    late = own_late_ref[...]
+    total = own_ref[...]
     for k in range(part_ref.shape[0]):
-        total = total + (part_ref[k, :half].astype(F32) + part_ref[k, half : 2 * half].astype(F32))
-        late = late + jnp.where(at_ref[1] == k, 0.0, part_ref[k, 2 * half :].astype(F32))
-    late_ref[...] = late.astype(BF16).astype(F32)
-    rounded = total.astype(BF16).astype(F32)
-    x = jnp.where(lane_group(total.shape) < 2, rounded, total)
+        total = total + jnp.where(at_ref[1] == k, 0.0, part_ref[k].astype(F32))
+    x = total[:half]
     x_ref[...] = x
+    late_ref[...] = total[half:]
     store_signal(x, sig)
     decay = [decay_ref[m : m + 1, :] for m in range(MODE_ROWS)]
     chunks = rows // STEPS
@@ -295,27 +291,18 @@
     )
     kept = transposed(kept, False, False)
     given = transposed(given, True, False)
-    tokens_too = swapped(tokens)
-    grads_too = swapped(grad_out)
-    kept, given, tokens_too, grads_too = lax.optimization_barrier(
-        (kept, given, tokens_too, grads_too)
-    )
     spread = call(
         spread_body, jax.ShapeDtypeStruct((chips, 2 * owned, 128), BF16), 4, inputs=3
     )(at, kept, given)
     weights = lax.all_to_all(spread, CHIPS, 0, 0, tiled=True).reshape(size_z, -1, 128)
 
 
+    tokens_too = swapped(tokens)
+    grads_too = swapped(grad_out)
     conv_own = jnp.where(core == 0, conv_out[:, :mine], conv_out[:, mine:])
     conv_sent = jnp.where(core == 0, conv_out[:, mine:], conv_out[:, :mine])
     conv = jnp.concatenate([swapped(conv_sent), conv_own], axis=1)
     conv = jnp.tile(conv, (1, 2))
-    flip = call(
-        transpose_body, jax.ShapeDtypeStruct((depth, rows), BF16), 8, moved=4 * depth * rows
-    )
-    tokens_t = flip(tokens, tokens_too)
-    grads_t = flip(grad_out, grads_too)
-
     pick = residues.shape[1] // 2
     res = jnp.where(core == 0, residues[:, :pick], residues[:, pick:])
     length = jnp.where(core == 0, decay_length[:, :pick], decay_length[:, pick:])
@@ -336,14 +323,13 @@
 
     project = call(
         project_body,
-        (pltpu.HBM((size_x, 3 * half, 128), BF16), jax.ShapeDtypeStruct((half, 128), F32)),
-        48,
+        (pltpu.HBM((size_x, rows, 128), BF16), jax.ShapeDtypeStruct((rows, 128), F32)),
+        20,
         inputs=6,
         flops=4 * rows * depth * size_x * 128,
         moved=8 * rows * depth,
     )
-    weights, tokens_t, grads_t = lax.optimization_barrier((weights, tokens_t, grads_t))
-    parts, own_late = project(
+    parts, own = project(
         at, in_hbm(tokens), in_hbm(tokens_too), in_hbm(grad_out), in_hbm(grads_too), weights
     )
     parts = lax.all_to_all(parts, "chan", 0, 0, tiled=True)
@@ -360,8 +346,16 @@
         scratch=[pltpu.VMEM((rows, 128), F32), pltpu.VMEM((MODE_ROWS * chunks, 128), F32)],
         inputs=5,
     )
-    x, late, left, state = first(at, parts, own_late, decay, far)
+    x, late, left, state = first(at, parts, own, decay, far)
+    _, *turned = lax.optimization_barrier((left, tokens, tokens_too, grad_out, grads_too))
+    turned = [in_hbm(t) for t in turned]
+    flip = call(
+        transpose_body, jax.ShapeDtypeStruct((depth, rows), BF16), 8, moved=4 * depth * rows
+    )
+    tokens_t = flip(*turned[:2])
+    grads_t = flip(*turned[2:])
     states = lax.all_to_all(state, CHIPS, 0, 0, tiled=True)
+    states, tokens_t, grads_t = lax.optimization_barrier((states, tokens_t, grads_t))
     second = call(
         second_body,
         jax.ShapeDtypeStruct((size_x, rows, 128), BF16),

time: 184 us -> 176 us (0.957)
  waiting for transfers between devices: 65 us -> 53.6 us
  blocking collectives: 44.3 us -> 48.5 us
  local copies, waits for them, and re-layouts: 6.46 us -> 2.29 us
  Pallas kernels: 18.8 us -> 21.7 us
    all_to_all x1, waiting for transfers between devices: 13.8 us -> 7.61 us  [local(): parts = lax.all_to_all(parts, 'chan', 0, 0, tiled=True)]
    all_to_all x1, waiting for transfers between devices: 11.8 us -> 6.1 us  [local(): states = lax.all_to_all(state, CHIPS, 0, 0, tiled=True)]
    all_to_all x1, blocking collectives: 29.7 us -> 34 us  [local(): partial = lax.all_to_all(partial, CHIPS, 0, 0, tiled=True)]
    unnamed x26 -> x14, local copies, waits for them, and re-layouts: 5.51 us -> 1.35 us
    pallas_call x3, Pallas kernels: 3.52 us -> 6.53 us  [the longest x1 2.18 us: local(): tokens_t = flip(*turned[:2])]
    ppermute x3, waiting for transfers between devices: 0.01 us -> 2.39 us  [swapped(): return lax.ppermute(value, 'seq_2', [(0, 1), (1, 0)])]
    all_to_all x1, waiting for transfers between devices: 24.7 us -> 22.8 us  [local(): lax.all_to_all(spread, CHIPS, 0, 0, tiled=True).reshape(size_z, -1, 128)]
  transfers between devices with their start and end apart: 10 -> 10, of which waited for: 6 -> 8; matrix products, arithmetic and copies ran while one was open for 1% -> 1% of each run, Pallas kernels for 2% -> 4%
where the time goes in v4:
time: 176 us; the launch traced here: 175 us
  waiting for transfers between devices  53.6 us (30%)
  blocking collectives  48.5 us (28%)
  starting transfers between devices  47.6 us (27%)
  Pallas kernels  21.7 us (12%)
  local copies, waits for them, and re-layouts  2.29 us (1%)
    all_to_all x1, blocking collectives, local(): partial = lax.all_to_all(partial, CHIPS, 0, 0, tiled=True)  34 us
    all_to_all x1, waiting for transfers between devices, local(): lax.all_to_all(spread, CHIPS, 0, 0, tiled=True).reshape(size_z, -1, 128)  22.8 us
    ppermute x4, starting transfers between devices, transposed(): return lax.ppermute(value, ('seq_0', 'seq_2', 'chan'), pairs)  19.3 us
    ppermute x4, waiting for transfers between devices, transposed(): return lax.ppermute(value, ('seq_0', 'seq_2', 'chan'), pairs)  14.7 us
    all_to_all x1, blocking collectives, local(): grads = lax.all_to_all(grads, 'chan', 0, 0, tiled=True)  14.6 us
    all_to_all x1, starting transfers between devices, local(): lax.all_to_all(spread, CHIPS, 0, 0, tiled=True).reshape(size_z, -1, 128)  9.09 us
    all_to_all x1, starting transfers between devices, local(): states = lax.all_to_all(state, CHIPS, 0, 0, tiled=True)  8.28 us
    all_to_all x1, waiting for transfers between devices, local(): parts = lax.all_to_all(parts, 'chan', 0, 0, tiled=True)  7.61 us
  transfers between devices with their start and end apart: 10, of which 8 were waited for; matrix products, arithmetic and copies ran while one was open for 1% of the time, Pallas kernels for 4%

profile of v4, /device:TPU:6, one launch (start us, length us, event | category | flops | bytes accessed | tf_op | source)
XLA Modules:
  0.0 175.2 jit_solution(4507286006462736968)
XLA Ops:
  1.8 10.9 %collective-permute-start.2 = (bf16[32,128]{1,0:T(8,128)(2,1)S(1)}, bf16[32,128]{1,0:T(8,128)(2,1)S(1)}, u32[]{:S(2)}, u32[]{:S(2)}) collective-permute-start(bf16[32,128]{1,0:T(8,128)(2,1)S(1)} %get-tuple-element.21), channel_id=1, source_target_pairs={{0,320},{1,128},{2,0},{3,384},{4,324},{5,132},{6,4},{7,388},{64,25... | collective-permute-start | bytes 24584 | tf_op jit(solution)/shard_map/ppermute | solution.py:283
  12.6 1.9 %collective-permute-start.3 = (bf16[32,128]{1,0:T(8,128)(2,1)S(1)}, bf16[32,128]{1,0:T(8,128)(2,1)S(1)}, u32[]{:S(2)}, u32[]{:S(2)}) collective-permute-start(bf16[32,128]{1,0:T(8,128)(2,1)S(1)} %get-tuple-element.22), channel_id=1, source_target_pairs={{0,324},{1,132},{2,4},{3,388},{4,320},{5,128},{6,0},{7,384},{64,26... | collective-permute-start | bytes 24584 | tf_op jit(solution)/shard_map/ppermute | solution.py:283
  14.6 7.3 %collective-permute-done.3.given_ref = bf16[32,128]{1,0:T(8,128)(2,1)S(1)} collective-permute-done((bf16[32,128]{1,0:T(8,128)(2,1)S(1)}, bf16[32,128]{1,0:T(8,128)(2,1)S(1)}, u32[]{:S(2)}, u32[]{:S(2)}) %collective-permute-start.3) | collective-permute-done | bytes 8224 | tf_op jit(solution)/shard_map/ppermute | solution.py:283
  23.5 9.1 %all-to-all-start = ((bf16[64,64,128]{2,1,0:T(8,128)(2,1)}), bf16[64,64,128]{2,1,0:T(8,128)(2,1)S(1)}, u32[]{:S(2)}, u32[]{:S(2)}) async-start(bf16[64,64,128]{2,1,0:T(8,128)(2,1)} %shard_map.87), calls=%async_computation | async-start | bytes 2097152 | tf_op jit(solution)/shard_map/all_to_all | solution.py:297
  32.6 1.9 %collective-permute-start = (bf16[512,1024]{1,0:T(8,128)(2,1)S(1)}, bf16[512,1024]{1,0:T(8,128)(2,1)}, u32[]{:S(2)}, u32[]{:S(2)}) collective-permute-start(bf16[512,1024]{1,0:T(8,128)(2,1)S(1)} %copy-done.2), channel_id=1, source_target_pairs={{0,4},{4,0},{1,5},{5,1},{2,6},{6,2},{3,7},{7,3},{8,12},{12,8},{9,1... | collective-permute-start | bytes 3145736 | tf_op jit(solution)/shard_map/ppermute | solution.py:286
  34.5 2.4 %collective-permute-start.1 = (bf16[512,1024]{1,0:T(8,128)(2,1)S(1)}, bf16[512,1024]{1,0:T(8,128)(2,1)}, u32[]{:S(2)}, u32[]{:S(2)}) collective-permute-start(bf16[512,1024]{1,0:T(8,128)(2,1)S(1)} %copy-done.3), channel_id=1, source_target_pairs={{0,4},{4,0},{1,5},{5,1},{2,6},{6,2},{3,7},{7,3},{8,12},{12,8},{9,1... | collective-permute-start | bytes 3145736 | tf_op jit(solution)/shard_map/ppermute | solution.py:286
  37.3 2.1 %collective-permute-done.1.other_g.b_ref = bf16[512,1024]{1,0:T(8,128)(2,1)} collective-permute-done((bf16[512,1024]{1,0:T(8,128)(2,1)S(1)}, bf16[512,1024]{1,0:T(8,128)(2,1)}, u32[]{:S(2)}, u32[]{:S(2)}) %collective-permute-start.1) | collective-permute-done | bytes 1048608 | tf_op jit(solution)/shard_map/ppermute | solution.py:286
  39.4 22.8 %all-to-all-done = bf16[64,64,128]{2,1,0:T(8,128)(2,1)S(1)} async-done(((bf16[64,64,128]{2,1,0:T(8,128)(2,1)}), bf16[64,64,128]{2,1,0:T(8,128)(2,1)S(1)}, u32[]{:S(2)}, u32[]{:S(2)}) %all-to-all-start) | async-done | bytes 1048608 | tf_op jit(solution)/shard_map/all_to_all | solution.py:297
  62.1 5.6 %shard_map.88 = (bf16[4,1024,128]{2,1,0:T(8,128)(2,1)}, f32[1024,128]{1,0:T(8,128)S(1)}) custom-call(s32[2]{0:T(128)S(1)} %pad_add_fusion.at_ref, bf16[512,1024]{1,0:T(8,128)(2,1)} %a_ref, bf16[512,1024]{1,0:T(8,128)(2,1)} %collective-permute-done.other_t.b_ref, bf16[512,1024]{1,0:T(8,128)(2,1)} %a_ref.1, ...), custom_call_target="tpu_custom_call" | custom-call | flops 2147483648 | bytes 8388608 | tf_op jit(solution)/shard_map/pallas_call | solution.py:332
  67.7 4.6 %all-to-all-start.1 = ((bf16[4,1024,128]{2,1,0:T(8,128)(2,1)}), bf16[4,1024,128]{2,1,0:T(8,128)(2,1)S(1)}, u32[]{:S(2)}, u32[]{:S(2)}) async-start(bf16[4,1024,128]{2,1,0:T(8,128)(2,1)} %get-tuple-element.23), calls=%async_computation.1 | async-start | bytes 2097152 | tf_op jit(solution)/shard_map/all_to_all | solution.py:335
  72.4 1.9 %collective-permute-start.4 = (bf16[512,32]{0,1:T(8,128)(2,1)S(1)}, bf16[512,32]{0,1:T(8,128)(2,1)S(1)}, u32[]{:S(2)}, u32[]{:S(2)}) collective-permute-start(bf16[512,32]{0,1:T(8,128)(2,1)S(1)} %get-tuple-element.42), channel_id=1, source_target_pairs={{0,4},{4,0},{1,5},{5,1},{2,6},{6,2},{3,7},{7,3},{8,12},{12,8},{9,1... | collective-permute-start | bytes 98312 | tf_op jit(solution)/shard_map/ppermute | solution.py:286
  74.9 7.6 %all-to-all-done.1.part_ref = bf16[4,1024,128]{2,1,0:T(8,128)(2,1)S(1)} async-done(((bf16[4,1024,128]{2,1,0:T(8,128)(2,1)}), bf16[4,1024,128]{2,1,0:T(8,128)(2,1)S(1)}, u32[]{:S(2)}, u32[]{:S(2)}) %all-to-all-start.1) | async-done | bytes 1048608 | tf_op jit(solution)/shard_map/all_to_all | solution.py:335
  82.5 2.2 %shard_map.89 = (f32[512,128]{1,0:T(8,128)S(1)}, f32[512,128]{1,0:T(8,128)S(1)}, f32[64,128]{1,0:T(8,128)S(1)}, f32[64,4,128]{2,1,0:T(4,128)}) custom-call(s32[2]{0:T(128)S(1)} %pad_add_fusion.at_ref, bf16[4,1024,128]{2,1,0:T(8,128)(2,1)S(1)} %all-to-all-done.1.part_ref, f32[1024,128]{1,0:T(8,128)S(1)} %get-tuple-element.24.own_ref, ...), custom_call_target="tpu_custom_call" | custom-call | tf_op jit(solution)/shard_map/pallas_call | solution.py:349
  84.7 8.3 %all-to-all-start.2 = ((f32[64,4,128]{2,1,0:T(4,128)}), f32[64,4,128]{2,1,0:T(4,128)S(1)}, u32[]{:S(2)}, u32[]{:S(2)}) async-start(f32[64,4,128]{2,1,0:T(4,128)} %get-tuple-element.25), calls=%async_computation.2 | async-start | bytes 262144 | tf_op jit(solution)/shard_map/all_to_all | solution.py:357
  93.9 2.2 %shard_map.90.tt_ref = bf16[1024,1024]{1,0:T(8,128)(2,1)S(1)} custom-call(bf16[512,1024]{1,0:T(8,128)(2,1)} %a_ref, bf16[512,1024]{1,0:T(8,128)(2,1)} %collective-permute-done.other_t.b_ref), custom_call_target="tpu_custom_call" | custom-call | bytes 4194304 | tf_op jit(solution)/shard_map/pallas_call | solution.py:355
  96.1 2.2 %shard_map.91.gt_ref = bf16[1024,1024]{1,0:T(8,128)(2,1)S(1)} custom-call(bf16[512,1024]{1,0:T(8,128)(2,1)} %a_ref.1, bf16[512,1024]{1,0:T(8,128)(2,1)} %collective-permute-done.1.other_g.b_ref), custom_call_target="tpu_custom_call" | custom-call | bytes 4194304 | tf_op jit(solution)/shard_map/pallas_call | solution.py:356
  99.6 6.1 %all-to-all-done.2.states_ref = f32[64,4,128]{2,1,0:T(4,128)S(1)} async-done(((f32[64,4,128]{2,1,0:T(4,128)}), f32[64,4,128]{2,1,0:T(4,128)S(1)}, u32[]{:S(2)}, u32[]{:S(2)}) %all-to-all-start.2) | async-done | bytes 131104 | tf_op jit(solution)/shard_map/all_to_all | solution.py:357
  105.7 2.0 %shard_map.92 = bf16[4,1024,128]{2,1,0:T(8,128)(2,1)S(1)} custom-call(s32[2]{0:T(128)S(1)} %pad_add_fusion.at_ref, f32[512,128]{1,0:T(8,128)S(1)} %get-tuple-element.33.x_ref, f32[512,128]{1,0:T(8,128)S(1)} %get-tuple-element.34.late_ref, f32[64,128]{1,0:T(8,128)S(1)} %get-tuple-element.26.left_ref, f32[64,4,128]{2,1,0:T(4,128)S(1)} %all-to-all-done.2.states_ref, ...), custom_call_target="tpu_custom_call" | custom-call | tf_op jit(solution)/shard_map/pallas_call | solution.py:366
  107.7 14.6 %all_to_all.25.grads_ref = bf16[4,1024,128]{2,1,0:T(8,128)(2,1)S(1)} all-to-all(bf16[4,1024,128]{2,1,0:T(8,128)(2,1)S(1)} %shard_map.92), channel_id=1, replica_groups=mesh['seq_0'=8,'seq_1'=8,'seq_2'=2,'chan'=4] {'chan'}, dimensions={0} | all-to-all | bytes 2097152 | tf_op jit(solution)/shard_map/all_to_all | solution.py:367
  122.3 2.9 %shard_map.93 = bf16[8,512,128]{2,1,0:T(8,128)(2,1)S(1)} custom-call(s32[2]{0:T(128)S(1)} %pad_add_fusion.at_ref, bf16[1024,1024]{1,0:T(8,128)(2,1)S(1)} %shard_map.90.tt_ref, bf16[1024,1024]{1,0:T(8,128)(2,1)S(1)} %copy-done.1, bf16[4,1024,128]{2,1,0:T(8,128)(2,1)S(1)} %all_to_all.25.grads_ref), custom_call_target="tpu_custom_call" | custom-call | flops 2147483648 | bytes 8388608 | tf_op jit(solution)/shard_map/pallas_call | solution.py:377
  125.2 34.0 %all_to_all.26.part_ref = bf16[64,64,128]{2,1,0:T(8,128)(2,1)S(1)} all-to-all(bf16[64,64,128]{2,1,0:T(8,128)(2,1)S(1)} %bitcast.18), channel_id=1, replica_groups=mesh['seq_0'=8,'seq_1'=8,'seq_2'=2,'chan'=4] {'seq_0','seq_1'}, dimensions={0} | all-to-all | bytes 2097152 | tf_op jit(solution)/shard_map/all_to_all | solution.py:378
  159.9 4.6 %collective-permute-start.5 = (f32[32,128]{1,0:T(8,128)S(1)}, f32[32,128]{1,0:T(8,128)S(1)}, u32[]{:S(2)}, u32[]{:S(2)}) collective-permute-start(f32[32,128]{1,0:T(8,128)S(1)} %get-tuple-element.36), channel_id=1, source_target_pairs={{320,0},{128,1},{0,2},{384,3},{324,4},{132,5},{4,6},{388,7},{256,6... | collective-permute-start | bytes 49160 | tf_op jit(solution)/shard_map/ppermute | solution.py:283
  166.4 3.3 %collective-permute-done.5.kept_ref = f32[32,128]{1,0:T(8,128)S(1)} collective-permute-done((f32[32,128]{1,0:T(8,128)S(1)}, f32[32,128]{1,0:T(8,128)S(1)}, u32[]{:S(2)}, u32[]{:S(2)}) %collective-permute-start.5) | collective-permute-done | bytes 16416 | tf_op jit(solution)/shard_map/ppermute | solution.py:283
  169.7 4.2 %collective-permute-done.6.given_ref = f32[32,128]{1,0:T(8,128)S(1)} collective-permute-done((f32[32,128]{1,0:T(8,128)S(1)}, f32[32,128]{1,0:T(8,128)S(1)}, u32[]{:S(2)}, u32[]{:S(2)}) %collective-permute-start.6) | collective-permute-done | bytes 16416 | tf_op jit(solution)/shard_map/ppermute | solution.py:283
  (46 shorter events, 9.7 us)
Async XLA Ops:
  0.6 32.0 %copy-start.2 = (bf16[512,1024]{1,0:T(8,128)(2,1)S(1)}, bf16[512,1024]{1,0:T(8,128)(2,1)}, u32[]{:S(2)}) copy-start(bf16[512,1024]{1,0:T(8,128)(2,1)} %a_ref) | copy-start | bytes 3145732
  0.6 33.9 %copy-start.3 = (bf16[512,1024]{1,0:T(8,128)(2,1)S(1)}, bf16[512,1024]{1,0:T(8,128)(2,1)}, u32[]{:S(2)}) copy-start(bf16[512,1024]{1,0:T(8,128)(2,1)} %a_ref.1) | copy-start | bytes 3145732
  1.8 12.8 %collective-permute-start.2 = (bf16[32,128]{1,0:T(8,128)(2,1)S(1)}, bf16[32,128]{1,0:T(8,128)(2,1)S(1)}, u32[]{:S(2)}, u32[]{:S(2)}) collective-permute-start(bf16[32,128]{1,0:T(8,128)(2,1)S(1)} %get-tuple-element.21), channel_id=1, source_target_pairs={{0,320},{1,128},{2,0},{3,384},{4,324},{5,132},{6,4},{7,388},{64,25... | collective-permute-start | bytes 24584 | tf_op jit(solution)/shard_map/ppermute | solution.py:283
  12.6 9.2 %collective-permute-start.3 = (bf16[32,128]{1,0:T(8,128)(2,1)S(1)}, bf16[32,128]{1,0:T(8,128)(2,1)S(1)}, u32[]{:S(2)}, u32[]{:S(2)}) collective-permute-start(bf16[32,128]{1,0:T(8,128)(2,1)S(1)} %get-tuple-element.22), channel_id=1, source_target_pairs={{0,324},{1,132},{2,4},{3,388},{4,320},{5,128},{6,0},{7,384},{64,26... | collective-permute-start | bytes 24584 | tf_op jit(solution)/shard_map/ppermute | solution.py:283
  23.5 38.6 %all-to-all-start = ((bf16[64,64,128]{2,1,0:T(8,128)(2,1)}), bf16[64,64,128]{2,1,0:T(8,128)(2,1)S(1)}, u32[]{:S(2)}, u32[]{:S(2)}) async-start(bf16[64,64,128]{2,1,0:T(8,128)(2,1)} %shard_map.87), calls=%async_computation | async-start | bytes 2097152 | tf_op jit(solution)/shard_map/all_to_all | solution.py:297
  32.6 4.7 %collective-permute-start = (bf16[512,1024]{1,0:T(8,128)(2,1)S(1)}, bf16[512,1024]{1,0:T(8,128)(2,1)}, u32[]{:S(2)}, u32[]{:S(2)}) collective-permute-start(bf16[512,1024]{1,0:T(8,128)(2,1)S(1)} %copy-done.2), channel_id=1, source_target_pairs={{0,4},{4,0},{1,5},{5,1},{2,6},{6,2},{3,7},{7,3},{8,12},{12,8},{9,1... | collective-permute-start | bytes 3145736 | tf_op jit(solution)/shard_map/ppermute | solution.py:286
  34.5 4.8 %collective-permute-start.1 = (bf16[512,1024]{1,0:T(8,128)(2,1)S(1)}, bf16[512,1024]{1,0:T(8,128)(2,1)}, u32[]{:S(2)}, u32[]{:S(2)}) collective-permute-start(bf16[512,1024]{1,0:T(8,128)(2,1)S(1)} %copy-done.3), channel_id=1, source_target_pairs={{0,4},{4,0},{1,5},{5,1},{2,6},{6,2},{3,7},{7,3},{8,12},{12,8},{9,1... | collective-permute-start | bytes 3145736 | tf_op jit(solution)/shard_map/ppermute | solution.py:286
  67.7 4.7 %copy-start.4 = (bf16[512,64]{0,1:T(8,128)(2,1)S(1)}, bf16[512,64]{0,1:T(8,128)(2,1)}, u32[]{:S(2)}) copy-start(bf16[512,64]{0,1:T(8,128)(2,1)} %param.11) | copy-start | bytes 196612
  67.7 6.6 %copy-start.5 = (f32[16,32]{1,0:T(8,128)S(1)}, f32[16,32]{1,0:T(8,128)}, u32[]{:S(2)}) copy-start(f32[16,32]{1,0:T(8,128)} %param.12) | copy-start | bytes 6148
  67.7 6.6 %copy-start.6 = (f32[16,32]{1,0:T(8,128)S(1)}, f32[16,32]{1,0:T(8,128)}, u32[]{:S(2)}) copy-start(f32[16,32]{1,0:T(8,128)} %param.13) | copy-start | bytes 6148
  67.7 14.7 %all-to-all-start.1 = ((bf16[4,1024,128]{2,1,0:T(8,128)(2,1)}), bf16[4,1024,128]{2,1,0:T(8,128)(2,1)S(1)}, u32[]{:S(2)}, u32[]{:S(2)}) async-start(bf16[4,1024,128]{2,1,0:T(8,128)(2,1)} %get-tuple-element.23), calls=%async_computation.1 | async-start | bytes 2097152 | tf_op jit(solution)/shard_map/all_to_all | solution.py:335
  72.4 21.3 %collective-permute-start.4 = (bf16[512,32]{0,1:T(8,128)(2,1)S(1)}, bf16[512,32]{0,1:T(8,128)(2,1)S(1)}, u32[]{:S(2)}, u32[]{:S(2)}) collective-permute-start(bf16[512,32]{0,1:T(8,128)(2,1)S(1)} %get-tuple-element.42), channel_id=1, source_target_pairs={{0,4},{4,0},{1,5},{5,1},{2,6},{6,2},{3,7},{7,3},{8,12},{12,8},{9,1... | collective-permute-start | bytes 98312 | tf_op jit(solution)/shard_map/ppermute | solution.py:286
  84.7 21.0 %all-to-all-start.2 = ((f32[64,4,128]{2,1,0:T(4,128)}), f32[64,4,128]{2,1,0:T(4,128)S(1)}, u32[]{:S(2)}, u32[]{:S(2)}) async-start(f32[64,4,128]{2,1,0:T(4,128)} %get-tuple-element.25), calls=%async_computation.2 | async-start | bytes 262144 | tf_op jit(solution)/shard_map/all_to_all | solution.py:357
  98.3 1.3 copy-start
  105.7 16.6 %copy-start.1 = (bf16[1024,1024]{1,0:T(8,128)(2,1)S(1)}, bf16[1024,1024]{1,0:T(8,128)(2,1)}, u32[]{:S(2)}) copy-start(bf16[1024,1024]{1,0:T(8,128)(2,1)} %copy-done) | copy-start | bytes 6291460
  159.9 9.9 %collective-permute-start.5 = (f32[32,128]{1,0:T(8,128)S(1)}, f32[32,128]{1,0:T(8,128)S(1)}, u32[]{:S(2)}, u32[]{:S(2)}) collective-permute-start(f32[32,128]{1,0:T(8,128)S(1)} %get-tuple-element.36), channel_id=1, source_target_pairs={{320,0},{128,1},{0,2},{384,3},{324,4},{132,5},{4,6},{388,7},{256,6... | collective-permute-start | bytes 49160 | tf_op jit(solution)/shard_map/ppermute | solution.py:283
  164.5 9.4 %collective-permute-start.6 = (f32[32,128]{1,0:T(8,128)S(1)}, f32[32,128]{1,0:T(8,128)S(1)}, u32[]{:S(2)}, u32[]{:S(2)}) collective-permute-start(f32[32,128]{1,0:T(8,128)S(1)} %get-tuple-element.37), channel_id=1, source_target_pairs={{324,0},{132,1},{4,2},{388,3},{320,4},{128,5},{0,6},{384,7},{260,6... | collective-permute-start | bytes 49160 | tf_op jit(solution)/shard_map/ppermute | solution.py:283

commit v5 on v4

--- a/solution.py
+++ b/solution.py
@@ -61,45 +61,35 @@
     out_ref[:, half:] = b_ref[...].T
 
 
-def pack_body(at_ref, in_ref, out_w_ref, kept_ref, given_ref):
-    core = at_ref[0]
+def pack_body(in_ref, out_w_ref, out_ref):
     width = out_w_ref.shape[1]
     row = lax.broadcasted_iota(jnp.int32, (width, 128), 0)
     lane = lax.broadcasted_iota(jnp.int32, (width, 128), 1)
     streams = [in_ref[0], in_ref[1], in_ref[2], out_w_ref[...]]
-    for half, ref in ((core, kept_ref), (1 - core, given_ref)):
-        total = jnp.zeros(ref.shape, F32)
+    for half in range(2):
+        total = jnp.zeros(out_ref.shape[1:], F32)
         for s, w in enumerate(streams):
             chosen = (lane // 32 == s) & (row == half * 32 + lane % 32)
             total = total + jnp.dot(w, chosen.astype(F32).astype(BF16), preferred_element_type=F32)
-        ref[...] = total.astype(BF16)
-
-
-def spread_body(at_ref, kept_ref, given_ref, out_ref):
-    first = at_ref[0] == 0
-    kept = kept_ref[...].astype(F32)
-    given = given_ref[...].astype(F32)
-    low = jnp.where(first, kept, given)
-    high = jnp.where(first, given, kept)
-    piece = jnp.concatenate([low, high], axis=0).astype(BF16)
+        out_ref[half] = total.astype(BF16)
+
+
+def spread_body(piece_ref, out_ref):
     for k in range(out_ref.shape[0]):
-        out_ref[k] = piece
-
-
-def total_body(at_ref, part_ref, kept_ref, given_ref):
-    first = at_ref[0] == 0
-    owned = kept_ref.shape[0]
-    total = part_ref[0].astype(F32)
-    for k in range(1, part_ref.shape[0]):
-        total = total + part_ref[k].astype(F32)
-    kept_ref[...] = jnp.where(first, total[:owned], total[owned:])
-    given_ref[...] = jnp.where(first, total[owned:], total[:owned])
-
-
-def unpack_body(at_ref, kept_ref, given_ref, in_ref, out_w_ref):
-    first = at_ref[0] == 0
-    low = jnp.where(first, kept_ref[...], given_ref[...])
-    high = jnp.where(first, given_ref[...], kept_ref[...])
+        out_ref[k] = piece_ref[k % 2]
+
+
+def total_body(part_ref, out_ref):
+    for core in range(2):
+        total = part_ref[core].astype(F32)
+        for k in range(core + 2, part_ref.shape[0], 2):
+            total = total + part_ref[k].astype(F32)
+        out_ref[core] = total
+
+
+def unpack_body(part_ref, in_ref, out_w_ref):
+    low = part_ref[0]
+    high = part_ref[1]
     for s, group in enumerate((0, 3, 2, 1)):
         left = low if group == 0 else turn(low, 128 - 32 * group)
         right = high if group == 1 else turn(high, (160 - 32 * group) % 128)
@@ -161,9 +151,10 @@
     total = own_ref[...]
     for k in range(part_ref.shape[0]):
         total = total + jnp.where(at_ref[1] == k, 0.0, part_ref[k].astype(F32))
-    x = total[:half]
+    rounded = total.astype(BF16).astype(F32)
+    x = jnp.where(lane_group((half, 128)) < 2, rounded[:half], total[:half])
     x_ref[...] = x
-    late_ref[...] = total[half:]
+    late_ref[...] = rounded[half:]
     store_signal(x, sig)
     decay = [decay_ref[m : m + 1, :] for m in range(MODE_ROWS)]
     chunks = rows // STEPS
@@ -270,32 +261,25 @@
 
     at = jnp.stack([core, lax.axis_index("chan")]).astype(jnp.int32)
 
-    def transposed(value, swap, to_owner):
+    def transposed(value, to_owner):
         pairs = []
         for z in range(size_z):
-            for k in range(2):
-                for x in range(size_x):
-                    j, l = z // 2, z % 2
-                    held_z = (2 * j + OFFSETS[(x - j) % size_x][l]) % size_z
-                    owner = (z * 2 + k) * size_x + x
-                    held = (held_z * 2 + (1 - k if swap else k)) * size_x + j
-                    pairs.append((held, owner) if to_owner else (owner, held))
-        return lax.ppermute(value, ("seq_0", "seq_2", "chan"), pairs)
+            for x in range(size_x):
+                j, l = z // 2, z % 2
+                held = ((2 * j + OFFSETS[(x - j) % size_x][l]) % size_z) * size_x + j
+                owner = z * size_x + x
+                pairs.append((held, owner) if to_owner else (owner, held))
+        return lax.ppermute(value, ("seq_0", "chan"), pairs)
 
     def swapped(value):
         return lax.ppermute(value, "seq_2", [(0, 1), (1, 0)])
 
-    piece = jax.ShapeDtypeStruct((owned, 128), BF16)
-    kept, given = call(pack_body, (piece, piece), 4, inputs=3)(
-        at, in_hbm(in_weight.transpose(1, 0, 2)), in_hbm(out_weight)
-    )
-    kept = transposed(kept, False, False)
-    given = transposed(given, True, False)
-    spread = call(
-        spread_body, jax.ShapeDtypeStruct((chips, 2 * owned, 128), BF16), 4, inputs=3
-    )(at, kept, given)
-    weights = lax.all_to_all(spread, CHIPS, 0, 0, tiled=True).reshape(size_z, -1, 128)
-
+    piece = call(pack_body, jax.ShapeDtypeStruct((2, owned, 128), BF16), 4)(
+        in_hbm(in_weight.transpose(1, 0, 2)), in_hbm(out_weight)
+    )
+    piece = transposed(piece, False)
+    spread = call(spread_body, jax.ShapeDtypeStruct((2 * chips, owned, 128), BF16), 4)(piece)
+    weights = lax.all_to_all(spread, SEQ, 0, 0, tiled=True).reshape(size_z, -1, 128)
 
     tokens_too = swapped(tokens)
     grads_too = swapped(grad_out)
@@ -374,12 +358,10 @@
         flops=4 * rows * depth * size_x * 128,
         moved=8 * rows * depth,
     )
-    partial = weigh(at, tokens_t, grads_t, grads).reshape(chips, 2 * owned, 128)
-    partial = lax.all_to_all(partial, CHIPS, 0, 0, tiled=True)
-    piece = jax.ShapeDtypeStruct((owned, 128), F32)
-    kept, given = call(total_body, (piece, piece), 6, inputs=2)(at, partial)
-    kept = transposed(kept, False, True)
-    given = transposed(given, True, True)
+    partial = weigh(at, tokens_t, grads_t, grads).reshape(2 * chips, owned, 128)
+    partial = lax.all_to_all(partial, SEQ, 0, 0, tiled=True)
+    total = call(total_body, jax.ShapeDtypeStruct((2, owned, 128), F32), 6)(partial)
+    total = transposed(total, True)
     grad_in, grad_proj = call(
         unpack_body,
         (
@@ -387,8 +369,7 @@
             jax.ShapeDtypeStruct((owned, channels), F32),
         ),
         4,
-        inputs=3,
-    )(at, kept, given)
+    )(total)
     return (grad_in.transpose(1, 0, 2), grad_proj)
 
 

time: 176 us -> 177 us (level)
  blocking collectives: 48.5 us -> 55.1 us
  waiting for transfers between devices: 53.6 us -> 51.5 us
  starting transfers between devices: 47.6 us -> 45.6 us
    ppermute x4 -> x2, waiting for transfers between devices: 14.7 us -> 8.38 us  [transposed(): return lax.ppermute(value, ('seq_0', 'chan'), pairs)]
    all_to_all x1, blocking collectives: 34 us -> 38.8 us  [local(): partial = lax.all_to_all(partial, SEQ, 0, 0, tiled=True)]
    ppermute x4 -> x2, starting transfers between devices: 19.3 us -> 14.6 us  [transposed(): return lax.ppermute(value, ('seq_0', 'chan'), pairs)]
    all_to_all x1, waiting for transfers between devices: 7.61 us -> 11.2 us  [local(): parts = lax.all_to_all(parts, 'chan', 0, 0, tiled=True)]
    all_to_all x1, starting transfers between devices: 9.09 us -> 12.7 us  [local(): lax.all_to_all(spread, SEQ, 0, 0, tiled=True).reshape(size_z, -1, 128)]
    all_to_all x1, starting transfers between devices: 8.28 us -> 5.56 us  [local(): states = lax.all_to_all(state, CHIPS, 0, 0, tiled=True)]
    all_to_all x1, starting transfers between devices: 4.65 us -> 6.55 us  [local(): parts = lax.all_to_all(parts, 'chan', 0, 0, tiled=True)]
  transfers between devices with their start and end apart: 10 -> 8, of which waited for: 8 -> 7; matrix products, arithmetic and copies ran while one was open for 1% -> 1% of each run, Pallas kernels for 4% -> 4%
where the time goes in v5:
time: 177 us; the launch traced here: 176 us
  blocking collectives  55.1 us (31%)
  waiting for transfers between devices  51.5 us (29%)
  starting transfers between devices  45.6 us (26%)
  Pallas kernels  20.1 us (11%)
  local copies, waits for them, and re-layouts  2.29 us (1%)
    all_to_all x1, blocking collectives, local(): partial = lax.all_to_all(partial, SEQ, 0, 0, tiled=True)  38.8 us
    all_to_all x1, waiting for transfers between devices, local(): lax.all_to_all(spread, SEQ, 0, 0, tiled=True).reshape(size_z, -1, 128)  23.5 us
    all_to_all x1, blocking collectives, local(): grads = lax.all_to_all(grads, 'chan', 0, 0, tiled=True)  16.2 us
    ppermute x2, starting transfers between devices, transposed(): return lax.ppermute(value, ('seq_0', 'chan'), pairs)  14.6 us
    all_to_all x1, starting transfers between devices, local(): lax.all_to_all(spread, SEQ, 0, 0, tiled=True).reshape(size_z, -1, 128)  12.7 us
    all_to_all x1, waiting for transfers between devices, local(): parts = lax.all_to_all(parts, 'chan', 0, 0, tiled=True)  11.2 us
    ppermute x2, waiting for transfers between devices, transposed(): return lax.ppermute(value, ('seq_0', 'chan'), pairs)  8.38 us
    all_to_all x1, starting transfers between devices, local(): parts = lax.all_to_all(parts, 'chan', 0, 0, tiled=True)  6.55 us
  transfers between devices with their start and end apart: 8, of which 7 were waited for; matrix products, arithmetic and copies ran while one was open for 1% of the time, Pallas kernels for 4%

profile of v5, /device:TPU:6, one launch (start us, length us, event | category | flops | bytes accessed | tf_op | source)
XLA Modules:
  0.0 176.0 jit_solution(10121193889800210473)
XLA Ops:
  1.7 10.9 %collective-permute-start.2 = (bf16[2,32,128]{2,1,0:T(8,128)(2,1)S(1)}, bf16[2,32,128]{2,1,0:T(8,128)(2,1)S(1)}, u32[]{:S(2)}, u32[]{:S(2)}) collective-permute-start(bf16[2,32,128]{2,1,0:T(8,128)(2,1)S(1)} %shard_map.86), channel_id=1, source_target_pairs={{0,320},{1,128},{2,0},{3,384},{64,256},{65,192},{66,64},{67,448},{... | collective-permute-start | bytes 49160 | tf_op jit(solution)/shard_map/ppermute | solution.py:272
  12.6 1.7 collective-permute-done.2.piece_ref
  14.3 1.1 shard_map.87
  15.4 12.7 %all-to-all-start = ((bf16[128,32,128]{2,1,0:T(8,128)(2,1)}), bf16[128,32,128]{2,1,0:T(8,128)(2,1)S(1)}, u32[]{:S(2)}, u32[]{:S(2)}) async-start(bf16[128,32,128]{2,1,0:T(8,128)(2,1)} %shard_map.87), calls=%async_computation | async-start | bytes 2097152 | tf_op jit(solution)/shard_map/all_to_all | solution.py:282
  28.1 1.9 %collective-permute-start = (bf16[512,1024]{1,0:T(8,128)(2,1)S(1)}, bf16[512,1024]{1,0:T(8,128)(2,1)}, u32[]{:S(2)}, u32[]{:S(2)}) collective-permute-start(bf16[512,1024]{1,0:T(8,128)(2,1)S(1)} %copy-done.2), channel_id=1, source_target_pairs={{0,4},{4,0},{1,5},{5,1},{2,6},{6,2},{3,7},{7,3},{8,12},{12,8},{9,1... | collective-permute-start | bytes 3145736 | tf_op jit(solution)/shard_map/ppermute | solution.py:275
  30.0 2.4 %collective-permute-start.1 = (bf16[512,1024]{1,0:T(8,128)(2,1)S(1)}, bf16[512,1024]{1,0:T(8,128)(2,1)}, u32[]{:S(2)}, u32[]{:S(2)}) collective-permute-start(bf16[512,1024]{1,0:T(8,128)(2,1)S(1)} %copy-done.3), channel_id=1, source_target_pairs={{0,4},{4,0},{1,5},{5,1},{2,6},{6,2},{3,7},{7,3},{8,12},{12,8},{9,1... | collective-permute-start | bytes 3145736 | tf_op jit(solution)/shard_map/ppermute | solution.py:275
  32.8 2.1 %collective-permute-done.1.other_g.b_ref = bf16[512,1024]{1,0:T(8,128)(2,1)} collective-permute-done((bf16[512,1024]{1,0:T(8,128)(2,1)S(1)}, bf16[512,1024]{1,0:T(8,128)(2,1)}, u32[]{:S(2)}, u32[]{:S(2)}) %collective-permute-start.1) | collective-permute-done | bytes 1048608 | tf_op jit(solution)/shard_map/ppermute | solution.py:275
  34.8 23.5 %all-to-all-done = bf16[128,32,128]{2,1,0:T(8,128)(2,1)S(1)} async-done(((bf16[128,32,128]{2,1,0:T(8,128)(2,1)}), bf16[128,32,128]{2,1,0:T(8,128)(2,1)S(1)}, u32[]{:S(2)}, u32[]{:S(2)}) %all-to-all-start) | async-done | bytes 1048608 | tf_op jit(solution)/shard_map/all_to_all | solution.py:282
  58.3 5.6 %shard_map.88 = (bf16[4,1024,128]{2,1,0:T(8,128)(2,1)}, f32[1024,128]{1,0:T(8,128)S(1)}) custom-call(s32[2]{0:T(128)S(1)} %pad_add_fusion.at_ref, bf16[512,1024]{1,0:T(8,128)(2,1)} %a_ref, bf16[512,1024]{1,0:T(8,128)(2,1)} %collective-permute-done.other_t.b_ref, bf16[512,1024]{1,0:T(8,128)(2,1)} %a_ref.1, ...), custom_call_target="tpu_custom_call" | custom-call | flops 2147483648 | bytes 8388608 | tf_op jit(solution)/shard_map/pallas_call | solution.py:316
  64.0 6.5 %all-to-all-start.1 = ((bf16[4,1024,128]{2,1,0:T(8,128)(2,1)}), bf16[4,1024,128]{2,1,0:T(8,128)(2,1)S(1)}, u32[]{:S(2)}, u32[]{:S(2)}) async-start(bf16[4,1024,128]{2,1,0:T(8,128)(2,1)} %get-tuple-element.17), calls=%async_computation.1 | async-start | bytes 2097152 | tf_op jit(solution)/shard_map/all_to_all | solution.py:319
  70.5 1.9 %collective-permute-start.3 = (bf16[512,32]{0,1:T(8,128)(2,1)S(1)}, bf16[512,32]{0,1:T(8,128)(2,1)S(1)}, u32[]{:S(2)}, u32[]{:S(2)}) collective-permute-start(bf16[512,32]{0,1:T(8,128)(2,1)S(1)} %get-tuple-element.34), channel_id=1, source_target_pairs={{0,4},{4,0},{1,5},{5,1},{2,6},{6,2},{3,7},{7,3},{8,12},{12,8},{9,1... | collective-permute-start | bytes 98312 | tf_op jit(solution)/shard_map/ppermute | solution.py:275
  73.0 11.2 %all-to-all-done.1.part_ref = bf16[4,1024,128]{2,1,0:T(8,128)(2,1)S(1)} async-done(((bf16[4,1024,128]{2,1,0:T(8,128)(2,1)}), bf16[4,1024,128]{2,1,0:T(8,128)(2,1)S(1)}, u32[]{:S(2)}, u32[]{:S(2)}) %all-to-all-start.1) | async-done | bytes 1048608 | tf_op jit(solution)/shard_map/all_to_all | solution.py:319
  84.2 2.2 %shard_map.89 = (f32[512,128]{1,0:T(8,128)S(1)}, f32[512,128]{1,0:T(8,128)S(1)}, f32[64,128]{1,0:T(8,128)S(1)}, f32[64,4,128]{2,1,0:T(4,128)}) custom-call(s32[2]{0:T(128)S(1)} %pad_add_fusion.at_ref, bf16[4,1024,128]{2,1,0:T(8,128)(2,1)S(1)} %all-to-all-done.1.part_ref, f32[1024,128]{1,0:T(8,128)S(1)} %get-tuple-element.18.own_ref, ...), custom_call_target="tpu_custom_call" | custom-call | tf_op jit(solution)/shard_map/pallas_call | solution.py:333
  86.4 5.6 %all-to-all-start.2 = ((f32[64,4,128]{2,1,0:T(4,128)}), f32[64,4,128]{2,1,0:T(4,128)S(1)}, u32[]{:S(2)}, u32[]{:S(2)}) async-start(f32[64,4,128]{2,1,0:T(4,128)} %get-tuple-element.19), calls=%async_computation.2 | async-start | bytes 262144 | tf_op jit(solution)/shard_map/all_to_all | solution.py:341
  92.9 2.2 %shard_map.90.tt_ref = bf16[1024,1024]{1,0:T(8,128)(2,1)S(1)} custom-call(bf16[512,1024]{1,0:T(8,128)(2,1)} %a_ref, bf16[512,1024]{1,0:T(8,128)(2,1)} %collective-permute-done.other_t.b_ref), custom_call_target="tpu_custom_call" | custom-call | bytes 4194304 | tf_op jit(solution)/shard_map/pallas_call | solution.py:339
  95.1 2.2 %shard_map.91.gt_ref = bf16[1024,1024]{1,0:T(8,128)(2,1)S(1)} custom-call(bf16[512,1024]{1,0:T(8,128)(2,1)} %a_ref.1, bf16[512,1024]{1,0:T(8,128)(2,1)} %collective-permute-done.1.other_g.b_ref), custom_call_target="tpu_custom_call" | custom-call | bytes 4194304 | tf_op jit(solution)/shard_map/pallas_call | solution.py:340
  97.3 1.3 copy-done
  98.7 6.1 %all-to-all-done.2.states_ref = f32[64,4,128]{2,1,0:T(4,128)S(1)} async-done(((f32[64,4,128]{2,1,0:T(4,128)}), f32[64,4,128]{2,1,0:T(4,128)S(1)}, u32[]{:S(2)}, u32[]{:S(2)}) %all-to-all-start.2) | async-done | bytes 131104 | tf_op jit(solution)/shard_map/all_to_all | solution.py:341
  104.7 2.0 %shard_map.92 = bf16[4,1024,128]{2,1,0:T(8,128)(2,1)S(1)} custom-call(s32[2]{0:T(128)S(1)} %pad_add_fusion.at_ref, f32[512,128]{1,0:T(8,128)S(1)} %get-tuple-element.27.x_ref, f32[512,128]{1,0:T(8,128)S(1)} %get-tuple-element.28.late_ref, f32[64,128]{1,0:T(8,128)S(1)} %get-tuple-element.20.left_ref, f32[64,4,128]{2,1,0:T(4,128)S(1)} %all-to-all-done.2.states_ref, ...), custom_call_target="tpu_custom_call" | custom-call | tf_op jit(solution)/shard_map/pallas_call | solution.py:350
  106.7 16.2 %all_to_all.25.grads_ref = bf16[4,1024,128]{2,1,0:T(8,128)(2,1)S(1)} all-to-all(bf16[4,1024,128]{2,1,0:T(8,128)(2,1)S(1)} %shard_map.92), channel_id=1, replica_groups=mesh['seq_0'=8,'seq_1'=8,'seq_2'=2,'chan'=4] {'chan'}, dimensions={0} | all-to-all | bytes 2097152 | tf_op jit(solution)/shard_map/all_to_all | solution.py:351
  123.0 2.9 %shard_map.93 = bf16[8,512,128]{2,1,0:T(8,128)(2,1)S(1)} custom-call(s32[2]{0:T(128)S(1)} %pad_add_fusion.at_ref, bf16[1024,1024]{1,0:T(8,128)(2,1)S(1)} %shard_map.90.tt_ref, bf16[1024,1024]{1,0:T(8,128)(2,1)S(1)} %copy-done.1, bf16[4,1024,128]{2,1,0:T(8,128)(2,1)S(1)} %all_to_all.25.grads_ref), custom_call_target="tpu_custom_call" | custom-call | flops 2147483648 | bytes 8388608 | tf_op jit(solution)/shard_map/pallas_call | solution.py:361
  125.9 38.8 %all_to_all.26.part_ref = bf16[128,32,128]{2,1,0:T(8,128)(2,1)S(1)} all-to-all(bf16[128,32,128]{2,1,0:T(8,128)(2,1)S(1)} %bitcast.18), channel_id=1, replica_groups=mesh['seq_0'=8,'seq_1'=8,'seq_2'=2,'chan'=4] {'seq_0','seq_1','seq_2'}, dimensions={0} | all-to-all | bytes 2097152 | tf_op jit(solution)/shard_map/all_to_all | solution.py:362
  164.9 3.8 %collective-permute-start.4 = (f32[2,32,128]{2,1,0:T(8,128)S(1)}, f32[2,32,128]{2,1,0:T(8,128)S(1)}, u32[]{:S(2)}, u32[]{:S(2)}) collective-permute-start(f32[2,32,128]{2,1,0:T(8,128)S(1)} %shard_map.94), channel_id=1, source_target_pairs={{320,0},{128,1},{0,2},{384,3},{256,64},{192,65},{64,66},{448,67},{... | collective-permute-start | bytes 98312 | tf_op jit(solution)/shard_map/ppermute | solution.py:272
  168.6 6.7 %collective-permute-done.4.part_ref = f32[2,32,128]{2,1,0:T(8,128)S(1)} collective-permute-done((f32[2,32,128]{2,1,0:T(8,128)S(1)}, f32[2,32,128]{2,1,0:T(8,128)S(1)}, u32[]{:S(2)}, u32[]{:S(2)}) %collective-permute-start.4) | collective-permute-done | bytes 32800 | tf_op jit(solution)/shard_map/ppermute | solution.py:272
  (42 shorter events, 3.7 us)
Async XLA Ops:
  0.6 27.4 %copy-start.2 = (bf16[512,1024]{1,0:T(8,128)(2,1)S(1)}, bf16[512,1024]{1,0:T(8,128)(2,1)}, u32[]{:S(2)}) copy-start(bf16[512,1024]{1,0:T(8,128)(2,1)} %a_ref) | copy-start | bytes 3145732
  0.6 29.4 %copy-start.3 = (bf16[512,1024]{1,0:T(8,128)(2,1)S(1)}, bf16[512,1024]{1,0:T(8,128)(2,1)}, u32[]{:S(2)}) copy-start(bf16[512,1024]{1,0:T(8,128)(2,1)} %a_ref.1) | copy-start | bytes 3145732
  1.7 12.6 %collective-permute-start.2 = (bf16[2,32,128]{2,1,0:T(8,128)(2,1)S(1)}, bf16[2,32,128]{2,1,0:T(8,128)(2,1)S(1)}, u32[]{:S(2)}, u32[]{:S(2)}) collective-permute-start(bf16[2,32,128]{2,1,0:T(8,128)(2,1)S(1)} %shard_map.86), channel_id=1, source_target_pairs={{0,320},{1,128},{2,0},{3,384},{64,256},{65,192},{66,64},{67,448},{... | collective-permute-start | bytes 49160 | tf_op jit(solution)/shard_map/ppermute | solution.py:272
  15.4 43.0 %all-to-all-start = ((bf16[128,32,128]{2,1,0:T(8,128)(2,1)}), bf16[128,32,128]{2,1,0:T(8,128)(2,1)S(1)}, u32[]{:S(2)}, u32[]{:S(2)}) async-start(bf16[128,32,128]{2,1,0:T(8,128)(2,1)} %shard_map.87), calls=%async_computation | async-start | bytes 2097152 | tf_op jit(solution)/shard_map/all_to_all | solution.py:282
  28.1 4.7 %collective-permute-start = (bf16[512,1024]{1,0:T(8,128)(2,1)S(1)}, bf16[512,1024]{1,0:T(8,128)(2,1)}, u32[]{:S(2)}, u32[]{:S(2)}) collective-permute-start(bf16[512,1024]{1,0:T(8,128)(2,1)S(1)} %copy-done.2), channel_id=1, source_target_pairs={{0,4},{4,0},{1,5},{5,1},{2,6},{6,2},{3,7},{7,3},{8,12},{12,8},{9,1... | collective-permute-start | bytes 3145736 | tf_op jit(solution)/shard_map/ppermute | solution.py:275
  30.0 4.8 %collective-permute-start.1 = (bf16[512,1024]{1,0:T(8,128)(2,1)S(1)}, bf16[512,1024]{1,0:T(8,128)(2,1)}, u32[]{:S(2)}, u32[]{:S(2)}) collective-permute-start(bf16[512,1024]{1,0:T(8,128)(2,1)S(1)} %copy-done.3), channel_id=1, source_target_pairs={{0,4},{4,0},{1,5},{5,1},{2,6},{6,2},{3,7},{7,3},{8,12},{12,8},{9,1... | collective-permute-start | bytes 3145736 | tf_op jit(solution)/shard_map/ppermute | solution.py:275
  63.9 6.6 %copy-start.4 = (bf16[512,64]{0,1:T(8,128)(2,1)S(1)}, bf16[512,64]{0,1:T(8,128)(2,1)}, u32[]{:S(2)}) copy-start(bf16[512,64]{0,1:T(8,128)(2,1)} %param.11) | copy-start | bytes 196612
  64.0 8.5 %copy-start.5 = (f32[16,32]{1,0:T(8,128)S(1)}, f32[16,32]{1,0:T(8,128)}, u32[]{:S(2)}) copy-start(f32[16,32]{1,0:T(8,128)} %param.12) | copy-start | bytes 6148
  64.0 8.5 %copy-start.6 = (f32[16,32]{1,0:T(8,128)S(1)}, f32[16,32]{1,0:T(8,128)}, u32[]{:S(2)}) copy-start(f32[16,32]{1,0:T(8,128)} %param.13) | copy-start | bytes 6148
  64.0 20.3 %all-to-all-start.1 = ((bf16[4,1024,128]{2,1,0:T(8,128)(2,1)}), bf16[4,1024,128]{2,1,0:T(8,128)(2,1)S(1)}, u32[]{:S(2)}, u32[]{:S(2)}) async-start(bf16[4,1024,128]{2,1,0:T(8,128)(2,1)} %get-tuple-element.17), calls=%async_computation.1 | async-start | bytes 2097152 | tf_op jit(solution)/shard_map/all_to_all | solution.py:319
  70.5 22.3 %collective-permute-start.3 = (bf16[512,32]{0,1:T(8,128)(2,1)S(1)}, bf16[512,32]{0,1:T(8,128)(2,1)S(1)}, u32[]{:S(2)}, u32[]{:S(2)}) collective-permute-start(bf16[512,32]{0,1:T(8,128)(2,1)S(1)} %get-tuple-element.34), channel_id=1, source_target_pairs={{0,4},{4,0},{1,5},{5,1},{2,6},{6,2},{3,7},{7,3},{8,12},{12,8},{9,1... | collective-permute-start | bytes 98312 | tf_op jit(solution)/shard_map/ppermute | solution.py:275
  86.4 18.3 %all-to-all-start.2 = ((f32[64,4,128]{2,1,0:T(4,128)}), f32[64,4,128]{2,1,0:T(4,128)S(1)}, u32[]{:S(2)}, u32[]{:S(2)}) async-start(f32[64,4,128]{2,1,0:T(4,128)} %get-tuple-element.19), calls=%async_computation.2 | async-start | bytes 262144 | tf_op jit(solution)/shard_map/all_to_all | solution.py:341
  97.3 1.3 copy-start
  104.7 18.2 %copy-start.1 = (bf16[1024,1024]{1,0:T(8,128)(2,1)S(1)}, bf16[1024,1024]{1,0:T(8,128)(2,1)}, u32[]{:S(2)}) copy-start(bf16[1024,1024]{1,0:T(8,128)(2,1)} %copy-done) | copy-start | bytes 6291460
  164.9 10.4 %collective-permute-start.4 = (f32[2,32,128]{2,1,0:T(8,128)S(1)}, f32[2,32,128]{2,1,0:T(8,128)S(1)}, u32[]{:S(2)}, u32[]{:S(2)}) collective-permute-start(f32[2,32,128]{2,1,0:T(8,128)S(1)} %shard_map.94), channel_id=1, source_target_pairs={{320,0},{128,1},{0,2},{384,3},{256,64},{192,65},{64,66},{448,67},{... | collective-permute-start | bytes 98312 | tf_op jit(solution)/shard_map/ppermute | solution.py:272

commit v6 on v5

--- a/solution.py
+++ b/solution.py
@@ -74,6 +74,19 @@
         out_ref[half] = total.astype(BF16)
 
 
+def conv_body(at_ref, own_ref, other_ref, out_ref):
+    core = at_ref[0]
+    row = lax.broadcasted_iota(jnp.int32, (own_ref.shape[1], 128), 0)
+    lane = lax.broadcasted_iota(jnp.int32, (own_ref.shape[1], 128), 1)
+    total = jnp.zeros(out_ref.shape, F32)
+    for odd, ref in ((1, own_ref), (0, other_ref)):
+        chosen = (lane // 32 % 2 == odd) & (row == core * 32 + lane % 32)
+        total = total + jnp.dot(
+            ref[...], chosen.astype(F32).astype(BF16), preferred_element_type=F32
+        )
+    out_ref[...] = total.astype(BF16)
+
+
 def spread_body(piece_ref, out_ref):
     for k in range(out_ref.shape[0]):
         out_ref[k] = piece_ref[k % 2]
@@ -120,8 +133,14 @@
             chunk = chunk_of(plane, e + k)
             early = jnp.where(odd, own, turn(other, 96))
             late = jnp.where(odd, turn(other, 32), own)
-            out_ref[chunk, :half] = early.astype(BF16)
-            out_ref[chunk, half:] = late.astype(BF16)
+            high = early.astype(BF16)
+            low = early - high.astype(F32)
+            low = jnp.where(
+                lane_group((half // 2, 128)) < 2, low[: half // 2], turn(low[half // 2 :], 64)
+            )
+            out_ref[chunk, :half] = high
+            out_ref[chunk, half : 2 * half] = late.astype(BF16)
+            out_ref[chunk, 2 * half :] = low.astype(BF16)
             if e + k == 0:
                 own_ref[:half] = early
                 own_ref[half:] = late
@@ -149,12 +168,16 @@
     rows = sig.shape[0]
     half = rows // 2
     total = own_ref[...]
+    low = jnp.zeros((half // 2, 128), F32)
     for k in range(part_ref.shape[0]):
-        total = total + jnp.where(at_ref[1] == k, 0.0, part_ref[k].astype(F32))
-    rounded = total.astype(BF16).astype(F32)
-    x = jnp.where(lane_group((half, 128)) < 2, rounded[:half], total[:half])
+        mine = at_ref[1] == k
+        total = total + jnp.where(mine, 0.0, part_ref[k, :rows].astype(F32))
+        low = low + jnp.where(mine, 0.0, part_ref[k, rows:].astype(F32))
+    low = jnp.concatenate([low, turn(low, 64)], axis=0)
+    early = total[:half] + jnp.where(lane_group(low.shape) < 2, low, 0.0)
+    x = jnp.where(lane_group(early.shape) < 2, early.astype(BF16).astype(F32), early)
     x_ref[...] = x
-    late_ref[...] = rounded[half:]
+    late_ref[...] = total[half:].astype(BF16).astype(F32)
     store_signal(x, sig)
     decay = [decay_ref[m : m + 1, :] for m in range(MODE_ROWS)]
     chunks = rows // STEPS
@@ -253,7 +276,6 @@
     rows = 2 * half
     owned = in_weight.shape[0]
     channels = out_weight.shape[1]
-    mine = channels // 2
     size_z, size_y, size_x = (lax.axis_size(a) for a in ("seq_0", "seq_1", "chan"))
     chips = size_z * size_y
     core = lax.axis_index("seq_2")
@@ -283,10 +305,10 @@
 
     tokens_too = swapped(tokens)
     grads_too = swapped(grad_out)
-    conv_own = jnp.where(core == 0, conv_out[:, :mine], conv_out[:, mine:])
-    conv_sent = jnp.where(core == 0, conv_out[:, mine:], conv_out[:, :mine])
-    conv = jnp.concatenate([swapped(conv_sent), conv_own], axis=1)
-    conv = jnp.tile(conv, (1, 2))
+    conv = call(conv_body, jax.ShapeDtypeStruct((half, 128), BF16), 4, inputs=3)(
+        at, conv_out, swapped(conv_out)
+    )
+
     pick = residues.shape[1] // 2
     res = jnp.where(core == 0, residues[:, :pick], residues[:, pick:])
     length = jnp.where(core == 0, decay_length[:, :pick], decay_length[:, pick:])
@@ -305,9 +327,12 @@
         0.0,
     )
 
+    weights, conv, weight, decay, far, power, reach = lax.optimization_barrier(
+        (weights, conv, weight, decay, far, power, reach)
+    )
     project = call(
         project_body,
-        (pltpu.HBM((size_x, rows, 128), BF16), jax.ShapeDtypeStruct((rows, 128), F32)),
+        (jax.ShapeDtypeStruct((size_x, rows + half // 2, 128), BF16), jax.ShapeDtypeStruct((rows, 128), F32)),
         20,
         inputs=6,
         flops=4 * rows * depth * size_x * 128,

time: 177 us -> 177 us (level)
  blocking collectives: 55.1 us -> 76 us
  waiting for transfers between devices: 51.5 us -> 37.1 us
  starting transfers between devices: 45.6 us -> 39.1 us
    all_to_all x0 -> x1, blocking collectives: none -> 21.9 us  [local(): parts = lax.all_to_all(parts, 'chan', 0, 0, tiled=True)]
    all_to_all x1 -> x0, waiting for transfers between devices: 11.2 us -> none  [local(): parts = lax.all_to_all(parts, 'chan', 0, 0, tiled=True)]
    all_to_all x1 -> x0, starting transfers between devices: 6.55 us -> none  [local(): parts = lax.all_to_all(parts, 'chan', 0, 0, tiled=True)]
    ppermute x3, waiting for transfers between devices: 2.32 us -> 0.01 us  [swapped(): return lax.ppermute(value, 'seq_2', [(0, 1), (1, 0)])]
    all_to_all x1, waiting for transfers between devices: 23.5 us -> 21.7 us  [local(): lax.all_to_all(spread, SEQ, 0, 0, tiled=True).reshape(size_z, -1, 128)]
  transfers between devices with their start and end apart: 8 -> 7, of which waited for: 7 -> 4; matrix products, arithmetic and copies ran while one was open for 1% -> 1% of each run, Pallas kernels for 4% -> 3%
where the time goes in v6:
time: 177 us; the launch traced here: 176 us
  blocking collectives  76 us (43%)
  starting transfers between devices  39.1 us (22%)
  waiting for transfers between devices  37.1 us (21%)
  Pallas kernels  20 us (11%)
  local copies, waits for them, and re-layouts  2.29 us (1%)
    all_to_all x1, blocking collectives, local(): partial = lax.all_to_all(partial, SEQ, 0, 0, tiled=True)  37.9 us
    all_to_all x1, blocking collectives, local(): parts = lax.all_to_all(parts, 'chan', 0, 0, tiled=True)  21.9 us
    all_to_all x1, waiting for transfers between devices, local(): lax.all_to_all(spread, SEQ, 0, 0, tiled=True).reshape(size_z, -1, 128)  21.7 us
    all_to_all x1, blocking collectives, local(): grads = lax.all_to_all(grads, 'chan', 0, 0, tiled=True)  16.2 us
    ppermute x2, starting transfers between devices, transposed(): return lax.ppermute(value, ('seq_0', 'chan'), pairs)  14.6 us
    all_to_all x1, starting transfers between devices, local(): lax.all_to_all(spread, SEQ, 0, 0, tiled=True).reshape(size_z, -1, 128)  12.7 us
    ppermute x2, waiting for transfers between devices, transposed(): return lax.ppermute(value, ('seq_0', 'chan'), pairs)  8.38 us
    all_to_all x1, waiting for transfers between devices, local(): states = lax.all_to_all(state, CHIPS, 0, 0, tiled=True)  6.99 us
  transfers between devices with their start and end apart: 7, of which 4 were waited for; matrix products, arithmetic and copies ran while one was open for 1% of the time, Pallas kernels for 3%

profile of v6, /device:TPU:6, one launch (start us, length us, event | category | flops | bytes accessed | tf_op | source)
XLA Modules:
  0.0 175.8 jit_solution(6484968905743227762)
XLA Ops:
  0.7 0.9 shard_map.86
  1.6 10.9 %collective-permute-start.2 = (bf16[2,32,128]{2,1,0:T(8,128)(2,1)S(1)}, bf16[2,32,128]{2,1,0:T(8,128)(2,1)S(1)}, u32[]{:S(2)}, u32[]{:S(2)}) collective-permute-start(bf16[2,32,128]{2,1,0:T(8,128)(2,1)S(1)} %shard_map.86), channel_id=1, source_target_pairs={{0,320},{1,128},{2,0},{3,384},{64,256},{65,192},{66,64},{67,448},{... | collective-permute-start | bytes 49160 | tf_op jit(solution)/shard_map/ppermute | solution.py:294
  12.5 1.7 collective-permute-done.2.piece_ref
  14.2 1.1 shard_map.87
  15.3 12.7 %all-to-all-start = ((bf16[128,32,128]{2,1,0:T(8,128)(2,1)}), bf16[128,32,128]{2,1,0:T(8,128)(2,1)S(1)}, u32[]{:S(2)}, u32[]{:S(2)}) async-start(bf16[128,32,128]{2,1,0:T(8,128)(2,1)} %shard_map.87), calls=%async_computation | async-start | bytes 2097152 | tf_op jit(solution)/shard_map/all_to_all | solution.py:304
  28.1 1.9 %collective-permute-start.3 = (bf16[512,64]{1,0:T(8,128)(2,1)S(1)}, bf16[512,64]{1,0:T(8,128)(2,1)S(1)}, u32[]{:S(2)}, u32[]{:S(2)}) collective-permute-start(bf16[512,64]{1,0:T(8,128)(2,1)S(1)} %copy.12.own_ref), channel_id=1, source_target_pairs={{0,4},{4,0},{1,5},{5,1},{2,6},{6,2},{3,7},{7,3},{8,12},{12,8},{9,1... | collective-permute-start | bytes 196616 | tf_op jit(solution)/shard_map/ppermute | solution.py:297
  30.0 2.4 %collective-permute-start = (bf16[512,1024]{1,0:T(8,128)(2,1)}, bf16[512,1024]{1,0:T(8,128)(2,1)}, u32[]{:S(2)}, u32[]{:S(2)}) collective-permute-start(bf16[512,1024]{1,0:T(8,128)(2,1)} %a_ref), channel_id=1, source_target_pairs={{0,4},{4,0},{1,5},{5,1},{2,6},{6,2},{3,7},{7,3},{8,12},{12,8},{9,1... | collective-permute-start | bytes 3145736 | tf_op jit(solution)/shard_map/ppermute | solution.py:297
  32.4 1.9 %collective-permute-start.1 = (bf16[512,1024]{1,0:T(8,128)(2,1)}, bf16[512,1024]{1,0:T(8,128)(2,1)}, u32[]{:S(2)}, u32[]{:S(2)}) collective-permute-start(bf16[512,1024]{1,0:T(8,128)(2,1)} %a_ref.1), channel_id=1, source_target_pairs={{0,4},{4,0},{1,5},{5,1},{2,6},{6,2},{3,7},{7,3},{8,12},{12,8},{9,1... | collective-permute-start | bytes 3145736 | tf_op jit(solution)/shard_map/ppermute | solution.py:297
  35.8 0.8 shard_map.88.conv_ref
  36.5 21.7 %all-to-all-done = bf16[128,32,128]{2,1,0:T(8,128)(2,1)S(1)} async-done(((bf16[128,32,128]{2,1,0:T(8,128)(2,1)}), bf16[128,32,128]{2,1,0:T(8,128)(2,1)S(1)}, u32[]{:S(2)}, u32[]{:S(2)}) %all-to-all-start) | async-done | bytes 1048608 | tf_op jit(solution)/shard_map/all_to_all | solution.py:304
  58.2 4.7 %shard_map.89 = (bf16[4,1280,128]{2,1,0:T(8,128)(2,1)S(1)}, f32[1024,128]{1,0:T(8,128)S(1)}) custom-call(s32[2]{0:T(128)S(1)} %pad_add_fusion.at_ref, bf16[512,1024]{1,0:T(8,128)(2,1)} %a_ref, bf16[512,1024]{1,0:T(8,128)(2,1)} %collective-permute-done.other_t.b_ref, bf16[512,1024]{1,0:T(8,128)(2,1)} %a_ref.1, ...), custom_call_target="tpu_custom_call" | custom-call | flops 2147483648 | bytes 8388608 | tf_op jit(solution)/shard_map/pallas_call | solution.py:341
  63.0 21.9 %all_to_all.25.part_ref = bf16[4,1280,128]{2,1,0:T(8,128)(2,1)S(1)} all-to-all(bf16[4,1280,128]{2,1,0:T(8,128)(2,1)S(1)} %get-tuple-element.25), channel_id=1, replica_groups=mesh['seq_0'=8,'seq_1'=8,'seq_2'=2,'chan'=4] {'chan'}, dimensions={0} | all-to-all | bytes 2621440 | tf_op jit(solution)/shard_map/all_to_all | solution.py:344
  84.8 2.3 %shard_map.90 = (f32[512,128]{1,0:T(8,128)S(1)}, f32[512,128]{1,0:T(8,128)S(1)}, f32[64,128]{1,0:T(8,128)S(1)}, f32[64,4,128]{2,1,0:T(4,128)}) custom-call(s32[2]{0:T(128)S(1)} %pad_add_fusion.at_ref, bf16[4,1280,128]{2,1,0:T(8,128)(2,1)S(1)} %all_to_all.25.part_ref, f32[1024,128]{1,0:T(8,128)S(1)} %get-tuple-element.26.own_ref, ...), custom_call_target="tpu_custom_call" | custom-call | tf_op jit(solution)/shard_map/pallas_call | solution.py:358
  87.1 5.5 %all-to-all-start.2 = ((f32[64,4,128]{2,1,0:T(4,128)}), f32[64,4,128]{2,1,0:T(4,128)S(1)}, u32[]{:S(2)}, u32[]{:S(2)}) async-start(f32[64,4,128]{2,1,0:T(4,128)} %get-tuple-element.29), calls=%async_computation.2 | async-start | bytes 262144 | tf_op jit(solution)/shard_map/all_to_all | solution.py:366
  92.7 2.2 %shard_map.91.tt_ref = bf16[1024,1024]{1,0:T(8,128)(2,1)S(1)} custom-call(bf16[512,1024]{1,0:T(8,128)(2,1)} %a_ref, bf16[512,1024]{1,0:T(8,128)(2,1)} %collective-permute-done.other_t.b_ref), custom_call_target="tpu_custom_call" | custom-call | bytes 4194304 | tf_op jit(solution)/shard_map/pallas_call | solution.py:364
  94.9 2.2 %shard_map.92.gt_ref = bf16[1024,1024]{1,0:T(8,128)(2,1)S(1)} custom-call(bf16[512,1024]{1,0:T(8,128)(2,1)} %a_ref.1, bf16[512,1024]{1,0:T(8,128)(2,1)} %collective-permute-done.1.other_g.b_ref), custom_call_target="tpu_custom_call" | custom-call | bytes 4194304 | tf_op jit(solution)/shard_map/pallas_call | solution.py:365
  97.1 1.3 copy-done
  98.4 7.0 %all-to-all-done.2.states_ref = f32[64,4,128]{2,1,0:T(4,128)S(1)} async-done(((f32[64,4,128]{2,1,0:T(4,128)}), f32[64,4,128]{2,1,0:T(4,128)S(1)}, u32[]{:S(2)}, u32[]{:S(2)}) %all-to-all-start.2) | async-done | bytes 131104 | tf_op jit(solution)/shard_map/all_to_all | solution.py:366
  105.4 2.0 %shard_map.93 = bf16[4,1024,128]{2,1,0:T(8,128)(2,1)S(1)} custom-call(s32[2]{0:T(128)S(1)} %pad_add_fusion.at_ref, f32[512,128]{1,0:T(8,128)S(1)} %get-tuple-element.37.x_ref, f32[512,128]{1,0:T(8,128)S(1)} %get-tuple-element.38.late_ref, f32[64,128]{1,0:T(8,128)S(1)} %get-tuple-element.30.left_ref, f32[64,4,128]{2,1,0:T(4,128)S(1)} %all-to-all-done.2.states_ref, ...), custom_call_target="tpu_custom_call" | custom-call | tf_op jit(solution)/shard_map/pallas_call | solution.py:375
  107.4 16.2 %all_to_all.26.grads_ref = bf16[4,1024,128]{2,1,0:T(8,128)(2,1)S(1)} all-to-all(bf16[4,1024,128]{2,1,0:T(8,128)(2,1)S(1)} %shard_map.93), channel_id=1, replica_groups=mesh['seq_0'=8,'seq_1'=8,'seq_2'=2,'chan'=4] {'chan'}, dimensions={0} | all-to-all | bytes 2097152 | tf_op jit(solution)/shard_map/all_to_all | solution.py:376
  123.6 2.9 %shard_map.94 = bf16[8,512,128]{2,1,0:T(8,128)(2,1)S(1)} custom-call(s32[2]{0:T(128)S(1)} %pad_add_fusion.at_ref, bf16[1024,1024]{1,0:T(8,128)(2,1)S(1)} %shard_map.91.tt_ref, bf16[1024,1024]{1,0:T(8,128)(2,1)S(1)} %copy-done.1, bf16[4,1024,128]{2,1,0:T(8,128)(2,1)S(1)} %all_to_all.26.grads_ref), custom_call_target="tpu_custom_call" | custom-call | flops 2147483648 | bytes 8388608 | tf_op jit(solution)/shard_map/pallas_call | solution.py:386
  126.6 37.9 %all_to_all.27.part_ref = bf16[128,32,128]{2,1,0:T(8,128)(2,1)S(1)} all-to-all(bf16[128,32,128]{2,1,0:T(8,128)(2,1)S(1)} %bitcast.17), channel_id=1, replica_groups=mesh['seq_0'=8,'seq_1'=8,'seq_2'=2,'chan'=4] {'seq_0','seq_1','seq_2'}, dimensions={0} | all-to-all | bytes 2097152 | tf_op jit(solution)/shard_map/all_to_all | solution.py:387
  164.6 3.8 %collective-permute-start.4 = (f32[2,32,128]{2,1,0:T(8,128)S(1)}, f32[2,32,128]{2,1,0:T(8,128)S(1)}, u32[]{:S(2)}, u32[]{:S(2)}) collective-permute-start(f32[2,32,128]{2,1,0:T(8,128)S(1)} %shard_map.95), channel_id=1, source_target_pairs={{320,0},{128,1},{0,2},{384,3},{256,64},{192,65},{64,66},{448,67},{... | collective-permute-start | bytes 98312 | tf_op jit(solution)/shard_map/ppermute | solution.py:294
  168.4 6.7 %collective-permute-done.4.part_ref = f32[2,32,128]{2,1,0:T(8,128)S(1)} collective-permute-done((f32[2,32,128]{2,1,0:T(8,128)S(1)}, f32[2,32,128]{2,1,0:T(8,128)S(1)}, u32[]{:S(2)}, u32[]{:S(2)}) %collective-permute-start.4) | collective-permute-done | bytes 32800 | tf_op jit(solution)/shard_map/ppermute | solution.py:294
  (35 shorter events, 2.3 us)
Async XLA Ops:
  0.6 27.3 %copy-start.2 = (bf16[512,64]{0,1:T(8,128)(2,1)S(1)}, bf16[512,64]{0,1:T(8,128)(2,1)}, u32[]{:S(2)}) copy-start(bf16[512,64]{0,1:T(8,128)(2,1)} %param.11) | copy-start | bytes 196612
  0.6 33.8 %copy-start.4 = (f32[16,32]{1,0:T(8,128)S(1)}, f32[16,32]{1,0:T(8,128)}, u32[]{:S(2)}) copy-start(f32[16,32]{1,0:T(8,128)} %param.13) | copy-start | bytes 6148
  0.7 33.8 %copy-start.3 = (f32[16,32]{1,0:T(8,128)S(1)}, f32[16,32]{1,0:T(8,128)}, u32[]{:S(2)}) copy-start(f32[16,32]{1,0:T(8,128)} %param.12) | copy-start | bytes 6148
  1.6 12.6 %collective-permute-start.2 = (bf16[2,32,128]{2,1,0:T(8,128)(2,1)S(1)}, bf16[2,32,128]{2,1,0:T(8,128)(2,1)S(1)}, u32[]{:S(2)}, u32[]{:S(2)}) collective-permute-start(bf16[2,32,128]{2,1,0:T(8,128)(2,1)S(1)} %shard_map.86), channel_id=1, source_target_pairs={{0,320},{1,128},{2,0},{3,384},{64,256},{65,192},{66,64},{67,448},{... | collective-permute-start | bytes 49160 | tf_op jit(solution)/shard_map/ppermute | solution.py:294
  15.3 43.0 %all-to-all-start = ((bf16[128,32,128]{2,1,0:T(8,128)(2,1)}), bf16[128,32,128]{2,1,0:T(8,128)(2,1)S(1)}, u32[]{:S(2)}, u32[]{:S(2)}) async-start(bf16[128,32,128]{2,1,0:T(8,128)(2,1)} %shard_map.87), calls=%async_computation | async-start | bytes 2097152 | tf_op jit(solution)/shard_map/all_to_all | solution.py:304
  28.1 7.7 %collective-permute-start.3 = (bf16[512,64]{1,0:T(8,128)(2,1)S(1)}, bf16[512,64]{1,0:T(8,128)(2,1)S(1)}, u32[]{:S(2)}, u32[]{:S(2)}) collective-permute-start(bf16[512,64]{1,0:T(8,128)(2,1)S(1)} %copy.12.own_ref), channel_id=1, source_target_pairs={{0,4},{4,0},{1,5},{5,1},{2,6},{6,2},{3,7},{7,3},{8,12},{12,8},{9,1... | collective-permute-start | bytes 196616 | tf_op jit(solution)/shard_map/ppermute | solution.py:297
  30.0 28.2 %collective-permute-start = (bf16[512,1024]{1,0:T(8,128)(2,1)}, bf16[512,1024]{1,0:T(8,128)(2,1)}, u32[]{:S(2)}, u32[]{:S(2)}) collective-permute-start(bf16[512,1024]{1,0:T(8,128)(2,1)} %a_ref), channel_id=1, source_target_pairs={{0,4},{4,0},{1,5},{5,1},{2,6},{6,2},{3,7},{7,3},{8,12},{12,8},{9,1... | collective-permute-start | bytes 3145736 | tf_op jit(solution)/shard_map/ppermute | solution.py:297
  32.4 25.8 %collective-permute-start.1 = (bf16[512,1024]{1,0:T(8,128)(2,1)}, bf16[512,1024]{1,0:T(8,128)(2,1)}, u32[]{:S(2)}, u32[]{:S(2)}) collective-permute-start(bf16[512,1024]{1,0:T(8,128)(2,1)} %a_ref.1), channel_id=1, source_target_pairs={{0,4},{4,0},{1,5},{5,1},{2,6},{6,2},{3,7},{7,3},{8,12},{12,8},{9,1... | collective-permute-start | bytes 3145736 | tf_op jit(solution)/shard_map/ppermute | solution.py:297
  87.1 18.3 %all-to-all-start.2 = ((f32[64,4,128]{2,1,0:T(4,128)}), f32[64,4,128]{2,1,0:T(4,128)S(1)}, u32[]{:S(2)}, u32[]{:S(2)}) async-start(f32[64,4,128]{2,1,0:T(4,128)} %get-tuple-element.29), calls=%async_computation.2 | async-start | bytes 262144 | tf_op jit(solution)/shard_map/all_to_all | solution.py:366
  97.1 1.3 copy-start
  105.4 18.2 %copy-start.1 = (bf16[1024,1024]{1,0:T(8,128)(2,1)S(1)}, bf16[1024,1024]{1,0:T(8,128)(2,1)}, u32[]{:S(2)}) copy-start(bf16[1024,1024]{1,0:T(8,128)(2,1)} %copy-done) | copy-start | bytes 6291460
  164.6 10.4 %collective-permute-start.4 = (f32[2,32,128]{2,1,0:T(8,128)S(1)}, f32[2,32,128]{2,1,0:T(8,128)S(1)}, u32[]{:S(2)}, u32[]{:S(2)}) collective-permute-start(f32[2,32,128]{2,1,0:T(8,128)S(1)} %shard_map.95), channel_id=1, source_target_pairs={{320,0},{128,1},{0,2},{384,3},{256,64},{192,65},{64,66},{448,67},{... | collective-permute-start | bytes 98312 | tf_op jit(solution)/shard_map/ppermute | solution.py:294

commit v7 on v6

--- a/solution.py
+++ b/solution.py
@@ -333,7 +333,7 @@
     project = call(
         project_body,
         (jax.ShapeDtypeStruct((size_x, rows + half // 2, 128), BF16), jax.ShapeDtypeStruct((rows, 128), F32)),
-        20,
+        48,
         inputs=6,
         flops=4 * rows * depth * size_x * 128,
         moved=8 * rows * depth,
@@ -378,14 +378,14 @@
     weigh = call(
         weigh_body,
         jax.ShapeDtypeStruct((size_z, depth // 2, 128), BF16),
-        16,
+        48,
         inputs=4,
         flops=4 * rows * depth * size_x * 128,
         moved=8 * rows * depth,
     )
     partial = weigh(at, tokens_t, grads_t, grads).reshape(2 * chips, owned, 128)
     partial = lax.all_to_all(partial, SEQ, 0, 0, tiled=True)
-    total = call(total_body, jax.ShapeDtypeStruct((2, owned, 128), F32), 6)(partial)
+    total = call(total_body, jax.ShapeDtypeStruct((2, owned, 128), F32), 48)(partial)
     total = transposed(total, True)
     grad_in, grad_proj = call(
         unpack_body,

time: 177 us -> 178 us (level)
  no operation moved by 1% of the time
where the time goes in v7:
time: 178 us; the launch traced here: 177 us
  blocking collectives  76 us (43%)
  starting transfers between devices  39.1 us (22%)
  waiting for transfers between devices  37.1 us (21%)
  Pallas kernels  21 us (12%)
  local copies, waits for them, and re-layouts  2.29 us (1%)
    all_to_all x1, blocking collectives, local(): partial = lax.all_to_all(partial, SEQ, 0, 0, tiled=True)  37.9 us
    all_to_all x1, blocking collectives, local(): parts = lax.all_to_all(parts, 'chan', 0, 0, tiled=True)  21.9 us
    all_to_all x1, waiting for transfers between devices, local(): lax.all_to_all(spread, SEQ, 0, 0, tiled=True).reshape(size_z, -1, 128)  21.7 us
    all_to_all x1, blocking collectives, local(): grads = lax.all_to_all(grads, 'chan', 0, 0, tiled=True)  16.2 us
    ppermute x2, starting transfers between devices, transposed(): return lax.ppermute(value, ('seq_0', 'chan'), pairs)  14.6 us
    all_to_all x1, starting transfers between devices, local(): lax.all_to_all(spread, SEQ, 0, 0, tiled=True).reshape(size_z, -1, 128)  12.7 us
    ppermute x2, waiting for transfers between devices, transposed(): return lax.ppermute(value, ('seq_0', 'chan'), pairs)  8.38 us
    all_to_all x1, waiting for transfers between devices, local(): states = lax.all_to_all(state, CHIPS, 0, 0, tiled=True)  6.98 us
  transfers between devices with their start and end apart: 7, of which 4 were waited for; matrix products, arithmetic and copies ran while one was open for 1% of the time, Pallas kernels for 3%

profile of v7, /device:TPU:6, one launch (start us, length us, event | category | flops | bytes accessed | tf_op | source)
XLA Modules:
  0.0 176.8 jit_solution(3084934703382288786)
XLA Ops:
  0.7 0.9 shard_map.86
  1.6 10.9 %collective-permute-start.2 = (bf16[2,32,128]{2,1,0:T(8,128)(2,1)S(1)}, bf16[2,32,128]{2,1,0:T(8,128)(2,1)S(1)}, u32[]{:S(2)}, u32[]{:S(2)}) collective-permute-start(bf16[2,32,128]{2,1,0:T(8,128)(2,1)S(1)} %shard_map.86), channel_id=1, source_target_pairs={{0,320},{1,128},{2,0},{3,384},{64,256},{65,192},{66,64},{67,448},{... | collective-permute-start | bytes 49160 | tf_op jit(solution)/shard_map/ppermute | solution.py:294
  12.5 1.7 collective-permute-done.2.piece_ref
  14.2 1.1 shard_map.87
  15.3 12.7 %all-to-all-start = ((bf16[128,32,128]{2,1,0:T(8,128)(2,1)}), bf16[128,32,128]{2,1,0:T(8,128)(2,1)S(1)}, u32[]{:S(2)}, u32[]{:S(2)}) async-start(bf16[128,32,128]{2,1,0:T(8,128)(2,1)} %shard_map.87), calls=%async_computation | async-start | bytes 2097152 | tf_op jit(solution)/shard_map/all_to_all | solution.py:304
  28.1 1.9 %collective-permute-start.3 = (bf16[512,64]{1,0:T(8,128)(2,1)S(1)}, bf16[512,64]{1,0:T(8,128)(2,1)S(1)}, u32[]{:S(2)}, u32[]{:S(2)}) collective-permute-start(bf16[512,64]{1,0:T(8,128)(2,1)S(1)} %copy.12.own_ref), channel_id=1, source_target_pairs={{0,4},{4,0},{1,5},{5,1},{2,6},{6,2},{3,7},{7,3},{8,12},{12,8},{9,1... | collective-permute-start | bytes 196616 | tf_op jit(solution)/shard_map/ppermute | solution.py:297
  30.0 2.4 %collective-permute-start = (bf16[512,1024]{1,0:T(8,128)(2,1)}, bf16[512,1024]{1,0:T(8,128)(2,1)}, u32[]{:S(2)}, u32[]{:S(2)}) collective-permute-start(bf16[512,1024]{1,0:T(8,128)(2,1)} %a_ref), channel_id=1, source_target_pairs={{0,4},{4,0},{1,5},{5,1},{2,6},{6,2},{3,7},{7,3},{8,12},{12,8},{9,1... | collective-permute-start | bytes 3145736 | tf_op jit(solution)/shard_map/ppermute | solution.py:297
  32.4 1.9 %collective-permute-start.1 = (bf16[512,1024]{1,0:T(8,128)(2,1)}, bf16[512,1024]{1,0:T(8,128)(2,1)}, u32[]{:S(2)}, u32[]{:S(2)}) collective-permute-start(bf16[512,1024]{1,0:T(8,128)(2,1)} %a_ref.1), channel_id=1, source_target_pairs={{0,4},{4,0},{1,5},{5,1},{2,6},{6,2},{3,7},{7,3},{8,12},{12,8},{9,1... | collective-permute-start | bytes 3145736 | tf_op jit(solution)/shard_map/ppermute | solution.py:297
  35.8 0.8 shard_map.88.conv_ref
  36.5 21.7 %all-to-all-done = bf16[128,32,128]{2,1,0:T(8,128)(2,1)S(1)} async-done(((bf16[128,32,128]{2,1,0:T(8,128)(2,1)}), bf16[128,32,128]{2,1,0:T(8,128)(2,1)S(1)}, u32[]{:S(2)}, u32[]{:S(2)}) %all-to-all-start) | async-done | bytes 1048608 | tf_op jit(solution)/shard_map/all_to_all | solution.py:304
  58.2 4.7 %shard_map.89 = (bf16[4,1280,128]{2,1,0:T(8,128)(2,1)S(1)}, f32[1024,128]{1,0:T(8,128)S(1)}) custom-call(s32[2]{0:T(128)S(1)} %pad_add_fusion.at_ref, bf16[512,1024]{1,0:T(8,128)(2,1)} %a_ref, bf16[512,1024]{1,0:T(8,128)(2,1)} %collective-permute-done.other_t.b_ref, bf16[512,1024]{1,0:T(8,128)(2,1)} %a_ref.1, ...), custom_call_target="tpu_custom_call" | custom-call | flops 2147483648 | bytes 8388608 | tf_op jit(solution)/shard_map/pallas_call | solution.py:341
  63.0 21.9 %all_to_all.25.part_ref = bf16[4,1280,128]{2,1,0:T(8,128)(2,1)S(1)} all-to-all(bf16[4,1280,128]{2,1,0:T(8,128)(2,1)S(1)} %get-tuple-element.25), channel_id=1, replica_groups=mesh['seq_0'=8,'seq_1'=8,'seq_2'=2,'chan'=4] {'chan'}, dimensions={0} | all-to-all | bytes 2621440 | tf_op jit(solution)/shard_map/all_to_all | solution.py:344
  84.8 2.3 %shard_map.90 = (f32[512,128]{1,0:T(8,128)S(1)}, f32[512,128]{1,0:T(8,128)S(1)}, f32[64,128]{1,0:T(8,128)S(1)}, f32[64,4,128]{2,1,0:T(4,128)}) custom-call(s32[2]{0:T(128)S(1)} %pad_add_fusion.at_ref, bf16[4,1280,128]{2,1,0:T(8,128)(2,1)S(1)} %all_to_all.25.part_ref, f32[1024,128]{1,0:T(8,128)S(1)} %get-tuple-element.26.own_ref, ...), custom_call_target="tpu_custom_call" | custom-call | tf_op jit(solution)/shard_map/pallas_call | solution.py:358
  87.1 5.6 %all-to-all-start.2 = ((f32[64,4,128]{2,1,0:T(4,128)}), f32[64,4,128]{2,1,0:T(4,128)S(1)}, u32[]{:S(2)}, u32[]{:S(2)}) async-start(f32[64,4,128]{2,1,0:T(4,128)} %get-tuple-element.29), calls=%async_computation.2 | async-start | bytes 262144 | tf_op jit(solution)/shard_map/all_to_all | solution.py:366
  92.7 2.2 %shard_map.91.tt_ref = bf16[1024,1024]{1,0:T(8,128)(2,1)S(1)} custom-call(bf16[512,1024]{1,0:T(8,128)(2,1)} %a_ref, bf16[512,1024]{1,0:T(8,128)(2,1)} %collective-permute-done.other_t.b_ref), custom_call_target="tpu_custom_call" | custom-call | bytes 4194304 | tf_op jit(solution)/shard_map/pallas_call | solution.py:364
  94.9 2.2 %shard_map.92.gt_ref = bf16[1024,1024]{1,0:T(8,128)(2,1)S(1)} custom-call(bf16[512,1024]{1,0:T(8,128)(2,1)} %a_ref.1, bf16[512,1024]{1,0:T(8,128)(2,1)} %collective-permute-done.1.other_g.b_ref), custom_call_target="tpu_custom_call" | custom-call | bytes 4194304 | tf_op jit(solution)/shard_map/pallas_call | solution.py:365
  97.1 1.3 copy-done
  98.4 7.0 %all-to-all-done.2.states_ref = f32[64,4,128]{2,1,0:T(4,128)S(1)} async-done(((f32[64,4,128]{2,1,0:T(4,128)}), f32[64,4,128]{2,1,0:T(4,128)S(1)}, u32[]{:S(2)}, u32[]{:S(2)}) %all-to-all-start.2) | async-done | bytes 131104 | tf_op jit(solution)/shard_map/all_to_all | solution.py:366
  105.4 2.0 %shard_map.93 = bf16[4,1024,128]{2,1,0:T(8,128)(2,1)S(1)} custom-call(s32[2]{0:T(128)S(1)} %pad_add_fusion.at_ref, f32[512,128]{1,0:T(8,128)S(1)} %get-tuple-element.37.x_ref, f32[512,128]{1,0:T(8,128)S(1)} %get-tuple-element.38.late_ref, f32[64,128]{1,0:T(8,128)S(1)} %get-tuple-element.30.left_ref, f32[64,4,128]{2,1,0:T(4,128)S(1)} %all-to-all-done.2.states_ref, ...), custom_call_target="tpu_custom_call" | custom-call | tf_op jit(solution)/shard_map/pallas_call | solution.py:375
  107.4 16.2 %all_to_all.26.grads_ref = bf16[4,1024,128]{2,1,0:T(8,128)(2,1)S(1)} all-to-all(bf16[4,1024,128]{2,1,0:T(8,128)(2,1)S(1)} %shard_map.93), channel_id=1, replica_groups=mesh['seq_0'=8,'seq_1'=8,'seq_2'=2,'chan'=4] {'chan'}, dimensions={0} | all-to-all | bytes 2097152 | tf_op jit(solution)/shard_map/all_to_all | solution.py:376
  123.6 4.0 %shard_map.94 = bf16[8,512,128]{2,1,0:T(8,128)(2,1)S(1)} custom-call(s32[2]{0:T(128)S(1)} %pad_add_fusion.at_ref, bf16[1024,1024]{1,0:T(8,128)(2,1)S(1)} %shard_map.91.tt_ref, bf16[1024,1024]{1,0:T(8,128)(2,1)} %copy-done, bf16[4,1024,128]{2,1,0:T(8,128)(2,1)S(1)} %all_to_all.26.grads_ref), custom_call_target="tpu_custom_call" | custom-call | flops 2147483648 | bytes 8388608 | tf_op jit(solution)/shard_map/pallas_call | solution.py:386
  127.6 37.9 %all_to_all.27.part_ref = bf16[128,32,128]{2,1,0:T(8,128)(2,1)S(1)} all-to-all(bf16[128,32,128]{2,1,0:T(8,128)(2,1)S(1)} %bitcast.17), channel_id=1, replica_groups=mesh['seq_0'=8,'seq_1'=8,'seq_2'=2,'chan'=4] {'seq_0','seq_1','seq_2'}, dimensions={0} | all-to-all | bytes 2097152 | tf_op jit(solution)/shard_map/all_to_all | solution.py:387
  165.7 3.8 %collective-permute-start.4 = (f32[2,32,128]{2,1,0:T(8,128)S(1)}, f32[2,32,128]{2,1,0:T(8,128)S(1)}, u32[]{:S(2)}, u32[]{:S(2)}) collective-permute-start(f32[2,32,128]{2,1,0:T(8,128)S(1)} %shard_map.95), channel_id=1, source_target_pairs={{320,0},{128,1},{0,2},{384,3},{256,64},{192,65},{64,66},{448,67},{... | collective-permute-start | bytes 98312 | tf_op jit(solution)/shard_map/ppermute | solution.py:294
  169.4 6.7 %collective-permute-done.4.part_ref = f32[2,32,128]{2,1,0:T(8,128)S(1)} collective-permute-done((f32[2,32,128]{2,1,0:T(8,128)S(1)}, f32[2,32,128]{2,1,0:T(8,128)S(1)}, u32[]{:S(2)}, u32[]{:S(2)}) %collective-permute-start.4) | collective-permute-done | bytes 32800 | tf_op jit(solution)/shard_map/ppermute | solution.py:294
  (33 shorter events, 2.3 us)
Async XLA Ops:
  0.6 27.3 %copy-start.1 = (bf16[512,64]{0,1:T(8,128)(2,1)S(1)}, bf16[512,64]{0,1:T(8,128)(2,1)}, u32[]{:S(2)}) copy-start(bf16[512,64]{0,1:T(8,128)(2,1)} %param.11) | copy-start | bytes 196612
  0.6 33.8 %copy-start.3 = (f32[16,32]{1,0:T(8,128)S(1)}, f32[16,32]{1,0:T(8,128)}, u32[]{:S(2)}) copy-start(f32[16,32]{1,0:T(8,128)} %param.13) | copy-start | bytes 6148
  0.7 33.8 %copy-start.2 = (f32[16,32]{1,0:T(8,128)S(1)}, f32[16,32]{1,0:T(8,128)}, u32[]{:S(2)}) copy-start(f32[16,32]{1,0:T(8,128)} %param.12) | copy-start | bytes 6148
  1.6 12.6 %collective-permute-start.2 = (bf16[2,32,128]{2,1,0:T(8,128)(2,1)S(1)}, bf16[2,32,128]{2,1,0:T(8,128)(2,1)S(1)}, u32[]{:S(2)}, u32[]{:S(2)}) collective-permute-start(bf16[2,32,128]{2,1,0:T(8,128)(2,1)S(1)} %shard_map.86), channel_id=1, source_target_pairs={{0,320},{1,128},{2,0},{3,384},{64,256},{65,192},{66,64},{67,448},{... | collective-permute-start | bytes 49160 | tf_op jit(solution)/shard_map/ppermute | solution.py:294
  15.3 43.0 %all-to-all-start = ((bf16[128,32,128]{2,1,0:T(8,128)(2,1)}), bf16[128,32,128]{2,1,0:T(8,128)(2,1)S(1)}, u32[]{:S(2)}, u32[]{:S(2)}) async-start(bf16[128,32,128]{2,1,0:T(8,128)(2,1)} %shard_map.87), calls=%async_computation | async-start | bytes 2097152 | tf_op jit(solution)/shard_map/all_to_all | solution.py:304
  28.1 7.7 %collective-permute-start.3 = (bf16[512,64]{1,0:T(8,128)(2,1)S(1)}, bf16[512,64]{1,0:T(8,128)(2,1)S(1)}, u32[]{:S(2)}, u32[]{:S(2)}) collective-permute-start(bf16[512,64]{1,0:T(8,128)(2,1)S(1)} %copy.12.own_ref), channel_id=1, source_target_pairs={{0,4},{4,0},{1,5},{5,1},{2,6},{6,2},{3,7},{7,3},{8,12},{12,8},{9,1... | collective-permute-start | bytes 196616 | tf_op jit(solution)/shard_map/ppermute | solution.py:297
  30.0 28.2 %collective-permute-start = (bf16[512,1024]{1,0:T(8,128)(2,1)}, bf16[512,1024]{1,0:T(8,128)(2,1)}, u32[]{:S(2)}, u32[]{:S(2)}) collective-permute-start(bf16[512,1024]{1,0:T(8,128)(2,1)} %a_ref), channel_id=1, source_target_pairs={{0,4},{4,0},{1,5},{5,1},{2,6},{6,2},{3,7},{7,3},{8,12},{12,8},{9,1... | collective-permute-start | bytes 3145736 | tf_op jit(solution)/shard_map/ppermute | solution.py:297
  32.4 25.8 %collective-permute-start.1 = (bf16[512,1024]{1,0:T(8,128)(2,1)}, bf16[512,1024]{1,0:T(8,128)(2,1)}, u32[]{:S(2)}, u32[]{:S(2)}) collective-permute-start(bf16[512,1024]{1,0:T(8,128)(2,1)} %a_ref.1), channel_id=1, source_target_pairs={{0,4},{4,0},{1,5},{5,1},{2,6},{6,2},{3,7},{7,3},{8,12},{12,8},{9,1... | collective-permute-start | bytes 3145736 | tf_op jit(solution)/shard_map/ppermute | solution.py:297
  87.1 18.3 %all-to-all-start.2 = ((f32[64,4,128]{2,1,0:T(4,128)}), f32[64,4,128]{2,1,0:T(4,128)S(1)}, u32[]{:S(2)}, u32[]{:S(2)}) async-start(f32[64,4,128]{2,1,0:T(4,128)} %get-tuple-element.29), calls=%async_computation.2 | async-start | bytes 262144 | tf_op jit(solution)/shard_map/all_to_all | solution.py:366
  97.1 1.3 copy-start
  165.7 10.4 %collective-permute-start.4 = (f32[2,32,128]{2,1,0:T(8,128)S(1)}, f32[2,32,128]{2,1,0:T(8,128)S(1)}, u32[]{:S(2)}, u32[]{:S(2)}) collective-permute-start(f32[2,32,128]{2,1,0:T(8,128)S(1)} %shard_map.95), channel_id=1, source_target_pairs={{320,0},{128,1},{0,2},{384,3},{256,64},{192,65},{64,66},{448,67},{... | collective-permute-start | bytes 98312 | tf_op jit(solution)/shard_map/ppermute | solution.py:294

commit v8 on v6

--- a/solution.py
+++ b/solution.py
@@ -162,7 +162,8 @@
 
 
 def first_body(
-    at_ref, part_ref, own_ref, decay_ref, far_ref, x_ref, late_ref, left_ref, state_ref, sig, st
+    at_ref, part_ref, own_ref, decay_ref, far_ref, conv_ref, x_ref, late_ref, left_ref, state_ref,
+    early_ref, sig, st,
 ):
     core = at_ref[0]
     rows = sig.shape[0]
@@ -178,6 +179,9 @@
     x = jnp.where(lane_group(early.shape) < 2, early.astype(BF16).astype(F32), early)
     x_ref[...] = x
     late_ref[...] = total[half:].astype(BF16).astype(F32)
+    grads = x * conv_ref[...].astype(F32)
+    odd = lane_group(grads.shape) % 2 == 1
+    early_ref[...] = jnp.where(odd, grads, turn(grads, 64))
     store_signal(x, sig)
     decay = [decay_ref[m : m + 1, :] for m in range(MODE_ROWS)]
     chunks = rows // STEPS
@@ -206,7 +210,7 @@
 
 def second_body(
     at_ref, x_ref, late_ref, left_ref, states_ref, reach_ref, power_ref, decay_ref, weight_ref,
-    conv_ref, out_ref, sig, ys,
+    out_ref, sig, ys,
 ):
     core = at_ref[0]
     rows = sig.shape[0]
@@ -241,27 +245,32 @@
     y = y + turn(y, 64)
     y = y + turn(y, 32)
     odd = lane_group((half, 128)) % 2 == 1
-    late = turn(late_ref[...], 64) * jnp.where(odd, y[half:], y[:half])
-    early = x_ref[...] * conv_ref[...].astype(F32)
-    own = jnp.where(odd, early, late)
-    other = turn(jnp.where(odd, late, turn(early, 64)), 96)
-    out = jnp.concatenate([own, other], axis=0).astype(BF16)
+    out = (turn(late_ref[...], 64) * jnp.where(odd, y[half:], y[:half])).astype(BF16)
     for k in range(out_ref.shape[0]):
         out_ref[k] = out
 
 
-def weigh_body(at_ref, tt_ref, gt_ref, grads_ref, out_ref):
+def weigh_body(at_ref, tt_ref, gt_ref, early_ref, late_ref, out_ref):
     plane = at_ref[1]
     block = out_ref.shape[1]
-    for l in range(2):
-        r = l * block
-        for c in range(0, grads_ref.shape[0], 2):
-            g = jnp.concatenate([grads_ref[chunk_of(plane, c + k)] for k in range(2)], axis=1)
-            from_t = jnp.dot(tt_ref[r : r + block, :], g, preferred_element_type=F32)
-            from_g = jnp.dot(gt_ref[r : r + block, :], g, preferred_element_type=F32)
+
+    def columns(e):
+        early = early_ref[chunk_of(plane, e)]
+        late = late_ref[chunk_of(plane, e)].astype(F32)
+        odd = lane_group(early.shape) % 2 == 1
+        own = jnp.where(odd, early, late)
+        other = turn(jnp.where(odd, late, early), 96)
+        return jnp.concatenate([own, other], axis=0).astype(BF16)
+
+    for e in range(0, early_ref.shape[0], 2):
+        g = jnp.concatenate([columns(e), columns(e + 1)], axis=1)
+        for l in range(2):
+            here = slice(l * block, (l + 1) * block)
+            from_t = jnp.dot(tt_ref[here, :], g, preferred_element_type=F32)
+            from_g = jnp.dot(gt_ref[here, :], g, preferred_element_type=F32)
             both = jnp.where(lane_group(from_t.shape) % GROUPS != 1, from_t, from_g).astype(BF16)
-            out_ref[holder(plane, c, l)] = both[:, :128]
-            out_ref[holder(plane, c + 1, l)] = both[:, 128:]
+            out_ref[holder(plane, e, l)] = both[:, :128]
+            out_ref[holder(plane, e + 1, l)] = both[:, 128:]
 
 
 def by_lanes(table):
@@ -350,12 +359,14 @@
             jax.ShapeDtypeStruct((half, 128), F32),
             jax.ShapeDtypeStruct((MODE_ROWS * chunks, 128), F32),
             jax.ShapeDtypeStruct((chips, MODE_ROWS, 128), F32),
+            pltpu.HBM((half, 128), F32),
         ),
         10,
         scratch=[pltpu.VMEM((rows, 128), F32), pltpu.VMEM((MODE_ROWS * chunks, 128), F32)],
-        inputs=5,
-    )
-    x, late, left, state = first(at, parts, own, decay, far)
+        inputs=6,
+    )
+    x, late, left, state, early = first(at, parts, own, decay, far, conv)
+    early = lax.all_gather(early, "chan", axis=0)
     _, *turned = lax.optimization_barrier((left, tokens, tokens_too, grad_out, grads_too))
     turned = [in_hbm(t) for t in turned]
     flip = call(
@@ -367,23 +378,23 @@
     states, tokens_t, grads_t = lax.optimization_barrier((states, tokens_t, grads_t))
     second = call(
         second_body,
-        jax.ShapeDtypeStruct((size_x, rows, 128), BF16),
+        jax.ShapeDtypeStruct((size_x, half, 128), BF16),
         10,
         scratch=[pltpu.VMEM((rows, 128), F32), pltpu.VMEM((rows, 128), F32)],
-        inputs=10,
-    )
-    grads = second(at, x, late, left, states, reach, power, decay, weight, conv)
+        inputs=9,
+    )
+    grads = second(at, x, late, left, states, reach, power, decay, weight)
     grads = lax.all_to_all(grads, "chan", 0, 0, tiled=True)
 
     weigh = call(
         weigh_body,
         jax.ShapeDtypeStruct((size_z, depth // 2, 128), BF16),
         16,
-        inputs=4,
+        inputs=5,
         flops=4 * rows * depth * size_x * 128,
         moved=8 * rows * depth,
     )
-    partial = weigh(at, tokens_t, grads_t, grads).reshape(2 * chips, owned, 128)
+    partial = weigh(at, tokens_t, grads_t, in_hbm(early), grads).reshape(2 * chips, owned, 128)
     partial = lax.all_to_all(partial, SEQ, 0, 0, tiled=True)
     total = call(total_body, jax.ShapeDtypeStruct((2, owned, 128), F32), 6)(partial)
     total = transposed(total, True)

time: 177 us -> 189 us (1.068)
  between operations: 0.89 us -> 14.3 us
  blocking collectives: 76 us -> 72.9 us
    all_to_all x1, blocking collectives: 16.2 us -> 10.6 us  [local(): grads = lax.all_to_all(grads, 'chan', 0, 0, tiled=True)]
    all_to_all x1, blocking collectives: 37.9 us -> 40.4 us  [local(): partial = lax.all_to_all(partial, SEQ, 0, 0, tiled=True)]
  transfers between devices with their start and end apart: 7 -> 8, of which waited for: 4 -> 4; matrix products, arithmetic and copies ran while one was open for 1% -> 1% of each run, Pallas kernels for 3% -> 4%
where the time goes in v8:
time: 189 us; the launch traced here: 188 us
  blocking collectives  72.9 us (39%)
  starting transfers between devices  38.1 us (20%)
  waiting for transfers between devices  37.6 us (20%)
  Pallas kernels  20.8 us (11%)
  between operations  14.3 us (8%)
  local copies, waits for them, and re-layouts  3.88 us (2%)
    all_to_all x1, blocking collectives, local(): partial = lax.all_to_all(partial, SEQ, 0, 0, tiled=True)  40.4 us
    all_to_all x1, blocking collectives, local(): parts = lax.all_to_all(parts, 'chan', 0, 0, tiled=True)  21.9 us
    all_to_all x1, waiting for transfers between devices, local(): lax.all_to_all(spread, SEQ, 0, 0, tiled=True).reshape(size_z, -1, 128)  21.7 us
    ppermute x2, starting transfers between devices, transposed(): return lax.ppermute(value, ('seq_0', 'chan'), pairs)  13.6 us
    all_to_all x1, starting transfers between devices, local(): lax.all_to_all(spread, SEQ, 0, 0, tiled=True).reshape(size_z, -1, 128)  12.7 us
    all_to_all x1, blocking collectives, local(): grads = lax.all_to_all(grads, 'chan', 0, 0, tiled=True)  10.6 us
    ppermute x2, waiting for transfers between devices, transposed(): return lax.ppermute(value, ('seq_0', 'chan'), pairs)  8.96 us
    all_to_all x1, waiting for transfers between devices, local(): states = lax.all_to_all(state, CHIPS, 0, 0, tiled=True)  6.94 us
  transfers between devices with their start and end apart: 8, of which 4 were waited for; matrix products, arithmetic and copies ran while one was open for 1% of the time, Pallas kernels for 4%

profile of v8, /device:TPU:6, one launch (start us, length us, event | category | flops | bytes accessed | tf_op | source)
XLA Modules:
  0.0 188.0 jit_solution(6276008253211187081)
XLA Ops:
  7.2 0.9 shard_map.86
  8.1 10.9 %collective-permute-start.2 = (bf16[2,32,128]{2,1,0:T(8,128)(2,1)S(1)}, bf16[2,32,128]{2,1,0:T(8,128)(2,1)S(1)}, u32[]{:S(2)}, u32[]{:S(2)}) collective-permute-start(bf16[2,32,128]{2,1,0:T(8,128)(2,1)S(1)} %shard_map.86), channel_id=1, source_target_pairs={{0,320},{1,128},{2,0},{3,384},{64,256},{65,192},{66,64},{67,448},{... | collective-permute-start | bytes 49160 | tf_op jit(solution)/shard_map/ppermute | solution.py:303
  19.0 1.7 collective-permute-done.2.piece_ref
  20.7 1.1 shard_map.87
  21.8 12.7 %all-to-all-start = ((bf16[128,32,128]{2,1,0:T(8,128)(2,1)}), bf16[128,32,128]{2,1,0:T(8,128)(2,1)S(1)}, u32[]{:S(2)}, u32[]{:S(2)}) async-start(bf16[128,32,128]{2,1,0:T(8,128)(2,1)} %shard_map.87), calls=%async_computation | async-start | bytes 2097152 | tf_op jit(solution)/shard_map/all_to_all | solution.py:313
  34.7 1.9 %collective-permute-start.3 = (bf16[512,64]{1,0:T(8,128)(2,1)S(1)}, bf16[512,64]{1,0:T(8,128)(2,1)S(1)}, u32[]{:S(2)}, u32[]{:S(2)}) collective-permute-start(bf16[512,64]{1,0:T(8,128)(2,1)S(1)} %copy.12.own_ref), channel_id=1, source_target_pairs={{0,4},{4,0},{1,5},{5,1},{2,6},{6,2},{3,7},{7,3},{8,12},{12,8},{9,1... | collective-permute-start | bytes 196616 | tf_op jit(solution)/shard_map/ppermute | solution.py:306
  36.6 2.4 %collective-permute-start = (bf16[512,1024]{1,0:T(8,128)(2,1)}, bf16[512,1024]{1,0:T(8,128)(2,1)}, u32[]{:S(2)}, u32[]{:S(2)}) collective-permute-start(bf16[512,1024]{1,0:T(8,128)(2,1)} %a_ref), channel_id=1, source_target_pairs={{0,4},{4,0},{1,5},{5,1},{2,6},{6,2},{3,7},{7,3},{8,12},{12,8},{9,1... | collective-permute-start | bytes 3145736 | tf_op jit(solution)/shard_map/ppermute | solution.py:306
  39.0 1.9 %collective-permute-start.1 = (bf16[512,1024]{1,0:T(8,128)(2,1)}, bf16[512,1024]{1,0:T(8,128)(2,1)}, u32[]{:S(2)}, u32[]{:S(2)}) collective-permute-start(bf16[512,1024]{1,0:T(8,128)(2,1)} %a_ref.1), channel_id=1, source_target_pairs={{0,4},{4,0},{1,5},{5,1},{2,6},{6,2},{3,7},{7,3},{8,12},{12,8},{9,1... | collective-permute-start | bytes 3145736 | tf_op jit(solution)/shard_map/ppermute | solution.py:306
  43.1 21.7 %all-to-all-done = bf16[128,32,128]{2,1,0:T(8,128)(2,1)S(1)} async-done(((bf16[128,32,128]{2,1,0:T(8,128)(2,1)}), bf16[128,32,128]{2,1,0:T(8,128)(2,1)S(1)}, u32[]{:S(2)}, u32[]{:S(2)}) %all-to-all-start) | async-done | bytes 1048608 | tf_op jit(solution)/shard_map/all_to_all | solution.py:313
  64.8 4.7 %shard_map.89 = (bf16[4,1280,128]{2,1,0:T(8,128)(2,1)S(1)}, f32[1024,128]{1,0:T(8,128)S(1)}) custom-call(s32[2]{0:T(128)S(1)} %pad_add_fusion.at_ref, bf16[512,1024]{1,0:T(8,128)(2,1)} %a_ref, bf16[512,1024]{1,0:T(8,128)(2,1)} %collective-permute-done.other_t.b_ref, bf16[512,1024]{1,0:T(8,128)(2,1)} %a_ref.1, ...), custom_call_target="tpu_custom_call" | custom-call | flops 2147483648 | bytes 8388608 | tf_op jit(solution)/shard_map/pallas_call | solution.py:350
  69.5 21.9 %all_to_all.25.part_ref = bf16[4,1280,128]{2,1,0:T(8,128)(2,1)S(1)} all-to-all(bf16[4,1280,128]{2,1,0:T(8,128)(2,1)S(1)} %get-tuple-element.26), channel_id=1, replica_groups=mesh['seq_0'=8,'seq_1'=8,'seq_2'=2,'chan'=4] {'chan'}, dimensions={0} | all-to-all | bytes 2621440 | tf_op jit(solution)/shard_map/all_to_all | solution.py:353
  91.4 2.4 %shard_map.90 = (f32[512,128]{1,0:T(8,128)S(1)}, f32[512,128]{1,0:T(8,128)S(1)}, f32[64,128]{1,0:T(8,128)S(1)}, f32[64,4,128]{2,1,0:T(4,128)}, f32[512,128]{1,0:T(8,128)}) custom-call(s32[2]{0:T(128)S(1)} %pad_add_fusion.at_ref, bf16[4,1280,128]{2,1,0:T(8,128)(2,1)S(1)} %all_to_all.25.part_ref, f32[1024,128]{1,0:T(8,128)S(1)} %get-tuple-element.27.own_ref, ...), custom_call_target="tpu_custom_call" | custom-call | tf_op jit(solution)/shard_map/pallas_call | solution.py:368
  93.8 5.6 %all-to-all-start.2 = ((f32[64,4,128]{2,1,0:T(4,128)}), f32[64,4,128]{2,1,0:T(4,128)S(1)}, u32[]{:S(2)}, u32[]{:S(2)}) async-start(f32[64,4,128]{2,1,0:T(4,128)} %get-tuple-element.31), calls=%async_computation.2 | async-start | bytes 262144 | tf_op jit(solution)/shard_map/all_to_all | solution.py:377
  99.4 2.2 %shard_map.92.gt_ref = bf16[1024,1024]{1,0:T(8,128)(2,1)S(1)} custom-call(bf16[512,1024]{1,0:T(8,128)(2,1)} %a_ref.1, bf16[512,1024]{1,0:T(8,128)(2,1)} %collective-permute-done.1.other_g.b_ref), custom_call_target="tpu_custom_call" | custom-call | bytes 4194304 | tf_op jit(solution)/shard_map/pallas_call | solution.py:376
  101.6 2.2 %shard_map.91.tt_ref = bf16[1024,1024]{1,0:T(8,128)(2,1)S(1)} custom-call(bf16[512,1024]{1,0:T(8,128)(2,1)} %a_ref, bf16[512,1024]{1,0:T(8,128)(2,1)} %collective-permute-done.other_t.b_ref), custom_call_target="tpu_custom_call" | custom-call | bytes 4194304 | tf_op jit(solution)/shard_map/pallas_call | solution.py:375
  103.9 1.3 copy-done
  105.2 6.9 %all-to-all-done.2.states_ref = f32[64,4,128]{2,1,0:T(4,128)S(1)} async-done(((f32[64,4,128]{2,1,0:T(4,128)}), f32[64,4,128]{2,1,0:T(4,128)S(1)}, u32[]{:S(2)}, u32[]{:S(2)}) %all-to-all-start.2) | async-done | bytes 131104 | tf_op jit(solution)/shard_map/all_to_all | solution.py:377
  112.1 1.9 %shard_map.93 = bf16[4,512,128]{2,1,0:T(8,128)(2,1)S(1)} custom-call(s32[2]{0:T(128)S(1)} %pad_add_fusion.at_ref, f32[512,128]{1,0:T(8,128)S(1)} %get-tuple-element.40.x_ref, f32[512,128]{1,0:T(8,128)S(1)} %get-tuple-element.41.late_ref, f32[64,128]{1,0:T(8,128)S(1)} %get-tuple-element.32.left_ref, f32[64,4,128]{2,1,0:T(4,128)S(1)} %all-to-all-done.2.states_ref, ...), custom_call_target="tpu_custom_call" | custom-call | tf_op jit(solution)/shard_map/pallas_call | solution.py:386
  114.0 10.6 %all_to_all.26.late_ref = bf16[4,512,128]{2,1,0:T(8,128)(2,1)S(1)} all-to-all(bf16[4,512,128]{2,1,0:T(8,128)(2,1)S(1)} %shard_map.93), channel_id=1, replica_groups=mesh['seq_0'=8,'seq_1'=8,'seq_2'=2,'chan'=4] {'chan'}, dimensions={0} | all-to-all | bytes 1048576 | tf_op jit(solution)/shard_map/all_to_all | solution.py:387
  124.7 1.6 copy-done.1
  126.2 3.6 %shard_map.94 = bf16[8,512,128]{2,1,0:T(8,128)(2,1)S(1)} custom-call(s32[2]{0:T(128)S(1)} %pad_add_fusion.at_ref, bf16[1024,1024]{1,0:T(8,128)(2,1)S(1)} %copy-done.1, bf16[1024,1024]{1,0:T(8,128)(2,1)S(1)} %shard_map.92.gt_ref, f32[4,512,128]{2,1,0:T(8,128)} %bitcast.22, bf16[4,512,128]{2,1,0:T(8,128)(2,1)S(1)} %all_to_all.26.late_ref), custom_call_target="tpu_custom_call" | custom-call | flops 2147483648 | bytes 8388608 | tf_op jit(solution)/shard_map/pallas_call | solution.py:397
  129.9 40.4 %all_to_all.27.part_ref = bf16[128,32,128]{2,1,0:T(8,128)(2,1)S(1)} all-to-all(bf16[128,32,128]{2,1,0:T(8,128)(2,1)S(1)} %bitcast.18), channel_id=1, replica_groups=mesh['seq_0'=8,'seq_1'=8,'seq_2'=2,'chan'=4] {'seq_0','seq_1','seq_2'}, dimensions={0} | all-to-all | bytes 2097152 | tf_op jit(solution)/shard_map/all_to_all | solution.py:398
  170.4 2.8 %collective-permute-start.4 = (f32[2,32,128]{2,1,0:T(8,128)S(1)}, f32[2,32,128]{2,1,0:T(8,128)S(1)}, u32[]{:S(2)}, u32[]{:S(2)}) collective-permute-start(f32[2,32,128]{2,1,0:T(8,128)S(1)} %shard_map.95), channel_id=1, source_target_pairs={{320,0},{128,1},{0,2},{384,3},{256,64},{192,65},{64,66},{448,67},{... | collective-permute-start | bytes 98312 | tf_op jit(solution)/shard_map/ppermute | solution.py:303
  173.2 7.3 %collective-permute-done.4.part_ref = f32[2,32,128]{2,1,0:T(8,128)S(1)} collective-permute-done((f32[2,32,128]{2,1,0:T(8,128)S(1)}, f32[2,32,128]{2,1,0:T(8,128)S(1)}, u32[]{:S(2)}, u32[]{:S(2)}) %collective-permute-start.4) | collective-permute-done | bytes 32800 | tf_op jit(solution)/shard_map/ppermute | solution.py:303
  (38 shorter events, 3.2 us)
Async XLA Ops:
  7.2 27.4 %copy-start.2 = (bf16[512,64]{0,1:T(8,128)(2,1)S(1)}, bf16[512,64]{0,1:T(8,128)(2,1)}, u32[]{:S(2)}) copy-start(bf16[512,64]{0,1:T(8,128)(2,1)} %param.11) | copy-start | bytes 196612
  7.2 33.8 %copy-start.3 = (f32[16,32]{1,0:T(8,128)S(1)}, f32[16,32]{1,0:T(8,128)}, u32[]{:S(2)}) copy-start(f32[16,32]{1,0:T(8,128)} %param.12) | copy-start | bytes 6148
  7.2 33.8 %copy-start.4 = (f32[16,32]{1,0:T(8,128)S(1)}, f32[16,32]{1,0:T(8,128)}, u32[]{:S(2)}) copy-start(f32[16,32]{1,0:T(8,128)} %param.13) | copy-start | bytes 6148
  8.1 12.6 %collective-permute-start.2 = (bf16[2,32,128]{2,1,0:T(8,128)(2,1)S(1)}, bf16[2,32,128]{2,1,0:T(8,128)(2,1)S(1)}, u32[]{:S(2)}, u32[]{:S(2)}) collective-permute-start(bf16[2,32,128]{2,1,0:T(8,128)(2,1)S(1)} %shard_map.86), channel_id=1, source_target_pairs={{0,320},{1,128},{2,0},{3,384},{64,256},{65,192},{66,64},{67,448},{... | collective-permute-start | bytes 49160 | tf_op jit(solution)/shard_map/ppermute | solution.py:303
  21.8 43.0 %all-to-all-start = ((bf16[128,32,128]{2,1,0:T(8,128)(2,1)}), bf16[128,32,128]{2,1,0:T(8,128)(2,1)S(1)}, u32[]{:S(2)}, u32[]{:S(2)}) async-start(bf16[128,32,128]{2,1,0:T(8,128)(2,1)} %shard_map.87), calls=%async_computation | async-start | bytes 2097152 | tf_op jit(solution)/shard_map/all_to_all | solution.py:313
  34.5 90.2 %all-gather.3.cloned.1.call-start = ((), (), s32[]{:S(2)}) async-start(), calls=%async_computation.5 | async-start | bytes 1310720 | tf_op jit(solution)/shard_map/all_gather | solution.py:369
  34.7 7.7 %collective-permute-start.3 = (bf16[512,64]{1,0:T(8,128)(2,1)S(1)}, bf16[512,64]{1,0:T(8,128)(2,1)S(1)}, u32[]{:S(2)}, u32[]{:S(2)}) collective-permute-start(bf16[512,64]{1,0:T(8,128)(2,1)S(1)} %copy.12.own_ref), channel_id=1, source_target_pairs={{0,4},{4,0},{1,5},{5,1},{2,6},{6,2},{3,7},{7,3},{8,12},{12,8},{9,1... | collective-permute-start | bytes 196616 | tf_op jit(solution)/shard_map/ppermute | solution.py:306
  36.6 28.2 %collective-permute-start = (bf16[512,1024]{1,0:T(8,128)(2,1)}, bf16[512,1024]{1,0:T(8,128)(2,1)}, u32[]{:S(2)}, u32[]{:S(2)}) collective-permute-start(bf16[512,1024]{1,0:T(8,128)(2,1)} %a_ref), channel_id=1, source_target_pairs={{0,4},{4,0},{1,5},{5,1},{2,6},{6,2},{3,7},{7,3},{8,12},{12,8},{9,1... | collective-permute-start | bytes 3145736 | tf_op jit(solution)/shard_map/ppermute | solution.py:306
  39.0 25.8 %collective-permute-start.1 = (bf16[512,1024]{1,0:T(8,128)(2,1)}, bf16[512,1024]{1,0:T(8,128)(2,1)}, u32[]{:S(2)}, u32[]{:S(2)}) collective-permute-start(bf16[512,1024]{1,0:T(8,128)(2,1)} %a_ref.1), channel_id=1, source_target_pairs={{0,4},{4,0},{1,5},{5,1},{2,6},{6,2},{3,7},{7,3},{8,12},{12,8},{9,1... | collective-permute-start | bytes 3145736 | tf_op jit(solution)/shard_map/ppermute | solution.py:306
  93.8 18.3 %all-to-all-start.2 = ((f32[64,4,128]{2,1,0:T(4,128)}), f32[64,4,128]{2,1,0:T(4,128)S(1)}, u32[]{:S(2)}, u32[]{:S(2)}) async-start(f32[64,4,128]{2,1,0:T(4,128)} %get-tuple-element.31), calls=%async_computation.2 | async-start | bytes 262144 | tf_op jit(solution)/shard_map/all_to_all | solution.py:377
  103.8 1.3 copy-start
  124.7 1.6 copy-start.1
  170.4 10.0 %collective-permute-start.4 = (f32[2,32,128]{2,1,0:T(8,128)S(1)}, f32[2,32,128]{2,1,0:T(8,128)S(1)}, u32[]{:S(2)}, u32[]{:S(2)}) collective-permute-start(f32[2,32,128]{2,1,0:T(8,128)S(1)} %shard_map.95), channel_id=1, source_target_pairs={{320,0},{128,1},{0,2},{384,3},{256,64},{192,65},{64,66},{448,67},{... | collective-permute-start | bytes 98312 | tf_op jit(solution)/shard_map/ppermute | solution.py:303
Sparse Core Ops, SparseCore 0:
  94.0 21.3 all-gather.2

commit v9 on v8

--- a/solution.py
+++ b/solution.py
@@ -181,7 +181,7 @@
     late_ref[...] = total[half:].astype(BF16).astype(F32)
     grads = x * conv_ref[...].astype(F32)
     odd = lane_group(grads.shape) % 2 == 1
-    early_ref[...] = jnp.where(odd, grads, turn(grads, 64))
+    early_ref[...] = jnp.where(odd, grads, turn(grads, 64)).astype(BF16)
     store_signal(x, sig)
     decay = [decay_ref[m : m + 1, :] for m in range(MODE_ROWS)]
     chunks = rows // STEPS
@@ -250,19 +250,20 @@
         out_ref[k] = out
 
 
-def weigh_body(at_ref, tt_ref, gt_ref, early_ref, late_ref, out_ref):
+def weigh_body(at_ref, tt_ref, gt_ref, early_a, early_b, early_c, early_d, late_ref, out_ref):
     plane = at_ref[1]
     block = out_ref.shape[1]
+    early_refs = (early_a, early_b, early_c, early_d)
 
     def columns(e):
-        early = early_ref[chunk_of(plane, e)]
+        early = early_refs[e][...].astype(F32)
         late = late_ref[chunk_of(plane, e)].astype(F32)
         odd = lane_group(early.shape) % 2 == 1
         own = jnp.where(odd, early, late)
         other = turn(jnp.where(odd, late, early), 96)
         return jnp.concatenate([own, other], axis=0).astype(BF16)
 
-    for e in range(0, early_ref.shape[0], 2):
+    for e in range(0, len(early_refs), 2):
         g = jnp.concatenate([columns(e), columns(e + 1)], axis=1)
         for l in range(2):
             here = slice(l * block, (l + 1) * block)
@@ -359,14 +360,13 @@
             jax.ShapeDtypeStruct((half, 128), F32),
             jax.ShapeDtypeStruct((MODE_ROWS * chunks, 128), F32),
             jax.ShapeDtypeStruct((chips, MODE_ROWS, 128), F32),
-            pltpu.HBM((half, 128), F32),
+            jax.ShapeDtypeStruct((half, 128), BF16),
         ),
         10,
         scratch=[pltpu.VMEM((rows, 128), F32), pltpu.VMEM((MODE_ROWS * chunks, 128), F32)],
         inputs=6,
     )
     x, late, left, state, early = first(at, parts, own, decay, far, conv)
-    early = lax.all_gather(early, "chan", axis=0)
     _, *turned = lax.optimization_barrier((left, tokens, tokens_too, grad_out, grads_too))
     turned = [in_hbm(t) for t in turned]
     flip = call(
@@ -374,8 +374,15 @@
     )
     tokens_t = flip(*turned[:2])
     grads_t = flip(*turned[2:])
+    early, tokens_t = lax.optimization_barrier((early, tokens_t))
+    early = [early] + [
+        lax.ppermute(early, "chan", [(k, (k - e) % size_x) for k in range(size_x)])
+        for e in range(1, size_x)
+    ]
     states = lax.all_to_all(state, CHIPS, 0, 0, tiled=True)
-    states, tokens_t, grads_t = lax.optimization_barrier((states, tokens_t, grads_t))
+    states, tokens_t, grads_t, *early = lax.optimization_barrier(
+        (states, tokens_t, grads_t, *early)
+    )
     second = call(
         second_body,
         jax.ShapeDtypeStruct((size_x, half, 128), BF16),
@@ -390,11 +397,11 @@
         weigh_body,
         jax.ShapeDtypeStruct((size_z, depth // 2, 128), BF16),
         16,
-        inputs=5,
+        inputs=8,
         flops=4 * rows * depth * size_x * 128,
         moved=8 * rows * depth,
     )
-    partial = weigh(at, tokens_t, grads_t, in_hbm(early), grads).reshape(2 * chips, owned, 128)
+    partial = weigh(at, tokens_t, grads_t, *early, grads).reshape(2 * chips, owned, 128)
     partial = lax.all_to_all(partial, SEQ, 0, 0, tiled=True)
     total = call(total_body, jax.ShapeDtypeStruct((2, owned, 128), F32), 6)(partial)
     total = transposed(total, True)

time: 189 us -> 182 us (0.963)
  between operations: 14.3 us -> 0.9 us
  starting transfers between devices: 38.1 us -> 49.5 us
  waiting for transfers between devices: 37.6 us -> 30.3 us
  blocking collectives: 72.9 us -> 76.9 us
    ppermute x0 -> x3, starting transfers between devices: none -> 10.4 us  [local(): lax.ppermute(early, 'chan', [(k, (k - e) % size_x) for k in range(size_x)])]
    all_to_all x1, waiting for transfers between devices: 6.94 us -> 0.01 us  [local(): states = lax.all_to_all(state, CHIPS, 0, 0, tiled=True)]
    all_to_all x1, blocking collectives: 40.4 us -> 43.8 us  [local(): partial = lax.all_to_all(partial, SEQ, 0, 0, tiled=True)]
  transfers between devices with their start and end apart: 8 -> 10, of which waited for: 4 -> 4; matrix products, arithmetic and copies ran while one was open for 1% -> 1% of each run, Pallas kernels for 4% -> 3%
where the time goes in v9:
time: 182 us; the launch traced here: 180 us
  blocking collectives  76.9 us (42%)
  starting transfers between devices  49.5 us (27%)
  waiting for transfers between devices  30.3 us (17%)
  Pallas kernels  20 us (11%)
  local copies, waits for them, and re-layouts  2.29 us (1%)
    all_to_all x1, blocking collectives, local(): partial = lax.all_to_all(partial, SEQ, 0, 0, tiled=True)  43.8 us
    all_to_all x1, blocking collectives, local(): parts = lax.all_to_all(parts, 'chan', 0, 0, tiled=True)  21.9 us
    all_to_all x1, waiting for transfers between devices, local(): lax.all_to_all(spread, SEQ, 0, 0, tiled=True).reshape(size_z, -1, 128)  21.7 us
    ppermute x2, starting transfers between devices, transposed(): return lax.ppermute(value, ('seq_0', 'chan'), pairs)  14.6 us
    all_to_all x1, starting transfers between devices, local(): lax.all_to_all(spread, SEQ, 0, 0, tiled=True).reshape(size_z, -1, 128)  12.7 us
    all_to_all x1, blocking collectives, local(): grads = lax.all_to_all(grads, 'chan', 0, 0, tiled=True)  11.3 us
    ppermute x3, starting transfers between devices, local(): lax.ppermute(early, 'chan', [(k, (k - e) % size_x) for k in range(size_x)])  10.4 us
    ppermute x2, waiting for transfers between devices, transposed(): return lax.ppermute(value, ('seq_0', 'chan'), pairs)  8.38 us
  transfers between devices with their start and end apart: 10, of which 4 were waited for; matrix products, arithmetic and copies ran while one was open for 1% of the time, Pallas kernels for 3%

profile of v9, /device:TPU:6, one launch (start us, length us, event | category | flops | bytes accessed | tf_op | source)
XLA Modules:
  0.0 180.4 jit_solution(7656151265064325855)
XLA Ops:
  1.6 10.9 %collective-permute-start.2 = (bf16[2,32,128]{2,1,0:T(8,128)(2,1)S(1)}, bf16[2,32,128]{2,1,0:T(8,128)(2,1)S(1)}, u32[]{:S(2)}, u32[]{:S(2)}) collective-permute-start(bf16[2,32,128]{2,1,0:T(8,128)(2,1)S(1)} %shard_map.86), channel_id=1, source_target_pairs={{0,320},{1,128},{2,0},{3,384},{64,256},{65,192},{66,64},{67,448},{... | collective-permute-start | bytes 49160 | tf_op jit(solution)/shard_map/ppermute | solution.py:304
  12.5 1.7 collective-permute-done.2.piece_ref
  14.2 1.1 shard_map.87
  15.3 12.7 %all-to-all-start = ((bf16[128,32,128]{2,1,0:T(8,128)(2,1)}), bf16[128,32,128]{2,1,0:T(8,128)(2,1)S(1)}, u32[]{:S(2)}, u32[]{:S(2)}) async-start(bf16[128,32,128]{2,1,0:T(8,128)(2,1)} %shard_map.87), calls=%async_computation | async-start | bytes 2097152 | tf_op jit(solution)/shard_map/all_to_all | solution.py:314
  28.1 1.9 %collective-permute-start.3 = (bf16[512,64]{1,0:T(8,128)(2,1)S(1)}, bf16[512,64]{1,0:T(8,128)(2,1)S(1)}, u32[]{:S(2)}, u32[]{:S(2)}) collective-permute-start(bf16[512,64]{1,0:T(8,128)(2,1)S(1)} %copy.12.own_ref), channel_id=1, source_target_pairs={{0,4},{4,0},{1,5},{5,1},{2,6},{6,2},{3,7},{7,3},{8,12},{12,8},{9,1... | collective-permute-start | bytes 196616 | tf_op jit(solution)/shard_map/ppermute | solution.py:307
  30.0 2.4 %collective-permute-start = (bf16[512,1024]{1,0:T(8,128)(2,1)}, bf16[512,1024]{1,0:T(8,128)(2,1)}, u32[]{:S(2)}, u32[]{:S(2)}) collective-permute-start(bf16[512,1024]{1,0:T(8,128)(2,1)} %a_ref), channel_id=1, source_target_pairs={{0,4},{4,0},{1,5},{5,1},{2,6},{6,2},{3,7},{7,3},{8,12},{12,8},{9,1... | collective-permute-start | bytes 3145736 | tf_op jit(solution)/shard_map/ppermute | solution.py:307
  32.4 1.9 %collective-permute-start.1 = (bf16[512,1024]{1,0:T(8,128)(2,1)}, bf16[512,1024]{1,0:T(8,128)(2,1)}, u32[]{:S(2)}, u32[]{:S(2)}) collective-permute-start(bf16[512,1024]{1,0:T(8,128)(2,1)} %a_ref.1), channel_id=1, source_target_pairs={{0,4},{4,0},{1,5},{5,1},{2,6},{6,2},{3,7},{7,3},{8,12},{12,8},{9,1... | collective-permute-start | bytes 3145736 | tf_op jit(solution)/shard_map/ppermute | solution.py:307
  36.5 21.7 %all-to-all-done = bf16[128,32,128]{2,1,0:T(8,128)(2,1)S(1)} async-done(((bf16[128,32,128]{2,1,0:T(8,128)(2,1)}), bf16[128,32,128]{2,1,0:T(8,128)(2,1)S(1)}, u32[]{:S(2)}, u32[]{:S(2)}) %all-to-all-start) | async-done | bytes 1048608 | tf_op jit(solution)/shard_map/all_to_all | solution.py:314
  58.2 4.7 %shard_map.89 = (bf16[4,1280,128]{2,1,0:T(8,128)(2,1)S(1)}, f32[1024,128]{1,0:T(8,128)S(1)}) custom-call(s32[2]{0:T(128)S(1)} %pad_add_fusion.at_ref, bf16[512,1024]{1,0:T(8,128)(2,1)} %a_ref, bf16[512,1024]{1,0:T(8,128)(2,1)} %collective-permute-done.other_t.b_ref, bf16[512,1024]{1,0:T(8,128)(2,1)} %a_ref.1, ...), custom_call_target="tpu_custom_call" | custom-call | flops 2147483648 | bytes 8388608 | tf_op jit(solution)/shard_map/pallas_call | solution.py:351
  63.0 21.9 %all_to_all.25.part_ref = bf16[4,1280,128]{2,1,0:T(8,128)(2,1)S(1)} all-to-all(bf16[4,1280,128]{2,1,0:T(8,128)(2,1)S(1)} %get-tuple-element.32), channel_id=1, replica_groups=mesh['seq_0'=8,'seq_1'=8,'seq_2'=2,'chan'=4] {'chan'}, dimensions={0} | all-to-all | bytes 2621440 | tf_op jit(solution)/shard_map/all_to_all | solution.py:354
  84.8 2.4 %shard_map.90 = (f32[512,128]{1,0:T(8,128)S(1)}, f32[512,128]{1,0:T(8,128)S(1)}, f32[64,128]{1,0:T(8,128)S(1)}, f32[64,4,128]{2,1,0:T(4,128)}, bf16[512,128]{1,0:T(8,128)(2,1)S(1)}) custom-call(s32[2]{0:T(128)S(1)} %pad_add_fusion.at_ref, bf16[4,1280,128]{2,1,0:T(8,128)(2,1)S(1)} %all_to_all.25.part_ref, f32[1024,128]{1,0:T(8,128)S(1)} %get-tuple-element.33.own_ref, ...), custom_call_target="tpu_custom_call" | custom-call | tf_op jit(solution)/shard_map/pallas_call | solution.py:369
  87.2 5.6 %all-to-all-start.2 = ((f32[64,4,128]{2,1,0:T(4,128)}), f32[64,4,128]{2,1,0:T(4,128)S(1)}, u32[]{:S(2)}, u32[]{:S(2)}) async-start(f32[64,4,128]{2,1,0:T(4,128)} %get-tuple-element.37), calls=%async_computation.2 | async-start | bytes 262144 | tf_op jit(solution)/shard_map/all_to_all | solution.py:382
  92.8 2.2 %shard_map.91.tt_ref = bf16[1024,1024]{1,0:T(8,128)(2,1)S(1)} custom-call(bf16[512,1024]{1,0:T(8,128)(2,1)} %a_ref, bf16[512,1024]{1,0:T(8,128)(2,1)} %collective-permute-done.other_t.b_ref), custom_call_target="tpu_custom_call" | custom-call | bytes 4194304 | tf_op jit(solution)/shard_map/pallas_call | solution.py:375
  95.0 2.1 %collective-permute-start.4 = (bf16[512,128]{1,0:T(8,128)(2,1)S(1)}, bf16[512,128]{1,0:T(8,128)(2,1)S(1)}, u32[]{:S(2)}, u32[]{:S(2)}) collective-permute-start(bf16[512,128]{1,0:T(8,128)(2,1)S(1)} %get-tuple-element.48.early_a), channel_id=1, source_target_pairs={{0,3},{1,0},{2,1},{3,2},{4,7},{5,4},{6,5},{7,6},{8,11},{9,8},{10,9... | collective-permute-start | bytes 393224 | tf_op jit(solution)/shard_map/ppermute | solution.py:379
  97.1 5.2 %collective-permute-start.5 = (bf16[512,128]{1,0:T(8,128)(2,1)S(1)}, bf16[512,128]{1,0:T(8,128)(2,1)S(1)}, u32[]{:S(2)}, u32[]{:S(2)}) collective-permute-start(bf16[512,128]{1,0:T(8,128)(2,1)S(1)} %get-tuple-element.48.early_a), channel_id=1, source_target_pairs={{0,2},{1,3},{2,0},{3,1},{4,6},{5,7},{6,4},{7,5},{8,10},{9,11},{10,... | collective-permute-start | bytes 393224 | tf_op jit(solution)/shard_map/ppermute | solution.py:379
  102.3 3.1 %collective-permute-start.6 = (bf16[512,128]{1,0:T(8,128)(2,1)S(1)}, bf16[512,128]{1,0:T(8,128)(2,1)S(1)}, u32[]{:S(2)}, u32[]{:S(2)}) collective-permute-start(bf16[512,128]{1,0:T(8,128)(2,1)S(1)} %get-tuple-element.48.early_a), channel_id=1, source_target_pairs={{0,1},{1,2},{2,3},{3,0},{4,5},{5,6},{6,7},{7,4},{8,9},{9,10},{10,1... | collective-permute-start | bytes 393224 | tf_op jit(solution)/shard_map/ppermute | solution.py:379
  105.4 2.2 %shard_map.92.gt_ref = bf16[1024,1024]{1,0:T(8,128)(2,1)S(1)} custom-call(bf16[512,1024]{1,0:T(8,128)(2,1)} %a_ref.1, bf16[512,1024]{1,0:T(8,128)(2,1)} %collective-permute-done.1.other_g.b_ref), custom_call_target="tpu_custom_call" | custom-call | bytes 4194304 | tf_op jit(solution)/shard_map/pallas_call | solution.py:376
  107.6 1.3 copy-done
  109.2 1.9 %shard_map.93 = bf16[4,512,128]{2,1,0:T(8,128)(2,1)S(1)} custom-call(s32[2]{0:T(128)S(1)} %pad_add_fusion.at_ref, f32[512,128]{1,0:T(8,128)S(1)} %get-tuple-element.52.x_ref, f32[512,128]{1,0:T(8,128)S(1)} %get-tuple-element.53.late_ref, f32[64,128]{1,0:T(8,128)S(1)} %get-tuple-element.39.left_ref, f32[64,4,128]{2,1,0:T(4,128)S(1)} %all-to-all-done.2.states_ref, ...), custom_call_target="tpu_custom_call" | custom-call | tf_op jit(solution)/shard_map/pallas_call | solution.py:393
  111.1 11.3 %all_to_all.26.late_ref = bf16[4,512,128]{2,1,0:T(8,128)(2,1)S(1)} all-to-all(bf16[4,512,128]{2,1,0:T(8,128)(2,1)S(1)} %shard_map.93), channel_id=1, replica_groups=mesh['seq_0'=8,'seq_1'=8,'seq_2'=2,'chan'=4] {'chan'}, dimensions={0} | all-to-all | bytes 1048576 | tf_op jit(solution)/shard_map/all_to_all | solution.py:394
  122.4 2.9 %shard_map.94 = bf16[8,512,128]{2,1,0:T(8,128)(2,1)S(1)} custom-call(s32[2]{0:T(128)S(1)} %pad_add_fusion.at_ref, bf16[1024,1024]{1,0:T(8,128)(2,1)S(1)} %shard_map.91.tt_ref, bf16[1024,1024]{1,0:T(8,128)(2,1)S(1)} %copy-done.1, bf16[512,128]{1,0:T(8,128)(2,1)S(1)} %get-tuple-element.48.early_a, bf16[512,128]{1,0:T(8,128)(2,1)S(1)} %collective-permute-done.4.early_b, ...), custom_call_target="tpu_custom_call" | custom-call | flops 2147483648 | bytes 8388608 | tf_op jit(solution)/shard_map/pallas_call | solution.py:404
  125.4 43.8 %all_to_all.27.part_ref = bf16[128,32,128]{2,1,0:T(8,128)(2,1)S(1)} all-to-all(bf16[128,32,128]{2,1,0:T(8,128)(2,1)S(1)} %bitcast.17), channel_id=1, replica_groups=mesh['seq_0'=8,'seq_1'=8,'seq_2'=2,'chan'=4] {'seq_0','seq_1','seq_2'}, dimensions={0} | all-to-all | bytes 2097152 | tf_op jit(solution)/shard_map/all_to_all | solution.py:405
  169.3 3.8 %collective-permute-start.7 = (f32[2,32,128]{2,1,0:T(8,128)S(1)}, f32[2,32,128]{2,1,0:T(8,128)S(1)}, u32[]{:S(2)}, u32[]{:S(2)}) collective-permute-start(f32[2,32,128]{2,1,0:T(8,128)S(1)} %shard_map.95), channel_id=1, source_target_pairs={{320,0},{128,1},{0,2},{384,3},{256,64},{192,65},{64,66},{448,67},{... | collective-permute-start | bytes 98312 | tf_op jit(solution)/shard_map/ppermute | solution.py:304
  173.0 6.7 %collective-permute-done.7.part_ref = f32[2,32,128]{2,1,0:T(8,128)S(1)} collective-permute-done((f32[2,32,128]{2,1,0:T(8,128)S(1)}, f32[2,32,128]{2,1,0:T(8,128)S(1)}, u32[]{:S(2)}, u32[]{:S(2)}) %collective-permute-start.7) | collective-permute-done | bytes 32800 | tf_op jit(solution)/shard_map/ppermute | solution.py:304
  (41 shorter events, 4.3 us)
Async XLA Ops:
  0.6 27.3 %copy-start.2 = (bf16[512,64]{0,1:T(8,128)(2,1)S(1)}, bf16[512,64]{0,1:T(8,128)(2,1)}, u32[]{:S(2)}) copy-start(bf16[512,64]{0,1:T(8,128)(2,1)} %param.11) | copy-start | bytes 196612
  0.6 33.7 %copy-start.3 = (f32[16,32]{1,0:T(8,128)S(1)}, f32[16,32]{1,0:T(8,128)}, u32[]{:S(2)}) copy-start(f32[16,32]{1,0:T(8,128)} %param.12) | copy-start | bytes 6148
  0.7 33.7 %copy-start.4 = (f32[16,32]{1,0:T(8,128)S(1)}, f32[16,32]{1,0:T(8,128)}, u32[]{:S(2)}) copy-start(f32[16,32]{1,0:T(8,128)} %param.13) | copy-start | bytes 6148
  1.6 12.6 %collective-permute-start.2 = (bf16[2,32,128]{2,1,0:T(8,128)(2,1)S(1)}, bf16[2,32,128]{2,1,0:T(8,128)(2,1)S(1)}, u32[]{:S(2)}, u32[]{:S(2)}) collective-permute-start(bf16[2,32,128]{2,1,0:T(8,128)(2,1)S(1)} %shard_map.86), channel_id=1, source_target_pairs={{0,320},{1,128},{2,0},{3,384},{64,256},{65,192},{66,64},{67,448},{... | collective-permute-start | bytes 49160 | tf_op jit(solution)/shard_map/ppermute | solution.py:304
  15.3 43.0 %all-to-all-start = ((bf16[128,32,128]{2,1,0:T(8,128)(2,1)}), bf16[128,32,128]{2,1,0:T(8,128)(2,1)S(1)}, u32[]{:S(2)}, u32[]{:S(2)}) async-start(bf16[128,32,128]{2,1,0:T(8,128)(2,1)} %shard_map.87), calls=%async_computation | async-start | bytes 2097152 | tf_op jit(solution)/shard_map/all_to_all | solution.py:314
  28.1 7.7 %collective-permute-start.3 = (bf16[512,64]{1,0:T(8,128)(2,1)S(1)}, bf16[512,64]{1,0:T(8,128)(2,1)S(1)}, u32[]{:S(2)}, u32[]{:S(2)}) collective-permute-start(bf16[512,64]{1,0:T(8,128)(2,1)S(1)} %copy.12.own_ref), channel_id=1, source_target_pairs={{0,4},{4,0},{1,5},{5,1},{2,6},{6,2},{3,7},{7,3},{8,12},{12,8},{9,1... | collective-permute-start | bytes 196616 | tf_op jit(solution)/shard_map/ppermute | solution.py:307
  30.0 28.2 %collective-permute-start = (bf16[512,1024]{1,0:T(8,128)(2,1)}, bf16[512,1024]{1,0:T(8,128)(2,1)}, u32[]{:S(2)}, u32[]{:S(2)}) collective-permute-start(bf16[512,1024]{1,0:T(8,128)(2,1)} %a_ref), channel_id=1, source_target_pairs={{0,4},{4,0},{1,5},{5,1},{2,6},{6,2},{3,7},{7,3},{8,12},{12,8},{9,1... | collective-permute-start | bytes 3145736 | tf_op jit(solution)/shard_map/ppermute | solution.py:307
  32.4 25.8 %collective-permute-start.1 = (bf16[512,1024]{1,0:T(8,128)(2,1)}, bf16[512,1024]{1,0:T(8,128)(2,1)}, u32[]{:S(2)}, u32[]{:S(2)}) collective-permute-start(bf16[512,1024]{1,0:T(8,128)(2,1)} %a_ref.1), channel_id=1, source_target_pairs={{0,4},{4,0},{1,5},{5,1},{2,6},{6,2},{3,7},{7,3},{8,12},{12,8},{9,1... | collective-permute-start | bytes 3145736 | tf_op jit(solution)/shard_map/ppermute | solution.py:307
  87.2 22.0 %all-to-all-start.2 = ((f32[64,4,128]{2,1,0:T(4,128)}), f32[64,4,128]{2,1,0:T(4,128)S(1)}, u32[]{:S(2)}, u32[]{:S(2)}) async-start(f32[64,4,128]{2,1,0:T(4,128)} %get-tuple-element.37), calls=%async_computation.2 | async-start | bytes 262144 | tf_op jit(solution)/shard_map/all_to_all | solution.py:382
  95.0 14.0 %collective-permute-start.4 = (bf16[512,128]{1,0:T(8,128)(2,1)S(1)}, bf16[512,128]{1,0:T(8,128)(2,1)S(1)}, u32[]{:S(2)}, u32[]{:S(2)}) collective-permute-start(bf16[512,128]{1,0:T(8,128)(2,1)S(1)} %get-tuple-element.48.early_a), channel_id=1, source_target_pairs={{0,3},{1,0},{2,1},{3,2},{4,7},{5,4},{6,5},{7,6},{8,11},{9,8},{10,9... | collective-permute-start | bytes 393224 | tf_op jit(solution)/shard_map/ppermute | solution.py:379
  97.1 11.8 %collective-permute-start.5 = (bf16[512,128]{1,0:T(8,128)(2,1)S(1)}, bf16[512,128]{1,0:T(8,128)(2,1)S(1)}, u32[]{:S(2)}, u32[]{:S(2)}) collective-permute-start(bf16[512,128]{1,0:T(8,128)(2,1)S(1)} %get-tuple-element.48.early_a), channel_id=1, source_target_pairs={{0,2},{1,3},{2,0},{3,1},{4,6},{5,7},{6,4},{7,5},{8,10},{9,11},{10,... | collective-permute-start | bytes 393224 | tf_op jit(solution)/shard_map/ppermute | solution.py:379
  102.3 6.9 %collective-permute-start.6 = (bf16[512,128]{1,0:T(8,128)(2,1)S(1)}, bf16[512,128]{1,0:T(8,128)(2,1)S(1)}, u32[]{:S(2)}, u32[]{:S(2)}) collective-permute-start(bf16[512,128]{1,0:T(8,128)(2,1)S(1)} %get-tuple-element.48.early_a), channel_id=1, source_target_pairs={{0,1},{1,2},{2,3},{3,0},{4,5},{5,6},{6,7},{7,4},{8,9},{9,10},{10,1... | collective-permute-start | bytes 393224 | tf_op jit(solution)/shard_map/ppermute | solution.py:379
  107.6 1.3 copy-start
  109.2 13.2 %copy-start.1 = (bf16[1024,1024]{1,0:T(8,128)(2,1)S(1)}, bf16[1024,1024]{1,0:T(8,128)(2,1)}, u32[]{:S(2)}) copy-start(bf16[1024,1024]{1,0:T(8,128)(2,1)} %copy-done) | copy-start | bytes 6291460
  169.3 10.4 %collective-permute-start.7 = (f32[2,32,128]{2,1,0:T(8,128)S(1)}, f32[2,32,128]{2,1,0:T(8,128)S(1)}, u32[]{:S(2)}, u32[]{:S(2)}) collective-permute-start(f32[2,32,128]{2,1,0:T(8,128)S(1)} %shard_map.95), channel_id=1, source_target_pairs={{320,0},{128,1},{0,2},{384,3},{256,64},{192,65},{64,66},{448,67},{... | collective-permute-start | bytes 98312 | tf_op jit(solution)/shard_map/ppermute | solution.py:304

commit v10 on v6

--- a/solution.py
+++ b/solution.py
@@ -93,11 +93,12 @@
 
 
 def total_body(part_ref, out_ref):
-    for core in range(2):
-        total = part_ref[core].astype(F32)
-        for k in range(core + 2, part_ref.shape[0], 2):
-            total = total + part_ref[k].astype(F32)
-        out_ref[core] = total
+    owned = out_ref.shape[1]
+    total = part_ref[0].astype(F32)
+    for k in range(1, part_ref.shape[0]):
+        total = total + part_ref[k].astype(F32)
+    out_ref[0] = total[:owned]
+    out_ref[1] = total[owned:]
 
 
 def unpack_body(part_ref, in_ref, out_w_ref):
@@ -339,7 +340,7 @@
         moved=8 * rows * depth,
     )
     parts, own = project(
-        at, in_hbm(tokens), in_hbm(tokens_too), in_hbm(grad_out), in_hbm(grads_too), weights
+        at, tokens, in_hbm(tokens_too), grad_out, in_hbm(grads_too), weights
     )
     parts = lax.all_to_all(parts, "chan", 0, 0, tiled=True)
 
@@ -377,15 +378,16 @@
 
     weigh = call(
         weigh_body,
-        jax.ShapeDtypeStruct((size_z, depth // 2, 128), BF16),
+        pltpu.HBM((size_z, depth // 2, 128), BF16),
         16,
         inputs=4,
         flops=4 * rows * depth * size_x * 128,
         moved=8 * rows * depth,
     )
-    partial = weigh(at, tokens_t, grads_t, grads).reshape(2 * chips, owned, 128)
-    partial = lax.all_to_all(partial, SEQ, 0, 0, tiled=True)
+    partial = weigh(at, tokens_t, grads_t, grads).reshape(chips, 2 * owned, 128)
+    partial = in_hbm(lax.all_to_all(partial, CHIPS, 0, 0, tiled=True))
     total = call(total_body, jax.ShapeDtypeStruct((2, owned, 128), F32), 6)(partial)
+    total = lax.all_to_all(total, "seq_2", 0, 0, tiled=True)
     total = transposed(total, True)
     grad_in, grad_proj = call(
         unpack_body,

time: 177 us -> 179 us (1.011)
  waiting for transfers between devices: 37.1 us -> 34 us
    all_to_all x1, waiting for transfers between devices: 21.7 us -> 19.5 us  [local(): lax.all_to_all(spread, SEQ, 0, 0, tiled=True).reshape(size_z, -1, 128)]
    all_to_all x1 -> x2, blocking collectives: 37.9 us -> 38.4 us  [the longest x1 34.6 us: local(): partial = in_hbm(lax.all_to_all(partial, CHIPS, 0, 0, tiled=True))]
where the time goes in v10:
time: 179 us; the launch traced here: 178 us
  blocking collectives  76.5 us (43%)
  starting transfers between devices  39.9 us (22%)
  waiting for transfers between devices  34 us (19%)
  Pallas kernels  21.7 us (12%)
  local copies, waits for them, and re-layouts  3.84 us (2%)
    all_to_all x1, blocking collectives, local(): partial = in_hbm(lax.all_to_all(partial, CHIPS, 0, 0, tiled=True))  34.6 us
    all_to_all x1, blocking collectives, local(): parts = lax.all_to_all(parts, 'chan', 0, 0, tiled=True)  21.9 us
    all_to_all x1, waiting for transfers between devices, local(): lax.all_to_all(spread, SEQ, 0, 0, tiled=True).reshape(size_z, -1, 128)  19.5 us
    all_to_all x1, blocking collectives, local(): grads = lax.all_to_all(grads, 'chan', 0, 0, tiled=True)  16.2 us
    ppermute x2, starting transfers between devices, transposed(): return lax.ppermute(value, ('seq_0', 'chan'), pairs)  15.5 us
    all_to_all x1, starting transfers between devices, local(): lax.all_to_all(spread, SEQ, 0, 0, tiled=True).reshape(size_z, -1, 128)  12.7 us
    ppermute x2, waiting for transfers between devices, transposed(): return lax.ppermute(value, ('seq_0', 'chan'), pairs)  7.44 us
    all_to_all x1, waiting for transfers between devices, local(): states = lax.all_to_all(state, CHIPS, 0, 0, tiled=True)  6.99 us
  transfers between devices with their start and end apart: 7, of which 4 were waited for; matrix products, arithmetic and copies ran while one was open for 1% of the time, Pallas kernels for 3%

profile of v10, /device:TPU:6, one launch (start us, length us, event | category | flops | bytes accessed | tf_op | source)
XLA Modules:
  0.0 177.9 jit_solution(5780264610697329133)
XLA Ops:
  1.7 10.9 %collective-permute-start.2 = (bf16[2,32,128]{2,1,0:T(8,128)(2,1)S(1)}, bf16[2,32,128]{2,1,0:T(8,128)(2,1)S(1)}, u32[]{:S(2)}, u32[]{:S(2)}) collective-permute-start(bf16[2,32,128]{2,1,0:T(8,128)(2,1)S(1)} %shard_map.86), channel_id=1, source_target_pairs={{0,320},{1,128},{2,0},{3,384},{64,256},{65,192},{66,64},{67,448},{... | collective-permute-start | bytes 49160 | tf_op jit(solution)/shard_map/ppermute | solution.py:295
  12.6 1.7 collective-permute-done.2.piece_ref
  14.3 1.1 shard_map.87
  15.4 12.7 %all-to-all-start = ((bf16[128,32,128]{2,1,0:T(8,128)(2,1)}), bf16[128,32,128]{2,1,0:T(8,128)(2,1)S(1)}, u32[]{:S(2)}, u32[]{:S(2)}) async-start(bf16[128,32,128]{2,1,0:T(8,128)(2,1)} %shard_map.87), calls=%async_computation | async-start | bytes 2097152 | tf_op jit(solution)/shard_map/all_to_all | solution.py:305
  28.2 1.9 %collective-permute-start.3 = (bf16[512,64]{1,0:T(8,128)(2,1)S(1)}, bf16[512,64]{1,0:T(8,128)(2,1)S(1)}, u32[]{:S(2)}, u32[]{:S(2)}) collective-permute-start(bf16[512,64]{1,0:T(8,128)(2,1)S(1)} %copy.12.own_ref), channel_id=1, source_target_pairs={{0,4},{4,0},{1,5},{5,1},{2,6},{6,2},{3,7},{7,3},{8,12},{12,8},{9,1... | collective-permute-start | bytes 196616 | tf_op jit(solution)/shard_map/ppermute | solution.py:298
  30.2 2.4 %collective-permute-start = (bf16[512,1024]{1,0:T(8,128)(2,1)S(1)}, bf16[512,1024]{1,0:T(8,128)(2,1)}, u32[]{:S(2)}, u32[]{:S(2)}) collective-permute-start(bf16[512,1024]{1,0:T(8,128)(2,1)S(1)} %copy-done.2), channel_id=1, source_target_pairs={{0,4},{4,0},{1,5},{5,1},{2,6},{6,2},{3,7},{7,3},{8,12},{12,8},{9,1... | collective-permute-start | bytes 3145736 | tf_op jit(solution)/shard_map/ppermute | solution.py:298
  32.6 1.9 %collective-permute-start.1 = (bf16[512,1024]{1,0:T(8,128)(2,1)S(1)}, bf16[512,1024]{1,0:T(8,128)(2,1)}, u32[]{:S(2)}, u32[]{:S(2)}) collective-permute-start(bf16[512,1024]{1,0:T(8,128)(2,1)S(1)} %copy-done.3), channel_id=1, source_target_pairs={{0,4},{4,0},{1,5},{5,1},{2,6},{6,2},{3,7},{7,3},{8,12},{12,8},{9,1... | collective-permute-start | bytes 3145736 | tf_op jit(solution)/shard_map/ppermute | solution.py:298
  38.8 19.5 %all-to-all-done = bf16[128,32,128]{2,1,0:T(8,128)(2,1)S(1)} async-done(((bf16[128,32,128]{2,1,0:T(8,128)(2,1)}), bf16[128,32,128]{2,1,0:T(8,128)(2,1)S(1)}, u32[]{:S(2)}, u32[]{:S(2)}) %all-to-all-start) | async-done | bytes 1048608 | tf_op jit(solution)/shard_map/all_to_all | solution.py:305
  58.4 4.1 %shard_map.89 = (bf16[4,1280,128]{2,1,0:T(8,128)(2,1)S(1)}, f32[1024,128]{1,0:T(8,128)S(1)}) custom-call(s32[2]{0:T(128)S(1)} %pad_add_fusion.at_ref, bf16[512,1024]{1,0:T(8,128)(2,1)S(1)} %copy-done.2, bf16[512,1024]{1,0:T(8,128)(2,1)} %collective-permute-done.other_t.b_ref, bf16[512,1024]{1,0:T(8,128)(2,1)S(1)} %copy-done.3, ...), custom_call_target="tpu_custom_call" | custom-call | flops 2147483648 | bytes 8388608 | tf_op jit(solution)/shard_map/pallas_call | solution.py:342
  62.5 21.9 %all_to_all.30.part_ref = bf16[4,1280,128]{2,1,0:T(8,128)(2,1)S(1)} all-to-all(bf16[4,1280,128]{2,1,0:T(8,128)(2,1)S(1)} %get-tuple-element.25), channel_id=1, replica_groups=mesh['seq_0'=8,'seq_1'=8,'seq_2'=2,'chan'=4] {'chan'}, dimensions={0} | all-to-all | bytes 2621440 | tf_op jit(solution)/shard_map/all_to_all | solution.py:345
  84.4 2.3 %shard_map.90 = (f32[512,128]{1,0:T(8,128)S(1)}, f32[512,128]{1,0:T(8,128)S(1)}, f32[64,128]{1,0:T(8,128)S(1)}, f32[64,4,128]{2,1,0:T(4,128)}) custom-call(s32[2]{0:T(128)S(1)} %pad_add_fusion.at_ref, bf16[4,1280,128]{2,1,0:T(8,128)(2,1)S(1)} %all_to_all.30.part_ref, f32[1024,128]{1,0:T(8,128)S(1)} %get-tuple-element.26.own_ref, ...), custom_call_target="tpu_custom_call" | custom-call | tf_op jit(solution)/shard_map/pallas_call | solution.py:359
  86.7 5.6 %all-to-all-start.2 = ((f32[64,4,128]{2,1,0:T(4,128)}), f32[64,4,128]{2,1,0:T(4,128)S(1)}, u32[]{:S(2)}, u32[]{:S(2)}) async-start(f32[64,4,128]{2,1,0:T(4,128)} %get-tuple-element.29), calls=%async_computation.2 | async-start | bytes 262144 | tf_op jit(solution)/shard_map/all_to_all | solution.py:367
  92.2 2.2 %shard_map.91.tt_ref = bf16[1024,1024]{1,0:T(8,128)(2,1)S(1)} custom-call(bf16[512,1024]{1,0:T(8,128)(2,1)} %a_ref, bf16[512,1024]{1,0:T(8,128)(2,1)} %collective-permute-done.other_t.b_ref), custom_call_target="tpu_custom_call" | custom-call | bytes 4194304 | tf_op jit(solution)/shard_map/pallas_call | solution.py:365
  94.4 2.2 %shard_map.92.gt_ref = bf16[1024,1024]{1,0:T(8,128)(2,1)S(1)} custom-call(bf16[512,1024]{1,0:T(8,128)(2,1)} %a_ref.1, bf16[512,1024]{1,0:T(8,128)(2,1)} %collective-permute-done.1.other_g.b_ref), custom_call_target="tpu_custom_call" | custom-call | bytes 4194304 | tf_op jit(solution)/shard_map/pallas_call | solution.py:366
  96.6 1.3 copy-done
  97.9 7.0 %all-to-all-done.2.states_ref = f32[64,4,128]{2,1,0:T(4,128)S(1)} async-done(((f32[64,4,128]{2,1,0:T(4,128)}), f32[64,4,128]{2,1,0:T(4,128)S(1)}, u32[]{:S(2)}, u32[]{:S(2)}) %all-to-all-start.2) | async-done | bytes 131104 | tf_op jit(solution)/shard_map/all_to_all | solution.py:367
  104.9 2.0 %shard_map.93 = bf16[4,1024,128]{2,1,0:T(8,128)(2,1)S(1)} custom-call(s32[2]{0:T(128)S(1)} %pad_add_fusion.at_ref, f32[512,128]{1,0:T(8,128)S(1)} %get-tuple-element.37.x_ref, f32[512,128]{1,0:T(8,128)S(1)} %get-tuple-element.38.late_ref, f32[64,128]{1,0:T(8,128)S(1)} %get-tuple-element.30.left_ref, f32[64,4,128]{2,1,0:T(4,128)S(1)} %all-to-all-done.2.states_ref, ...), custom_call_target="tpu_custom_call" | custom-call | tf_op jit(solution)/shard_map/pallas_call | solution.py:376
  106.9 16.2 %all_to_all.31.grads_ref = bf16[4,1024,128]{2,1,0:T(8,128)(2,1)S(1)} all-to-all(bf16[4,1024,128]{2,1,0:T(8,128)(2,1)S(1)} %shard_map.93), channel_id=1, replica_groups=mesh['seq_0'=8,'seq_1'=8,'seq_2'=2,'chan'=4] {'chan'}, dimensions={0} | all-to-all | bytes 2097152 | tf_op jit(solution)/shard_map/all_to_all | solution.py:377
  123.2 3.9 %shard_map.94 = bf16[8,512,128]{2,1,0:T(8,128)(2,1)} custom-call(s32[2]{0:T(128)S(1)} %pad_add_fusion.at_ref, bf16[1024,1024]{1,0:T(8,128)(2,1)S(1)} %shard_map.91.tt_ref, bf16[1024,1024]{1,0:T(8,128)(2,1)S(1)} %copy-done.1, bf16[4,1024,128]{2,1,0:T(8,128)(2,1)S(1)} %all_to_all.31.grads_ref), custom_call_target="tpu_custom_call" | custom-call | flops 2147483648 | bytes 8388608 | tf_op jit(solution)/shard_map/pallas_call | solution.py:387
  127.0 34.6 %all_to_all.32.part_ref = bf16[64,64,128]{2,1,0:T(8,128)(2,1)} all-to-all(bf16[64,64,128]{2,1,0:T(8,128)(2,1)} %bitcast.17), channel_id=1, replica_groups=mesh['seq_0'=8,'seq_1'=8,'seq_2'=2,'chan'=4] {'seq_0','seq_1'}, dimensions={0} | all-to-all | bytes 2097152 | tf_op jit(solution)/shard_map/all_to_all | solution.py:388
  161.7 1.4 shard_map.95
  163.1 3.7 %all_to_all.33 = f32[2,32,128]{2,1,0:T(8,128)S(1)} all-to-all(f32[2,32,128]{2,1,0:T(8,128)S(1)} %shard_map.95), channel_id=1, replica_groups=mesh['seq_0'=8,'seq_1'=8,'seq_2'=2,'chan'=4] {'seq_2'}, dimensions={0} | all-to-all | bytes 65536 | tf_op jit(solution)/shard_map/all_to_all | solution.py:390
  166.8 4.6 %collective-permute-start.4 = (f32[2,32,128]{2,1,0:T(8,128)S(1)}, f32[2,32,128]{2,1,0:T(8,128)S(1)}, u32[]{:S(2)}, u32[]{:S(2)}) collective-permute-start(f32[2,32,128]{2,1,0:T(8,128)S(1)} %all_to_all.33), channel_id=1, source_target_pairs={{320,0},{128,1},{0,2},{384,3},{256,64},{192,65},{64,66},{448,67},{... | collective-permute-start | bytes 98312 | tf_op jit(solution)/shard_map/ppermute | solution.py:295
  171.4 5.7 %collective-permute-done.4.part_ref = f32[2,32,128]{2,1,0:T(8,128)S(1)} collective-permute-done((f32[2,32,128]{2,1,0:T(8,128)S(1)}, f32[2,32,128]{2,1,0:T(8,128)S(1)}, u32[]{:S(2)}, u32[]{:S(2)}) %collective-permute-start.4) | collective-permute-done | bytes 32800 | tf_op jit(solution)/shard_map/ppermute | solution.py:295
  (46 shorter events, 6.1 us)
Async XLA Ops:
  0.6 27.5 %copy-start.7 = (bf16[512,64]{0,1:T(8,128)(2,1)S(1)}, bf16[512,64]{0,1:T(8,128)(2,1)}, u32[]{:S(2)}) copy-start(bf16[512,64]{0,1:T(8,128)(2,1)} %param.11) | copy-start | bytes 196612
  0.6 29.5 %copy-start.2 = (bf16[512,1024]{1,0:T(8,128)(2,1)S(1)}, bf16[512,1024]{1,0:T(8,128)(2,1)}, u32[]{:S(2)}) copy-start(bf16[512,1024]{1,0:T(8,128)(2,1)} %a_ref) | copy-start | bytes 3145732
  0.7 31.9 %copy-start.3 = (bf16[512,1024]{1,0:T(8,128)(2,1)S(1)}, bf16[512,1024]{1,0:T(8,128)(2,1)}, u32[]{:S(2)}) copy-start(bf16[512,1024]{1,0:T(8,128)(2,1)} %a_ref.1) | copy-start | bytes 3145732
  0.7 34.0 %copy-start.9 = (f32[16,32]{1,0:T(8,128)S(1)}, f32[16,32]{1,0:T(8,128)}, u32[]{:S(2)}) copy-start(f32[16,32]{1,0:T(8,128)} %param.13) | copy-start | bytes 6148
  0.7 34.0 %copy-start.8 = (f32[16,32]{1,0:T(8,128)S(1)}, f32[16,32]{1,0:T(8,128)}, u32[]{:S(2)}) copy-start(f32[16,32]{1,0:T(8,128)} %param.12) | copy-start | bytes 6148
  1.7 12.6 %collective-permute-start.2 = (bf16[2,32,128]{2,1,0:T(8,128)(2,1)S(1)}, bf16[2,32,128]{2,1,0:T(8,128)(2,1)S(1)}, u32[]{:S(2)}, u32[]{:S(2)}) collective-permute-start(bf16[2,32,128]{2,1,0:T(8,128)(2,1)S(1)} %shard_map.86), channel_id=1, source_target_pairs={{0,320},{1,128},{2,0},{3,384},{64,256},{65,192},{66,64},{67,448},{... | collective-permute-start | bytes 49160 | tf_op jit(solution)/shard_map/ppermute | solution.py:295
  15.4 43.0 %all-to-all-start = ((bf16[128,32,128]{2,1,0:T(8,128)(2,1)}), bf16[128,32,128]{2,1,0:T(8,128)(2,1)S(1)}, u32[]{:S(2)}, u32[]{:S(2)}) async-start(bf16[128,32,128]{2,1,0:T(8,128)(2,1)} %shard_map.87), calls=%async_computation | async-start | bytes 2097152 | tf_op jit(solution)/shard_map/all_to_all | solution.py:305
  28.2 8.3 %collective-permute-start.3 = (bf16[512,64]{1,0:T(8,128)(2,1)S(1)}, bf16[512,64]{1,0:T(8,128)(2,1)S(1)}, u32[]{:S(2)}, u32[]{:S(2)}) collective-permute-start(bf16[512,64]{1,0:T(8,128)(2,1)S(1)} %copy.12.own_ref), channel_id=1, source_target_pairs={{0,4},{4,0},{1,5},{5,1},{2,6},{6,2},{3,7},{7,3},{8,12},{12,8},{9,1... | collective-permute-start | bytes 196616 | tf_op jit(solution)/shard_map/ppermute | solution.py:298
  30.2 28.2 %collective-permute-start = (bf16[512,1024]{1,0:T(8,128)(2,1)S(1)}, bf16[512,1024]{1,0:T(8,128)(2,1)}, u32[]{:S(2)}, u32[]{:S(2)}) collective-permute-start(bf16[512,1024]{1,0:T(8,128)(2,1)S(1)} %copy-done.2), channel_id=1, source_target_pairs={{0,4},{4,0},{1,5},{5,1},{2,6},{6,2},{3,7},{7,3},{8,12},{12,8},{9,1... | collective-permute-start | bytes 3145736 | tf_op jit(solution)/shard_map/ppermute | solution.py:298
  32.6 25.8 %collective-permute-start.1 = (bf16[512,1024]{1,0:T(8,128)(2,1)S(1)}, bf16[512,1024]{1,0:T(8,128)(2,1)}, u32[]{:S(2)}, u32[]{:S(2)}) collective-permute-start(bf16[512,1024]{1,0:T(8,128)(2,1)S(1)} %copy-done.3), channel_id=1, source_target_pairs={{0,4},{4,0},{1,5},{5,1},{2,6},{6,2},{3,7},{7,3},{8,12},{12,8},{9,1... | collective-permute-start | bytes 3145736 | tf_op jit(solution)/shard_map/ppermute | solution.py:298
  36.5 0.6 copy-start.5
  37.2 0.9 copy-start.6
  86.7 18.3 %all-to-all-start.2 = ((f32[64,4,128]{2,1,0:T(4,128)}), f32[64,4,128]{2,1,0:T(4,128)S(1)}, u32[]{:S(2)}, u32[]{:S(2)}) async-start(f32[64,4,128]{2,1,0:T(4,128)} %get-tuple-element.29), calls=%async_computation.2 | async-start | bytes 262144 | tf_op jit(solution)/shard_map/all_to_all | solution.py:367
  94.4 10.5 %copy-start.4 = (f32[64,128]{1,0:T(8,128)S(1)}, f32[64,128]{1,0:T(8,128)}, u32[]{:S(2)}) copy-start(f32[64,128]{1,0:T(8,128)} %fusion.power_ref) | copy-start | bytes 98308
  96.6 1.3 copy-start
  104.9 18.2 %copy-start.1 = (bf16[1024,1024]{1,0:T(8,128)(2,1)S(1)}, bf16[1024,1024]{1,0:T(8,128)(2,1)}, u32[]{:S(2)}) copy-start(bf16[1024,1024]{1,0:T(8,128)(2,1)} %copy-done) | copy-start | bytes 6291460
  166.8 10.4 %collective-permute-start.4 = (f32[2,32,128]{2,1,0:T(8,128)S(1)}, f32[2,32,128]{2,1,0:T(8,128)S(1)}, u32[]{:S(2)}, u32[]{:S(2)}) collective-permute-start(f32[2,32,128]{2,1,0:T(8,128)S(1)} %all_to_all.33), channel_id=1, source_target_pairs={{320,0},{128,1},{0,2},{384,3},{256,64},{192,65},{64,66},{448,67},{... | collective-permute-start | bytes 98312 | tf_op jit(solution)/shard_map/ppermute | solution.py:295

commit v11 on v10

--- a/solution.py
+++ b/solution.py
@@ -378,14 +378,14 @@
 
     weigh = call(
         weigh_body,
-        pltpu.HBM((size_z, depth // 2, 128), BF16),
+        jax.ShapeDtypeStruct((size_z, depth // 2, 128), BF16),
         16,
         inputs=4,
         flops=4 * rows * depth * size_x * 128,
         moved=8 * rows * depth,
     )
     partial = weigh(at, tokens_t, grads_t, grads).reshape(chips, 2 * owned, 128)
-    partial = in_hbm(lax.all_to_all(partial, CHIPS, 0, 0, tiled=True))
+    partial = lax.all_to_all(partial, CHIPS, 0, 0, tiled=True)
     total = call(total_body, jax.ShapeDtypeStruct((2, owned, 128), F32), 6)(partial)
     total = lax.all_to_all(total, "seq_2", 0, 0, tiled=True)
     total = transposed(total, True)

time: 179 us -> 176 us (0.983)
  Pallas kernels: 21.7 us -> 19.5 us
where the time goes in v11:
time: 176 us; the launch traced here: 175 us
  blocking collectives  76.2 us (43%)
  starting transfers between devices  39.9 us (23%)
  waiting for transfers between devices  34 us (19%)
  Pallas kernels  19.5 us (11%)
  local copies, waits for them, and re-layouts  3.84 us (2%)
    all_to_all x1, blocking collectives, local(): partial = lax.all_to_all(partial, CHIPS, 0, 0, tiled=True)  34.3 us
    all_to_all x1, blocking collectives, local(): parts = lax.all_to_all(parts, 'chan', 0, 0, tiled=True)  21.9 us
    all_to_all x1, waiting for transfers between devices, local(): lax.all_to_all(spread, SEQ, 0, 0, tiled=True).reshape(size_z, -1, 128)  19.5 us
    all_to_all x1, blocking collectives, local(): grads = lax.all_to_all(grads, 'chan', 0, 0, tiled=True)  16.2 us
    ppermute x2, starting transfers between devices, transposed(): return lax.ppermute(value, ('seq_0', 'chan'), pairs)  15.5 us
    all_to_all x1, starting transfers between devices, local(): lax.all_to_all(spread, SEQ, 0, 0, tiled=True).reshape(size_z, -1, 128)  12.7 us
    ppermute x2, waiting for transfers between devices, transposed(): return lax.ppermute(value, ('seq_0', 'chan'), pairs)  7.44 us
    all_to_all x1, waiting for transfers between devices, local(): states = lax.all_to_all(state, CHIPS, 0, 0, tiled=True)  6.99 us
  transfers between devices with their start and end apart: 7, of which 4 were waited for; matrix products, arithmetic and copies ran while one was open for 1% of the time, Pallas kernels for 3%

profile of v11, /device:TPU:6, one launch (start us, length us, event | category | flops | bytes accessed | tf_op | source)
XLA Modules:
  0.0 175.4 jit_solution(6762854039433809526)
XLA Ops:
  0.7 1.0 shard_map.86
  1.7 10.9 %collective-permute-start.2 = (bf16[2,32,128]{2,1,0:T(8,128)(2,1)S(1)}, bf16[2,32,128]{2,1,0:T(8,128)(2,1)S(1)}, u32[]{:S(2)}, u32[]{:S(2)}) collective-permute-start(bf16[2,32,128]{2,1,0:T(8,128)(2,1)S(1)} %shard_map.86), channel_id=1, source_target_pairs={{0,320},{1,128},{2,0},{3,384},{64,256},{65,192},{66,64},{67,448},{... | collective-permute-start | bytes 49160 | tf_op jit(solution)/shard_map/ppermute | solution.py:295
  12.6 1.7 collective-permute-done.2.piece_ref
  14.3 1.1 shard_map.87
  15.4 12.7 %all-to-all-start = ((bf16[128,32,128]{2,1,0:T(8,128)(2,1)}), bf16[128,32,128]{2,1,0:T(8,128)(2,1)S(1)}, u32[]{:S(2)}, u32[]{:S(2)}) async-start(bf16[128,32,128]{2,1,0:T(8,128)(2,1)} %shard_map.87), calls=%async_computation | async-start | bytes 2097152 | tf_op jit(solution)/shard_map/all_to_all | solution.py:305
  28.2 1.9 %collective-permute-start.3 = (bf16[512,64]{1,0:T(8,128)(2,1)S(1)}, bf16[512,64]{1,0:T(8,128)(2,1)S(1)}, u32[]{:S(2)}, u32[]{:S(2)}) collective-permute-start(bf16[512,64]{1,0:T(8,128)(2,1)S(1)} %copy.12.own_ref), channel_id=1, source_target_pairs={{0,4},{4,0},{1,5},{5,1},{2,6},{6,2},{3,7},{7,3},{8,12},{12,8},{9,1... | collective-permute-start | bytes 196616 | tf_op jit(solution)/shard_map/ppermute | solution.py:298
  30.2 2.4 %collective-permute-start = (bf16[512,1024]{1,0:T(8,128)(2,1)S(1)}, bf16[512,1024]{1,0:T(8,128)(2,1)}, u32[]{:S(2)}, u32[]{:S(2)}) collective-permute-start(bf16[512,1024]{1,0:T(8,128)(2,1)S(1)} %copy-done.2), channel_id=1, source_target_pairs={{0,4},{4,0},{1,5},{5,1},{2,6},{6,2},{3,7},{7,3},{8,12},{12,8},{9,1... | collective-permute-start | bytes 3145736 | tf_op jit(solution)/shard_map/ppermute | solution.py:298
  32.6 1.9 %collective-permute-start.1 = (bf16[512,1024]{1,0:T(8,128)(2,1)S(1)}, bf16[512,1024]{1,0:T(8,128)(2,1)}, u32[]{:S(2)}, u32[]{:S(2)}) collective-permute-start(bf16[512,1024]{1,0:T(8,128)(2,1)S(1)} %copy-done.3), channel_id=1, source_target_pairs={{0,4},{4,0},{1,5},{5,1},{2,6},{6,2},{3,7},{7,3},{8,12},{12,8},{9,1... | collective-permute-start | bytes 3145736 | tf_op jit(solution)/shard_map/ppermute | solution.py:298
  38.8 19.5 %all-to-all-done = bf16[128,32,128]{2,1,0:T(8,128)(2,1)S(1)} async-done(((bf16[128,32,128]{2,1,0:T(8,128)(2,1)}), bf16[128,32,128]{2,1,0:T(8,128)(2,1)S(1)}, u32[]{:S(2)}, u32[]{:S(2)}) %all-to-all-start) | async-done | bytes 1048608 | tf_op jit(solution)/shard_map/all_to_all | solution.py:305
  58.4 4.1 %shard_map.89 = (bf16[4,1280,128]{2,1,0:T(8,128)(2,1)S(1)}, f32[1024,128]{1,0:T(8,128)S(1)}) custom-call(s32[2]{0:T(128)S(1)} %pad_add_fusion.at_ref, bf16[512,1024]{1,0:T(8,128)(2,1)S(1)} %copy-done.2, bf16[512,1024]{1,0:T(8,128)(2,1)} %collective-permute-done.other_t.b_ref, bf16[512,1024]{1,0:T(8,128)(2,1)S(1)} %copy-done.3, ...), custom_call_target="tpu_custom_call" | custom-call | flops 2147483648 | bytes 8388608 | tf_op jit(solution)/shard_map/pallas_call | solution.py:342
  62.5 21.9 %all_to_all.30.part_ref = bf16[4,1280,128]{2,1,0:T(8,128)(2,1)S(1)} all-to-all(bf16[4,1280,128]{2,1,0:T(8,128)(2,1)S(1)} %get-tuple-element.25), channel_id=1, replica_groups=mesh['seq_0'=8,'seq_1'=8,'seq_2'=2,'chan'=4] {'chan'}, dimensions={0} | all-to-all | bytes 2621440 | tf_op jit(solution)/shard_map/all_to_all | solution.py:345
  84.4 2.3 %shard_map.90 = (f32[512,128]{1,0:T(8,128)S(1)}, f32[512,128]{1,0:T(8,128)S(1)}, f32[64,128]{1,0:T(8,128)S(1)}, f32[64,4,128]{2,1,0:T(4,128)}) custom-call(s32[2]{0:T(128)S(1)} %pad_add_fusion.at_ref, bf16[4,1280,128]{2,1,0:T(8,128)(2,1)S(1)} %all_to_all.30.part_ref, f32[1024,128]{1,0:T(8,128)S(1)} %get-tuple-element.26.own_ref, ...), custom_call_target="tpu_custom_call" | custom-call | tf_op jit(solution)/shard_map/pallas_call | solution.py:359
  86.7 5.6 %all-to-all-start.2 = ((f32[64,4,128]{2,1,0:T(4,128)}), f32[64,4,128]{2,1,0:T(4,128)S(1)}, u32[]{:S(2)}, u32[]{:S(2)}) async-start(f32[64,4,128]{2,1,0:T(4,128)} %get-tuple-element.29), calls=%async_computation.2 | async-start | bytes 262144 | tf_op jit(solution)/shard_map/all_to_all | solution.py:367
  92.2 2.2 %shard_map.91.tt_ref = bf16[1024,1024]{1,0:T(8,128)(2,1)S(1)} custom-call(bf16[512,1024]{1,0:T(8,128)(2,1)} %a_ref, bf16[512,1024]{1,0:T(8,128)(2,1)} %collective-permute-done.other_t.b_ref), custom_call_target="tpu_custom_call" | custom-call | bytes 4194304 | tf_op jit(solution)/shard_map/pallas_call | solution.py:365
  94.4 2.2 %shard_map.92.gt_ref = bf16[1024,1024]{1,0:T(8,128)(2,1)S(1)} custom-call(bf16[512,1024]{1,0:T(8,128)(2,1)} %a_ref.1, bf16[512,1024]{1,0:T(8,128)(2,1)} %collective-permute-done.1.other_g.b_ref), custom_call_target="tpu_custom_call" | custom-call | bytes 4194304 | tf_op jit(solution)/shard_map/pallas_call | solution.py:366
  96.6 1.3 copy-done
  97.9 7.0 %all-to-all-done.2.states_ref = f32[64,4,128]{2,1,0:T(4,128)S(1)} async-done(((f32[64,4,128]{2,1,0:T(4,128)}), f32[64,4,128]{2,1,0:T(4,128)S(1)}, u32[]{:S(2)}, u32[]{:S(2)}) %all-to-all-start.2) | async-done | bytes 131104 | tf_op jit(solution)/shard_map/all_to_all | solution.py:367
  104.9 2.0 %shard_map.93 = bf16[4,1024,128]{2,1,0:T(8,128)(2,1)S(1)} custom-call(s32[2]{0:T(128)S(1)} %pad_add_fusion.at_ref, f32[512,128]{1,0:T(8,128)S(1)} %get-tuple-element.37.x_ref, f32[512,128]{1,0:T(8,128)S(1)} %get-tuple-element.38.late_ref, f32[64,128]{1,0:T(8,128)S(1)} %get-tuple-element.30.left_ref, f32[64,4,128]{2,1,0:T(4,128)S(1)} %all-to-all-done.2.states_ref, ...), custom_call_target="tpu_custom_call" | custom-call | tf_op jit(solution)/shard_map/pallas_call | solution.py:376
  106.9 16.2 %all_to_all.31.grads_ref = bf16[4,1024,128]{2,1,0:T(8,128)(2,1)S(1)} all-to-all(bf16[4,1024,128]{2,1,0:T(8,128)(2,1)S(1)} %shard_map.93), channel_id=1, replica_groups=mesh['seq_0'=8,'seq_1'=8,'seq_2'=2,'chan'=4] {'chan'}, dimensions={0} | all-to-all | bytes 2097152 | tf_op jit(solution)/shard_map/all_to_all | solution.py:377
  123.2 2.9 %shard_map.94 = bf16[8,512,128]{2,1,0:T(8,128)(2,1)S(1)} custom-call(s32[2]{0:T(128)S(1)} %pad_add_fusion.at_ref, bf16[1024,1024]{1,0:T(8,128)(2,1)S(1)} %shard_map.91.tt_ref, bf16[1024,1024]{1,0:T(8,128)(2,1)S(1)} %copy-done.1, bf16[4,1024,128]{2,1,0:T(8,128)(2,1)S(1)} %all_to_all.31.grads_ref), custom_call_target="tpu_custom_call" | custom-call | flops 2147483648 | bytes 8388608 | tf_op jit(solution)/shard_map/pallas_call | solution.py:387
  126.1 34.3 %all_to_all.32.part_ref = bf16[64,64,128]{2,1,0:T(8,128)(2,1)S(1)} all-to-all(bf16[64,64,128]{2,1,0:T(8,128)(2,1)S(1)} %bitcast.17), channel_id=1, replica_groups=mesh['seq_0'=8,'seq_1'=8,'seq_2'=2,'chan'=4] {'seq_0','seq_1'}, dimensions={0} | all-to-all | bytes 2097152 | tf_op jit(solution)/shard_map/all_to_all | solution.py:388
  160.6 3.7 %all_to_all.33 = f32[2,32,128]{2,1,0:T(8,128)S(1)} all-to-all(f32[2,32,128]{2,1,0:T(8,128)S(1)} %shard_map.95), channel_id=1, replica_groups=mesh['seq_0'=8,'seq_1'=8,'seq_2'=2,'chan'=4] {'seq_2'}, dimensions={0} | all-to-all | bytes 65536 | tf_op jit(solution)/shard_map/all_to_all | solution.py:390
  164.3 4.6 %collective-permute-start.4 = (f32[2,32,128]{2,1,0:T(8,128)S(1)}, f32[2,32,128]{2,1,0:T(8,128)S(1)}, u32[]{:S(2)}, u32[]{:S(2)}) collective-permute-start(f32[2,32,128]{2,1,0:T(8,128)S(1)} %all_to_all.33), channel_id=1, source_target_pairs={{320,0},{128,1},{0,2},{384,3},{256,64},{192,65},{64,66},{448,67},{... | collective-permute-start | bytes 98312 | tf_op jit(solution)/shard_map/ppermute | solution.py:295
  168.9 5.7 %collective-permute-done.4.part_ref = f32[2,32,128]{2,1,0:T(8,128)S(1)} collective-permute-done((f32[2,32,128]{2,1,0:T(8,128)S(1)}, f32[2,32,128]{2,1,0:T(8,128)S(1)}, u32[]{:S(2)}, u32[]{:S(2)}) %collective-permute-start.4) | collective-permute-done | bytes 32800 | tf_op jit(solution)/shard_map/ppermute | solution.py:295
  (46 shorter events, 5.3 us)
Async XLA Ops:
  0.6 27.5 %copy-start.7 = (bf16[512,64]{0,1:T(8,128)(2,1)S(1)}, bf16[512,64]{0,1:T(8,128)(2,1)}, u32[]{:S(2)}) copy-start(bf16[512,64]{0,1:T(8,128)(2,1)} %param.11) | copy-start | bytes 196612
  0.6 29.5 %copy-start.2 = (bf16[512,1024]{1,0:T(8,128)(2,1)S(1)}, bf16[512,1024]{1,0:T(8,128)(2,1)}, u32[]{:S(2)}) copy-start(bf16[512,1024]{1,0:T(8,128)(2,1)} %a_ref) | copy-start | bytes 3145732
  0.7 31.9 %copy-start.3 = (bf16[512,1024]{1,0:T(8,128)(2,1)S(1)}, bf16[512,1024]{1,0:T(8,128)(2,1)}, u32[]{:S(2)}) copy-start(bf16[512,1024]{1,0:T(8,128)(2,1)} %a_ref.1) | copy-start | bytes 3145732
  0.7 34.0 %copy-start.9 = (f32[16,32]{1,0:T(8,128)S(1)}, f32[16,32]{1,0:T(8,128)}, u32[]{:S(2)}) copy-start(f32[16,32]{1,0:T(8,128)} %param.13) | copy-start | bytes 6148
  0.7 34.0 %copy-start.8 = (f32[16,32]{1,0:T(8,128)S(1)}, f32[16,32]{1,0:T(8,128)}, u32[]{:S(2)}) copy-start(f32[16,32]{1,0:T(8,128)} %param.12) | copy-start | bytes 6148
  1.7 12.6 %collective-permute-start.2 = (bf16[2,32,128]{2,1,0:T(8,128)(2,1)S(1)}, bf16[2,32,128]{2,1,0:T(8,128)(2,1)S(1)}, u32[]{:S(2)}, u32[]{:S(2)}) collective-permute-start(bf16[2,32,128]{2,1,0:T(8,128)(2,1)S(1)} %shard_map.86), channel_id=1, source_target_pairs={{0,320},{1,128},{2,0},{3,384},{64,256},{65,192},{66,64},{67,448},{... | collective-permute-start | bytes 49160 | tf_op jit(solution)/shard_map/ppermute | solution.py:295
  15.4 43.0 %all-to-all-start = ((bf16[128,32,128]{2,1,0:T(8,128)(2,1)}), bf16[128,32,128]{2,1,0:T(8,128)(2,1)S(1)}, u32[]{:S(2)}, u32[]{:S(2)}) async-start(bf16[128,32,128]{2,1,0:T(8,128)(2,1)} %shard_map.87), calls=%async_computation | async-start | bytes 2097152 | tf_op jit(solution)/shard_map/all_to_all | solution.py:305
  28.2 8.3 %collective-permute-start.3 = (bf16[512,64]{1,0:T(8,128)(2,1)S(1)}, bf16[512,64]{1,0:T(8,128)(2,1)S(1)}, u32[]{:S(2)}, u32[]{:S(2)}) collective-permute-start(bf16[512,64]{1,0:T(8,128)(2,1)S(1)} %copy.12.own_ref), channel_id=1, source_target_pairs={{0,4},{4,0},{1,5},{5,1},{2,6},{6,2},{3,7},{7,3},{8,12},{12,8},{9,1... | collective-permute-start | bytes 196616 | tf_op jit(solution)/shard_map/ppermute | solution.py:298
  30.2 28.2 %collective-permute-start = (bf16[512,1024]{1,0:T(8,128)(2,1)S(1)}, bf16[512,1024]{1,0:T(8,128)(2,1)}, u32[]{:S(2)}, u32[]{:S(2)}) collective-permute-start(bf16[512,1024]{1,0:T(8,128)(2,1)S(1)} %copy-done.2), channel_id=1, source_target_pairs={{0,4},{4,0},{1,5},{5,1},{2,6},{6,2},{3,7},{7,3},{8,12},{12,8},{9,1... | collective-permute-start | bytes 3145736 | tf_op jit(solution)/shard_map/ppermute | solution.py:298
  32.6 25.8 %collective-permute-start.1 = (bf16[512,1024]{1,0:T(8,128)(2,1)S(1)}, bf16[512,1024]{1,0:T(8,128)(2,1)}, u32[]{:S(2)}, u32[]{:S(2)}) collective-permute-start(bf16[512,1024]{1,0:T(8,128)(2,1)S(1)} %copy-done.3), channel_id=1, source_target_pairs={{0,4},{4,0},{1,5},{5,1},{2,6},{6,2},{3,7},{7,3},{8,12},{12,8},{9,1... | collective-permute-start | bytes 3145736 | tf_op jit(solution)/shard_map/ppermute | solution.py:298
  36.5 0.6 copy-start.5
  37.2 0.9 copy-start.6
  86.7 18.3 %all-to-all-start.2 = ((f32[64,4,128]{2,1,0:T(4,128)}), f32[64,4,128]{2,1,0:T(4,128)S(1)}, u32[]{:S(2)}, u32[]{:S(2)}) async-start(f32[64,4,128]{2,1,0:T(4,128)} %get-tuple-element.29), calls=%async_computation.2 | async-start | bytes 262144 | tf_op jit(solution)/shard_map/all_to_all | solution.py:367
  94.4 10.5 %copy-start.4 = (f32[64,128]{1,0:T(8,128)S(1)}, f32[64,128]{1,0:T(8,128)}, u32[]{:S(2)}) copy-start(f32[64,128]{1,0:T(8,128)} %fusion.power_ref) | copy-start | bytes 98308
  96.6 1.3 copy-start
  104.9 18.2 %copy-start.1 = (bf16[1024,1024]{1,0:T(8,128)(2,1)S(1)}, bf16[1024,1024]{1,0:T(8,128)(2,1)}, u32[]{:S(2)}) copy-start(bf16[1024,1024]{1,0:T(8,128)(2,1)} %copy-done) | copy-start | bytes 6291460
  164.3 10.4 %collective-permute-start.4 = (f32[2,32,128]{2,1,0:T(8,128)S(1)}, f32[2,32,128]{2,1,0:T(8,128)S(1)}, u32[]{:S(2)}, u32[]{:S(2)}) collective-permute-start(f32[2,32,128]{2,1,0:T(8,128)S(1)} %all_to_all.33), channel_id=1, source_target_pairs={{320,0},{128,1},{0,2},{384,3},{256,64},{192,65},{64,66},{448,67},{... | collective-permute-start | bytes 98312 | tf_op jit(solution)/shard_map/ppermute | solution.py:295

commit v12 on v11

--- a/solution.py
+++ b/solution.py
@@ -170,10 +170,10 @@
     half = rows // 2
     total = own_ref[...]
     low = jnp.zeros((half // 2, 128), F32)
-    for k in range(part_ref.shape[0]):
-        mine = at_ref[1] == k
-        total = total + jnp.where(mine, 0.0, part_ref[k, :rows].astype(F32))
-        low = low + jnp.where(mine, 0.0, part_ref[k, rows:].astype(F32))
+    for e in range(1, part_ref.shape[0]):
+        k = chunk_of(at_ref[1], e)
+        total = total + part_ref[k, :rows].astype(F32)
+        low = low + part_ref[k, rows:].astype(F32)
     low = jnp.concatenate([low, turn(low, 64)], axis=0)
     early = total[:half] + jnp.where(lane_group(low.shape) < 2, low, 0.0)
     x = jnp.where(lane_group(early.shape) < 2, early.astype(BF16).astype(F32), early)
@@ -192,7 +192,7 @@
         )
 
     zero = jnp.zeros((per, 128), F32)
-    held = lax.fori_loop(0, STEPS, step, (zero,) * (2 * MODE_ROWS), unroll=8)
+    held = lax.fori_loop(0, STEPS, step, (zero,) * (2 * MODE_ROWS), unroll=16)
     for m in range(MODE_ROWS):
         for h in range(2):
             st[m * chunks + h * per : m * chunks + (h + 1) * per, :] = held[2 * m + h]
@@ -237,7 +237,7 @@
             new.append(states)
         return tuple(new[h][m] for m in range(MODE_ROWS) for h in range(2))
 
-    lax.fori_loop(0, STEPS, step, tuple(begin), unroll=8)
+    lax.fori_loop(0, STEPS, step, tuple(begin), unroll=16)
     y = ys[...]
     y = y + turn(y, 64)
     y = y + turn(y, 32)

time: 176 us -> 176 us (level)
  no operation moved by 1% of the time
where the time goes in v12:
time: 176 us; the launch traced here: 175 us
  blocking collectives  76.2 us (43%)
  starting transfers between devices  39.9 us (23%)
  waiting for transfers between devices  34 us (19%)
  Pallas kernels  19.2 us (11%)
  local copies, waits for them, and re-layouts  3.84 us (2%)
    all_to_all x1, blocking collectives, local(): partial = lax.all_to_all(partial, CHIPS, 0, 0, tiled=True)  34.3 us
    all_to_all x1, blocking collectives, local(): parts = lax.all_to_all(parts, 'chan', 0, 0, tiled=True)  21.9 us
    all_to_all x1, waiting for transfers between devices, local(): lax.all_to_all(spread, SEQ, 0, 0, tiled=True).reshape(size_z, -1, 128)  19.5 us
    all_to_all x1, blocking collectives, local(): grads = lax.all_to_all(grads, 'chan', 0, 0, tiled=True)  16.2 us
    ppermute x2, starting transfers between devices, transposed(): return lax.ppermute(value, ('seq_0', 'chan'), pairs)  15.5 us
    all_to_all x1, starting transfers between devices, local(): lax.all_to_all(spread, SEQ, 0, 0, tiled=True).reshape(size_z, -1, 128)  12.7 us
    ppermute x2, waiting for transfers between devices, transposed(): return lax.ppermute(value, ('seq_0', 'chan'), pairs)  7.43 us
    all_to_all x1, waiting for transfers between devices, local(): states = lax.all_to_all(state, CHIPS, 0, 0, tiled=True)  6.99 us
  transfers between devices with their start and end apart: 7, of which 4 were waited for; matrix products, arithmetic and copies ran while one was open for 1% of the time, Pallas kernels for 3%

profile of v12, /device:TPU:6, one launch (start us, length us, event | category | flops | bytes accessed | tf_op | source)
XLA Modules:
  0.0 175.2 jit_solution(5107895564104976511)
XLA Ops:
  0.7 1.0 shard_map.86
  1.7 10.9 %collective-permute-start.2 = (bf16[2,32,128]{2,1,0:T(8,128)(2,1)S(1)}, bf16[2,32,128]{2,1,0:T(8,128)(2,1)S(1)}, u32[]{:S(2)}, u32[]{:S(2)}) collective-permute-start(bf16[2,32,128]{2,1,0:T(8,128)(2,1)S(1)} %shard_map.86), channel_id=1, source_target_pairs={{0,320},{1,128},{2,0},{3,384},{64,256},{65,192},{66,64},{67,448},{... | collective-permute-start | bytes 49160 | tf_op jit(solution)/shard_map/ppermute | solution.py:295
  12.6 1.7 collective-permute-done.2.piece_ref
  14.3 1.1 shard_map.87
  15.4 12.7 %all-to-all-start = ((bf16[128,32,128]{2,1,0:T(8,128)(2,1)}), bf16[128,32,128]{2,1,0:T(8,128)(2,1)S(1)}, u32[]{:S(2)}, u32[]{:S(2)}) async-start(bf16[128,32,128]{2,1,0:T(8,128)(2,1)} %shard_map.87), calls=%async_computation | async-start | bytes 2097152 | tf_op jit(solution)/shard_map/all_to_all | solution.py:305
  28.2 1.9 %collective-permute-start.3 = (bf16[512,64]{1,0:T(8,128)(2,1)S(1)}, bf16[512,64]{1,0:T(8,128)(2,1)S(1)}, u32[]{:S(2)}, u32[]{:S(2)}) collective-permute-start(bf16[512,64]{1,0:T(8,128)(2,1)S(1)} %copy.12.own_ref), channel_id=1, source_target_pairs={{0,4},{4,0},{1,5},{5,1},{2,6},{6,2},{3,7},{7,3},{8,12},{12,8},{9,1... | collective-permute-start | bytes 196616 | tf_op jit(solution)/shard_map/ppermute | solution.py:298
  30.2 2.4 %collective-permute-start = (bf16[512,1024]{1,0:T(8,128)(2,1)S(1)}, bf16[512,1024]{1,0:T(8,128)(2,1)}, u32[]{:S(2)}, u32[]{:S(2)}) collective-permute-start(bf16[512,1024]{1,0:T(8,128)(2,1)S(1)} %copy-done.2), channel_id=1, source_target_pairs={{0,4},{4,0},{1,5},{5,1},{2,6},{6,2},{3,7},{7,3},{8,12},{12,8},{9,1... | collective-permute-start | bytes 3145736 | tf_op jit(solution)/shard_map/ppermute | solution.py:298
  32.6 1.9 %collective-permute-start.1 = (bf16[512,1024]{1,0:T(8,128)(2,1)S(1)}, bf16[512,1024]{1,0:T(8,128)(2,1)}, u32[]{:S(2)}, u32[]{:S(2)}) collective-permute-start(bf16[512,1024]{1,0:T(8,128)(2,1)S(1)} %copy-done.3), channel_id=1, source_target_pairs={{0,4},{4,0},{1,5},{5,1},{2,6},{6,2},{3,7},{7,3},{8,12},{12,8},{9,1... | collective-permute-start | bytes 3145736 | tf_op jit(solution)/shard_map/ppermute | solution.py:298
  38.8 19.5 %all-to-all-done = bf16[128,32,128]{2,1,0:T(8,128)(2,1)S(1)} async-done(((bf16[128,32,128]{2,1,0:T(8,128)(2,1)}), bf16[128,32,128]{2,1,0:T(8,128)(2,1)S(1)}, u32[]{:S(2)}, u32[]{:S(2)}) %all-to-all-start) | async-done | bytes 1048608 | tf_op jit(solution)/shard_map/all_to_all | solution.py:305
  58.4 4.1 %shard_map.89 = (bf16[4,1280,128]{2,1,0:T(8,128)(2,1)S(1)}, f32[1024,128]{1,0:T(8,128)S(1)}) custom-call(s32[2]{0:T(128)S(1)} %pad_add_fusion.at_ref, bf16[512,1024]{1,0:T(8,128)(2,1)S(1)} %copy-done.2, bf16[512,1024]{1,0:T(8,128)(2,1)} %collective-permute-done.other_t.b_ref, bf16[512,1024]{1,0:T(8,128)(2,1)S(1)} %copy-done.3, ...), custom_call_target="tpu_custom_call" | custom-call | flops 2147483648 | bytes 8388608 | tf_op jit(solution)/shard_map/pallas_call | solution.py:342
  62.5 21.9 %all_to_all.30.part_ref = bf16[4,1280,128]{2,1,0:T(8,128)(2,1)S(1)} all-to-all(bf16[4,1280,128]{2,1,0:T(8,128)(2,1)S(1)} %get-tuple-element.25), channel_id=1, replica_groups=mesh['seq_0'=8,'seq_1'=8,'seq_2'=2,'chan'=4] {'chan'}, dimensions={0} | all-to-all | bytes 2621440 | tf_op jit(solution)/shard_map/all_to_all | solution.py:345
  84.4 2.1 %shard_map.90 = (f32[512,128]{1,0:T(8,128)S(1)}, f32[512,128]{1,0:T(8,128)S(1)}, f32[64,128]{1,0:T(8,128)S(1)}, f32[64,4,128]{2,1,0:T(4,128)}) custom-call(s32[2]{0:T(128)S(1)} %pad_add_fusion.at_ref, bf16[4,1280,128]{2,1,0:T(8,128)(2,1)S(1)} %all_to_all.30.part_ref, f32[1024,128]{1,0:T(8,128)S(1)} %get-tuple-element.26.own_ref, ...), custom_call_target="tpu_custom_call" | custom-call | tf_op jit(solution)/shard_map/pallas_call | solution.py:359
  86.5 5.6 %all-to-all-start.2 = ((f32[64,4,128]{2,1,0:T(4,128)}), f32[64,4,128]{2,1,0:T(4,128)S(1)}, u32[]{:S(2)}, u32[]{:S(2)}) async-start(f32[64,4,128]{2,1,0:T(4,128)} %get-tuple-element.29), calls=%async_computation.2 | async-start | bytes 262144 | tf_op jit(solution)/shard_map/all_to_all | solution.py:367
  92.0 2.2 %shard_map.91.tt_ref = bf16[1024,1024]{1,0:T(8,128)(2,1)S(1)} custom-call(bf16[512,1024]{1,0:T(8,128)(2,1)} %a_ref, bf16[512,1024]{1,0:T(8,128)(2,1)} %collective-permute-done.other_t.b_ref), custom_call_target="tpu_custom_call" | custom-call | bytes 4194304 | tf_op jit(solution)/shard_map/pallas_call | solution.py:365
  94.2 2.2 %shard_map.92.gt_ref = bf16[1024,1024]{1,0:T(8,128)(2,1)S(1)} custom-call(bf16[512,1024]{1,0:T(8,128)(2,1)} %a_ref.1, bf16[512,1024]{1,0:T(8,128)(2,1)} %collective-permute-done.1.other_g.b_ref), custom_call_target="tpu_custom_call" | custom-call | bytes 4194304 | tf_op jit(solution)/shard_map/pallas_call | solution.py:366
  96.4 1.3 copy-done
  97.8 7.0 %all-to-all-done.2.states_ref = f32[64,4,128]{2,1,0:T(4,128)S(1)} async-done(((f32[64,4,128]{2,1,0:T(4,128)}), f32[64,4,128]{2,1,0:T(4,128)S(1)}, u32[]{:S(2)}, u32[]{:S(2)}) %all-to-all-start.2) | async-done | bytes 131104 | tf_op jit(solution)/shard_map/all_to_all | solution.py:367
  104.8 1.9 %shard_map.93 = bf16[4,1024,128]{2,1,0:T(8,128)(2,1)S(1)} custom-call(s32[2]{0:T(128)S(1)} %pad_add_fusion.at_ref, f32[512,128]{1,0:T(8,128)S(1)} %get-tuple-element.37.x_ref, f32[512,128]{1,0:T(8,128)S(1)} %get-tuple-element.38.late_ref, f32[64,128]{1,0:T(8,128)S(1)} %get-tuple-element.30.left_ref, f32[64,4,128]{2,1,0:T(4,128)S(1)} %all-to-all-done.2.states_ref, ...), custom_call_target="tpu_custom_call" | custom-call | tf_op jit(solution)/shard_map/pallas_call | solution.py:376
  106.7 16.2 %all_to_all.31.grads_ref = bf16[4,1024,128]{2,1,0:T(8,128)(2,1)S(1)} all-to-all(bf16[4,1024,128]{2,1,0:T(8,128)(2,1)S(1)} %shard_map.93), channel_id=1, replica_groups=mesh['seq_0'=8,'seq_1'=8,'seq_2'=2,'chan'=4] {'chan'}, dimensions={0} | all-to-all | bytes 2097152 | tf_op jit(solution)/shard_map/all_to_all | solution.py:377
  122.9 2.9 %shard_map.94 = bf16[8,512,128]{2,1,0:T(8,128)(2,1)S(1)} custom-call(s32[2]{0:T(128)S(1)} %pad_add_fusion.at_ref, bf16[1024,1024]{1,0:T(8,128)(2,1)S(1)} %shard_map.91.tt_ref, bf16[1024,1024]{1,0:T(8,128)(2,1)S(1)} %copy-done.1, bf16[4,1024,128]{2,1,0:T(8,128)(2,1)S(1)} %all_to_all.31.grads_ref), custom_call_target="tpu_custom_call" | custom-call | flops 2147483648 | bytes 8388608 | tf_op jit(solution)/shard_map/pallas_call | solution.py:387
  125.8 34.3 %all_to_all.32.part_ref = bf16[64,64,128]{2,1,0:T(8,128)(2,1)S(1)} all-to-all(bf16[64,64,128]{2,1,0:T(8,128)(2,1)S(1)} %bitcast.17), channel_id=1, replica_groups=mesh['seq_0'=8,'seq_1'=8,'seq_2'=2,'chan'=4] {'seq_0','seq_1'}, dimensions={0} | all-to-all | bytes 2097152 | tf_op jit(solution)/shard_map/all_to_all | solution.py:388
  160.3 3.7 %all_to_all.33 = f32[2,32,128]{2,1,0:T(8,128)S(1)} all-to-all(f32[2,32,128]{2,1,0:T(8,128)S(1)} %shard_map.95), channel_id=1, replica_groups=mesh['seq_0'=8,'seq_1'=8,'seq_2'=2,'chan'=4] {'seq_2'}, dimensions={0} | all-to-all | bytes 65536 | tf_op jit(solution)/shard_map/all_to_all | solution.py:390
  164.1 4.6 %collective-permute-start.4 = (f32[2,32,128]{2,1,0:T(8,128)S(1)}, f32[2,32,128]{2,1,0:T(8,128)S(1)}, u32[]{:S(2)}, u32[]{:S(2)}) collective-permute-start(f32[2,32,128]{2,1,0:T(8,128)S(1)} %all_to_all.33), channel_id=1, source_target_pairs={{320,0},{128,1},{0,2},{384,3},{256,64},{192,65},{64,66},{448,67},{... | collective-permute-start | bytes 98312 | tf_op jit(solution)/shard_map/ppermute | solution.py:295
  168.7 5.7 %collective-permute-done.4.part_ref = f32[2,32,128]{2,1,0:T(8,128)S(1)} collective-permute-done((f32[2,32,128]{2,1,0:T(8,128)S(1)}, f32[2,32,128]{2,1,0:T(8,128)S(1)}, u32[]{:S(2)}, u32[]{:S(2)}) %collective-permute-start.4) | collective-permute-done | bytes 32800 | tf_op jit(solution)/shard_map/ppermute | solution.py:295
  (46 shorter events, 5.3 us)
Async XLA Ops:
  0.6 27.5 %copy-start.7 = (bf16[512,64]{0,1:T(8,128)(2,1)S(1)}, bf16[512,64]{0,1:T(8,128)(2,1)}, u32[]{:S(2)}) copy-start(bf16[512,64]{0,1:T(8,128)(2,1)} %param.11) | copy-start | bytes 196612
  0.6 29.5 %copy-start.2 = (bf16[512,1024]{1,0:T(8,128)(2,1)S(1)}, bf16[512,1024]{1,0:T(8,128)(2,1)}, u32[]{:S(2)}) copy-start(bf16[512,1024]{1,0:T(8,128)(2,1)} %a_ref) | copy-start | bytes 3145732
  0.7 31.9 %copy-start.3 = (bf16[512,1024]{1,0:T(8,128)(2,1)S(1)}, bf16[512,1024]{1,0:T(8,128)(2,1)}, u32[]{:S(2)}) copy-start(bf16[512,1024]{1,0:T(8,128)(2,1)} %a_ref.1) | copy-start | bytes 3145732
  0.7 34.0 %copy-start.9 = (f32[16,32]{1,0:T(8,128)S(1)}, f32[16,32]{1,0:T(8,128)}, u32[]{:S(2)}) copy-start(f32[16,32]{1,0:T(8,128)} %param.13) | copy-start | bytes 6148
  0.7 34.0 %copy-start.8 = (f32[16,32]{1,0:T(8,128)S(1)}, f32[16,32]{1,0:T(8,128)}, u32[]{:S(2)}) copy-start(f32[16,32]{1,0:T(8,128)} %param.12) | copy-start | bytes 6148
  1.7 12.6 %collective-permute-start.2 = (bf16[2,32,128]{2,1,0:T(8,128)(2,1)S(1)}, bf16[2,32,128]{2,1,0:T(8,128)(2,1)S(1)}, u32[]{:S(2)}, u32[]{:S(2)}) collective-permute-start(bf16[2,32,128]{2,1,0:T(8,128)(2,1)S(1)} %shard_map.86), channel_id=1, source_target_pairs={{0,320},{1,128},{2,0},{3,384},{64,256},{65,192},{66,64},{67,448},{... | collective-permute-start | bytes 49160 | tf_op jit(solution)/shard_map/ppermute | solution.py:295
  15.4 43.0 %all-to-all-start = ((bf16[128,32,128]{2,1,0:T(8,128)(2,1)}), bf16[128,32,128]{2,1,0:T(8,128)(2,1)S(1)}, u32[]{:S(2)}, u32[]{:S(2)}) async-start(bf16[128,32,128]{2,1,0:T(8,128)(2,1)} %shard_map.87), calls=%async_computation | async-start | bytes 2097152 | tf_op jit(solution)/shard_map/all_to_all | solution.py:305
  28.2 8.3 %collective-permute-start.3 = (bf16[512,64]{1,0:T(8,128)(2,1)S(1)}, bf16[512,64]{1,0:T(8,128)(2,1)S(1)}, u32[]{:S(2)}, u32[]{:S(2)}) collective-permute-start(bf16[512,64]{1,0:T(8,128)(2,1)S(1)} %copy.12.own_ref), channel_id=1, source_target_pairs={{0,4},{4,0},{1,5},{5,1},{2,6},{6,2},{3,7},{7,3},{8,12},{12,8},{9,1... | collective-permute-start | bytes 196616 | tf_op jit(solution)/shard_map/ppermute | solution.py:298
  30.2 28.2 %collective-permute-start = (bf16[512,1024]{1,0:T(8,128)(2,1)S(1)}, bf16[512,1024]{1,0:T(8,128)(2,1)}, u32[]{:S(2)}, u32[]{:S(2)}) collective-permute-start(bf16[512,1024]{1,0:T(8,128)(2,1)S(1)} %copy-done.2), channel_id=1, source_target_pairs={{0,4},{4,0},{1,5},{5,1},{2,6},{6,2},{3,7},{7,3},{8,12},{12,8},{9,1... | collective-permute-start | bytes 3145736 | tf_op jit(solution)/shard_map/ppermute | solution.py:298
  32.6 25.8 %collective-permute-start.1 = (bf16[512,1024]{1,0:T(8,128)(2,1)S(1)}, bf16[512,1024]{1,0:T(8,128)(2,1)}, u32[]{:S(2)}, u32[]{:S(2)}) collective-permute-start(bf16[512,1024]{1,0:T(8,128)(2,1)S(1)} %copy-done.3), channel_id=1, source_target_pairs={{0,4},{4,0},{1,5},{5,1},{2,6},{6,2},{3,7},{7,3},{8,12},{12,8},{9,1... | collective-permute-start | bytes 3145736 | tf_op jit(solution)/shard_map/ppermute | solution.py:298
  36.5 0.6 copy-start.5
  37.2 0.9 copy-start.6
  86.5 18.3 %all-to-all-start.2 = ((f32[64,4,128]{2,1,0:T(4,128)}), f32[64,4,128]{2,1,0:T(4,128)S(1)}, u32[]{:S(2)}, u32[]{:S(2)}) async-start(f32[64,4,128]{2,1,0:T(4,128)} %get-tuple-element.29), calls=%async_computation.2 | async-start | bytes 262144 | tf_op jit(solution)/shard_map/all_to_all | solution.py:367
  94.2 10.5 %copy-start.4 = (f32[64,128]{1,0:T(8,128)S(1)}, f32[64,128]{1,0:T(8,128)}, u32[]{:S(2)}) copy-start(f32[64,128]{1,0:T(8,128)} %fusion.power_ref) | copy-start | bytes 98308
  96.4 1.3 copy-start
  104.8 18.2 %copy-start.1 = (bf16[1024,1024]{1,0:T(8,128)(2,1)S(1)}, bf16[1024,1024]{1,0:T(8,128)(2,1)}, u32[]{:S(2)}) copy-start(bf16[1024,1024]{1,0:T(8,128)(2,1)} %copy-done) | copy-start | bytes 6291460
  164.1 10.4 %collective-permute-start.4 = (f32[2,32,128]{2,1,0:T(8,128)S(1)}, f32[2,32,128]{2,1,0:T(8,128)S(1)}, u32[]{:S(2)}, u32[]{:S(2)}) collective-permute-start(f32[2,32,128]{2,1,0:T(8,128)S(1)} %all_to_all.33), channel_id=1, source_target_pairs={{320,0},{128,1},{0,2},{384,3},{256,64},{192,65},{64,66},{448,67},{... | collective-permute-start | bytes 98312 | tf_op jit(solution)/shard_map/ppermute | solution.py:295

commit v13 on v12

--- a/solution.py
+++ b/solution.py
@@ -254,15 +254,15 @@
 def weigh_body(at_ref, tt_ref, gt_ref, grads_ref, out_ref):
     plane = at_ref[1]
     block = out_ref.shape[1]
-    for l in range(2):
-        r = l * block
-        for c in range(0, grads_ref.shape[0], 2):
-            g = jnp.concatenate([grads_ref[chunk_of(plane, c + k)] for k in range(2)], axis=1)
-            from_t = jnp.dot(tt_ref[r : r + block, :], g, preferred_element_type=F32)
-            from_g = jnp.dot(gt_ref[r : r + block, :], g, preferred_element_type=F32)
+    for e in range(0, grads_ref.shape[0], 2):
+        g = jnp.concatenate([grads_ref[chunk_of(plane, e + k)] for k in range(2)], axis=1)
+        for l in range(2):
+            here = slice(l * block, (l + 1) * block)
+            from_t = jnp.dot(tt_ref[here, :], g, preferred_element_type=F32)
+            from_g = jnp.dot(gt_ref[here, :], g, preferred_element_type=F32)
             both = jnp.where(lane_group(from_t.shape) % GROUPS != 1, from_t, from_g).astype(BF16)
-            out_ref[holder(plane, c, l)] = both[:, :128]
-            out_ref[holder(plane, c + 1, l)] = both[:, 128:]
+            out_ref[holder(plane, e, l)] = both[:, :128]
+            out_ref[holder(plane, e + 1, l)] = both[:, 128:]
 
 
 def by_lanes(table):

time: 176 us -> 176 us (level)
  no operation moved by 1% of the time
where the time goes in v13:
time: 176 us; the launch traced here: 175 us
  blocking collectives  76.2 us (43%)
  starting transfers between devices  39.9 us (23%)
  waiting for transfers between devices  34 us (19%)
  Pallas kernels  19.2 us (11%)
  local copies, waits for them, and re-layouts  3.84 us (2%)
    all_to_all x1, blocking collectives, local(): partial = lax.all_to_all(partial, CHIPS, 0, 0, tiled=True)  34.3 us
    all_to_all x1, blocking collectives, local(): parts = lax.all_to_all(parts, 'chan', 0, 0, tiled=True)  21.9 us
    all_to_all x1, waiting for transfers between devices, local(): lax.all_to_all(spread, SEQ, 0, 0, tiled=True).reshape(size_z, -1, 128)  19.5 us
    all_to_all x1, blocking collectives, local(): grads = lax.all_to_all(grads, 'chan', 0, 0, tiled=True)  16.2 us
    ppermute x2, starting transfers between devices, transposed(): return lax.ppermute(value, ('seq_0', 'chan'), pairs)  15.5 us
    all_to_all x1, starting transfers between devices, local(): lax.all_to_all(spread, SEQ, 0, 0, tiled=True).reshape(size_z, -1, 128)  12.7 us
    ppermute x2, waiting for transfers between devices, transposed(): return lax.ppermute(value, ('seq_0', 'chan'), pairs)  7.43 us
    all_to_all x1, waiting for transfers between devices, local(): states = lax.all_to_all(state, CHIPS, 0, 0, tiled=True)  6.99 us
  transfers between devices with their start and end apart: 7, of which 4 were waited for; matrix products, arithmetic and copies ran while one was open for 1% of the time, Pallas kernels for 3%

profile of v13, /device:TPU:6, one launch (start us, length us, event | category | flops | bytes accessed | tf_op | source)
XLA Modules:
  0.0 175.2 jit_solution(6468584227324711325)
XLA Ops:
  0.7 1.0 shard_map.86
  1.7 10.9 %collective-permute-start.2 = (bf16[2,32,128]{2,1,0:T(8,128)(2,1)S(1)}, bf16[2,32,128]{2,1,0:T(8,128)(2,1)S(1)}, u32[]{:S(2)}, u32[]{:S(2)}) collective-permute-start(bf16[2,32,128]{2,1,0:T(8,128)(2,1)S(1)} %shard_map.86), channel_id=1, source_target_pairs={{0,320},{1,128},{2,0},{3,384},{64,256},{65,192},{66,64},{67,448},{... | collective-permute-start | bytes 49160 | tf_op jit(solution)/shard_map/ppermute | solution.py:295
  12.6 1.7 collective-permute-done.2.piece_ref
  14.3 1.1 shard_map.87
  15.4 12.7 %all-to-all-start = ((bf16[128,32,128]{2,1,0:T(8,128)(2,1)}), bf16[128,32,128]{2,1,0:T(8,128)(2,1)S(1)}, u32[]{:S(2)}, u32[]{:S(2)}) async-start(bf16[128,32,128]{2,1,0:T(8,128)(2,1)} %shard_map.87), calls=%async_computation | async-start | bytes 2097152 | tf_op jit(solution)/shard_map/all_to_all | solution.py:305
  28.2 1.9 %collective-permute-start.3 = (bf16[512,64]{1,0:T(8,128)(2,1)S(1)}, bf16[512,64]{1,0:T(8,128)(2,1)S(1)}, u32[]{:S(2)}, u32[]{:S(2)}) collective-permute-start(bf16[512,64]{1,0:T(8,128)(2,1)S(1)} %copy.12.own_ref), channel_id=1, source_target_pairs={{0,4},{4,0},{1,5},{5,1},{2,6},{6,2},{3,7},{7,3},{8,12},{12,8},{9,1... | collective-permute-start | bytes 196616 | tf_op jit(solution)/shard_map/ppermute | solution.py:298
  30.2 2.4 %collective-permute-start = (bf16[512,1024]{1,0:T(8,128)(2,1)S(1)}, bf16[512,1024]{1,0:T(8,128)(2,1)}, u32[]{:S(2)}, u32[]{:S(2)}) collective-permute-start(bf16[512,1024]{1,0:T(8,128)(2,1)S(1)} %copy-done.2), channel_id=1, source_target_pairs={{0,4},{4,0},{1,5},{5,1},{2,6},{6,2},{3,7},{7,3},{8,12},{12,8},{9,1... | collective-permute-start | bytes 3145736 | tf_op jit(solution)/shard_map/ppermute | solution.py:298
  32.6 1.9 %collective-permute-start.1 = (bf16[512,1024]{1,0:T(8,128)(2,1)S(1)}, bf16[512,1024]{1,0:T(8,128)(2,1)}, u32[]{:S(2)}, u32[]{:S(2)}) collective-permute-start(bf16[512,1024]{1,0:T(8,128)(2,1)S(1)} %copy-done.3), channel_id=1, source_target_pairs={{0,4},{4,0},{1,5},{5,1},{2,6},{6,2},{3,7},{7,3},{8,12},{12,8},{9,1... | collective-permute-start | bytes 3145736 | tf_op jit(solution)/shard_map/ppermute | solution.py:298
  38.8 19.5 %all-to-all-done = bf16[128,32,128]{2,1,0:T(8,128)(2,1)S(1)} async-done(((bf16[128,32,128]{2,1,0:T(8,128)(2,1)}), bf16[128,32,128]{2,1,0:T(8,128)(2,1)S(1)}, u32[]{:S(2)}, u32[]{:S(2)}) %all-to-all-start) | async-done | bytes 1048608 | tf_op jit(solution)/shard_map/all_to_all | solution.py:305
  58.4 4.1 %shard_map.89 = (bf16[4,1280,128]{2,1,0:T(8,128)(2,1)S(1)}, f32[1024,128]{1,0:T(8,128)S(1)}) custom-call(s32[2]{0:T(128)S(1)} %pad_add_fusion.at_ref, bf16[512,1024]{1,0:T(8,128)(2,1)S(1)} %copy-done.2, bf16[512,1024]{1,0:T(8,128)(2,1)} %collective-permute-done.other_t.b_ref, bf16[512,1024]{1,0:T(8,128)(2,1)S(1)} %copy-done.3, ...), custom_call_target="tpu_custom_call" | custom-call | flops 2147483648 | bytes 8388608 | tf_op jit(solution)/shard_map/pallas_call | solution.py:342
  62.5 21.9 %all_to_all.30.part_ref = bf16[4,1280,128]{2,1,0:T(8,128)(2,1)S(1)} all-to-all(bf16[4,1280,128]{2,1,0:T(8,128)(2,1)S(1)} %get-tuple-element.25), channel_id=1, replica_groups=mesh['seq_0'=8,'seq_1'=8,'seq_2'=2,'chan'=4] {'chan'}, dimensions={0} | all-to-all | bytes 2621440 | tf_op jit(solution)/shard_map/all_to_all | solution.py:345
  84.4 2.1 %shard_map.90 = (f32[512,128]{1,0:T(8,128)S(1)}, f32[512,128]{1,0:T(8,128)S(1)}, f32[64,128]{1,0:T(8,128)S(1)}, f32[64,4,128]{2,1,0:T(4,128)}) custom-call(s32[2]{0:T(128)S(1)} %pad_add_fusion.at_ref, bf16[4,1280,128]{2,1,0:T(8,128)(2,1)S(1)} %all_to_all.30.part_ref, f32[1024,128]{1,0:T(8,128)S(1)} %get-tuple-element.26.own_ref, ...), custom_call_target="tpu_custom_call" | custom-call | tf_op jit(solution)/shard_map/pallas_call | solution.py:359
  86.5 5.6 %all-to-all-start.2 = ((f32[64,4,128]{2,1,0:T(4,128)}), f32[64,4,128]{2,1,0:T(4,128)S(1)}, u32[]{:S(2)}, u32[]{:S(2)}) async-start(f32[64,4,128]{2,1,0:T(4,128)} %get-tuple-element.29), calls=%async_computation.2 | async-start | bytes 262144 | tf_op jit(solution)/shard_map/all_to_all | solution.py:367
  92.0 2.2 %shard_map.91.tt_ref = bf16[1024,1024]{1,0:T(8,128)(2,1)S(1)} custom-call(bf16[512,1024]{1,0:T(8,128)(2,1)} %a_ref, bf16[512,1024]{1,0:T(8,128)(2,1)} %collective-permute-done.other_t.b_ref), custom_call_target="tpu_custom_call" | custom-call | bytes 4194304 | tf_op jit(solution)/shard_map/pallas_call | solution.py:365
  94.2 2.2 %shard_map.92.gt_ref = bf16[1024,1024]{1,0:T(8,128)(2,1)S(1)} custom-call(bf16[512,1024]{1,0:T(8,128)(2,1)} %a_ref.1, bf16[512,1024]{1,0:T(8,128)(2,1)} %collective-permute-done.1.other_g.b_ref), custom_call_target="tpu_custom_call" | custom-call | bytes 4194304 | tf_op jit(solution)/shard_map/pallas_call | solution.py:366
  96.4 1.3 copy-done
  97.8 7.0 %all-to-all-done.2.states_ref = f32[64,4,128]{2,1,0:T(4,128)S(1)} async-done(((f32[64,4,128]{2,1,0:T(4,128)}), f32[64,4,128]{2,1,0:T(4,128)S(1)}, u32[]{:S(2)}, u32[]{:S(2)}) %all-to-all-start.2) | async-done | bytes 131104 | tf_op jit(solution)/shard_map/all_to_all | solution.py:367
  104.8 1.9 %shard_map.93 = bf16[4,1024,128]{2,1,0:T(8,128)(2,1)S(1)} custom-call(s32[2]{0:T(128)S(1)} %pad_add_fusion.at_ref, f32[512,128]{1,0:T(8,128)S(1)} %get-tuple-element.37.x_ref, f32[512,128]{1,0:T(8,128)S(1)} %get-tuple-element.38.late_ref, f32[64,128]{1,0:T(8,128)S(1)} %get-tuple-element.30.left_ref, f32[64,4,128]{2,1,0:T(4,128)S(1)} %all-to-all-done.2.states_ref, ...), custom_call_target="tpu_custom_call" | custom-call | tf_op jit(solution)/shard_map/pallas_call | solution.py:376
  106.7 16.2 %all_to_all.31.grads_ref = bf16[4,1024,128]{2,1,0:T(8,128)(2,1)S(1)} all-to-all(bf16[4,1024,128]{2,1,0:T(8,128)(2,1)S(1)} %shard_map.93), channel_id=1, replica_groups=mesh['seq_0'=8,'seq_1'=8,'seq_2'=2,'chan'=4] {'chan'}, dimensions={0} | all-to-all | bytes 2097152 | tf_op jit(solution)/shard_map/all_to_all | solution.py:377
  122.9 2.9 %shard_map.94 = bf16[8,512,128]{2,1,0:T(8,128)(2,1)S(1)} custom-call(s32[2]{0:T(128)S(1)} %pad_add_fusion.at_ref, bf16[1024,1024]{1,0:T(8,128)(2,1)S(1)} %shard_map.91.tt_ref, bf16[1024,1024]{1,0:T(8,128)(2,1)S(1)} %copy-done.1, bf16[4,1024,128]{2,1,0:T(8,128)(2,1)S(1)} %all_to_all.31.grads_ref), custom_call_target="tpu_custom_call" | custom-call | flops 2147483648 | bytes 8388608 | tf_op jit(solution)/shard_map/pallas_call | solution.py:387
  125.8 34.3 %all_to_all.32.part_ref = bf16[64,64,128]{2,1,0:T(8,128)(2,1)S(1)} all-to-all(bf16[64,64,128]{2,1,0:T(8,128)(2,1)S(1)} %bitcast.17), channel_id=1, replica_groups=mesh['seq_0'=8,'seq_1'=8,'seq_2'=2,'chan'=4] {'seq_0','seq_1'}, dimensions={0} | all-to-all | bytes 2097152 | tf_op jit(solution)/shard_map/all_to_all | solution.py:388
  160.3 3.7 %all_to_all.33 = f32[2,32,128]{2,1,0:T(8,128)S(1)} all-to-all(f32[2,32,128]{2,1,0:T(8,128)S(1)} %shard_map.95), channel_id=1, replica_groups=mesh['seq_0'=8,'seq_1'=8,'seq_2'=2,'chan'=4] {'seq_2'}, dimensions={0} | all-to-all | bytes 65536 | tf_op jit(solution)/shard_map/all_to_all | solution.py:390
  164.1 4.6 %collective-permute-start.4 = (f32[2,32,128]{2,1,0:T(8,128)S(1)}, f32[2,32,128]{2,1,0:T(8,128)S(1)}, u32[]{:S(2)}, u32[]{:S(2)}) collective-permute-start(f32[2,32,128]{2,1,0:T(8,128)S(1)} %all_to_all.33), channel_id=1, source_target_pairs={{320,0},{128,1},{0,2},{384,3},{256,64},{192,65},{64,66},{448,67},{... | collective-permute-start | bytes 98312 | tf_op jit(solution)/shard_map/ppermute | solution.py:295
  168.7 5.7 %collective-permute-done.4.part_ref = f32[2,32,128]{2,1,0:T(8,128)S(1)} collective-permute-done((f32[2,32,128]{2,1,0:T(8,128)S(1)}, f32[2,32,128]{2,1,0:T(8,128)S(1)}, u32[]{:S(2)}, u32[]{:S(2)}) %collective-permute-start.4) | collective-permute-done | bytes 32800 | tf_op jit(solution)/shard_map/ppermute | solution.py:295
  (46 shorter events, 5.3 us)
Async XLA Ops:
  0.6 27.5 %copy-start.7 = (bf16[512,64]{0,1:T(8,128)(2,1)S(1)}, bf16[512,64]{0,1:T(8,128)(2,1)}, u32[]{:S(2)}) copy-start(bf16[512,64]{0,1:T(8,128)(2,1)} %param.11) | copy-start | bytes 196612
  0.6 29.5 %copy-start.2 = (bf16[512,1024]{1,0:T(8,128)(2,1)S(1)}, bf16[512,1024]{1,0:T(8,128)(2,1)}, u32[]{:S(2)}) copy-start(bf16[512,1024]{1,0:T(8,128)(2,1)} %a_ref) | copy-start | bytes 3145732
  0.7 31.9 %copy-start.3 = (bf16[512,1024]{1,0:T(8,128)(2,1)S(1)}, bf16[512,1024]{1,0:T(8,128)(2,1)}, u32[]{:S(2)}) copy-start(bf16[512,1024]{1,0:T(8,128)(2,1)} %a_ref.1) | copy-start | bytes 3145732
  0.7 34.0 %copy-start.9 = (f32[16,32]{1,0:T(8,128)S(1)}, f32[16,32]{1,0:T(8,128)}, u32[]{:S(2)}) copy-start(f32[16,32]{1,0:T(8,128)} %param.13) | copy-start | bytes 6148
  0.7 34.0 %copy-start.8 = (f32[16,32]{1,0:T(8,128)S(1)}, f32[16,32]{1,0:T(8,128)}, u32[]{:S(2)}) copy-start(f32[16,32]{1,0:T(8,128)} %param.12) | copy-start | bytes 6148
  1.7 12.6 %collective-permute-start.2 = (bf16[2,32,128]{2,1,0:T(8,128)(2,1)S(1)}, bf16[2,32,128]{2,1,0:T(8,128)(2,1)S(1)}, u32[]{:S(2)}, u32[]{:S(2)}) collective-permute-start(bf16[2,32,128]{2,1,0:T(8,128)(2,1)S(1)} %shard_map.86), channel_id=1, source_target_pairs={{0,320},{1,128},{2,0},{3,384},{64,256},{65,192},{66,64},{67,448},{... | collective-permute-start | bytes 49160 | tf_op jit(solution)/shard_map/ppermute | solution.py:295
  15.4 43.0 %all-to-all-start = ((bf16[128,32,128]{2,1,0:T(8,128)(2,1)}), bf16[128,32,128]{2,1,0:T(8,128)(2,1)S(1)}, u32[]{:S(2)}, u32[]{:S(2)}) async-start(bf16[128,32,128]{2,1,0:T(8,128)(2,1)} %shard_map.87), calls=%async_computation | async-start | bytes 2097152 | tf_op jit(solution)/shard_map/all_to_all | solution.py:305
  28.2 8.3 %collective-permute-start.3 = (bf16[512,64]{1,0:T(8,128)(2,1)S(1)}, bf16[512,64]{1,0:T(8,128)(2,1)S(1)}, u32[]{:S(2)}, u32[]{:S(2)}) collective-permute-start(bf16[512,64]{1,0:T(8,128)(2,1)S(1)} %copy.12.own_ref), channel_id=1, source_target_pairs={{0,4},{4,0},{1,5},{5,1},{2,6},{6,2},{3,7},{7,3},{8,12},{12,8},{9,1... | collective-permute-start | bytes 196616 | tf_op jit(solution)/shard_map/ppermute | solution.py:298
  30.2 28.2 %collective-permute-start = (bf16[512,1024]{1,0:T(8,128)(2,1)S(1)}, bf16[512,1024]{1,0:T(8,128)(2,1)}, u32[]{:S(2)}, u32[]{:S(2)}) collective-permute-start(bf16[512,1024]{1,0:T(8,128)(2,1)S(1)} %copy-done.2), channel_id=1, source_target_pairs={{0,4},{4,0},{1,5},{5,1},{2,6},{6,2},{3,7},{7,3},{8,12},{12,8},{9,1... | collective-permute-start | bytes 3145736 | tf_op jit(solution)/shard_map/ppermute | solution.py:298
  32.6 25.8 %collective-permute-start.1 = (bf16[512,1024]{1,0:T(8,128)(2,1)S(1)}, bf16[512,1024]{1,0:T(8,128)(2,1)}, u32[]{:S(2)}, u32[]{:S(2)}) collective-permute-start(bf16[512,1024]{1,0:T(8,128)(2,1)S(1)} %copy-done.3), channel_id=1, source_target_pairs={{0,4},{4,0},{1,5},{5,1},{2,6},{6,2},{3,7},{7,3},{8,12},{12,8},{9,1... | collective-permute-start | bytes 3145736 | tf_op jit(solution)/shard_map/ppermute | solution.py:298
  36.5 0.6 copy-start.5
  37.2 0.9 copy-start.6
  86.5 18.3 %all-to-all-start.2 = ((f32[64,4,128]{2,1,0:T(4,128)}), f32[64,4,128]{2,1,0:T(4,128)S(1)}, u32[]{:S(2)}, u32[]{:S(2)}) async-start(f32[64,4,128]{2,1,0:T(4,128)} %get-tuple-element.29), calls=%async_computation.2 | async-start | bytes 262144 | tf_op jit(solution)/shard_map/all_to_all | solution.py:367
  94.2 10.5 %copy-start.4 = (f32[64,128]{1,0:T(8,128)S(1)}, f32[64,128]{1,0:T(8,128)}, u32[]{:S(2)}) copy-start(f32[64,128]{1,0:T(8,128)} %fusion.power_ref) | copy-start | bytes 98308
  96.4 1.3 copy-start
  104.8 18.2 %copy-start.1 = (bf16[1024,1024]{1,0:T(8,128)(2,1)S(1)}, bf16[1024,1024]{1,0:T(8,128)(2,1)}, u32[]{:S(2)}) copy-start(bf16[1024,1024]{1,0:T(8,128)(2,1)} %copy-done) | copy-start | bytes 6291460
  164.1 10.4 %collective-permute-start.4 = (f32[2,32,128]{2,1,0:T(8,128)S(1)}, f32[2,32,128]{2,1,0:T(8,128)S(1)}, u32[]{:S(2)}, u32[]{:S(2)}) collective-permute-start(f32[2,32,128]{2,1,0:T(8,128)S(1)} %all_to_all.33), channel_id=1, source_target_pairs={{320,0},{128,1},{0,2},{384,3},{256,64},{192,65},{64,66},{448,67},{... | collective-permute-start | bytes 98312 | tf_op jit(solution)/shard_map/ppermute | solution.py:295

commit v14 on v13

--- a/solution.py
+++ b/solution.py
@@ -8,7 +8,7 @@
 
 SEQ = ("seq_0", "seq_1", "seq_2")
 CHIPS = ("seq_0", "seq_1")
-STEPS = 64
+STEPS = 32
 MODE_ROWS = 4
 GROUPS = 4
 F32 = jnp.float32

time: 176 us -> 176 us (level)
  no operation moved by 1% of the time
where the time goes in v14:
time: 176 us; the launch traced here: 175 us
  blocking collectives  76.2 us (43%)
  starting transfers between devices  40 us (23%)
  waiting for transfers between devices  33.9 us (19%)
  Pallas kernels  19.6 us (11%)
  local copies, waits for them, and re-layouts  3.84 us (2%)
    all_to_all x1, blocking collectives, local(): partial = lax.all_to_all(partial, CHIPS, 0, 0, tiled=True)  34.3 us
    all_to_all x1, blocking collectives, local(): parts = lax.all_to_all(parts, 'chan', 0, 0, tiled=True)  21.9 us
    all_to_all x1, waiting for transfers between devices, local(): lax.all_to_all(spread, SEQ, 0, 0, tiled=True).reshape(size_z, -1, 128)  19.5 us
    all_to_all x1, blocking collectives, local(): grads = lax.all_to_all(grads, 'chan', 0, 0, tiled=True)  16.2 us
    ppermute x2, starting transfers between devices, transposed(): return lax.ppermute(value, ('seq_0', 'chan'), pairs)  15.5 us
    all_to_all x1, starting transfers between devices, local(): lax.all_to_all(spread, SEQ, 0, 0, tiled=True).reshape(size_z, -1, 128)  12.7 us
    ppermute x2, waiting for transfers between devices, transposed(): return lax.ppermute(value, ('seq_0', 'chan'), pairs)  7.42 us
    all_to_all x1, waiting for transfers between devices, local(): states = lax.all_to_all(state, CHIPS, 0, 0, tiled=True)  6.97 us
  transfers between devices with their start and end apart: 7, of which 4 were waited for; matrix products, arithmetic and copies ran while one was open for 1% of the time, Pallas kernels for 3%

profile of v14, /device:TPU:6, one launch (start us, length us, event | category | flops | bytes accessed | tf_op | source)
XLA Modules:
  0.0 175.5 jit_solution(11156138907099395864)
XLA Ops:
  0.7 1.0 shard_map.86
  1.7 10.9 %collective-permute-start.2 = (bf16[2,32,128]{2,1,0:T(8,128)(2,1)S(1)}, bf16[2,32,128]{2,1,0:T(8,128)(2,1)S(1)}, u32[]{:S(2)}, u32[]{:S(2)}) collective-permute-start(bf16[2,32,128]{2,1,0:T(8,128)(2,1)S(1)} %shard_map.86), channel_id=1, source_target_pairs={{0,320},{1,128},{2,0},{3,384},{64,256},{65,192},{66,64},{67,448},{... | collective-permute-start | bytes 49160 | tf_op jit(solution)/shard_map/ppermute | solution.py:295
  12.6 1.7 collective-permute-done.2.piece_ref
  14.3 1.1 shard_map.87
  15.4 12.7 %all-to-all-start = ((bf16[128,32,128]{2,1,0:T(8,128)(2,1)}), bf16[128,32,128]{2,1,0:T(8,128)(2,1)S(1)}, u32[]{:S(2)}, u32[]{:S(2)}) async-start(bf16[128,32,128]{2,1,0:T(8,128)(2,1)} %shard_map.87), calls=%async_computation | async-start | bytes 2097152 | tf_op jit(solution)/shard_map/all_to_all | solution.py:305
  28.2 1.9 %collective-permute-start.3 = (bf16[512,64]{1,0:T(8,128)(2,1)S(1)}, bf16[512,64]{1,0:T(8,128)(2,1)S(1)}, u32[]{:S(2)}, u32[]{:S(2)}) collective-permute-start(bf16[512,64]{1,0:T(8,128)(2,1)S(1)} %copy.12.own_ref), channel_id=1, source_target_pairs={{0,4},{4,0},{1,5},{5,1},{2,6},{6,2},{3,7},{7,3},{8,12},{12,8},{9,1... | collective-permute-start | bytes 196616 | tf_op jit(solution)/shard_map/ppermute | solution.py:298
  30.2 2.4 %collective-permute-start = (bf16[512,1024]{1,0:T(8,128)(2,1)S(1)}, bf16[512,1024]{1,0:T(8,128)(2,1)}, u32[]{:S(2)}, u32[]{:S(2)}) collective-permute-start(bf16[512,1024]{1,0:T(8,128)(2,1)S(1)} %copy-done.2), channel_id=1, source_target_pairs={{0,4},{4,0},{1,5},{5,1},{2,6},{6,2},{3,7},{7,3},{8,12},{12,8},{9,1... | collective-permute-start | bytes 3145736 | tf_op jit(solution)/shard_map/ppermute | solution.py:298
  32.6 1.9 %collective-permute-start.1 = (bf16[512,1024]{1,0:T(8,128)(2,1)S(1)}, bf16[512,1024]{1,0:T(8,128)(2,1)}, u32[]{:S(2)}, u32[]{:S(2)}) collective-permute-start(bf16[512,1024]{1,0:T(8,128)(2,1)S(1)} %copy-done.3), channel_id=1, source_target_pairs={{0,4},{4,0},{1,5},{5,1},{2,6},{6,2},{3,7},{7,3},{8,12},{12,8},{9,1... | collective-permute-start | bytes 3145736 | tf_op jit(solution)/shard_map/ppermute | solution.py:298
  38.8 19.5 %all-to-all-done = bf16[128,32,128]{2,1,0:T(8,128)(2,1)S(1)} async-done(((bf16[128,32,128]{2,1,0:T(8,128)(2,1)}), bf16[128,32,128]{2,1,0:T(8,128)(2,1)S(1)}, u32[]{:S(2)}, u32[]{:S(2)}) %all-to-all-start) | async-done | bytes 1048608 | tf_op jit(solution)/shard_map/all_to_all | solution.py:305
  58.4 4.1 %shard_map.89 = (bf16[4,1280,128]{2,1,0:T(8,128)(2,1)S(1)}, f32[1024,128]{1,0:T(8,128)S(1)}) custom-call(s32[2]{0:T(128)S(1)} %pad_add_fusion.at_ref, bf16[512,1024]{1,0:T(8,128)(2,1)S(1)} %copy-done.2, bf16[512,1024]{1,0:T(8,128)(2,1)} %collective-permute-done.other_t.b_ref, bf16[512,1024]{1,0:T(8,128)(2,1)S(1)} %copy-done.3, ...), custom_call_target="tpu_custom_call" | custom-call | flops 2147483648 | bytes 8388608 | tf_op jit(solution)/shard_map/pallas_call | solution.py:342
  62.5 21.9 %all_to_all.30.part_ref = bf16[4,1280,128]{2,1,0:T(8,128)(2,1)S(1)} all-to-all(bf16[4,1280,128]{2,1,0:T(8,128)(2,1)S(1)} %get-tuple-element.25), channel_id=1, replica_groups=mesh['seq_0'=8,'seq_1'=8,'seq_2'=2,'chan'=4] {'chan'}, dimensions={0} | all-to-all | bytes 2621440 | tf_op jit(solution)/shard_map/all_to_all | solution.py:345
  84.4 2.2 %shard_map.90 = (f32[512,128]{1,0:T(8,128)S(1)}, f32[512,128]{1,0:T(8,128)S(1)}, f32[128,128]{1,0:T(8,128)S(1)}, f32[64,4,128]{2,1,0:T(4,128)}) custom-call(s32[2]{0:T(128)S(1)} %pad_add_fusion.at_ref, bf16[4,1280,128]{2,1,0:T(8,128)(2,1)S(1)} %all_to_all.30.part_ref, f32[1024,128]{1,0:T(8,128)S(1)} %get-tuple-element.26.own_ref, ...), custom_call_target="tpu_custom_call" | custom-call | tf_op jit(solution)/shard_map/pallas_call | solution.py:359
  86.5 5.6 %all-to-all-start.2 = ((f32[64,4,128]{2,1,0:T(4,128)}), f32[64,4,128]{2,1,0:T(4,128)S(1)}, u32[]{:S(2)}, u32[]{:S(2)}) async-start(f32[64,4,128]{2,1,0:T(4,128)} %get-tuple-element.29), calls=%async_computation.2 | async-start | bytes 262144 | tf_op jit(solution)/shard_map/all_to_all | solution.py:367
  92.1 2.2 %shard_map.91.tt_ref = bf16[1024,1024]{1,0:T(8,128)(2,1)S(1)} custom-call(bf16[512,1024]{1,0:T(8,128)(2,1)} %a_ref, bf16[512,1024]{1,0:T(8,128)(2,1)} %collective-permute-done.other_t.b_ref), custom_call_target="tpu_custom_call" | custom-call | bytes 4194304 | tf_op jit(solution)/shard_map/pallas_call | solution.py:365
  94.3 2.2 %shard_map.92.gt_ref = bf16[1024,1024]{1,0:T(8,128)(2,1)S(1)} custom-call(bf16[512,1024]{1,0:T(8,128)(2,1)} %a_ref.1, bf16[512,1024]{1,0:T(8,128)(2,1)} %collective-permute-done.1.other_g.b_ref), custom_call_target="tpu_custom_call" | custom-call | bytes 4194304 | tf_op jit(solution)/shard_map/pallas_call | solution.py:366
  96.5 1.3 copy-done
  97.8 7.0 %all-to-all-done.2.states_ref = f32[64,4,128]{2,1,0:T(4,128)S(1)} async-done(((f32[64,4,128]{2,1,0:T(4,128)}), f32[64,4,128]{2,1,0:T(4,128)S(1)}, u32[]{:S(2)}, u32[]{:S(2)}) %all-to-all-start.2) | async-done | bytes 131104 | tf_op jit(solution)/shard_map/all_to_all | solution.py:367
  104.8 2.2 %shard_map.93 = bf16[4,1024,128]{2,1,0:T(8,128)(2,1)S(1)} custom-call(s32[2]{0:T(128)S(1)} %pad_add_fusion.at_ref, f32[512,128]{1,0:T(8,128)S(1)} %get-tuple-element.37.x_ref, f32[512,128]{1,0:T(8,128)S(1)} %get-tuple-element.38.late_ref, f32[128,128]{1,0:T(8,128)S(1)} %get-tuple-element.30.left_ref, f32[64,4,128]{2,1,0:T(4,128)S(1)} %all-to-all-done.2.states_ref, ...), custom_call_target="tpu_custom_call" | custom-call | tf_op jit(solution)/shard_map/pallas_call | solution.py:376
  107.0 16.2 %all_to_all.31.grads_ref = bf16[4,1024,128]{2,1,0:T(8,128)(2,1)S(1)} all-to-all(bf16[4,1024,128]{2,1,0:T(8,128)(2,1)S(1)} %shard_map.93), channel_id=1, replica_groups=mesh['seq_0'=8,'seq_1'=8,'seq_2'=2,'chan'=4] {'chan'}, dimensions={0} | all-to-all | bytes 2097152 | tf_op jit(solution)/shard_map/all_to_all | solution.py:377
  123.2 2.9 %shard_map.94 = bf16[8,512,128]{2,1,0:T(8,128)(2,1)S(1)} custom-call(s32[2]{0:T(128)S(1)} %pad_add_fusion.at_ref, bf16[1024,1024]{1,0:T(8,128)(2,1)S(1)} %shard_map.91.tt_ref, bf16[1024,1024]{1,0:T(8,128)(2,1)S(1)} %copy-done.1, bf16[4,1024,128]{2,1,0:T(8,128)(2,1)S(1)} %all_to_all.31.grads_ref), custom_call_target="tpu_custom_call" | custom-call | flops 2147483648 | bytes 8388608 | tf_op jit(solution)/shard_map/pallas_call | solution.py:387
  126.1 34.3 %all_to_all.32.part_ref = bf16[64,64,128]{2,1,0:T(8,128)(2,1)S(1)} all-to-all(bf16[64,64,128]{2,1,0:T(8,128)(2,1)S(1)} %bitcast.17), channel_id=1, replica_groups=mesh['seq_0'=8,'seq_1'=8,'seq_2'=2,'chan'=4] {'seq_0','seq_1'}, dimensions={0} | all-to-all | bytes 2097152 | tf_op jit(solution)/shard_map/all_to_all | solution.py:388
  160.7 3.7 %all_to_all.33 = f32[2,32,128]{2,1,0:T(8,128)S(1)} all-to-all(f32[2,32,128]{2,1,0:T(8,128)S(1)} %shard_map.95), channel_id=1, replica_groups=mesh['seq_0'=8,'seq_1'=8,'seq_2'=2,'chan'=4] {'seq_2'}, dimensions={0} | all-to-all | bytes 65536 | tf_op jit(solution)/shard_map/all_to_all | solution.py:390
  164.4 4.6 %collective-permute-start.4 = (f32[2,32,128]{2,1,0:T(8,128)S(1)}, f32[2,32,128]{2,1,0:T(8,128)S(1)}, u32[]{:S(2)}, u32[]{:S(2)}) collective-permute-start(f32[2,32,128]{2,1,0:T(8,128)S(1)} %all_to_all.33), channel_id=1, source_target_pairs={{320,0},{128,1},{0,2},{384,3},{256,64},{192,65},{64,66},{448,67},{... | collective-permute-start | bytes 98312 | tf_op jit(solution)/shard_map/ppermute | solution.py:295
  169.0 5.7 %collective-permute-done.4.part_ref = f32[2,32,128]{2,1,0:T(8,128)S(1)} collective-permute-done((f32[2,32,128]{2,1,0:T(8,128)S(1)}, f32[2,32,128]{2,1,0:T(8,128)S(1)}, u32[]{:S(2)}, u32[]{:S(2)}) %collective-permute-start.4) | collective-permute-done | bytes 32800 | tf_op jit(solution)/shard_map/ppermute | solution.py:295
  (46 shorter events, 5.3 us)
Async XLA Ops:
  0.6 27.5 %copy-start.7 = (bf16[512,64]{0,1:T(8,128)(2,1)S(1)}, bf16[512,64]{0,1:T(8,128)(2,1)}, u32[]{:S(2)}) copy-start(bf16[512,64]{0,1:T(8,128)(2,1)} %param.11) | copy-start | bytes 196612
  0.6 29.5 %copy-start.2 = (bf16[512,1024]{1,0:T(8,128)(2,1)S(1)}, bf16[512,1024]{1,0:T(8,128)(2,1)}, u32[]{:S(2)}) copy-start(bf16[512,1024]{1,0:T(8,128)(2,1)} %a_ref) | copy-start | bytes 3145732
  0.7 31.9 %copy-start.3 = (bf16[512,1024]{1,0:T(8,128)(2,1)S(1)}, bf16[512,1024]{1,0:T(8,128)(2,1)}, u32[]{:S(2)}) copy-start(bf16[512,1024]{1,0:T(8,128)(2,1)} %a_ref.1) | copy-start | bytes 3145732
  0.7 34.0 %copy-start.9 = (f32[16,32]{1,0:T(8,128)S(1)}, f32[16,32]{1,0:T(8,128)}, u32[]{:S(2)}) copy-start(f32[16,32]{1,0:T(8,128)} %param.13) | copy-start | bytes 6148
  0.7 34.0 %copy-start.8 = (f32[16,32]{1,0:T(8,128)S(1)}, f32[16,32]{1,0:T(8,128)}, u32[]{:S(2)}) copy-start(f32[16,32]{1,0:T(8,128)} %param.12) | copy-start | bytes 6148
  1.7 12.6 %collective-permute-start.2 = (bf16[2,32,128]{2,1,0:T(8,128)(2,1)S(1)}, bf16[2,32,128]{2,1,0:T(8,128)(2,1)S(1)}, u32[]{:S(2)}, u32[]{:S(2)}) collective-permute-start(bf16[2,32,128]{2,1,0:T(8,128)(2,1)S(1)} %shard_map.86), channel_id=1, source_target_pairs={{0,320},{1,128},{2,0},{3,384},{64,256},{65,192},{66,64},{67,448},{... | collective-permute-start | bytes 49160 | tf_op jit(solution)/shard_map/ppermute | solution.py:295
  15.4 43.0 %all-to-all-start = ((bf16[128,32,128]{2,1,0:T(8,128)(2,1)}), bf16[128,32,128]{2,1,0:T(8,128)(2,1)S(1)}, u32[]{:S(2)}, u32[]{:S(2)}) async-start(bf16[128,32,128]{2,1,0:T(8,128)(2,1)} %shard_map.87), calls=%async_computation | async-start | bytes 2097152 | tf_op jit(solution)/shard_map/all_to_all | solution.py:305
  28.2 8.3 %collective-permute-start.3 = (bf16[512,64]{1,0:T(8,128)(2,1)S(1)}, bf16[512,64]{1,0:T(8,128)(2,1)S(1)}, u32[]{:S(2)}, u32[]{:S(2)}) collective-permute-start(bf16[512,64]{1,0:T(8,128)(2,1)S(1)} %copy.12.own_ref), channel_id=1, source_target_pairs={{0,4},{4,0},{1,5},{5,1},{2,6},{6,2},{3,7},{7,3},{8,12},{12,8},{9,1... | collective-permute-start | bytes 196616 | tf_op jit(solution)/shard_map/ppermute | solution.py:298
  30.2 28.2 %collective-permute-start = (bf16[512,1024]{1,0:T(8,128)(2,1)S(1)}, bf16[512,1024]{1,0:T(8,128)(2,1)}, u32[]{:S(2)}, u32[]{:S(2)}) collective-permute-start(bf16[512,1024]{1,0:T(8,128)(2,1)S(1)} %copy-done.2), channel_id=1, source_target_pairs={{0,4},{4,0},{1,5},{5,1},{2,6},{6,2},{3,7},{7,3},{8,12},{12,8},{9,1... | collective-permute-start | bytes 3145736 | tf_op jit(solution)/shard_map/ppermute | solution.py:298
  32.6 25.8 %collective-permute-start.1 = (bf16[512,1024]{1,0:T(8,128)(2,1)S(1)}, bf16[512,1024]{1,0:T(8,128)(2,1)}, u32[]{:S(2)}, u32[]{:S(2)}) collective-permute-start(bf16[512,1024]{1,0:T(8,128)(2,1)S(1)} %copy-done.3), channel_id=1, source_target_pairs={{0,4},{4,0},{1,5},{5,1},{2,6},{6,2},{3,7},{7,3},{8,12},{12,8},{9,1... | collective-permute-start | bytes 3145736 | tf_op jit(solution)/shard_map/ppermute | solution.py:298
  36.5 0.6 copy-start.5
  37.2 0.9 copy-start.6
  86.5 18.3 %all-to-all-start.2 = ((f32[64,4,128]{2,1,0:T(4,128)}), f32[64,4,128]{2,1,0:T(4,128)S(1)}, u32[]{:S(2)}, u32[]{:S(2)}) async-start(f32[64,4,128]{2,1,0:T(4,128)} %get-tuple-element.29), calls=%async_computation.2 | async-start | bytes 262144 | tf_op jit(solution)/shard_map/all_to_all | solution.py:367
  94.3 10.5 %copy-start.4 = (f32[128,128]{1,0:T(8,128)S(1)}, f32[128,128]{1,0:T(8,128)}, u32[]{:S(2)}) copy-start(f32[128,128]{1,0:T(8,128)} %fusion.power_ref) | copy-start | bytes 196612
  96.5 1.3 copy-start
  104.8 18.4 %copy-start.1 = (bf16[1024,1024]{1,0:T(8,128)(2,1)S(1)}, bf16[1024,1024]{1,0:T(8,128)(2,1)}, u32[]{:S(2)}) copy-start(bf16[1024,1024]{1,0:T(8,128)(2,1)} %copy-done) | copy-start | bytes 6291460
  164.4 10.4 %collective-permute-start.4 = (f32[2,32,128]{2,1,0:T(8,128)S(1)}, f32[2,32,128]{2,1,0:T(8,128)S(1)}, u32[]{:S(2)}, u32[]{:S(2)}) collective-permute-start(f32[2,32,128]{2,1,0:T(8,128)S(1)} %all_to_all.33), channel_id=1, source_target_pairs={{320,0},{128,1},{0,2},{384,3},{256,64},{192,65},{64,66},{448,67},{... | collective-permute-start | bytes 98312 | tf_op jit(solution)/shard_map/ppermute | solution.py:295

commit v15 on v14

--- a/solution.py
+++ b/solution.py
@@ -192,7 +192,7 @@
         )
 
     zero = jnp.zeros((per, 128), F32)
-    held = lax.fori_loop(0, STEPS, step, (zero,) * (2 * MODE_ROWS), unroll=16)
+    held = lax.fori_loop(0, STEPS, step, (zero,) * (2 * MODE_ROWS), unroll=8)
     for m in range(MODE_ROWS):
         for h in range(2):
             st[m * chunks + h * per : m * chunks + (h + 1) * per, :] = held[2 * m + h]
@@ -237,7 +237,7 @@
             new.append(states)
         return tuple(new[h][m] for m in range(MODE_ROWS) for h in range(2))
 
-    lax.fori_loop(0, STEPS, step, tuple(begin), unroll=16)
+    lax.fori_loop(0, STEPS, step, tuple(begin), unroll=8)
     y = ys[...]
     y = y + turn(y, 64)
     y = y + turn(y, 32)

time: 176 us -> 176 us (level)
  no operation moved by 1% of the time
where the time goes in v15:
time: 176 us
  blocking collectives  76.2 us (43%)
  starting transfers between devices  40 us (23%)
  waiting for transfers between devices  33.9 us (19%)
  Pallas kernels  19.6 us (11%)
  local copies, waits for them, and re-layouts  3.84 us (2%)
    all_to_all x1, blocking collectives, local(): partial = lax.all_to_all(partial, CHIPS, 0, 0, tiled=True)  34.4 us
    all_to_all x1, blocking collectives, local(): parts = lax.all_to_all(parts, 'chan', 0, 0, tiled=True)  21.9 us
    all_to_all x1, waiting for transfers between devices, local(): lax.all_to_all(spread, SEQ, 0, 0, tiled=True).reshape(size_z, -1, 128)  19.5 us
    all_to_all x1, blocking collectives, local(): grads = lax.all_to_all(grads, 'chan', 0, 0, tiled=True)  16.2 us
    ppermute x2, starting transfers between devices, transposed(): return lax.ppermute(value, ('seq_0', 'chan'), pairs)  15.5 us
    all_to_all x1, starting transfers between devices, local(): lax.all_to_all(spread, SEQ, 0, 0, tiled=True).reshape(size_z, -1, 128)  12.7 us
    ppermute x2, waiting for transfers between devices, transposed(): return lax.ppermute(value, ('seq_0', 'chan'), pairs)  7.42 us
    all_to_all x1, waiting for transfers between devices, local(): states = lax.all_to_all(state, CHIPS, 0, 0, tiled=True)  6.97 us
  transfers between devices with their start and end apart: 7, of which 4 were waited for; matrix products, arithmetic and copies ran while one was open for 1% of the time, Pallas kernels for 3%

profile of v15, /device:TPU:6, one launch (start us, length us, event | category | flops | bytes accessed | tf_op | source)
XLA Modules:
  0.0 175.5 jit_solution(3844017483045945779)
XLA Ops:
  0.7 1.0 shard_map.86
  1.7 10.9 %collective-permute-start.2 = (bf16[2,32,128]{2,1,0:T(8,128)(2,1)S(1)}, bf16[2,32,128]{2,1,0:T(8,128)(2,1)S(1)}, u32[]{:S(2)}, u32[]{:S(2)}) collective-permute-start(bf16[2,32,128]{2,1,0:T(8,128)(2,1)S(1)} %shard_map.86), channel_id=1, source_target_pairs={{0,320},{1,128},{2,0},{3,384},{64,256},{65,192},{66,64},{67,448},{... | collective-permute-start | bytes 49160 | tf_op jit(solution)/shard_map/ppermute | solution.py:295
  12.6 1.7 collective-permute-done.2.piece_ref
  14.3 1.1 shard_map.87
  15.4 12.7 %all-to-all-start = ((bf16[128,32,128]{2,1,0:T(8,128)(2,1)}), bf16[128,32,128]{2,1,0:T(8,128)(2,1)S(1)}, u32[]{:S(2)}, u32[]{:S(2)}) async-start(bf16[128,32,128]{2,1,0:T(8,128)(2,1)} %shard_map.87), calls=%async_computation | async-start | bytes 2097152 | tf_op jit(solution)/shard_map/all_to_all | solution.py:305
  28.2 1.9 %collective-permute-start.3 = (bf16[512,64]{1,0:T(8,128)(2,1)S(1)}, bf16[512,64]{1,0:T(8,128)(2,1)S(1)}, u32[]{:S(2)}, u32[]{:S(2)}) collective-permute-start(bf16[512,64]{1,0:T(8,128)(2,1)S(1)} %copy.12.own_ref), channel_id=1, source_target_pairs={{0,4},{4,0},{1,5},{5,1},{2,6},{6,2},{3,7},{7,3},{8,12},{12,8},{9,1... | collective-permute-start | bytes 196616 | tf_op jit(solution)/shard_map/ppermute | solution.py:298
  30.2 2.4 %collective-permute-start = (bf16[512,1024]{1,0:T(8,128)(2,1)S(1)}, bf16[512,1024]{1,0:T(8,128)(2,1)}, u32[]{:S(2)}, u32[]{:S(2)}) collective-permute-start(bf16[512,1024]{1,0:T(8,128)(2,1)S(1)} %copy-done.2), channel_id=1, source_target_pairs={{0,4},{4,0},{1,5},{5,1},{2,6},{6,2},{3,7},{7,3},{8,12},{12,8},{9,1... | collective-permute-start | bytes 3145736 | tf_op jit(solution)/shard_map/ppermute | solution.py:298
  32.6 1.9 %collective-permute-start.1 = (bf16[512,1024]{1,0:T(8,128)(2,1)S(1)}, bf16[512,1024]{1,0:T(8,128)(2,1)}, u32[]{:S(2)}, u32[]{:S(2)}) collective-permute-start(bf16[512,1024]{1,0:T(8,128)(2,1)S(1)} %copy-done.3), channel_id=1, source_target_pairs={{0,4},{4,0},{1,5},{5,1},{2,6},{6,2},{3,7},{7,3},{8,12},{12,8},{9,1... | collective-permute-start | bytes 3145736 | tf_op jit(solution)/shard_map/ppermute | solution.py:298
  38.8 19.5 %all-to-all-done = bf16[128,32,128]{2,1,0:T(8,128)(2,1)S(1)} async-done(((bf16[128,32,128]{2,1,0:T(8,128)(2,1)}), bf16[128,32,128]{2,1,0:T(8,128)(2,1)S(1)}, u32[]{:S(2)}, u32[]{:S(2)}) %all-to-all-start) | async-done | bytes 1048608 | tf_op jit(solution)/shard_map/all_to_all | solution.py:305
  58.4 4.1 %shard_map.89 = (bf16[4,1280,128]{2,1,0:T(8,128)(2,1)S(1)}, f32[1024,128]{1,0:T(8,128)S(1)}) custom-call(s32[2]{0:T(128)S(1)} %pad_add_fusion.at_ref, bf16[512,1024]{1,0:T(8,128)(2,1)S(1)} %copy-done.2, bf16[512,1024]{1,0:T(8,128)(2,1)} %collective-permute-done.other_t.b_ref, bf16[512,1024]{1,0:T(8,128)(2,1)S(1)} %copy-done.3, ...), custom_call_target="tpu_custom_call" | custom-call | flops 2147483648 | bytes 8388608 | tf_op jit(solution)/shard_map/pallas_call | solution.py:342
  62.5 21.9 %all_to_all.30.part_ref = bf16[4,1280,128]{2,1,0:T(8,128)(2,1)S(1)} all-to-all(bf16[4,1280,128]{2,1,0:T(8,128)(2,1)S(1)} %get-tuple-element.25), channel_id=1, replica_groups=mesh['seq_0'=8,'seq_1'=8,'seq_2'=2,'chan'=4] {'chan'}, dimensions={0} | all-to-all | bytes 2621440 | tf_op jit(solution)/shard_map/all_to_all | solution.py:345
  84.4 2.2 %shard_map.90 = (f32[512,128]{1,0:T(8,128)S(1)}, f32[512,128]{1,0:T(8,128)S(1)}, f32[128,128]{1,0:T(8,128)S(1)}, f32[64,4,128]{2,1,0:T(4,128)}) custom-call(s32[2]{0:T(128)S(1)} %pad_add_fusion.at_ref, bf16[4,1280,128]{2,1,0:T(8,128)(2,1)S(1)} %all_to_all.30.part_ref, f32[1024,128]{1,0:T(8,128)S(1)} %get-tuple-element.26.own_ref, ...), custom_call_target="tpu_custom_call" | custom-call | tf_op jit(solution)/shard_map/pallas_call | solution.py:359
  86.5 5.6 %all-to-all-start.2 = ((f32[64,4,128]{2,1,0:T(4,128)}), f32[64,4,128]{2,1,0:T(4,128)S(1)}, u32[]{:S(2)}, u32[]{:S(2)}) async-start(f32[64,4,128]{2,1,0:T(4,128)} %get-tuple-element.29), calls=%async_computation.2 | async-start | bytes 262144 | tf_op jit(solution)/shard_map/all_to_all | solution.py:367
  92.1 2.2 %shard_map.91.tt_ref = bf16[1024,1024]{1,0:T(8,128)(2,1)S(1)} custom-call(bf16[512,1024]{1,0:T(8,128)(2,1)} %a_ref, bf16[512,1024]{1,0:T(8,128)(2,1)} %collective-permute-done.other_t.b_ref), custom_call_target="tpu_custom_call" | custom-call | bytes 4194304 | tf_op jit(solution)/shard_map/pallas_call | solution.py:365
  94.3 2.2 %shard_map.92.gt_ref = bf16[1024,1024]{1,0:T(8,128)(2,1)S(1)} custom-call(bf16[512,1024]{1,0:T(8,128)(2,1)} %a_ref.1, bf16[512,1024]{1,0:T(8,128)(2,1)} %collective-permute-done.1.other_g.b_ref), custom_call_target="tpu_custom_call" | custom-call | bytes 4194304 | tf_op jit(solution)/shard_map/pallas_call | solution.py:366
  96.5 1.3 copy-done
  97.8 7.0 %all-to-all-done.2.states_ref = f32[64,4,128]{2,1,0:T(4,128)S(1)} async-done(((f32[64,4,128]{2,1,0:T(4,128)}), f32[64,4,128]{2,1,0:T(4,128)S(1)}, u32[]{:S(2)}, u32[]{:S(2)}) %all-to-all-start.2) | async-done | bytes 131104 | tf_op jit(solution)/shard_map/all_to_all | solution.py:367
  104.8 2.2 %shard_map.93 = bf16[4,1024,128]{2,1,0:T(8,128)(2,1)S(1)} custom-call(s32[2]{0:T(128)S(1)} %pad_add_fusion.at_ref, f32[512,128]{1,0:T(8,128)S(1)} %get-tuple-element.37.x_ref, f32[512,128]{1,0:T(8,128)S(1)} %get-tuple-element.38.late_ref, f32[128,128]{1,0:T(8,128)S(1)} %get-tuple-element.30.left_ref, f32[64,4,128]{2,1,0:T(4,128)S(1)} %all-to-all-done.2.states_ref, ...), custom_call_target="tpu_custom_call" | custom-call | tf_op jit(solution)/shard_map/pallas_call | solution.py:376
  107.0 16.2 %all_to_all.31.grads_ref = bf16[4,1024,128]{2,1,0:T(8,128)(2,1)S(1)} all-to-all(bf16[4,1024,128]{2,1,0:T(8,128)(2,1)S(1)} %shard_map.93), channel_id=1, replica_groups=mesh['seq_0'=8,'seq_1'=8,'seq_2'=2,'chan'=4] {'chan'}, dimensions={0} | all-to-all | bytes 2097152 | tf_op jit(solution)/shard_map/all_to_all | solution.py:377
  123.3 2.9 %shard_map.94 = bf16[8,512,128]{2,1,0:T(8,128)(2,1)S(1)} custom-call(s32[2]{0:T(128)S(1)} %pad_add_fusion.at_ref, bf16[1024,1024]{1,0:T(8,128)(2,1)S(1)} %shard_map.91.tt_ref, bf16[1024,1024]{1,0:T(8,128)(2,1)S(1)} %copy-done.1, bf16[4,1024,128]{2,1,0:T(8,128)(2,1)S(1)} %all_to_all.31.grads_ref), custom_call_target="tpu_custom_call" | custom-call | flops 2147483648 | bytes 8388608 | tf_op jit(solution)/shard_map/pallas_call | solution.py:387
  126.2 34.4 %all_to_all.32.part_ref = bf16[64,64,128]{2,1,0:T(8,128)(2,1)S(1)} all-to-all(bf16[64,64,128]{2,1,0:T(8,128)(2,1)S(1)} %bitcast.17), channel_id=1, replica_groups=mesh['seq_0'=8,'seq_1'=8,'seq_2'=2,'chan'=4] {'seq_0','seq_1'}, dimensions={0} | all-to-all | bytes 2097152 | tf_op jit(solution)/shard_map/all_to_all | solution.py:388
  160.7 3.7 %all_to_all.33 = f32[2,32,128]{2,1,0:T(8,128)S(1)} all-to-all(f32[2,32,128]{2,1,0:T(8,128)S(1)} %shard_map.95), channel_id=1, replica_groups=mesh['seq_0'=8,'seq_1'=8,'seq_2'=2,'chan'=4] {'seq_2'}, dimensions={0} | all-to-all | bytes 65536 | tf_op jit(solution)/shard_map/all_to_all | solution.py:390
  164.4 4.6 %collective-permute-start.4 = (f32[2,32,128]{2,1,0:T(8,128)S(1)}, f32[2,32,128]{2,1,0:T(8,128)S(1)}, u32[]{:S(2)}, u32[]{:S(2)}) collective-permute-start(f32[2,32,128]{2,1,0:T(8,128)S(1)} %all_to_all.33), channel_id=1, source_target_pairs={{320,0},{128,1},{0,2},{384,3},{256,64},{192,65},{64,66},{448,67},{... | collective-permute-start | bytes 98312 | tf_op jit(solution)/shard_map/ppermute | solution.py:295
  169.1 5.7 %collective-permute-done.4.part_ref = f32[2,32,128]{2,1,0:T(8,128)S(1)} collective-permute-done((f32[2,32,128]{2,1,0:T(8,128)S(1)}, f32[2,32,128]{2,1,0:T(8,128)S(1)}, u32[]{:S(2)}, u32[]{:S(2)}) %collective-permute-start.4) | collective-permute-done | bytes 32800 | tf_op jit(solution)/shard_map/ppermute | solution.py:295
  (46 shorter events, 5.3 us)
Async XLA Ops:
  0.6 27.5 %copy-start.7 = (bf16[512,64]{0,1:T(8,128)(2,1)S(1)}, bf16[512,64]{0,1:T(8,128)(2,1)}, u32[]{:S(2)}) copy-start(bf16[512,64]{0,1:T(8,128)(2,1)} %param.11) | copy-start | bytes 196612
  0.6 29.5 %copy-start.2 = (bf16[512,1024]{1,0:T(8,128)(2,1)S(1)}, bf16[512,1024]{1,0:T(8,128)(2,1)}, u32[]{:S(2)}) copy-start(bf16[512,1024]{1,0:T(8,128)(2,1)} %a_ref) | copy-start | bytes 3145732
  0.7 31.9 %copy-start.3 = (bf16[512,1024]{1,0:T(8,128)(2,1)S(1)}, bf16[512,1024]{1,0:T(8,128)(2,1)}, u32[]{:S(2)}) copy-start(bf16[512,1024]{1,0:T(8,128)(2,1)} %a_ref.1) | copy-start | bytes 3145732
  0.7 34.0 %copy-start.9 = (f32[16,32]{1,0:T(8,128)S(1)}, f32[16,32]{1,0:T(8,128)}, u32[]{:S(2)}) copy-start(f32[16,32]{1,0:T(8,128)} %param.13) | copy-start | bytes 6148
  0.7 34.0 %copy-start.8 = (f32[16,32]{1,0:T(8,128)S(1)}, f32[16,32]{1,0:T(8,128)}, u32[]{:S(2)}) copy-start(f32[16,32]{1,0:T(8,128)} %param.12) | copy-start | bytes 6148
  1.7 12.6 %collective-permute-start.2 = (bf16[2,32,128]{2,1,0:T(8,128)(2,1)S(1)}, bf16[2,32,128]{2,1,0:T(8,128)(2,1)S(1)}, u32[]{:S(2)}, u32[]{:S(2)}) collective-permute-start(bf16[2,32,128]{2,1,0:T(8,128)(2,1)S(1)} %shard_map.86), channel_id=1, source_target_pairs={{0,320},{1,128},{2,0},{3,384},{64,256},{65,192},{66,64},{67,448},{... | collective-permute-start | bytes 49160 | tf_op jit(solution)/shard_map/ppermute | solution.py:295
  15.4 43.0 %all-to-all-start = ((bf16[128,32,128]{2,1,0:T(8,128)(2,1)}), bf16[128,32,128]{2,1,0:T(8,128)(2,1)S(1)}, u32[]{:S(2)}, u32[]{:S(2)}) async-start(bf16[128,32,128]{2,1,0:T(8,128)(2,1)} %shard_map.87), calls=%async_computation | async-start | bytes 2097152 | tf_op jit(solution)/shard_map/all_to_all | solution.py:305
  28.2 8.3 %collective-permute-start.3 = (bf16[512,64]{1,0:T(8,128)(2,1)S(1)}, bf16[512,64]{1,0:T(8,128)(2,1)S(1)}, u32[]{:S(2)}, u32[]{:S(2)}) collective-permute-start(bf16[512,64]{1,0:T(8,128)(2,1)S(1)} %copy.12.own_ref), channel_id=1, source_target_pairs={{0,4},{4,0},{1,5},{5,1},{2,6},{6,2},{3,7},{7,3},{8,12},{12,8},{9,1... | collective-permute-start | bytes 196616 | tf_op jit(solution)/shard_map/ppermute | solution.py:298
  30.2 28.2 %collective-permute-start = (bf16[512,1024]{1,0:T(8,128)(2,1)S(1)}, bf16[512,1024]{1,0:T(8,128)(2,1)}, u32[]{:S(2)}, u32[]{:S(2)}) collective-permute-start(bf16[512,1024]{1,0:T(8,128)(2,1)S(1)} %copy-done.2), channel_id=1, source_target_pairs={{0,4},{4,0},{1,5},{5,1},{2,6},{6,2},{3,7},{7,3},{8,12},{12,8},{9,1... | collective-permute-start | bytes 3145736 | tf_op jit(solution)/shard_map/ppermute | solution.py:298
  32.6 25.8 %collective-permute-start.1 = (bf16[512,1024]{1,0:T(8,128)(2,1)S(1)}, bf16[512,1024]{1,0:T(8,128)(2,1)}, u32[]{:S(2)}, u32[]{:S(2)}) collective-permute-start(bf16[512,1024]{1,0:T(8,128)(2,1)S(1)} %copy-done.3), channel_id=1, source_target_pairs={{0,4},{4,0},{1,5},{5,1},{2,6},{6,2},{3,7},{7,3},{8,12},{12,8},{9,1... | collective-permute-start | bytes 3145736 | tf_op jit(solution)/shard_map/ppermute | solution.py:298
  36.5 0.6 copy-start.5
  37.2 0.9 copy-start.6
  86.5 18.3 %all-to-all-start.2 = ((f32[64,4,128]{2,1,0:T(4,128)}), f32[64,4,128]{2,1,0:T(4,128)S(1)}, u32[]{:S(2)}, u32[]{:S(2)}) async-start(f32[64,4,128]{2,1,0:T(4,128)} %get-tuple-element.29), calls=%async_computation.2 | async-start | bytes 262144 | tf_op jit(solution)/shard_map/all_to_all | solution.py:367
  94.3 10.5 %copy-start.4 = (f32[128,128]{1,0:T(8,128)S(1)}, f32[128,128]{1,0:T(8,128)}, u32[]{:S(2)}) copy-start(f32[128,128]{1,0:T(8,128)} %fusion.power_ref) | copy-start | bytes 196612
  96.5 1.3 copy-start
  104.8 18.5 %copy-start.1 = (bf16[1024,1024]{1,0:T(8,128)(2,1)S(1)}, bf16[1024,1024]{1,0:T(8,128)(2,1)}, u32[]{:S(2)}) copy-start(bf16[1024,1024]{1,0:T(8,128)(2,1)} %copy-done) | copy-start | bytes 6291460
  164.4 10.4 %collective-permute-start.4 = (f32[2,32,128]{2,1,0:T(8,128)S(1)}, f32[2,32,128]{2,1,0:T(8,128)S(1)}, u32[]{:S(2)}, u32[]{:S(2)}) collective-permute-start(f32[2,32,128]{2,1,0:T(8,128)S(1)} %all_to_all.33), channel_id=1, source_target_pairs={{320,0},{128,1},{0,2},{384,3},{256,64},{192,65},{64,66},{448,67},{... | collective-permute-start | bytes 98312 | tf_op jit(solution)/shard_map/ppermute | solution.py:295
